TPU v7x, 32 devices: a whole 2x2x4 slice. The times are simulated.
32 devices in a mesh: dp: 8 (over z, core), tensor: 4 (over y, x).
Axes of the slice: x: 2, y: 2, z: 4, core: 2. Of those that a mesh axis runs over, the one named last changes fastest.
Arguments:
- layer_input: bfloat16 [16384, 2048], P(('dp', 'tensor')), may hold values from -6 to 6
- cotangent: bfloat16 [16384, 2048], P(('dp', 'tensor')), may hold values from -6 to 6
- firstgain: bfloat16 [2048], P('dp'), may hold values from 0.5 to 1.5
- firstbias: bfloat16 [2048], P('dp'), may hold values from -1 to 1
- secondgain: bfloat16 [2048], P('dp'), may hold values from 0.5 to 1.5
- secondbias: bfloat16 [2048], P('dp'), may hold values from -1 to 1
- project: bfloat16 [2048, 8, 768], P('dp', 'tensor'), may hold values from -0.125 to 0.125
- projbias: bfloat16 [8, 768], P('tensor', 'dp'), may hold values from -3 to 3
- merging: bfloat16 [2048, 2048], P('tensor', 'dp'), may hold values from -1.5 to 1.5
- mergebias: bfloat16 [2048], P('dp'), may hold values from -2 to 2
- expand: bfloat16 [2048, 8192], P('dp', 'tensor'), may hold values from -0.125 to 0.125
- expandbias: bfloat16 [8192], P(('tensor', 'dp')), may hold values from -3 to 3
- shrink: bfloat16 [8192, 2048], P('tensor', 'dp'), may hold values from -0.0625 to 0.0625
- shrinkbias: bfloat16 [2048], P('dp'), may hold values from -2 to 2
Outputs:
- layer_output: bfloat16 [16384, 2048], P(('dp', 'tensor'))
- input_grad: float32 [16384, 2048], P(('dp', 'tensor'))
- firstgain_grad: float32 [2048], P('dp')
- firstbias_grad: float32 [2048], P('dp')
- secondgain_grad: float32 [2048], P('dp')
- secondbias_grad: float32 [2048], P('dp')
- project_grad: float32 [2048, 8, 768], P('dp', 'tensor')
- projbias_grad: float32 [8, 768], P('tensor', 'dp')
- merging_grad: float32 [2048, 2048], P('tensor', 'dp')
- mergebias_grad: float32 [2048], P('dp')
- expand_grad: float32 [2048, 8192], P('dp', 'tensor')
- expandbias_grad: float32 [8192], P(('tensor', 'dp'))
- shrink_grad: float32 [8192, 2048], P('tensor', 'dp')
- shrinkbias_grad: float32 [2048], P('dp')
All inputs are finite; a program needn't handle non-finite values.
Results may differ from a plain program's by a relative error of at most 0.015.
Values may be sent and summed in bfloat16 or wider, within the bound.
No kernel may reach another device: no remote copies, remote signals or barrier semaphores. Data moves between devices by JAX's collectives and lax.ppermute only.
A program may use at most 256 MiB of HBM per device.

v0:
```python
from functools import partial

import jax
import jax.numpy as jnp
from jax import lax
from jax.sharding import PartitionSpec as P

HEAD_DIM = 256
ROTARY = 64
LENGTH = 2048
QBLOCK = 512


epsilon = 1e-05


def normalize(row_data, gain_vec, shift_vec):
    centre = row_data - jnp.mean(row_data, axis=-1, keepdims=True)
    spread = jnp.mean(centre * centre, axis=-1, keepdims=True)
    return centre * lax.rsqrt(spread + epsilon) * gain_vec + shift_vec


def norm_backward(row_data, gain_vec, shift_vec, upstream):
    unused, pullback = jax.vjp(normalize, row_data, gain_vec, shift_vec)
    return pullback(upstream)


def rotary_tables(length, rotary):
    position = jnp.arange(length, dtype=jnp.float32)
    frequency = 10000.0 ** (-jnp.arange(0, rotary, 2, dtype=jnp.float32) / rotary)
    angles = position[:, None] * frequency[None, :]
    return (jnp.cos(angles), jnp.sin(angles))


def rotate_heads(values, cosine_table, sine_table):
    halfway = cosine_table.shape[-1]
    leading = values[..., :halfway]
    trailing = values[..., halfway : 2 * halfway]
    return jnp.concatenate(
        [
            leading * cosine_table - trailing * sine_table,
            trailing * cosine_table + leading * sine_table,
            values[..., 2 * halfway :],
        ],
        axis=-1,
    )


def masked_scores(query_block, key_block, begin_row, score_scale):
    scores = (
        jnp.einsum("bhqe,bhke->bhqk", query_block, key_block, preferred_element_type=jnp.float32)
        * score_scale
    )
    row_at = begin_row + jnp.arange(query_block.shape[2])[:, None]
    col_at = jnp.arange(key_block.shape[2])[None, :]
    return jnp.where(col_at <= row_at, scores, -1000000000.0)


def body(
    layer_input,
    cotangent,
    firstgain,
    firstbias,
    secondgain,
    secondbias,
    project,
    projbias,
    merging,
    mergebias,
    expand,
    expandbias,
    shrink,
    shrinkbias,
):
    vectors = jnp.stack([firstgain, firstbias, secondgain, secondbias, mergebias, shrinkbias])
    weights = (
        lax.all_gather(project, "dp", axis=0, tiled=True),
        lax.all_gather(projbias, "dp", axis=1, tiled=True),
        lax.all_gather(merging, "dp", axis=1, tiled=True),
        lax.all_gather(expand, "dp", axis=0, tiled=True),
        lax.all_gather(expandbias, "dp", axis=0, tiled=True),
        lax.all_gather(shrink, "dp", axis=1, tiled=True),
        lax.all_gather(vectors, "dp", axis=1, tiled=True),
    )
    w_project, b_project, w_merge, w_expand, b_expand, w_shrink, all_vectors = weights
    scaled = all_vectors.astype(jnp.float32)
    own_rows = layer_input.astype(jnp.float32)
    group_rows = lax.all_gather(layer_input, "tensor", axis=0, tiled=True).astype(jnp.float32)
    first_norm = normalize(group_rows, scaled[0], scaled[1]).astype(jnp.bfloat16)
    second_norm = normalize(group_rows, scaled[2], scaled[3]).astype(jnp.bfloat16)
    group_count = first_norm.shape[0]
    width = first_norm.shape[1]
    seq_count = group_count // LENGTH
    local_heads = w_project.shape[1]
    score_scale = HEAD_DIM ** (-0.5)
    cosine_table, sine_table = rotary_tables(LENGTH, ROTARY)
    first_seq = first_norm.reshape(seq_count, LENGTH, width)
    mixed_rows = jnp.einsum(
        "bsd,dhe->bhse", first_seq, w_project, preferred_element_type=jnp.float32
    )
    mixed_rows = mixed_rows + b_project.astype(jnp.float32)[None, :, None, :]
    queries = rotate_heads(mixed_rows[..., :HEAD_DIM], cosine_table, sine_table).astype(
        jnp.bfloat16
    )
    keyset = rotate_heads(
        mixed_rows[..., HEAD_DIM : 2 * HEAD_DIM], cosine_table, sine_table
    ).astype(jnp.bfloat16)
    valueset = mixed_rows[..., 2 * HEAD_DIM :].astype(jnp.bfloat16)
    context_parts = []
    total_parts = []
    for block_index in range(LENGTH // QBLOCK):
        begin_row = block_index * QBLOCK
        finish_row = begin_row + QBLOCK
        scores = masked_scores(
            queries[:, :, begin_row:finish_row], keyset[:, :, :finish_row], begin_row, score_scale
        )
        row_top = jnp.max(scores, axis=-1, keepdims=True)
        exponent = jnp.exp(scores - row_top)
        row_total = jnp.sum(exponent, axis=-1, keepdims=True)
        probability = (exponent / row_total).astype(jnp.bfloat16)
        context_parts.append(
            jnp.einsum(
                "bhqk,bhke->bhqe",
                probability,
                valueset[:, :, :finish_row],
                preferred_element_type=jnp.float32,
            )
        )
        total_parts.append(row_top[..., 0] + jnp.log(row_total[..., 0]))
    context_heads = jnp.concatenate(context_parts, axis=2)
    log_total = jnp.concatenate(total_parts, axis=2)
    context = jnp.transpose(context_heads, (0, 2, 1, 3)).reshape(
        group_count, local_heads * HEAD_DIM
    )
    context = context.astype(jnp.bfloat16)
    attended = jnp.dot(context, w_merge, preferred_element_type=jnp.float32)
    preact = jnp.dot(second_norm, w_expand, preferred_element_type=jnp.float32) + b_expand.astype(
        jnp.float32
    )
    hidden = jax.nn.gelu(preact, approximate=False).astype(jnp.bfloat16)
    branches = attended + jnp.dot(hidden, w_shrink, preferred_element_type=jnp.float32)
    summed = lax.psum_scatter(
        branches.astype(jnp.bfloat16), "tensor", scatter_dimension=0, tiled=True
    ).astype(jnp.float32)
    layer_output = (own_rows + summed + scaled[4] + scaled[5]).astype(jnp.bfloat16)
    weights = (
        lax.all_gather(project, "dp", axis=0, tiled=True),
        lax.all_gather(projbias, "dp", axis=1, tiled=True),
        lax.all_gather(merging, "dp", axis=1, tiled=True),
        lax.all_gather(expand, "dp", axis=0, tiled=True),
        lax.all_gather(expandbias, "dp", axis=0, tiled=True),
        lax.all_gather(shrink, "dp", axis=1, tiled=True),
        lax.all_gather(vectors, "dp", axis=1, tiled=True),
    )
    w_project, b_project, w_merge, w_expand, b_expand, w_shrink, all_vectors = weights
    scaled = all_vectors.astype(jnp.float32)
    seed_rows = lax.all_gather(cotangent, "tensor", axis=0, tiled=True)
    hidden_grad = jnp.einsum("sd,fd->sf", seed_rows, w_shrink, preferred_element_type=jnp.float32)
    unused, gelu_pull = jax.vjp(partial(jax.nn.gelu, approximate=False), preact)
    preact_grad = gelu_pull(hidden_grad)[0].astype(jnp.bfloat16)
    shrink_grad = jnp.einsum("sf,sd->fd", hidden, seed_rows, preferred_element_type=jnp.float32)
    expand_grad = jnp.einsum(
        "sd,sf->df", second_norm, preact_grad, preferred_element_type=jnp.float32
    )
    expandbias_grad = jnp.sum(preact_grad, axis=0, dtype=jnp.float32)
    second_back = jnp.einsum("sf,df->sd", preact_grad, w_expand, preferred_element_type=jnp.float32)
    context_grad = jnp.einsum("sd,ed->se", seed_rows, w_merge, preferred_element_type=jnp.float32)
    context_grad = context_grad.astype(jnp.bfloat16)
    merging_grad = jnp.einsum("se,sd->ed", context, seed_rows, preferred_element_type=jnp.float32)
    grad_heads = jnp.transpose(
        context_grad.reshape(seq_count, LENGTH, local_heads, HEAD_DIM), (0, 2, 1, 3)
    )
    query_grads = []
    key_grad = jnp.zeros(queries.shape, jnp.float32)
    value_grad = jnp.zeros(queries.shape, jnp.float32)
    for block_index in range(LENGTH // QBLOCK):
        begin_row = block_index * QBLOCK
        finish_row = begin_row + QBLOCK
        query_block = queries[:, :, begin_row:finish_row]
        scores = masked_scores(query_block, keyset[:, :, :finish_row], begin_row, score_scale)
        probability = jnp.exp(scores - log_total[:, :, begin_row:finish_row, None])
        prob_round = probability.astype(jnp.bfloat16)
        grad_block = grad_heads[:, :, begin_row:finish_row]
        prob_grad = jnp.einsum(
            "bhqe,bhke->bhqk",
            grad_block,
            valueset[:, :, :finish_row],
            preferred_element_type=jnp.float32,
        )
        inner_sum = jnp.sum(probability * prob_grad, axis=-1, keepdims=True)
        score_grad = (probability * (prob_grad - inner_sum)).astype(jnp.bfloat16)
        query_grads.append(
            jnp.einsum(
                "bhqk,bhke->bhqe",
                score_grad,
                keyset[:, :, :finish_row],
                preferred_element_type=jnp.float32,
            )
            * score_scale
        )
        key_grad = key_grad.at[:, :, :finish_row].add(
            jnp.einsum(
                "bhqk,bhqe->bhke", score_grad, query_block, preferred_element_type=jnp.float32
            )
            * score_scale
        )
        value_grad = value_grad.at[:, :, :finish_row].add(
            jnp.einsum(
                "bhqk,bhqe->bhke", prob_round, grad_block, preferred_element_type=jnp.float32
            )
        )
    query_grad = jnp.concatenate(query_grads, axis=2)
    mixed_grad = jnp.concatenate(
        [
            rotate_heads(query_grad, cosine_table, -sine_table),
            rotate_heads(key_grad, cosine_table, -sine_table),
            value_grad,
        ],
        axis=-1,
    ).astype(jnp.bfloat16)
    project_grad = jnp.einsum(
        "bsd,bhse->dhe", first_seq, mixed_grad, preferred_element_type=jnp.float32
    )
    projbias_grad = jnp.sum(mixed_grad, axis=(0, 2), dtype=jnp.float32)
    first_back = jnp.einsum(
        "bhse,dhe->bsd", mixed_grad, w_project, preferred_element_type=jnp.float32
    ).reshape(group_count, width)
    row_first, gain_first, shift_first = norm_backward(group_rows, scaled[0], scaled[1], first_back)
    row_second, gain_second, shift_second = norm_backward(
        group_rows, scaled[2], scaled[3], second_back
    )
    row_part = lax.psum_scatter(
        (row_first + row_second).astype(jnp.bfloat16), "tensor", scatter_dimension=0, tiled=True
    ).astype(jnp.float32)
    seed_own = cotangent.astype(jnp.float32)
    input_grad = seed_own + row_part
    seed_total = jnp.sum(seed_own, axis=0)
    vector_part = jnp.stack(
        [gain_first, shift_first, gain_second, shift_second, seed_total, seed_total]
    )
    summed_grads = (
        lax.psum_scatter(
            project_grad.astype(jnp.bfloat16), "dp", scatter_dimension=0, tiled=True
        ).astype(jnp.float32),
        lax.psum_scatter(
            projbias_grad.astype(jnp.bfloat16), "dp", scatter_dimension=1, tiled=True
        ).astype(jnp.float32),
        lax.psum_scatter(
            merging_grad.astype(jnp.bfloat16), "dp", scatter_dimension=1, tiled=True
        ).astype(jnp.float32),
        lax.psum_scatter(
            expand_grad.astype(jnp.bfloat16), "dp", scatter_dimension=0, tiled=True
        ).astype(jnp.float32),
        lax.psum_scatter(
            expandbias_grad.astype(jnp.bfloat16), "dp", scatter_dimension=0, tiled=True
        ).astype(jnp.float32),
        lax.psum_scatter(
            shrink_grad.astype(jnp.bfloat16), "dp", scatter_dimension=1, tiled=True
        ).astype(jnp.float32),
        lax.psum_scatter(
            vector_part.astype(jnp.bfloat16), "dp", scatter_dimension=1, tiled=True
        ).astype(jnp.float32),
    )
    vector_total = lax.psum(summed_grads[6], "tensor")
    return (
        layer_output,
        input_grad,
        vector_total[0],
        vector_total[1],
        vector_total[2],
        vector_total[3],
        summed_grads[0],
        summed_grads[1],
        summed_grads[2],
        vector_total[4],
        summed_grads[3],
        summed_grads[4],
        summed_grads[5],
        vector_total[5],
    )


def solution(mesh):
    return jax.shard_map(
        body,
        mesh=mesh,
        in_specs=(
            P(("dp", "tensor"), None),
            P(("dp", "tensor"), None),
            P("dp"),
            P("dp"),
            P("dp"),
            P("dp"),
            P("dp", "tensor", None),
            P("tensor", "dp"),
            P("tensor", "dp"),
            P("dp"),
            P("dp", "tensor"),
            P(("tensor", "dp")),
            P("tensor", "dp"),
            P("dp"),
        ),
        out_specs=(
            P(("dp", "tensor"), None),
            P(("dp", "tensor"), None),
            P("dp"),
            P("dp"),
            P("dp"),
            P("dp"),
            P("dp", "tensor", None),
            P("tensor", "dp"),
            P("tensor", "dp"),
            P("dp"),
            P("dp", "tensor"),
            P(("tensor", "dp")),
            P("tensor", "dp"),
            P("dp"),
        ),
        check_vma=False,
    )
```

profile of v0, /device:TPU:0, one launch (start us, length us, event | category | flops | bytes accessed | tf_op | source)
XLA Modules:
  0.0 1090.9 jit_solution(890005800705977737)
XLA Ops:
  14.6 13.4 %all-gather = bf16[8,96,2]{1,2,0:T(2,128)(2,1)S(1)} all-gather(bf16[1,96,2]{1,2,0:T(2,128)(2,1)S(1)} %bitcast.296), channel_id=1, replica_groups=mesh['dp'=8,'tensor'=4] {'dp'}, dimensions={0}, use_global_device_ids=true | all-gather | bytes 3456 | tf_op jit(solution)/shard_map/all_gather | solution.py:78
  38.3 14.0 %all_gather.33 = bf16[6,2048]{1,0:T(8,128)(2,1)S(1)} all-gather(bf16[6,256]{1,0:T(8,128)(2,1)S(1)} %stack.43), channel_id=1, replica_groups=mesh['dp'=8,'tensor'=4] {'dp'}, dimensions={1}, use_global_device_ids=true | all-gather | bytes 27648 | tf_op jit(solution)/shard_map/all_gather | solution.py:83
  59.0 41.3 %all-gather.9.cloned.1.call-done = bf16[2048,2048]{1,0:T(8,128)(2,1)} async-done(((bf16[512,2048]{1,0:T(8,128)(2,1)}), bf16[2048,2048]{1,0:T(8,128)(2,1)}) %all-gather.9.cloned.1.call-update) | async-done | bytes 8388624 | tf_op jit(solution)/shard_map/all_gather | solution.py:88
  108.4 59.2 %all-gather.11.cloned.1.call-done = bf16[2048,2,768]{0,2,1:T(8,128)(2,1)} async-done(((bf16[256,2,768]{0,2,1:T(8,128)(2,1)}), bf16[2048,2,768]{0,2,1:T(8,128)(2,1)}) %all-gather.11.cloned.1.call-update) | async-done | bytes 6291472 | tf_op jit(solution)/shard_map/all_gather | solution.py:77
  167.7 20.3 %fusion.98 = (bf16[1,2,2048,768]{2,3,1,0:T(8,128)(2,1)S(1)}, f32[1,2,2048,768]{2,3,1,0:T(8,128)}) fusion(f32[2,768]{1,0:T(2,128)S(1)} %bitcast.289, bf16[2048,2,768]{0,2,1:T(8,128)(2,1)} %all-gather.11.cloned.1.call-done, bf16[2048,2048]{1,0:T(8,128)(2,1)} %all-gather.9.cloned.1.call-done, f32[2048]{0:T(1024)S(1)} %bitcast.287, f32[2048]{0:T(1024)S(1)} %bitcast.275, ...), kind=kOutput, calls=%fused_computation.217 | convolution fusion | flops 12916359168 | bytes 33593344 | tf_op jit(solution)/shard_map/bsd,dhe->bhse/dot_general | solution.py:98
  203.4 83.4 %all-gather.19.cloned.1.call-done = bf16[2048,2048]{1,0:T(8,128)(2,1)} async-done(((bf16[512,2048]{1,0:T(8,128)(2,1)}), bf16[2048,2048]{1,0:T(8,128)(2,1)}) %all-gather.19.cloned.1.call-update) | async-done | bytes 8388624 | tf_op jit(solution)/shard_map/all_gather | solution.py:157
  398.2 24.7 %fusion.89 = f32[2048,2048]{1,0:T(8,128)} fusion(bf16[2048,2048]{1,0:T(8,128)(2,1)} %all-gather.15.cloned.1.call-done, bf16[2048,2048]{1,0:T(8,128)(2,1)} %all-gather.9.cloned.1.call-done, f32[2048]{0:T(1024)S(1)} %bitcast.285, f32[2048]{0:T(1024)S(1)} %bitcast.270, f32[2048]{0:T(1024)S(1)} %fusion.85, f32[2048]{0:T(1024)S(1)} %broadcast_multiply_fusion), kind=kOutput, calls=%fused_computation.210 | convolution fusion | flops 17205035008 | bytes 33587200 | tf_op jit(solution)/shard_map/dot_general | solution.py:137
  423.0 29.8 %all-gather.17.cloned.1.call-done = bf16[2048,2048]{1,0:T(8,128)(2,1)} async-done(((bf16[2048,256]{1,0:T(8,128)(2,1)}), bf16[2048,2048]{1,0:T(8,128)(2,1)}) %all-gather.17.cloned.1.call-update) | async-done | bytes 8388624 | tf_op jit(solution)/shard_map/all_gather | solution.py:82
  452.8 63.4 %fusion.94 = (bf16[2048]{0:T(1024)(128)(2,1)}, bf16[2048,2048]{1,0:T(8,128)(2,1)S(1)}, f32[2048,2048]{1,0:T(8,128)}) fusion(f32[2048,2048]{1,0:T(8,128)} %fusion.89, f32[2048]{0:T(1024)S(1)} %bitcast.282, bf16[2048,2048]{1,0:T(8,128)(2,1)} %all-gather.19.cloned.1.call-done, bf16[2048,2048]{1,0:T(8,128)(2,1)} %all-gather.17.cloned.1.call-done), kind=kOutput, calls=%fused_computation.214 | convolution fusion | flops 17490245632 | bytes 58732544 | tf_op jit(solution)/shard_map/sd,fd->sf/dot_general | solution.py:158
  516.2 20.5 %fusion.104 = f32[2048,2048]{1,0:T(8,128)} fusion(bf16[2048,2048]{1,0:T(8,128)(2,1)S(1)} %get-tuple-element.193, bf16[2048,2048]{1,0:T(8,128)(2,1)S(1)} %copy-done.55), kind=kOutput, calls=%fused_computation.224 | convolution fusion | flops 17179869184 | bytes 33554432 | tf_op jit(solution)/shard_map/sf,df->sd/dot_general | solution.py:166
  536.8 30.1 %bitcast_reduce_fusion = (bf16[2048]{0:T(1024)(128)(2,1)S(1)}, f32[2048]{0:T(1024)S(1)}, f32[2048]{0:T(1024)S(1)}, bf16[2048]{0:T(1024)(128)(2,1)S(1)}, f32[2048,2048,1]{1,0,2:T(8,128)}) fusion(f32[2048]{0:T(1024)S(1)} %bitcast.276, f32[2048]{0:T(1024)S(1)} %copy-done.36, bf16[2048,2048]{1,0:T(8,128)(2,1)} %all-gather.9.cloned.1.call-done, ...), kind=kOutput, calls=%fused_computation.25 | convolution fusion | flops 12926836736 | bytes 54575104 | tf_op jit(solution)/shard_map/bhse,dhe->bsd/dot_general | solution.py:225
  566.9 17.8 %fusion.15 = (bf16[2048]{0:T(1024)(128)(2,1)S(1)}, f32[2048]{0:T(1024)S(1)}, f32[2048]{0:T(1024)S(1)}, bf16[2048]{0:T(1024)(128)(2,1)S(1)}) fusion(f32[2048,2048]{1,0:T(8,128)} %fusion.104, bf16[2048,2048]{1,0:T(8,128)(2,1)} %all-gather.9.cloned.1.call-done, f32[2048]{0:T(1024)S(1)} %copy-done.45, f32[2048]{0:T(1024)S(1)} %copy-done.36, ...), kind=kLoop, calls=%fused_computation.20 | loop fusion | flops 79683584 | bytes 42016768 | tf_op jit(solution)/shard_map/transpose(jvp())/reduce_sum | solution.py:20
  594.6 20.5 %convolution_convert_fusion.2 = bf16[2048,2,768]{2,0,1:T(8,128)(2,1)} fusion(bf16[2,2048,768]{1,2,0:T(8,128)(2,1)} %get-tuple-element.246, bf16[2048,2048]{1,0:T(8,128)(2,1)} %all-gather.9.cloned.1.call-done, f32[2048]{0:T(1024)S(1)} %bitcast.288, f32[2048]{0:T(1024)S(1)} %bitcast.278, f32[2048]{0:T(1024)S(1)} %copy-done.45, f32[2048]{0:T(1024)S(1)} %copy-done.36), kind=kOutput, calls=%fused_computation.65 | convolution fusion | flops 12913213440 | bytes 21004288 | tf_op jit(solution)/shard_map/bsd,bhse->dhe/dot_general | solution.py:221
  615.2 12.7 %multiply_convert_fusion = bf16[2048,2048]{1,0:T(8,128)(2,1)S(1)} fusion(f32[2048,2048]{1,0:T(8,128)} %get-tuple-element.194, f32[2048,2048]{1,0:T(8,128)} %fusion.89, f32[2048]{0:T(1024)S(1)} %bitcast.283), kind=kLoop, calls=%fused_computation.30 | loop fusion | flops 16777216 | bytes 41951232 | tf_op jit(solution)/shard_map/convert_element_type | solution.py:140
  631.2 22.1 %convolution_convert_fusion = bf16[2048,2048]{1,0:T(8,128)(2,1)} fusion(bf16[2048,2048]{1,0:T(8,128)(2,1)S(1)} %multiply_convert_fusion, bf16[2048,2048]{1,0:T(8,128)(2,1)} %all-gather.19.cloned.1.call-done), kind=kOutput, calls=%fused_computation.53 | convolution fusion | flops 17184063488 | bytes 25165824 | tf_op jit(solution)/shard_map/sf,sd->fd/dot_general | solution.py:161
  654.0 25.4 %convolution_convert_fusion.1 = bf16[2048,2048]{1,0:T(8,128)(2,1)} fusion(bf16[2048,2048]{1,0:T(8,128)(2,1)} %copy-done.64, bf16[2048,2048]{1,0:T(8,128)(2,1)} %all-gather.9.cloned.1.call-done, f32[2048]{0:T(1024)S(1)} %bitcast.286, f32[2048]{0:T(1024)S(1)} %bitcast.273, f32[2048]{0:T(1024)S(1)} %copy-done.45, f32[2048]{0:T(1024)S(1)} %copy-done.36), kind=kOutput, calls=%fused_computation.54 | convolution fusion | flops 17209229312 | bytes 25198592 | tf_op jit(solution)/shard_map/sd,sf->df/dot_general | solution.py:162
  679.5 19.5 %add_convert_fusion = bf16[2048,2048]{1,0:T(8,128)(2,1)} fusion(f32[2048]{0:T(1024)S(1)} %negate_multiply_fusion.1, f32[2048]{0:T(1024)S(1)} %negate_multiply_fusion.2, f32[2048]{0:T(1024)S(1)} %get-tuple-element.223, f32[2048]{0:T(1024)S(1)} %copy-done.36, bf16[2048,2048]{1,0:T(8,128)(2,1)} %all-gather.9.cloned.1.call-done, f32[2048]{0:T(1024)S(1)} %copy-done.45, ...), kind=kLoop, calls=%fused_computation.27 | loop fusion | flops 67108864 | bytes 50397184 | tf_op jit(solution)/shard_map/convert_element_type | solution.py:233
  709.0 25.4 %add_convert_fusion.2 = bf16[2048,2048]{1,0:T(8,128)(2,1)} fusion(f32[2048,2048]{1,0:T(8,128)} %fusion.103, bf16[2048,2048]{1,0:T(8,128)(2,1)} %copy-done.18, bf16[2048,2048]{1,0:T(8,128)(2,1)} %all-gather.17.cloned.1.call-done), kind=kOutput, calls=%fused_computation.29 | convolution fusion | flops 17188257792 | bytes 41943040 | tf_op jit(solution)/shard_map/dot_general | solution.py:141
  737.7 15.1 %all-reduce.2 = bf16[2048]{0:T(1024)(128)(2,1)S(1)} all-reduce(bf16[2048]{0:T(1024)(128)(2,1)S(1)} %copy-done.53), channel_id=9, replica_groups=mesh['dp'=8,'tensor'=4] {'dp'}, use_global_device_ids=true, to_apply=%region_33.34.clone | all-reduce | flops 2048 | bytes 8192
  753.5 10.1 psum.7
  769.1 42.8 %reduce-scatter.23.cloned.1.call-done = bf16[2048,256]{1,0:T(8,128)(2,1)} async-done(((bf16[2048,2048]{1,0:T(8,128)(2,1)}), bf16[2048,256]{1,0:T(8,128)(2,1)}) %reduce-scatter.23.cloned.1.call-update) | async-done | bytes 1048592 | tf_op jit(solution)/shard_map/reduce_scatter | solution.py:257
  814.6 87.4 %reduce-scatter.21.cloned.1.call-done = bf16[256,2048]{1,0:T(8,128)(2,1)} async-done(((bf16[2048,2048]{1,0:T(8,128)(2,1)}), bf16[256,2048]{1,0:T(8,128)(2,1)}) %reduce-scatter.21.cloned.1.call-update) | async-done | bytes 1048592 | tf_op jit(solution)/shard_map/reduce_scatter | solution.py:251
  904.8 85.1 %reduce-scatter.13.cloned.1.call-done = bf16[512,2048]{1,0:T(8,128)(2,1)} async-done(((bf16[2048,2048]{1,0:T(8,128)(2,1)}), bf16[512,2048]{1,0:T(8,128)(2,1)}) %reduce-scatter.13.cloned.1.call-update) | async-done | bytes 2097168 | tf_op jit(solution)/shard_map/reduce_scatter | solution.py:232
  994.3 85.3 %reduce-scatter.11.cloned.1.call-done = bf16[512,2048]{1,0:T(8,128)(2,1)} async-done(((bf16[2048,2048]{1,0:T(8,128)(2,1)}), bf16[512,2048]{1,0:T(8,128)(2,1)}) %reduce-scatter.11.cloned.1.call-update) | async-done | bytes 2097168 | tf_op jit(solution)/shard_map/reduce_scatter | solution.py:142
  (292 shorter events, 205.6 us)
Async XLA Ops:
  7.3 93.0 %all-gather.9.cloned.1.call-start = ((), (), s32[]{:S(2)}) async-start(), calls=%async_computation.8 | async-start | bytes 10485760 | tf_op jit(solution)/shard_map/all_gather | solution.py:88
  8.0 159.7 %all-gather.11.cloned.1.call-start = ((), (), s32[]{:S(2)}) async-start(), calls=%async_computation.9 | async-start | bytes 7077888 | tf_op jit(solution)/shard_map/all_gather | solution.py:77
  11.1 192.3 %all-gather.13.cloned.1.call-start = ((), (), s32[]{:S(2)}) async-start(), calls=%async_computation.10 | async-start | bytes 2359296 | tf_op jit(solution)/shard_map/all_gather | solution.py:79
  11.8 274.9 %all-gather.19.cloned.1.call-start = ((), (), s32[]{:S(2)}) async-start(), calls=%async_computation.14 | async-start | bytes 10485760 | tf_op jit(solution)/shard_map/all_gather | solution.py:157
  12.4 385.7 %all-gather.15.cloned.1.call-start = ((), (), s32[]{:S(2)}) async-start(), calls=%async_computation.11 | async-start | bytes 9437184 | tf_op jit(solution)/shard_map/all_gather | solution.py:80
  13.0 439.8 %all-gather.17.cloned.1.call-start = ((), (), s32[]{:S(2)}) async-start(), calls=%async_computation.12 | async-start | bytes 9437184 | tf_op jit(solution)/shard_map/all_gather | solution.py:82
  13.6 722.8 %reduce-scatter.25.cloned.1.call-start = ((), (), s32[]{:S(2)}) async-start(), calls=%async_computation.21 | async-start | bytes 221184
  53.0 114.7 %copy-start.42 = (f32[1,2048]{1,0:T(1,128)}, f32[1,2048]{1,0:T(1,128)S(1)}, u32[]{:S(2)}) copy-start(f32[1,2048]{1,0:T(1,128)S(1)} %get-tuple-element.215) | copy-start | bytes 24580
  53.0 114.7 %copy-start.51 = (f32[1,2048]{1,0:T(1,128)}, f32[1,2048]{1,0:T(1,128)S(1)}, u32[]{:S(2)}) copy-start(f32[1,2048]{1,0:T(1,128)S(1)} %get-tuple-element.216) | copy-start | bytes 24580
  106.1 292.1 %copy-start.35 = (f32[2048]{0:T(1024)}, f32[2048]{0:T(1024)S(1)}, u32[]{:S(2)}) copy-start(f32[2048]{0:T(1024)S(1)} %broadcast_multiply_fusion) | copy-start | bytes 24580
  108.4 79.6 %copy-start.38 = (f32[2048]{0:T(1024)}, f32[2048]{0:T(1024)S(1)}, u32[]{:S(2)}) copy-start(f32[2048]{0:T(1024)S(1)} %fusion.16) | copy-start | bytes 24580
  108.4 289.8 %copy-start.44 = (f32[2048]{0:T(1024)}, f32[2048]{0:T(1024)S(1)}, u32[]{:S(2)}) copy-start(f32[2048]{0:T(1024)S(1)} %fusion.85) | copy-start | bytes 24580
  197.7 116.3 %copy-start.22 = (bf16[1,2,2048,32]{2,3,1,0:T(8,128)(2,1)}, bf16[1,2,2048,32]{2,3,1,0:T(8,128)(2,1)S(1)}, u32[]{:S(2)}) copy-start(bf16[1,2,2048,32]{2,3,1,0:T(8,128)(2,1)S(1)} %get-tuple-element.206) | copy-start | bytes 786436
  197.7 116.3 %copy-start.24 = (bf16[1,2,2048,32]{2,3,1,0:T(8,128)(2,1)}, bf16[1,2,2048,32]{2,3,1,0:T(8,128)(2,1)S(1)}, u32[]{:S(2)}) copy-start(bf16[1,2,2048,32]{2,3,1,0:T(8,128)(2,1)S(1)} %get-tuple-element.207) | copy-start | bytes 786436
  398.1 355.4 %reduce-scatter.15.cloned.1.call-start = ((), (), s32[]{:S(2)}) async-start(), calls=%async_computation.16 | async-start | bytes 36864 | tf_op jit(solution)/shard_map/reduce_scatter | solution.py:260
  585.4 178.8 %reduce-scatter.19.cloned.1.call-start = ((), (), s32[]{:S(2)}) async-start(), calls=%async_computation.18 | async-start | bytes 2359296 | tf_op jit(solution)/shard_map/reduce_scatter | solution.py:248
  594.6 171.4 %reduce-scatter.17.cloned.1.call-start = ((), (), s32[]{:S(2)}) async-start(), calls=%async_computation.17 | async-start | bytes 7077888 | tf_op jit(solution)/shard_map/reduce_scatter | solution.py:242
  615.1 196.8 %reduce-scatter.23.cloned.1.call-start = ((), (), s32[]{:S(2)}) async-start(), calls=%async_computation.20 | async-start | bytes 9437184 | tf_op jit(solution)/shard_map/reduce_scatter | solution.py:257
  653.3 248.7 %reduce-scatter.21.cloned.1.call-start = ((), (), s32[]{:S(2)}) async-start(), calls=%async_computation.19 | async-start | bytes 9437184 | tf_op jit(solution)/shard_map/reduce_scatter | solution.py:251
  679.4 310.5 %reduce-scatter.13.cloned.1.call-start = ((), (), s32[]{:S(2)}) async-start(), calls=%async_computation.15 | async-start | bytes 10485760 | tf_op jit(solution)/shard_map/reduce_scatter | solution.py:232
  699.0 380.5 %reduce-scatter.11.cloned.1.call-start = ((), (), s32[]{:S(2)}) async-start(), calls=%async_computation.13 | async-start | bytes 10485760 | tf_op jit(solution)/shard_map/reduce_scatter | solution.py:142
  734.5 255.4 %copy-start.8 = (bf16[512,2048]{1,0:T(8,128)(2,1)S(1)}, bf16[512,2048]{1,0:T(8,128)(2,1)}, u32[]{:S(2)}) copy-start(bf16[512,2048]{1,0:T(8,128)(2,1)} %param.35) | copy-start | bytes 6291460
  814.6 264.9 %copy-start.46 = (f32[1,2048]{1,0:T(1,128)S(1)}, f32[1,2048]{1,0:T(1,128)}, u32[]{:S(2)}) copy-start(f32[1,2048]{1,0:T(1,128)} %get-tuple-element.211) | copy-start | bytes 24580
  814.6 264.9 %copy-start.47 = (f32[1,2048]{1,0:T(1,128)S(1)}, f32[1,2048]{1,0:T(1,128)}, u32[]{:S(2)}) copy-start(f32[1,2048]{1,0:T(1,128)} %get-tuple-element.212) | copy-start | bytes 24580
  (61 other events, 562.4 us)
Sparse Core Ops, SparseCore 0:
  10.0 90.2 all-gather.8
  102.5 65.1 all-gather.10
  169.3 29.0 all-gather.12
  200.0 86.6 all-gather.18
  288.2 82.0 all-gather.14
  371.7 81.0 all-gather.16
  455.6 28.4 reduce-scatter.24
  585.6 28.1 reduce-scatter.14
  616.6 33.9 reduce-scatter.18
  652.7 68.5 reduce-scatter.16
  723.6 88.2 reduce-scatter.22
  814.1 87.9 reduce-scatter.20
  905.1 84.7 reduce-scatter.12
  993.1 86.3 reduce-scatter.10
where the time goes:
time: 1100 us; the launch traced here: 1090 us
  waiting for transfers between devices  517 us (47%)
  matrix products  332 us (30%)
  other arithmetic  108 us (10%)
  blocking collectives  61.3 us (6%)
  local copies, waits for them, and re-layouts  55.3 us (5%)
  between operations  15.8 us (1%)
    reduce_scatter x1, waiting for transfers between devices, body(): lax.psum_scatter(expand_grad.astype(jnp.bfloat16), 'dp', scatter_dimensio...  87.4 us
    reduce_scatter x1, waiting for transfers between devices, body(): lax.psum_scatter(branches.astype(jnp.bfloat16), 'tensor', scatter_dimensi...  85.3 us
    reduce_scatter x1, waiting for transfers between devices, body(): lax.psum_scatter((row_first + row_second).astype(jnp.bfloat16), 'tensor',...  85.1 us
    all_gather x1, waiting for transfers between devices, body(): seed_rows = lax.all_gather(cotangent, 'tensor', axis=0, tiled=True)  83.4 us
    dot_general x1, matrix products, body(): jnp.einsum('sd,fd->sf', seed_rows, w_shrink, preferred_element_type=jnp.f...  63.4 us
    all_gather x1, waiting for transfers between devices, body(): lax.all_gather(project, 'dp', axis=0, tiled=True)  59.2 us
    reduce_scatter x1, waiting for transfers between devices, body(): lax.psum_scatter(shrink_grad.astype(jnp.bfloat16), 'dp', scatter_dimensio...  42.8 us
    all_gather x1, waiting for transfers between devices, body(): lax.all_gather(layer_input, 'tensor', axis=0, tiled=True)  41.3 us
  transfers between devices with their start and end apart: 14, of which 8 were waited for; matrix products, arithmetic and copies ran while one was open for 44% of the time, Pallas kernels for 0%

commit v1 on v0

v1 whole, which is shorter than its diff:
```python
import jax
import jax.numpy as jnp
from jax import lax
from jax.experimental import pallas as pl
from jax.experimental.pallas import tpu as pltpu
from jax.sharding import PartitionSpec as P

HEAD_DIM = 256
ROTARY = 64
LENGTH = 2048
EPSILON = 1e-05
BIG = -1e30
F32 = jnp.float32
BF16 = jnp.bfloat16
DIMS = {
    "NN": (((1,), (0,)), ((), ())),
    "NT": (((1,), (1,)), ((), ())),
    "TN": (((0,), (0,)), ((), ())),
}


def product(left, right, mode):
    return lax.dot_general(left, right, DIMS[mode], preferred_element_type=F32)


def params():
    return pltpu.CompilerParams(vmem_limit_bytes=56 << 20)


def cost(flops, nbytes, transcendentals=0):
    return pl.CostEstimate(
        flops=int(flops), bytes_accessed=int(nbytes), transcendentals=int(transcendentals)
    )


def tile_of(width, most):
    best = 128
    for size in range(128, most + 1, 128):
        if width % size == 0:
            best = size
    return best


def call(kernel, ids, grid, in_specs, out_specs, out_shape, args, cost_of, scratch=()):
    return pl.pallas_call(
        kernel,
        grid_spec=pltpu.PrefetchScalarGridSpec(
            num_scalar_prefetch=1,
            grid=grid,
            in_specs=in_specs,
            out_specs=out_specs,
            scratch_shapes=list(scratch),
        ),
        out_shape=out_shape,
        compiler_params=params(),
        cost_estimate=cost_of,
    )(ids, *args)


def norm_kernel(ids, pieces, vectors, unit):
    rows = sum(piece.shape[0] for piece in pieces)
    width = pieces[0].shape[1]
    starts = []
    for piece in pieces:
        starts.append((starts[-1][1] if starts else 0,) * 2)
        starts[-1] = (starts[-1][0], starts[-1][0] + piece.shape[0] // unit)

    def kernel(ids_ref, *refs):
        step = pl.program_id(0)
        vec = refs[len(pieces)]
        first_ref, second_ref = refs[len(pieces) + 1 :]
        for (low, high), piece_ref in zip(starts, refs):

            @pl.when((step >= low) & (step < high))
            def _(piece_ref=piece_ref):
                data = piece_ref[...].astype(F32)
                centre = data - jnp.mean(data, axis=-1, keepdims=True)
                spread = jnp.mean(centre * centre, axis=-1, keepdims=True)
                scaled = centre * lax.rsqrt(spread + EPSILON)
                first_ref[...] = (scaled * vec[0:1, :] + vec[1:2, :]).astype(BF16)
                second_ref[...] = (scaled * vec[2:3, :] + vec[3:4, :]).astype(BF16)

    def spec(low, high):
        return pl.BlockSpec((unit, width), lambda i, ids: (jnp.clip(i - low, 0, high - low - 1), 0))

    out = pl.BlockSpec((unit, width), lambda i, ids: (i, 0))
    shape = jax.ShapeDtypeStruct((rows, width), BF16)
    return call(
        kernel,
        ids,
        (rows // unit,),
        [spec(low, high) for low, high in starts] + [pl.BlockSpec(vectors.shape, lambda i, ids: (0, 0))],
        [out, out],
        [shape, shape],
        (*pieces, vectors),
        cost(12 * rows * width, 6 * rows * width),
    )


def rotate(block, cos, sin_low, sin_high, sign):
    lead = block[:, :128]
    turned = (
        lead * cos
        + sign * (pltpu.roll(lead, 96, 1) * sin_low + pltpu.roll(lead, 32, 1) * sin_high)
    )
    return jnp.concatenate([turned, block[:, 128:]], axis=1)


def mixed_kernel(ids, first, weight, bias, tables, blocks):
    rows, depth = first.shape
    heads = weight.shape[1] // (3 * HEAD_DIM)
    unit = rows // blocks
    wide = 3 * HEAD_DIM

    def kernel(ids_ref, a_ref, w_ref, b_ref, cos, low, high, out_ref):
        for part in range(3):
            here = slice(part * HEAD_DIM, (part + 1) * HEAD_DIM)
            value = product(a_ref[...], w_ref[:, here], "NN") + b_ref[:, here]
            if part < 2:
                value = rotate(value, cos[...], low[...], high[...], 1.0)
            out_ref[:, here] = value.astype(BF16)

    table = pl.BlockSpec((unit, 128), lambda j, i, ids: (ids[0] ^ i, 0))
    return call(
        kernel,
        ids,
        (heads, blocks),
        [
            pl.BlockSpec((unit, depth), lambda j, i, ids: (i, 0)),
            pl.BlockSpec((depth, wide), lambda j, i, ids: (0, j)),
            pl.BlockSpec((1, wide), lambda j, i, ids: (0, j)),
            table,
            table,
            table,
        ],
        pl.BlockSpec((unit, wide), lambda j, i, ids: (i, j)),
        jax.ShapeDtypeStruct((rows, heads * wide), BF16),
        (first, weight, bias, *tables),
        cost(2 * rows * depth * heads * wide, 2 * (heads * rows * depth + depth * heads * wide + rows * heads * wide)),
    )


def attend_kernel(ids, mixed, blocks):
    rows, width = mixed.shape
    heads = width // (3 * HEAD_DIM)
    unit = rows // blocks
    scale = HEAD_DIM ** (-0.5)

    def kernel(ids_ref, x_ref, ctx_ref, lse_ref, top_s, total_s, acc_s):
        block = pl.program_id(0)
        me = ids_ref[0]
        here = pl.ds(pl.multiple_of((me ^ block) * unit, unit), unit)

        def step(other, diagonal):
            there = pl.ds(pl.multiple_of((me ^ other) * unit, unit), unit)
            for head in range(heads):
                at = 3 * HEAD_DIM * head
                scores = (
                    product(
                        x_ref[here, at : at + HEAD_DIM],
                        x_ref[there, at + HEAD_DIM : at + 2 * HEAD_DIM],
                        "NT",
                    )
                    * scale
                )
                value = x_ref[there, at + 2 * HEAD_DIM : at + 3 * HEAD_DIM]
                if diagonal:
                    row_at = lax.broadcasted_iota(jnp.int32, scores.shape, 0)
                    col_at = lax.broadcasted_iota(jnp.int32, scores.shape, 1)
                    scores = jnp.where(col_at <= row_at, scores, BIG)
                    top = jnp.max(scores, axis=1, keepdims=True)
                    weight = jnp.exp(scores - top)
                    top_s[head] = top
                    total_s[head] = jnp.sum(weight, axis=1, keepdims=True)
                    acc_s[head] = product(weight.astype(BF16), value, "NN")
                else:
                    before = top_s[head]
                    top = jnp.maximum(before, jnp.max(scores, axis=1, keepdims=True))
                    weight = jnp.exp(scores - top)
                    shrunk = jnp.exp(before - top)
                    top_s[head] = top
                    total_s[head] = total_s[head] * shrunk + jnp.sum(weight, axis=1, keepdims=True)
                    acc_s[head] = acc_s[head] * shrunk + product(weight.astype(BF16), value, "NN")

        step(block, True)

        @pl.loop(0, block)
        def _(other):
            step(other, False)

        for head in range(heads):
            at = HEAD_DIM * head
            ctx_ref[:, at : at + HEAD_DIM] = (acc_s[head] / total_s[head]).astype(BF16)
            log_total = top_s[head] + jnp.log(total_s[head])
            lse_ref[head, 0] = jnp.transpose(jnp.broadcast_to(log_total, (unit, 128)))[:8]

    return call(
        kernel,
        ids,
        (blocks,),
        [pl.BlockSpec((rows, width), lambda b, ids: (0, 0))],
        [
            pl.BlockSpec((unit, heads * HEAD_DIM), lambda b, ids: (ids[0] ^ b, 0)),
            pl.BlockSpec((heads, 1, 8, unit), lambda b, ids: (0, b, 0, 0)),
        ],
        [
            jax.ShapeDtypeStruct((rows, heads * HEAD_DIM), BF16),
            jax.ShapeDtypeStruct((heads, blocks, 8, unit), F32),
        ],
        (mixed,),
        cost(2 * heads * rows * rows * HEAD_DIM, 3 * rows * width, heads * rows * rows // 2),
        [
            pltpu.VMEM((heads, unit, 1), F32),
            pltpu.VMEM((heads, unit, 1), F32),
            pltpu.VMEM((heads, unit, HEAD_DIM), F32),
        ],
    )


def attend_back_kernel(ids, mixed, grad, context, lse, tables, blocks):
    rows, width = mixed.shape
    heads = width // (3 * HEAD_DIM)
    unit = rows // blocks
    scale = HEAD_DIM ** (-0.5)

    def kernel(ids_ref, x_ref, g_ref, c_ref, lse_ref, cos, low, high, out_ref, sum_ref, dk_s, dv_s, dq_s, inner_s):
        turn = pl.program_id(0)
        block = blocks - 1 - turn
        me = ids_ref[0]

        @pl.when(turn == 0)
        def _():
            dk_s[...] = jnp.zeros_like(dk_s)
            dv_s[...] = jnp.zeros_like(dv_s)
            sum_ref[...] = jnp.zeros_like(sum_ref)

        here = pl.ds(pl.multiple_of((me ^ block) * unit, unit), unit)
        for head in range(heads):
            cols = slice(HEAD_DIM * head, HEAD_DIM * (head + 1))
            inner = jnp.sum(g_ref[here, cols].astype(F32) * c_ref[here, cols].astype(F32), axis=1, keepdims=True)
            inner_s[head] = jnp.transpose(jnp.broadcast_to(inner, (unit, 128)))[:8]

        def step(other, diagonal):
            there = pl.ds(pl.multiple_of((me ^ other) * unit, unit), unit)
            for head in range(heads):
                at = 3 * HEAD_DIM * head
                query = x_ref[here, at : at + HEAD_DIM]
                seed = g_ref[here, HEAD_DIM * head : HEAD_DIM * (head + 1)]
                key = x_ref[there, at + HEAD_DIM : at + 2 * HEAD_DIM]
                value = x_ref[there, at + 2 * HEAD_DIM : at + 3 * HEAD_DIM]
                scores = product(key, query, "NT") * scale
                prob = jnp.exp(scores - lse_ref[head, 0][:1])
                if diagonal:
                    key_at = lax.broadcasted_iota(jnp.int32, scores.shape, 0)
                    row_at = lax.broadcasted_iota(jnp.int32, scores.shape, 1)
                    prob = jnp.where(key_at <= row_at, prob, 0.0)
                dprob = product(value, seed, "NT")
                dscore = (prob * (dprob - inner_s[head][:1])).astype(BF16)
                dv_s[head, other] += product(prob.astype(BF16), seed, "NN")
                dk_s[head, other] += product(dscore, query, "NN")
                dquery = product(dscore, key, "TN")
                if diagonal:
                    dq_s[head] = dquery
                else:
                    dq_s[head] += dquery

        step(block, True)

        @pl.loop(0, block)
        def _(other):
            step(other, False)

        for head in range(heads):
            at = 3 * HEAD_DIM * head
            dquery = rotate(dq_s[head] * scale, cos[...], low[...], high[...], -1.0)
            dkey = rotate(dk_s[head, block] * scale, cos[...], low[...], high[...], -1.0)
            for part, value in enumerate((dquery, dkey, dv_s[head, block])):
                cols = slice(at + part * HEAD_DIM, at + (part + 1) * HEAD_DIM)
                rounded = value.astype(BF16)
                out_ref[:, cols] = rounded
                sum_ref[:, cols] += jnp.sum(rounded.astype(F32), axis=0, keepdims=True)

    def whole(cols):
        return pl.BlockSpec((rows, cols), lambda b, ids: (0, 0))

    table = pl.BlockSpec((unit, 128), lambda b, ids: (blocks - 1 - b, 0))
    return call(
        kernel,
        ids,
        (blocks,),
        [
            whole(width),
            whole(heads * HEAD_DIM),
            whole(heads * HEAD_DIM),
            pl.BlockSpec((heads, 1, 8, unit), lambda b, ids: (0, blocks - 1 - b, 0, 0)),
            table,
            table,
            table,
        ],
        [
            pl.BlockSpec((unit, width), lambda b, ids: (ids[0] ^ (blocks - 1 - b), 0)),
            pl.BlockSpec((1, width), lambda b, ids: (0, 0)),
        ],
        [jax.ShapeDtypeStruct((rows, width), BF16), jax.ShapeDtypeStruct((1, width), F32)],
        (mixed, grad, context, lse, *tables),
        cost(5 * heads * rows * rows * HEAD_DIM, 6 * rows * width, heads * rows * rows // 2),
        [
            pltpu.VMEM((heads, blocks, unit, HEAD_DIM), F32),
            pltpu.VMEM((heads, blocks, unit, HEAD_DIM), F32),
            pltpu.VMEM((heads, unit, HEAD_DIM), F32),
            pltpu.VMEM((heads, 8, unit), F32),
        ],
    )


def expand_kernel(ids, second, weight, bias):
    rows, depth = second.shape
    width = weight.shape[1]
    tall, wide = tile_of(rows, 1024), tile_of(width, 1024)
    unit = tile_of(wide, 512)

    def kernel(ids_ref, a_ref, w_ref, b_ref, hidden_ref, slope_ref):
        for part in range(wide // unit):
            here = slice(part * unit, (part + 1) * unit)
            pre = product(a_ref[...], w_ref[:, here], "NN") + b_ref[:, here]
            phi = 0.5 + 0.5 * lax.erf(pre * 0.7071067811865476)
            hidden_ref[:, here] = (pre * phi).astype(BF16)
            slope = phi + pre * (jnp.exp(-0.5 * pre * pre) * 0.3989422804014327)
            slope_ref[:, here] = slope.astype(BF16)

    out = pl.BlockSpec((tall, wide), lambda i, j, ids: (i, j))
    shape = jax.ShapeDtypeStruct((rows, width), BF16)
    return call(
        kernel,
        ids,
        (rows // tall, width // wide),
        [
            pl.BlockSpec((tall, depth), lambda i, j, ids: (i, 0)),
            pl.BlockSpec((depth, wide), lambda i, j, ids: (0, j)),
            pl.BlockSpec((1, wide), lambda i, j, ids: (0, j)),
        ],
        [out, out],
        [shape, shape],
        (second, weight, bias),
        cost(2 * rows * depth * width, 2 * (rows * depth + 2 * depth * width + 2 * rows * width), 2 * rows * width),
    )


def shrink_back_kernel(ids, seed, weight, slope):
    rows, depth = seed.shape
    width = weight.shape[0]
    tall, wide = tile_of(rows, 1024), tile_of(width, 1024)
    unit = tile_of(wide, 512)

    def kernel(ids_ref, a_ref, w_ref, s_ref, out_ref, sum_ref):
        @pl.when(pl.program_id(1) == 0)
        def _():
            sum_ref[...] = jnp.zeros_like(sum_ref)

        for part in range(wide // unit):
            here = slice(part * unit, (part + 1) * unit)
            grad = product(a_ref[...], w_ref[here, :], "NT") * s_ref[:, here].astype(F32)
            rounded = grad.astype(BF16)
            out_ref[:, here] = rounded
            sum_ref[:, here] += jnp.sum(rounded.astype(F32), axis=0, keepdims=True)

    tile = pl.BlockSpec((tall, wide), lambda j, i, ids: (i, j))
    return call(
        kernel,
        ids,
        (width // wide, rows // tall),
        [
            pl.BlockSpec((tall, depth), lambda j, i, ids: (i, 0)),
            pl.BlockSpec((wide, depth), lambda j, i, ids: (j, 0)),
            tile,
        ],
        [tile, pl.BlockSpec((1, wide), lambda j, i, ids: (0, j))],
        [jax.ShapeDtypeStruct((rows, width), BF16), jax.ShapeDtypeStruct((1, width), F32)],
        (seed, weight, slope),
        cost(2 * rows * depth * width, 2 * (2 * rows * depth + depth * width + 2 * rows * width)),
    )


def plain_kernel(ids, left, right, mode):
    rows, depth = left.shape
    width = right.shape[1] if mode == "NN" else right.shape[0]
    tall = tile_of(rows, 512)

    def kernel(ids_ref, a_ref, b_ref, out_ref):
        out_ref[...] = product(a_ref[...], b_ref[...], mode).astype(BF16)

    return call(
        kernel,
        ids,
        (rows // tall,),
        [
            pl.BlockSpec((tall, depth), lambda i, ids: (i, 0)),
            pl.BlockSpec(right.shape, lambda i, ids: (0, 0)),
        ],
        pl.BlockSpec((tall, width), lambda i, ids: (i, 0)),
        jax.ShapeDtypeStruct((rows, width), BF16),
        (left, right),
        cost(2 * rows * depth * width, 2 * (rows * depth + depth * width + rows * width)),
    )


def pair_kernel(ids, left_a, right_a, left_b, right_b, mode, scales, blocks):
    rows = left_a.shape[0]
    width = right_a.shape[1] if mode == "NN" else right_a.shape[0]
    deep_a, deep_b = left_a.shape[1], left_b.shape[1]
    tall, wide = rows // blocks, tile_of(width, 1024)
    unit = tile_of(wide, 512)

    def kernel(ids_ref, a_ref, b_ref, c_ref, d_ref, s_ref, out_ref):
        for part in range(wide // unit):
            here = slice(part * unit, (part + 1) * unit)
            if mode == "NN":
                one = product(a_ref[...], b_ref[:, here], mode)
                two = product(c_ref[...], d_ref[:, here], mode)
            else:
                one = product(a_ref[...], b_ref[here, :], mode) * s_ref[0:1, here]
                two = product(c_ref[...], d_ref[here, :], mode) * s_ref[1:2, here]
            out_ref[:, here] = (one + two).astype(BF16)

    def weight(deep):
        if mode == "NN":
            return pl.BlockSpec((deep, wide), lambda j, i, ids: (0, j))
        return pl.BlockSpec((wide, deep), lambda j, i, ids: (j, 0))

    return call(
        kernel,
        ids,
        (width // wide, blocks),
        [
            pl.BlockSpec((tall, deep_a), lambda j, i, ids: (i, 0)),
            weight(deep_a),
            pl.BlockSpec((tall, deep_b), lambda j, i, ids: (i, 0)),
            weight(deep_b),
            pl.BlockSpec((2, wide), lambda j, i, ids: (0, j)),
        ],
        pl.BlockSpec((tall, wide), lambda j, i, ids: (ids[0] ^ i, j)),
        jax.ShapeDtypeStruct((rows, width), BF16),
        (left_a, right_a, left_b, right_b, scales),
        cost(2 * rows * (deep_a + deep_b) * width, 2 * (2 * rows + width) * (deep_a + deep_b) + 2 * rows * width),
    )


def half_grad_kernel(ids, left, right, mine, added=None):
    rows, depth = left.shape
    width = right.shape[1] // 2
    tall = tile_of(depth, 1024)
    unit = tile_of(width, 512)

    def kernel(ids_ref, a_ref, b_ref, *refs):
        out_ref = refs[-1]
        for part in range(width // unit):
            here = slice(part * unit, (part + 1) * unit)
            value = product(a_ref[...], b_ref[:, here], "TN")
            if added is not None:
                value = value + refs[0][:, here].astype(F32)
            out_ref[:, here] = value.astype(BF16)

    if mine:
        pick = pl.BlockSpec((rows, width), lambda i, ids: (0, ids[1]))
    else:
        pick = pl.BlockSpec((rows, width), lambda i, ids: (0, 1 - ids[1]))
    tile = pl.BlockSpec((tall, width), lambda i, ids: (i, 0))
    extra = [] if added is None else [added]
    return call(
        kernel,
        ids,
        (depth // tall,),
        [pl.BlockSpec((rows, tall), lambda i, ids: (0, i)), pick] + [tile] * len(extra),
        tile,
        jax.ShapeDtypeStruct((depth, width), BF16),
        (left, right, *extra),
        cost(2 * rows * depth * width, 2 * (rows * depth + rows * width + (1 + len(extra)) * depth * width)),
    )


def rotary_tables(length):
    position = jnp.arange(length, dtype=F32)[:, None]
    lane = jnp.arange(128)
    half = ROTARY // 2
    frequency = 10000.0 ** (-2.0 * (lane % half).astype(F32) / ROTARY)
    angles = position * frequency[None, :]
    sine = jnp.sin(angles)
    return (
        jnp.where(lane < ROTARY, jnp.cos(angles), 1.0),
        jnp.where(lane < half, -sine, 0.0),
        jnp.where((lane >= half) & (lane < ROTARY), sine, 0.0),
    )


def flip(value, axis, bit, size):
    return lax.ppermute(value, axis, [(i, i ^ bit) for i in range(size)])


def sum_over(value, axis, size):
    bit = 1
    while bit < size:
        value = value + flip(value, axis, bit, size)
        bit *= 2
    return value


def gather_rows(rows, size):
    if size != 4:
        return [rows] + [flip(rows, "tensor", k, size) for k in range(1, size)]
    half = rows.shape[0] // 2
    one = flip(rows, "tensor", 1, size)
    two = flip(rows, "tensor", 2, size)
    upper = flip(two[:half], "tensor", 1, size)
    lower = flip(one[half:], "tensor", 2, size)
    return [rows, one, two, upper, lower]


def swap_core(value, size):
    return flip(value, "dp", 1, size)


def line_sum(value, chip, core, size):
    chips = size // 2
    depth, width = value.shape
    chunks = value.reshape(chips, depth // chips, width)

    def chunk(index):
        return lax.dynamic_index_in_dim(chunks, jnp.clip(index, 0, chips - 1), 0, keepdims=False)

    up = down = None
    for step in range(1, chips):
        send_up, send_down = chunk(chips - step + chip), chunk(chip + step - chips)
        if step > 1:
            send_up = (send_up.astype(F32) + up.astype(F32)).astype(BF16)
            send_down = (send_down.astype(F32) + down.astype(F32)).astype(BF16)
        pairs = [(i, i + 1) for i in range(step)]
        up = lax.ppermute(send_up, "dp", [(2 * a + k, 2 * b + k) for a, b in pairs for k in (0, 1)])
        pairs = [(chips - 1 - i, chips - 2 - i) for i in range(step)]
        down = lax.ppermute(send_down, "dp", [(2 * a + k, 2 * b + k) for a, b in pairs for k in (0, 1)])
    total = chunk(chip).astype(F32)
    if chips > 1:
        total = total + up.astype(F32) + down.astype(F32)
    total = total.astype(BF16).reshape(2, depth // size, width)
    mine = lax.dynamic_index_in_dim(total, core, 0, keepdims=False)
    other = swap_core(lax.dynamic_index_in_dim(total, 1 - core, 0, keepdims=False), size)
    low = jnp.where(core == 0, mine, other)
    high = jnp.where(core == 0, other, mine)
    return jnp.concatenate([low, high], axis=1).astype(F32)


def body(
    layer_input,
    cotangent,
    firstgain,
    firstbias,
    secondgain,
    secondbias,
    project,
    projbias,
    merging,
    mergebias,
    expand,
    expandbias,
    shrink,
    shrinkbias,
):
    n_dp, n_tensor = lax.axis_size("dp"), lax.axis_size("tensor")
    dp_at, tensor_at = lax.axis_index("dp"), lax.axis_index("tensor")
    chip, core = dp_at // 2, dp_at % 2
    ids = jnp.stack([tensor_at, core]).astype(jnp.int32)
    own_count, width = layer_input.shape
    group_count = own_count * n_tensor
    assert group_count == LENGTH
    depth = width // n_dp
    heads = project.shape[1]
    mixed_width = heads * 3 * HEAD_DIM
    hidden_width = expand.shape[1]

    rows_pieces = gather_rows(layer_input, n_tensor)
    own_project = project.reshape(depth, mixed_width)
    w_project = lax.all_gather(own_project, "dp", axis=0, tiled=True)
    w_merge = lax.all_gather(merging, "dp", axis=1, tiled=True)
    w_expand = lax.all_gather(expand, "dp", axis=0, tiled=True)
    w_shrink = lax.all_gather(shrink, "dp", axis=1, tiled=True)
    seed_pieces = gather_rows(cotangent, n_tensor)

    packed = jnp.concatenate(
        [firstgain, firstbias, secondgain, secondbias, mergebias, shrinkbias, expandbias, projbias.reshape(-1)]
    )
    slots = jnp.where(jnp.arange(n_dp)[:, None] == dp_at, packed[None, :], jnp.zeros((), BF16))
    slots = sum_over(slots, "dp", n_dp).astype(F32)
    vectors = jnp.transpose(slots[:, : 6 * depth].reshape(n_dp, 6, depth), (1, 0, 2)).reshape(6, width)
    at = 6 * depth
    part = hidden_width // n_dp
    b_expand = slots[:, at : at + part].reshape(1, hidden_width)
    at += part
    b_project = jnp.transpose(slots[:, at:].reshape(n_dp, heads, -1), (1, 0, 2)).reshape(1, mixed_width)

    tables = rotary_tables(LENGTH)
    unit = own_count // 2
    first, second = norm_kernel(ids, rows_pieces, vectors, unit)
    seed = jnp.concatenate(seed_pieces, axis=0)

    mixed = mixed_kernel(ids, first, w_project, b_project, tables, n_tensor)
    context, lse = attend_kernel(ids, mixed, n_tensor)
    cgrad = plain_kernel(ids, seed, w_merge, "NT")
    mgrad, mixed_sum = attend_back_kernel(ids, mixed, cgrad, context, lse, tables, n_tensor)
    hidden, slope = expand_kernel(ids, second, w_expand, b_expand)
    pgrad, expand_sum = shrink_back_kernel(ids, seed, w_shrink, slope)

    def grad_of(left, right):
        other = half_grad_kernel(ids, left, right, False)
        came = swap_core(other, n_dp)
        return line_sum(half_grad_kernel(ids, left, right, True, came), chip, core, n_dp)

    merging_grad = jnp.transpose(grad_of(seed, context))
    project_grad = grad_of(first, mgrad)
    shrink_grad = jnp.transpose(grad_of(seed, hidden))
    expand_grad = grad_of(second, pgrad)

    ones = jnp.ones((2, width), F32)
    branches = pair_kernel(ids, context, w_merge, hidden, w_shrink, "NN", ones, n_tensor)
    summed = lax.psum_scatter(branches, "tensor", scatter_dimension=0, tiled=True).astype(F32)
    layer_output = (layer_input.astype(F32) + summed + (vectors[4] + vectors[5])).astype(BF16)

    gains = jnp.stack([vectors[0], vectors[2]])
    back = pair_kernel(ids, mgrad, w_project, pgrad, w_expand, "NT", gains, n_tensor)
    back = lax.psum_scatter(back, "tensor", scatter_dimension=0, tiled=True).astype(F32)
    data = layer_input.astype(F32)
    centre = data - jnp.mean(data, axis=-1, keepdims=True)
    rstd = lax.rsqrt(jnp.mean(centre * centre, axis=-1, keepdims=True) + EPSILON)
    scaled = centre * rstd
    inner = jnp.mean(back * scaled, axis=-1, keepdims=True)
    seed_own = cotangent.astype(F32)
    input_grad = seed_own + rstd * (back - jnp.mean(back, axis=-1, keepdims=True) - scaled * inner)

    seed_sum = sum_over(jnp.sum(seed_own, axis=0, keepdims=True), "tensor", n_tensor)
    sums = sum_over(jnp.concatenate([seed_sum, expand_sum, mixed_sum], axis=1), "dp", n_dp)
    seed_sum = lax.dynamic_slice_in_dim(sums[0, :width], dp_at * depth, depth)
    expand_sum = sums[0, width : width + hidden_width]
    mixed_sum = sums[0, width + hidden_width :]
    expandbias_grad = lax.dynamic_slice_in_dim(expand_sum, dp_at * part, part)
    piece = projbias.shape[1]
    projbias_grad = lax.dynamic_slice_in_dim(mixed_sum.reshape(heads, -1), dp_at * piece, piece, axis=1)

    def norm_grads(weight, weight_grad, total, gain, bias):
        weight = weight.astype(F32)
        gain, bias = gain.astype(F32), bias.astype(F32)
        scaled_sum = jnp.sum(weight * (weight_grad - bias[:, None] * total[None, :]), axis=1) / gain
        return scaled_sum, jnp.sum(weight * total[None, :], axis=1)

    norms = jnp.stack(
        norm_grads(own_project, project_grad, mixed_sum, firstgain, firstbias)
        + norm_grads(expand, expand_grad, expand_sum, secondgain, secondbias)
    )
    norms = sum_over(norms, "tensor", n_tensor)
    return (
        layer_output,
        input_grad,
        norms[0],
        norms[1],
        norms[2],
        norms[3],
        project_grad.reshape(project.shape),
        projbias_grad,
        merging_grad,
        seed_sum,
        expand_grad,
        expandbias_grad,
        shrink_grad,
        seed_sum,
    )


def solution(mesh):
    specs = (
        P(("dp", "tensor"), None),
        P(("dp", "tensor"), None),
        P("dp"),
        P("dp"),
        P("dp"),
        P("dp"),
        P("dp", "tensor", None),
        P("tensor", "dp"),
        P("tensor", "dp"),
        P("dp"),
        P("dp", "tensor"),
        P(("tensor", "dp")),
        P("tensor", "dp"),
        P("dp"),
    )
    return jax.shard_map(body, mesh=mesh, in_specs=specs, out_specs=specs, check_vma=False)
```

time: 1100 us -> 748 us (0.68)
  waiting for transfers between devices: 517 us -> 165 us
  matrix products: 332 us -> 0 us
  Pallas kernels: 0 us -> 322 us
  starting transfers between devices: 0.56 us -> 128 us
  blocking collectives: 61.3 us -> 0 us
  other arithmetic: 108 us -> 55.7 us
    dot_general x36 -> x0, matrix products: 332 us -> none  [the longest x1 63.4 us: body(): jnp.einsum('sd,fd->sf', seed_rows, w_shrink, preferred_element_type=jnp.f...]
    pallas_call x0 -> x17, Pallas kernels: none -> 322 us  [call(): pl.pallas_call(kernel, grid_spec=pltpu.PrefetchScalarGridSpec(num_scalar_...]
    reduce_scatter x7 -> x2, waiting for transfers between devices: 301 us -> 0.02 us  [the longest x1 0.02 us: body(): lax.psum_scatter(back, 'tensor', scatter_dimension=0, tiled=True)]
    all_gather x6 -> x4, waiting for transfers between devices: 214 us -> 11.9 us  [the longest x1 11.9 us: body(): w_shrink = lax.all_gather(shrink, 'dp', axis=1, tiled=True)]
    ppermute x0 -> x50, waiting for transfers between devices: none -> 152 us  [the longest x26 85.9 us: flip(): return lax.ppermute(value, axis, [(i, i ^ bit) for i in range(size)])]
    ppermute x0 -> x50, starting transfers between devices: none -> 128 us  [the longest x12 74.8 us: line_sum(): lax.ppermute(send_up, 'dp', [(2 * a + k, 2 * b + k) for a, b in pairs for...]
    all_gather x3 -> x0, blocking collectives: 36.1 us -> none  [the longest x1 14 us: body(): lax.all_gather(vectors, 'dp', axis=1, tiled=True)]
    convert_element_type x15 -> x21, other arithmetic: 54.8 us -> 28.2 us  [the longest x8 13.3 us: line_sum(): send_up = (send_up.astype(F32) + up.astype(F32)).astype(BF16)]
  transfers between devices with their start and end apart: 14 -> 56, of which waited for: 8 -> 20; matrix products, arithmetic and copies ran while one was open for 44% -> 13% of each run, Pallas kernels for 0% -> 35%
where the time goes in v1:
time: 748 us; the launch traced here: 738 us
  Pallas kernels  322 us (43%)
  waiting for transfers between devices  165 us (22%)
  starting transfers between devices  128 us (17%)
  other arithmetic  55.7 us (7%)
  local copies, waits for them, and re-layouts  50.3 us (7%)
  between operations  15.5 us (2%)
    pallas_call x17, Pallas kernels, call(): pl.pallas_call(kernel, grid_spec=pltpu.PrefetchScalarGridSpec(num_scalar_...  322 us
    ppermute x26, waiting for transfers between devices, flip(): return lax.ppermute(value, axis, [(i, i ^ bit) for i in range(size)])  85.9 us
    ppermute x12, starting transfers between devices, line_sum(): lax.ppermute(send_up, 'dp', [(2 * a + k, 2 * b + k) for a, b in pairs for...  74.8 us
    ppermute x12, waiting for transfers between devices, line_sum(): lax.ppermute(send_up, 'dp', [(2 * a + k, 2 * b + k) for a, b in pairs for...  55.5 us
    ppermute x26, starting transfers between devices, flip(): return lax.ppermute(value, axis, [(i, i ^ bit) for i in range(size)])  39.7 us
    unnamed x96, local copies, waits for them, and re-layouts  25.5 us
  transfers between devices with their start and end apart: 56, of which 20 were waited for; matrix products, arithmetic and copies ran while one was open for 13% of the time, Pallas kernels for 35%

profile of v1, /device:TPU:0, one launch (start us, length us, event | category | flops | bytes accessed | tf_op | source)
XLA Modules:
  0.0 737.7 jit_solution(7038115136604454160)
XLA Ops:
  38.1 23.2 %collective-permute-done.1.refs_2_ = bf16[512,2048]{1,0:T(8,128)(2,1)} collective-permute-done((bf16[512,2048]{1,0:T(8,128)(2,1)S(1)}, bf16[512,2048]{1,0:T(8,128)(2,1)}, u32[]{:S(2)}, u32[]{:S(2)}) %collective-permute-start.1) | collective-permute-done | bytes 2097184 | tf_op jit(solution)/shard_map/ppermute | solution.py:496
  69.5 36.7 %collective-permute-done.8 = bf16[512,2048]{1,0:T(8,128)(2,1)} collective-permute-done((bf16[512,2048]{1,0:T(8,128)(2,1)}, bf16[512,2048]{1,0:T(8,128)(2,1)}, u32[]{:S(2)}, u32[]{:S(2)}) %collective-permute-start.8) | collective-permute-done | bytes 2097184 | tf_op jit(solution)/shard_map/ppermute | solution.py:496
  132.0 15.2 %shard_map.245 = (bf16[2048,2048]{1,0:T(8,128)(2,1)}, bf16[2048,2048]{1,0:T(8,128)(2,1)}) custom-call(s32[2]{0:T(128)} %pad_add_fusion.ids_ref, bf16[512,2048]{1,0:T(8,128)(2,1)} %refs_0_.1, bf16[512,2048]{1,0:T(8,128)(2,1)} %collective-permute-done.refs_1_, bf16[512,2048]{1,0:T(8,128)(2,1)} %collective-permute-done.1.refs_2_, bf16[256,2048]{1,0:T(8,128)(2,1)} %copy-done.11, ...), custom_call_target="tpu_custom_call" | custom-call | flops 50331648 | bytes 25165824 | tf_op jit(solution)/shard_map/pallas_call | solution.py:45
  155.1 9.6 %shard_map.250.g_ref = bf16[2048,512]{1,0:T(8,128)(2,1)} custom-call(s32[2]{0:T(128)} %pad_add_fusion.ids_ref, bf16[2048,2048]{1,0:T(8,128)(2,1)} %constant_dynamic-update-slice_fusion.a_ref, bf16[512,2048]{1,0:T(8,128)(2,1)} %all-gather.7.cloned.1.call-done.b_ref), custom_call_target="tpu_custom_call" | custom-call | flops 4294967296 | bytes 12582912 | tf_op jit(solution)/shard_map/pallas_call | solution.py:45
  164.7 21.4 %shard_map.246.x_ref = bf16[2048,1536]{1,0:T(8,128)(2,1)} custom-call(s32[2]{0:T(128)} %pad_add_fusion.ids_ref, bf16[2048,2048]{1,0:T(8,128)(2,1)} %get-tuple-element.24.a_ref, bf16[2048,1536]{1,0:T(8,128)(2,1)} %all-gather.5.cloned.1.call-done.w_ref.b_ref, f32[1,1536]{1,0:T(1,128)} %reshape.196.b_ref, f32[2048,128]{1,0:T(8,128)} %get-tuple-element.112.cos, ...), custom_call_target="tpu_custom_call" | custom-call | flops 12884901888 | bytes 29360128 | tf_op jit(solution)/shard_map/pallas_call | solution.py:45
  186.1 22.8 %shard_map.247 = (bf16[2048,512]{1,0:T(8,128)(2,1)}, f32[2,4,8,512]{3,2,1,0:T(8,128)}) custom-call(s32[2]{0:T(128)} %pad_add_fusion.ids_ref, bf16[2048,1536]{1,0:T(8,128)(2,1)} %shard_map.246.x_ref), custom_call_target="tpu_custom_call" | custom-call | flops 4294967296 | bytes 9437184 | tf_op jit(solution)/shard_map/pallas_call | solution.py:45
  208.9 26.3 %shard_map.251 = (bf16[2048,1536]{1,0:T(8,128)(2,1)}, f32[1,1536]{1,0:T(1,128)}) custom-call(s32[2]{0:T(128)} %pad_add_fusion.ids_ref, bf16[2048,1536]{1,0:T(8,128)(2,1)} %shard_map.246.x_ref, bf16[2048,512]{1,0:T(8,128)(2,1)} %shard_map.250.g_ref, bf16[2048,512]{1,0:T(8,128)(2,1)} %get-tuple-element.25.a_ref.c_ref.b_ref, ...), custom_call_target="tpu_custom_call" | custom-call | flops 10737418240 | bytes 18874368 | tf_op jit(solution)/shard_map/pallas_call | solution.py:45
  235.2 30.1 %shard_map.248 = (bf16[2048,2048]{1,0:T(8,128)(2,1)}, bf16[2048,2048]{1,0:T(8,128)(2,1)}) custom-call(s32[2]{0:T(128)} %pad_add_fusion.ids_ref, bf16[2048,2048]{1,0:T(8,128)(2,1)} %get-tuple-element.26.a_ref, bf16[2048,2048]{1,0:T(8,128)(2,1)} %all-gather.9.cloned.1.call-done.w_ref.d_ref, f32[1,2048]{1,0:T(1,128)} %bitcast.201), custom_call_target="tpu_custom_call" | custom-call | flops 17179869184 | bytes 41943040 | tf_op jit(solution)/shard_map/pallas_call | solution.py:45
  265.3 11.9 %all-gather.11.cloned.1.call-done.d_ref.w_ref = bf16[2048,2048]{1,0:T(8,128)(2,1)} async-done(((bf16[2048,256]{1,0:T(8,128)(2,1)}), bf16[2048,2048]{1,0:T(8,128)(2,1)}) %all-gather.11.cloned.1.call-update) | async-done | bytes 8388624 | tf_op jit(solution)/shard_map/all_gather | solution.py:584
  277.1 25.1 %shard_map.252 = (bf16[2048,2048]{1,0:T(8,128)(2,1)}, f32[1,2048]{1,0:T(1,128)}) custom-call(s32[2]{0:T(128)} %pad_add_fusion.ids_ref, bf16[2048,2048]{1,0:T(8,128)(2,1)} %constant_dynamic-update-slice_fusion.a_ref, bf16[2048,2048]{1,0:T(8,128)(2,1)} %all-gather.11.cloned.1.call-done.d_ref.w_ref, bf16[2048,2048]{1,0:T(8,128)(2,1)} %get-tuple-element.30.s_ref), custom_call_target="tpu_custom_call" | custom-call | flops 17179869184 | bytes 41943040 | tf_op jit(solution)/shard_map/pallas_call | solution.py:45
  302.3 38.7 %shard_map.253 = bf16[2048,2048]{1,0:T(8,128)(2,1)} custom-call(s32[2]{0:T(128)} %pad_add_fusion.ids_ref, bf16[2048,1536]{1,0:T(8,128)(2,1)} %get-tuple-element.29.a_ref.b_ref, bf16[2048,1536]{1,0:T(8,128)(2,1)} %all-gather.5.cloned.1.call-done.w_ref.b_ref, bf16[2048,2048]{1,0:T(8,128)(2,1)} %get-tuple-element.31.c_ref.b_ref, ...), custom_call_target="tpu_custom_call" | custom-call | flops 30064771072 | bytes 52428800 | tf_op jit(solution)/shard_map/pallas_call | solution.py:45
  341.6 29.8 %shard_map.249 = bf16[2048,2048]{1,0:T(8,128)(2,1)} custom-call(s32[2]{0:T(128)} %pad_add_fusion.ids_ref, bf16[2048,512]{1,0:T(8,128)(2,1)} %get-tuple-element.25.a_ref.c_ref.b_ref, bf16[512,2048]{1,0:T(8,128)(2,1)} %all-gather.7.cloned.1.call-done.b_ref, bf16[2048,2048]{1,0:T(8,128)(2,1)} %get-tuple-element.27.c_ref.b_ref, ...), custom_call_target="tpu_custom_call" | custom-call | flops 21474836480 | bytes 39845888 | tf_op jit(solution)/shard_map/pallas_call | solution.py:45
  371.5 14.2 %shard_map.254 = bf16[2048,768]{1,0:T(8,128)(2,1)} custom-call(s32[2]{0:T(128)} %pad_add_fusion.ids_ref, bf16[2048,2048]{1,0:T(8,128)(2,1)} %get-tuple-element.24.a_ref, bf16[2048,1536]{1,0:T(8,128)(2,1)} %get-tuple-element.29.a_ref.b_ref), custom_call_target="tpu_custom_call" | custom-call | flops 6442450944 | bytes 14680064 | tf_op jit(solution)/shard_map/pallas_call | solution.py:45
  386.1 14.7 %shard_map.260 = bf16[2048,1024]{1,0:T(8,128)(2,1)} custom-call(s32[2]{0:T(128)} %pad_add_fusion.ids_ref, bf16[2048,2048]{1,0:T(8,128)(2,1)} %constant_dynamic-update-slice_fusion.a_ref, bf16[2048,2048]{1,0:T(8,128)(2,1)} %get-tuple-element.27.c_ref.b_ref), custom_call_target="tpu_custom_call" | custom-call | flops 8589934592 | bytes 16777216 | tf_op jit(solution)/shard_map/pallas_call | solution.py:45
  400.9 14.5 %shard_map.256 = bf16[2048,1024]{1,0:T(8,128)(2,1)} custom-call(s32[2]{0:T(128)} %pad_add_fusion.ids_ref, bf16[2048,2048]{1,0:T(8,128)(2,1)} %get-tuple-element.26.a_ref, bf16[2048,2048]{1,0:T(8,128)(2,1)} %get-tuple-element.31.c_ref.b_ref), custom_call_target="tpu_custom_call" | custom-call | flops 8589934592 | bytes 16777216 | tf_op jit(solution)/shard_map/pallas_call | solution.py:45
  422.9 14.7 %shard_map.255 = bf16[2048,768]{1,0:T(8,128)(2,1)} custom-call(s32[2]{0:T(128)} %pad_add_fusion.ids_ref, bf16[2048,2048]{1,0:T(8,128)(2,1)} %get-tuple-element.24.a_ref, bf16[2048,1536]{1,0:T(8,128)(2,1)} %get-tuple-element.29.a_ref.b_ref, bf16[2048,768]{1,0:T(8,128)(2,1)} %collective-permute-done.11.refs_0_), custom_call_target="tpu_custom_call" | custom-call | flops 6442450944 | bytes 17825792 | tf_op jit(solution)/shard_map/pallas_call | solution.py:45
  469.0 15.6 %shard_map.261 = bf16[2048,1024]{1,0:T(8,128)(2,1)} custom-call(s32[2]{0:T(128)} %pad_add_fusion.ids_ref, bf16[2048,2048]{1,0:T(8,128)(2,1)} %constant_dynamic-update-slice_fusion.a_ref, bf16[2048,2048]{1,0:T(8,128)(2,1)} %get-tuple-element.27.c_ref.b_ref, bf16[2048,1024]{1,0:T(8,128)(2,1)} %collective-permute-done.42.refs_0_), custom_call_target="tpu_custom_call" | custom-call | flops 8589934592 | bytes 20971520 | tf_op jit(solution)/shard_map/pallas_call | solution.py:45
  490.0 15.5 %shard_map.257 = bf16[2048,1024]{1,0:T(8,128)(2,1)} custom-call(s32[2]{0:T(128)} %pad_add_fusion.ids_ref, bf16[2048,2048]{1,0:T(8,128)(2,1)} %get-tuple-element.26.a_ref, bf16[2048,2048]{1,0:T(8,128)(2,1)} %get-tuple-element.31.c_ref.b_ref, bf16[2048,1024]{1,0:T(8,128)(2,1)} %collective-permute-done.24.refs_0_), custom_call_target="tpu_custom_call" | custom-call | flops 8589934592 | bytes 20971520 | tf_op jit(solution)/shard_map/pallas_call | solution.py:45
  520.3 20.5 %collective-permute-done.36 = bf16[512,256]{1,0:T(8,128)(2,1)S(1)} collective-permute-done((bf16[512,256]{1,0:T(8,128)(2,1)S(1)}, bf16[512,256]{1,0:T(8,128)(2,1)S(1)}, u32[]{:S(2)}, u32[]{:S(2)}) %collective-permute-start.36) | collective-permute-done | bytes 262176 | tf_op jit(solution)/shard_map/ppermute | solution.py:537
  542.9 10.8 %collective-permute-start.26 = (bf16[512,1024]{1,0:T(8,128)(2,1)S(1)}, bf16[512,1024]{1,0:T(8,128)(2,1)S(1)}, u32[]{:S(2)}, u32[]{:S(2)}) collective-permute-start(bf16[512,1024]{1,0:T(8,128)(2,1)S(1)} %fusion.19), channel_id=1, source_target_pairs={{0,8},{4,12},{8,16},{12,20},{1,9},{5,13},{9,17},{13,21},{2,10},{6,... | collective-permute-start | bytes 3145736 | tf_op jit(solution)/shard_map/ppermute | solution.py:537
  572.5 13.2 %collective-permute-done.26 = bf16[512,1024]{1,0:T(8,128)(2,1)S(1)} collective-permute-done((bf16[512,1024]{1,0:T(8,128)(2,1)S(1)}, bf16[512,1024]{1,0:T(8,128)(2,1)S(1)}, u32[]{:S(2)}, u32[]{:S(2)}) %collective-permute-start.26) | collective-permute-done | bytes 1048608 | tf_op jit(solution)/shard_map/ppermute | solution.py:537
  616.7 30.2 %collective-permute-start.27 = (bf16[512,1024]{1,0:T(8,128)(2,1)}, bf16[512,1024]{1,0:T(8,128)(2,1)}, u32[]{:S(2)}, u32[]{:S(2)}) collective-permute-start(bf16[512,1024]{1,0:T(8,128)(2,1)} %get-tuple-element.72), channel_id=1, source_target_pairs={{0,8},{4,12},{8,16},{12,20},{16,24},{20,28},{1,9},{5,13},{9,17},{1... | collective-permute-start | bytes 3145736 | tf_op jit(solution)/shard_map/ppermute | solution.py:537
  664.5 10.1 %collective-permute-done.30 = bf16[512,1024]{1,0:T(8,128)(2,1)} collective-permute-done((bf16[512,1024]{1,0:T(8,128)(2,1)}, bf16[512,1024]{1,0:T(8,128)(2,1)}, u32[]{:S(2)}, u32[]{:S(2)}) %collective-permute-start.30) | collective-permute-done | bytes 1048608 | tf_op jit(solution)/shard_map/ppermute | solution.py:539
  696.9 12.1 %collective-permute-start.22 = (f32[1,5632]{1,0:T(1,128)S(1)}, f32[1,5632]{1,0:T(1,128)S(1)}, u32[]{:S(2)}, u32[]{:S(2)}) collective-permute-start(f32[1,5632]{1,0:T(1,128)S(1)} %fusion.50), channel_id=1, source_target_pairs={{0,8},{4,12},{8,0},{12,4},{16,24},{20,28},{24,16},{28,20},{1,9},{5... | collective-permute-start | bytes 67592 | tf_op jit(solution)/shard_map/ppermute | solution.py:496
  (295 shorter events, 245.2 us)
Async XLA Ops:
  7.2 147.9 %all-gather.7.cloned.1.call-start = ((), (), s32[]{:S(2)}) async-start(), calls=%async_computation.3 | async-start | bytes 2359296 | tf_op jit(solution)/shard_map/all_gather | solution.py:582
  7.9 156.8 %all-gather.5.cloned.1.call-start = ((), (), s32[]{:S(2)}) async-start(), calls=%async_computation.2 | async-start | bytes 7077888 | tf_op jit(solution)/shard_map/all_gather | solution.py:581
  10.3 224.9 %all-gather.9.cloned.1.call-start = ((), (), s32[]{:S(2)}) async-start(), calls=%async_computation.4 | async-start | bytes 9437184 | tf_op jit(solution)/shard_map/all_gather | solution.py:583
  11.1 266.1 %all-gather.11.cloned.1.call-start = ((), (), s32[]{:S(2)}) async-start(), calls=%async_computation.5 | async-start | bytes 9437184 | tf_op jit(solution)/shard_map/all_gather | solution.py:584
  11.6 665.4 %reduce-scatter.5.cloned.1.call-start = ((), (), s32[]{:S(2)}) async-start(), calls=%async_computation.7 | async-start | bytes 10485760 | tf_op jit(solution)/shard_map/reduce_scatter | solution.py:628
  11.7 49.6 %collective-permute-start.1 = (bf16[512,2048]{1,0:T(8,128)(2,1)S(1)}, bf16[512,2048]{1,0:T(8,128)(2,1)}, u32[]{:S(2)}, u32[]{:S(2)}) collective-permute-start(bf16[512,2048]{1,0:T(8,128)(2,1)S(1)} %copy-done), channel_id=1, source_target_pairs={{0,2},{1,3},{2,0},{3,1},{4,6},{5,7},{6,4},{7,5},{8,10},{9,11},{10,... | collective-permute-start | bytes 6291464 | tf_op jit(solution)/shard_map/ppermute | solution.py:496
  14.7 50.9 %collective-permute-start = (bf16[512,2048]{1,0:T(8,128)(2,1)S(1)}, bf16[512,2048]{1,0:T(8,128)(2,1)}, u32[]{:S(2)}, u32[]{:S(2)}) collective-permute-start(bf16[512,2048]{1,0:T(8,128)(2,1)S(1)} %copy-done), channel_id=1, source_target_pairs={{0,1},{1,0},{2,3},{3,2},{4,5},{5,4},{6,7},{7,6},{8,9},{9,8},{10,11... | collective-permute-start | bytes 6291464 | tf_op jit(solution)/shard_map/ppermute | solution.py:496
  16.2 94.9 %collective-permute-start.7 = (bf16[512,2048]{1,0:T(8,128)(2,1)}, bf16[512,2048]{1,0:T(8,128)(2,1)}, u32[]{:S(2)}, u32[]{:S(2)}) collective-permute-start(bf16[512,2048]{1,0:T(8,128)(2,1)} %param.15), channel_id=1, source_target_pairs={{0,1},{1,0},{2,3},{3,2},{4,5},{5,4},{6,7},{7,6},{8,9},{9,8},{10,11... | collective-permute-start | bytes 6291464 | tf_op jit(solution)/shard_map/ppermute | solution.py:496
  16.8 89.5 %collective-permute-start.8 = (bf16[512,2048]{1,0:T(8,128)(2,1)}, bf16[512,2048]{1,0:T(8,128)(2,1)}, u32[]{:S(2)}, u32[]{:S(2)}) collective-permute-start(bf16[512,2048]{1,0:T(8,128)(2,1)} %param.15), channel_id=1, source_target_pairs={{0,2},{1,3},{2,0},{3,1},{4,6},{5,7},{6,4},{7,5},{8,10},{9,11},{10,... | collective-permute-start | bytes 6291464 | tf_op jit(solution)/shard_map/ppermute | solution.py:496
  63.6 67.1 %collective-permute-start.2 = (bf16[256,2048]{1,0:T(8,128)(2,1)}, bf16[256,2048]{1,0:T(8,128)(2,1)S(1)}, u32[]{:S(2)}, u32[]{:S(2)}) collective-permute-start(bf16[256,2048]{1,0:T(8,128)(2,1)} %slice.82), channel_id=1, source_target_pairs={{0,1},{1,0},{2,3},{3,2},{4,5},{5,4},{6,7},{7,6},{8,9},{9,8},{10,11... | collective-permute-start | bytes 3145736 | tf_op jit(solution)/shard_map/ppermute | solution.py:496
  68.0 62.7 %collective-permute-start.3 = (bf16[256,2048]{1,0:T(8,128)(2,1)}, bf16[256,2048]{1,0:T(8,128)(2,1)S(1)}, u32[]{:S(2)}, u32[]{:S(2)}) collective-permute-start(bf16[256,2048]{1,0:T(8,128)(2,1)} %slice.83), channel_id=1, source_target_pairs={{0,2},{1,3},{2,0},{3,1},{4,6},{5,7},{6,4},{7,5},{8,10},{9,11},{10,... | collective-permute-start | bytes 3145736 | tf_op jit(solution)/shard_map/ppermute | solution.py:496
  341.0 340.6 %reduce-scatter.3.cloned.1.call-start = ((), (), s32[]{:S(2)}) async-start(), calls=%async_computation.6 | async-start | bytes 10485760 | tf_op jit(solution)/shard_map/reduce_scatter | solution.py:623
  400.9 62.9 %collective-permute-start.42 = (bf16[2048,1024]{1,0:T(8,128)(2,1)}, bf16[2048,1024]{1,0:T(8,128)(2,1)}, u32[]{:S(2)}, u32[]{:S(2)}) collective-permute-start(bf16[2048,1024]{1,0:T(8,128)(2,1)} %shard_map.260), channel_id=1, source_target_pairs={{0,4},{4,0},{8,12},{12,8},{16,20},{20,16},{24,28},{28,24},{1,5},{5... | collective-permute-start | bytes 12582920 | tf_op jit(solution)/shard_map/ppermute | solution.py:496
  415.4 72.2 %collective-permute-start.24 = (bf16[2048,1024]{1,0:T(8,128)(2,1)}, bf16[2048,1024]{1,0:T(8,128)(2,1)}, u32[]{:S(2)}, u32[]{:S(2)}) collective-permute-start(bf16[2048,1024]{1,0:T(8,128)(2,1)} %shard_map.256), channel_id=1, source_target_pairs={{0,4},{4,0},{8,12},{12,8},{16,20},{20,16},{24,28},{28,24},{1,5},{5... | collective-permute-start | bytes 12582920 | tf_op jit(solution)/shard_map/ppermute | solution.py:496
  452.3 55.0 %collective-permute-start.35 = (bf16[512,256]{1,0:T(8,128)(2,1)S(1)}, bf16[512,256]{1,0:T(8,128)(2,1)}, u32[]{:S(2)}, u32[]{:S(2)}) collective-permute-start(bf16[512,256]{1,0:T(8,128)(2,1)S(1)} %get-tuple-element.91), channel_id=1, source_target_pairs={{0,8},{4,12},{1,9},{5,13},{2,10},{6,14},{3,11},{7,15}} | collective-permute-start | bytes 786440 | tf_op jit(solution)/shard_map/ppermute | solution.py:537
  454.3 63.5 %collective-permute-start.38 = (bf16[512,256]{1,0:T(8,128)(2,1)S(1)}, bf16[512,256]{1,0:T(8,128)(2,1)S(1)}, u32[]{:S(2)}, u32[]{:S(2)}) collective-permute-start(bf16[512,256]{1,0:T(8,128)(2,1)S(1)} %get-tuple-element.92), channel_id=1, source_target_pairs={{24,16},{28,20},{25,17},{29,21},{26,18},{30,22},{27,19},{31,23}} | collective-permute-start | bytes 786440 | tf_op jit(solution)/shard_map/ppermute | solution.py:539
  459.9 49.9 %collective-permute-start.15 = (bf16[512,768]{1,0:T(8,128)(2,1)}, bf16[512,768]{1,0:T(8,128)(2,1)}, u32[]{:S(2)}, u32[]{:S(2)}) collective-permute-start(bf16[512,768]{1,0:T(8,128)(2,1)} %get-tuple-element.79), channel_id=1, source_target_pairs={{24,16},{28,20},{25,17},{29,21},{26,18},{30,22},{27,19},{31,23}} | collective-permute-start | bytes 2359304 | tf_op jit(solution)/shard_map/ppermute | solution.py:539
  463.7 47.7 %collective-permute-start.13 = (bf16[512,768]{1,0:T(8,128)(2,1)}, bf16[512,768]{1,0:T(8,128)(2,1)}, u32[]{:S(2)}, u32[]{:S(2)}) collective-permute-start(bf16[512,768]{1,0:T(8,128)(2,1)} %fusion.27), channel_id=1, source_target_pairs={{0,8},{4,12},{8,16},{12,20},{1,9},{5,13},{9,17},{13,21},{2,10},{6,... | collective-permute-start | bytes 2359304 | tf_op jit(solution)/shard_map/ppermute | solution.py:537
  514.9 47.3 %collective-permute-start.46 = (bf16[512,1024]{1,0:T(8,128)(2,1)S(1)}, bf16[512,1024]{1,0:T(8,128)(2,1)S(1)}, u32[]{:S(2)}, u32[]{:S(2)}) collective-permute-start(bf16[512,1024]{1,0:T(8,128)(2,1)S(1)} %copy-done.10), channel_id=1, source_target_pairs={{24,16},{28,20},{25,17},{29,21},{26,18},{30,22},{27,19},{31,23}} | collective-permute-start | bytes 3145736 | tf_op jit(solution)/shard_map/ppermute | solution.py:539
  517.8 45.7 %collective-permute-start.44 = (bf16[512,1024]{1,0:T(8,128)(2,1)S(1)}, bf16[512,1024]{1,0:T(8,128)(2,1)S(1)}, u32[]{:S(2)}, u32[]{:S(2)}) collective-permute-start(bf16[512,1024]{1,0:T(8,128)(2,1)S(1)} %fusion.13), channel_id=1, source_target_pairs={{0,8},{4,12},{8,16},{12,20},{1,9},{5,13},{9,17},{13,21},{2,10},{6,... | collective-permute-start | bytes 3145736 | tf_op jit(solution)/shard_map/ppermute | solution.py:537
  563.5 43.5 %collective-permute-start.14 = (bf16[512,768]{1,0:T(8,128)(2,1)}, bf16[512,768]{1,0:T(8,128)(2,1)}, u32[]{:S(2)}, u32[]{:S(2)}) collective-permute-start(bf16[512,768]{1,0:T(8,128)(2,1)} %get-tuple-element.76), channel_id=1, source_target_pairs={{0,8},{4,12},{8,16},{12,20},{16,24},{20,28},{1,9},{5,13},{9,17},{1... | collective-permute-start | bytes 2359304 | tf_op jit(solution)/shard_map/ppermute | solution.py:537
  597.8 52.1 %collective-permute-start.41 = (bf16[256,256]{0,1:T(8,128)(2,1)S(1)}, bf16[256,256]{0,1:T(8,128)(2,1)S(1)}, u32[]{:S(2)}, u32[]{:S(2)}) collective-permute-start(bf16[256,256]{0,1:T(8,128)(2,1)S(1)} %bitcast.181), channel_id=1, source_target_pairs={{0,4},{4,0},{8,12},{12,8},{16,20},{20,16},{24,28},{28,24},{1,5},{5... | collective-permute-start | bytes 393224 | tf_op jit(solution)/shard_map/ppermute | solution.py:496
  608.9 45.6 %collective-permute-start.45 = (bf16[512,1024]{1,0:T(8,128)(2,1)}, bf16[512,1024]{1,0:T(8,128)(2,1)S(1)}, u32[]{:S(2)}, u32[]{:S(2)}) collective-permute-start(bf16[512,1024]{1,0:T(8,128)(2,1)} %get-tuple-element.68), channel_id=1, source_target_pairs={{0,8},{4,12},{8,16},{12,20},{16,24},{20,28},{1,9},{5,13},{9,17},{1... | collective-permute-start | bytes 3145736 | tf_op jit(solution)/shard_map/ppermute | solution.py:537
  616.7 47.8 %collective-permute-start.27 = (bf16[512,1024]{1,0:T(8,128)(2,1)}, bf16[512,1024]{1,0:T(8,128)(2,1)}, u32[]{:S(2)}, u32[]{:S(2)}) collective-permute-start(bf16[512,1024]{1,0:T(8,128)(2,1)} %get-tuple-element.72), channel_id=1, source_target_pairs={{0,8},{4,12},{8,16},{12,20},{16,24},{20,28},{1,9},{5,13},{9,17},{1... | collective-permute-start | bytes 3145736 | tf_op jit(solution)/shard_map/ppermute | solution.py:537
  (66 other events, 1271.2 us)
Sparse Core Ops, SparseCore 0:
  9.6 35.3 all-gather.6
  46.7 65.5 all-gather.4
  113.9 80.6 all-gather.8
  196.1 81.0 all-gather.10
  341.1 84.5 reduce-scatter.4
  428.9 86.3 reduce-scatter.2

commit v2 on v1

--- a/solution.py
+++ b/solution.py
@@ -41,23 +41,28 @@
     return best
 
 
-def call(kernel, ids, grid, in_specs, out_specs, out_shape, args, cost_of, scratch=()):
+def call(kernel, ids, grid, in_specs, out_specs, out_shape, args, cost_of, scratch=(), after=()):
+    count = len(args)
+
+    def run(ids_ref, *refs):
+        kernel(ids_ref, *refs[:count], *refs[count + len(after) :])
+
     return pl.pallas_call(
-        kernel,
+        run,
         grid_spec=pltpu.PrefetchScalarGridSpec(
             num_scalar_prefetch=1,
             grid=grid,
-            in_specs=in_specs,
+            in_specs=list(in_specs) + [pl.BlockSpec(memory_space=pl.ANY)] * len(after),
             out_specs=out_specs,
             scratch_shapes=list(scratch),
         ),
         out_shape=out_shape,
         compiler_params=params(),
         cost_estimate=cost_of,
-    )(ids, *args)
-
-
-def norm_kernel(ids, pieces, vectors, unit):
+    )(ids, *args, *after)
+
+
+def norm_kernel(ids, pieces, vectors, unit, after=()):
     rows = sum(piece.shape[0] for piece in pieces)
     width = pieces[0].shape[1]
     starts = []
@@ -94,6 +99,7 @@
         [shape, shape],
         (*pieces, vectors),
         cost(12 * rows * width, 6 * rows * width),
+        after=after,
     )
 
 
@@ -106,7 +112,7 @@
     return jnp.concatenate([turned, block[:, 128:]], axis=1)
 
 
-def mixed_kernel(ids, first, weight, bias, tables, blocks):
+def mixed_kernel(ids, first, weight, bias, tables, blocks, after=()):
     rows, depth = first.shape
     heads = weight.shape[1] // (3 * HEAD_DIM)
     unit = rows // blocks
@@ -137,10 +143,11 @@
         jax.ShapeDtypeStruct((rows, heads * wide), BF16),
         (first, weight, bias, *tables),
         cost(2 * rows * depth * heads * wide, 2 * (heads * rows * depth + depth * heads * wide + rows * heads * wide)),
-    )
-
-
-def attend_kernel(ids, mixed, blocks):
+        after=after,
+    )
+
+
+def attend_kernel(ids, mixed, blocks, after=()):
     rows, width = mixed.shape
     heads = width // (3 * HEAD_DIM)
     unit = rows // blocks
@@ -214,10 +221,11 @@
             pltpu.VMEM((heads, unit, 1), F32),
             pltpu.VMEM((heads, unit, HEAD_DIM), F32),
         ],
-    )
-
-
-def attend_back_kernel(ids, mixed, grad, context, lse, tables, blocks):
+        after=after,
+    )
+
+
+def attend_back_kernel(ids, mixed, grad, context, lse, tables, blocks, after=()):
     rows, width = mixed.shape
     heads = width // (3 * HEAD_DIM)
     unit = rows // blocks
@@ -310,10 +318,11 @@
             pltpu.VMEM((heads, unit, HEAD_DIM), F32),
             pltpu.VMEM((heads, 8, unit), F32),
         ],
-    )
-
-
-def expand_kernel(ids, second, weight, bias):
+        after=after,
+    )
+
+
+def expand_kernel(ids, second, weight, bias, after=()):
     rows, depth = second.shape
     width = weight.shape[1]
     tall, wide = tile_of(rows, 1024), tile_of(width, 1024)
@@ -343,10 +352,42 @@
         [shape, shape],
         (second, weight, bias),
         cost(2 * rows * depth * width, 2 * (rows * depth + 2 * depth * width + 2 * rows * width), 2 * rows * width),
-    )
-
-
-def shrink_back_kernel(ids, seed, weight, slope):
+        after=after,
+    )
+
+
+def stack_kernel(ids, pieces, unit, after=()):
+    rows = sum(piece.shape[0] for piece in pieces)
+    width = pieces[0].shape[1]
+    ends = [0]
+    for piece in pieces:
+        ends.append(ends[-1] + piece.shape[0] // unit)
+
+    def kernel(ids_ref, *refs):
+        step = pl.program_id(0)
+        for low, high, piece_ref in zip(ends, ends[1:], refs):
+
+            @pl.when((step >= low) & (step < high))
+            def _(piece_ref=piece_ref):
+                refs[-1][...] = piece_ref[...]
+
+    def spec(low, high):
+        return pl.BlockSpec((unit, width), lambda i, ids: (jnp.clip(i - low, 0, high - low - 1), 0))
+
+    return call(
+        kernel,
+        ids,
+        (rows // unit,),
+        [spec(low, high) for low, high in zip(ends, ends[1:])],
+        pl.BlockSpec((unit, width), lambda i, ids: (i, 0)),
+        jax.ShapeDtypeStruct((rows, width), BF16),
+        tuple(pieces),
+        cost(0, 4 * rows * width),
+        after=after,
+    )
+
+
+def shrink_back_kernel(ids, seed, weight, slope, after=()):
     rows, depth = seed.shape
     width = weight.shape[0]
     tall, wide = tile_of(rows, 1024), tile_of(width, 1024)
@@ -378,103 +419,199 @@
         [jax.ShapeDtypeStruct((rows, width), BF16), jax.ShapeDtypeStruct((1, width), F32)],
         (seed, weight, slope),
         cost(2 * rows * depth * width, 2 * (2 * rows * depth + depth * width + 2 * rows * width)),
-    )
-
-
-def plain_kernel(ids, left, right, mode):
+        after=after,
+    )
+
+
+def halves_kernel(ids, left, mine, other, after=()):
     rows, depth = left.shape
-    width = right.shape[1] if mode == "NN" else right.shape[0]
+    width = mine.shape[1]
     tall = tile_of(rows, 512)
 
-    def kernel(ids_ref, a_ref, b_ref, out_ref):
-        out_ref[...] = product(a_ref[...], b_ref[...], mode).astype(BF16)
-
+    def kernel(ids_ref, a_ref, m_ref, o_ref, out_ref):
+        @pl.when(ids_ref[1] == 0)
+        def _():
+            out_ref[:, :width] = product(a_ref[...], m_ref[...], "NN").astype(BF16)
+            out_ref[:, width:] = product(a_ref[...], o_ref[...], "NN").astype(BF16)
+
+        @pl.when(ids_ref[1] != 0)
+        def _():
+            out_ref[:, :width] = product(a_ref[...], o_ref[...], "NN").astype(BF16)
+            out_ref[:, width:] = product(a_ref[...], m_ref[...], "NN").astype(BF16)
+
+    whole = pl.BlockSpec((depth, width), lambda i, ids: (0, 0))
     return call(
         kernel,
         ids,
         (rows // tall,),
-        [
-            pl.BlockSpec((tall, depth), lambda i, ids: (i, 0)),
-            pl.BlockSpec(right.shape, lambda i, ids: (0, 0)),
-        ],
-        pl.BlockSpec((tall, width), lambda i, ids: (i, 0)),
-        jax.ShapeDtypeStruct((rows, width), BF16),
-        (left, right),
-        cost(2 * rows * depth * width, 2 * (rows * depth + depth * width + rows * width)),
-    )
-
-
-def pair_kernel(ids, left_a, right_a, left_b, right_b, mode, scales, blocks):
-    rows = left_a.shape[0]
-    width = right_a.shape[1] if mode == "NN" else right_a.shape[0]
-    deep_a, deep_b = left_a.shape[1], left_b.shape[1]
-    tall, wide = rows // blocks, tile_of(width, 1024)
+        [pl.BlockSpec((tall, depth), lambda i, ids: (i, 0)), whole, whole],
+        pl.BlockSpec((tall, 2 * width), lambda i, ids: (i, 0)),
+        jax.ShapeDtypeStruct((rows, 2 * width), BF16),
+        (left, mine, other),
+        cost(4 * rows * depth * width, 2 * (rows * depth + 2 * depth * width + 2 * rows * width)),
+        after=after,
+    )
+
+
+def branches_kernel(ids, context, mine, other, hidden, shrink, blocks, after=()):
+    rows, deep_b = hidden.shape
+    depth, half = mine.shape
+    tall, wide = rows // blocks, tile_of(depth, 1024)
     unit = tile_of(wide, 512)
 
-    def kernel(ids_ref, a_ref, b_ref, c_ref, d_ref, s_ref, out_ref):
+    def kernel(ids_ref, a_ref, b_ref, m_ref, o_ref, h_ref, s_ref, out_ref):
         for part in range(wide // unit):
             here = slice(part * unit, (part + 1) * unit)
-            if mode == "NN":
-                one = product(a_ref[...], b_ref[:, here], mode)
-                two = product(c_ref[...], d_ref[:, here], mode)
-            else:
-                one = product(a_ref[...], b_ref[here, :], mode) * s_ref[0:1, here]
-                two = product(c_ref[...], d_ref[here, :], mode) * s_ref[1:2, here]
-            out_ref[:, here] = (one + two).astype(BF16)
-
-    def weight(deep):
-        if mode == "NN":
-            return pl.BlockSpec((deep, wide), lambda j, i, ids: (0, j))
-        return pl.BlockSpec((wide, deep), lambda j, i, ids: (j, 0))
-
-    return call(
-        kernel,
-        ids,
-        (width // wide, blocks),
-        [
-            pl.BlockSpec((tall, deep_a), lambda j, i, ids: (i, 0)),
-            weight(deep_a),
+            value = product(h_ref[...], s_ref[:, here], "NN")
+            value = value + product(a_ref[...], m_ref[here, :], "NT")
+            value = value + product(b_ref[...], o_ref[here, :], "NT")
+            out_ref[:, here] = value.astype(BF16)
+
+    return call(
+        kernel,
+        ids,
+        (depth // wide, blocks),
+        [
+            pl.BlockSpec((tall, half), lambda j, i, ids: (i, ids[1])),
+            pl.BlockSpec((tall, half), lambda j, i, ids: (i, 1 - ids[1])),
+            pl.BlockSpec((wide, half), lambda j, i, ids: (j, 0)),
+            pl.BlockSpec((wide, half), lambda j, i, ids: (j, 0)),
             pl.BlockSpec((tall, deep_b), lambda j, i, ids: (i, 0)),
-            weight(deep_b),
-            pl.BlockSpec((2, wide), lambda j, i, ids: (0, j)),
+            pl.BlockSpec((deep_b, wide), lambda j, i, ids: (0, j)),
         ],
         pl.BlockSpec((tall, wide), lambda j, i, ids: (ids[0] ^ i, j)),
+        jax.ShapeDtypeStruct((rows, depth), BF16),
+        (context, context, mine, other, hidden, shrink),
+        cost(2 * rows * (2 * half + deep_b) * depth, 2 * (2 * rows + depth) * (2 * half + deep_b) + 2 * rows * depth),
+        after=after,
+    )
+
+
+def back_kernel(ids, left_a, right_a, left_b, right_b, scales, block, blocks, after=()):
+    rows = left_a.shape[0] // blocks
+    width = right_a.shape[0]
+    deep_a, deep_b = left_a.shape[1], left_b.shape[1]
+    wide = tile_of(width, 512)
+
+    def kernel(ids_ref, a_ref, b_ref, c_ref, d_ref, s_ref, out_ref):
+        one = product(a_ref[...], b_ref[...], "NT") * s_ref[0:1, :]
+        two = product(c_ref[...], d_ref[...], "NT") * s_ref[1:2, :]
+        out_ref[...] = (one + two).astype(BF16)
+
+    return call(
+        kernel,
+        ids,
+        (width // wide,),
+        [
+            pl.BlockSpec((rows, deep_a), lambda j, ids: (block, 0)),
+            pl.BlockSpec((wide, deep_a), lambda j, ids: (j, 0)),
+            pl.BlockSpec((rows, deep_b), lambda j, ids: (block, 0)),
+            pl.BlockSpec((wide, deep_b), lambda j, ids: (j, 0)),
+            pl.BlockSpec((2, wide), lambda j, ids: (0, j)),
+        ],
+        pl.BlockSpec((rows, wide), lambda j, ids: (0, j)),
         jax.ShapeDtypeStruct((rows, width), BF16),
         (left_a, right_a, left_b, right_b, scales),
-        cost(2 * rows * (deep_a + deep_b) * width, 2 * (2 * rows + width) * (deep_a + deep_b) + 2 * rows * width),
-    )
-
-
-def half_grad_kernel(ids, left, right, mine, added=None):
+        cost(2 * rows * (deep_a + deep_b) * width, 2 * (rows + width) * (deep_a + deep_b) + 2 * rows * width),
+        after=after,
+    )
+
+
+def grad_kernel(ids, left, right, weight=None, total=None, after=()):
     rows, depth = left.shape
     width = right.shape[1] // 2
-    tall = tile_of(depth, 1024)
+    tall = tile_of(depth, 512)
+    steps = depth // tall
     unit = tile_of(width, 512)
+    summed = weight is not None
 
     def kernel(ids_ref, a_ref, b_ref, *refs):
-        out_ref = refs[-1]
-        for part in range(width // unit):
-            here = slice(part * unit, (part + 1) * unit)
-            value = product(a_ref[...], b_ref[:, here], "TN")
-            if added is not None:
-                value = value + refs[0][:, here].astype(F32)
-            out_ref[:, here] = value.astype(BF16)
-
-    if mine:
-        pick = pl.BlockSpec((rows, width), lambda i, ids: (0, ids[1]))
-    else:
-        pick = pl.BlockSpec((rows, width), lambda i, ids: (0, 1 - ids[1]))
-    tile = pl.BlockSpec((tall, width), lambda i, ids: (i, 0))
-    extra = [] if added is None else [added]
-    return call(
-        kernel,
-        ids,
-        (depth // tall,),
-        [pl.BlockSpec((rows, tall), lambda i, ids: (0, i)), pick] + [tile] * len(extra),
-        tile,
-        jax.ShapeDtypeStruct((depth, width), BF16),
-        (left, right, *extra),
-        cost(2 * rows * depth * width, 2 * (rows * depth + rows * width + (1 + len(extra)) * depth * width)),
+        half = pl.program_id(0)
+        other_ref, mine_ref = refs[2:4] if summed else refs
+        at = pl.ds(pl.multiple_of(pl.program_id(1) * tall, tall), tall)
+        for turn, out_ref in ((0, other_ref), (1, mine_ref)):
+
+            @pl.when(half == turn)
+            def _(turn=turn, out_ref=out_ref):
+                gain = jnp.zeros((tall, 128), F32)
+                shift = jnp.zeros((tall, 128), F32)
+                for part in range(width // unit):
+                    here = slice(part * unit, (part + 1) * unit)
+                    value = product(a_ref[...], b_ref[:, here], "TN")
+                    out_ref[:, here] = value.astype(BF16)
+                    if summed:
+                        held = refs[0][:, here].astype(F32)
+                        one, two = held * value, held * refs[1][:, here]
+                        for lane in range(0, unit, 128):
+                            gain = gain + one[:, lane : lane + 128]
+                            shift = shift + two[:, lane : lane + 128]
+                if summed:
+                    if turn == 0:
+                        refs[4][at, :] = gain
+                        refs[5][at, :] = shift
+                    else:
+                        refs[4][at, :] += gain
+                        refs[5][at, :] += shift
+
+    def column(half, ids):
+        return ids[1] ^ 1 ^ half
+
+    in_specs = [
+        pl.BlockSpec((rows, tall), lambda half, i, ids: (0, i)),
+        pl.BlockSpec((rows, width), lambda half, i, ids: (0, column(half, ids))),
+    ]
+    out_specs = [
+        pl.BlockSpec((tall, width), lambda half, i, ids: (jnp.where(half == 0, i, steps - 1), 0)),
+        pl.BlockSpec((tall, width), lambda half, i, ids: (jnp.where(half == 0, 0, i), 0)),
+    ]
+    out_shape = [jax.ShapeDtypeStruct((depth, width), BF16)] * 2
+    args = (left, right)
+    if summed:
+        args += (weight, total)
+        in_specs += [
+            pl.BlockSpec((tall, width), lambda half, i, ids: (i, column(half, ids))),
+            pl.BlockSpec((1, width), lambda half, i, ids: (0, column(half, ids))),
+        ]
+        out_specs += [pl.BlockSpec((depth, 128), lambda half, i, ids: (0, 0))] * 2
+        out_shape += [jax.ShapeDtypeStruct((depth, 128), F32)] * 2
+    return call(
+        kernel,
+        ids,
+        (2, steps),
+        in_specs,
+        out_specs,
+        out_shape,
+        args,
+        cost(4 * rows * depth * width, 2 * (2 * rows * depth + 2 * rows * width + 4 * depth * width)),
+        after=after,
+    )
+
+
+def add_kernel(ids, arrays, places, count, rows, after=()):
+    width = arrays[0].shape[1]
+
+    def kernel(ids_ref, *refs):
+        total = refs[0][...].astype(F32)
+        for ref in refs[1:-1]:
+            total = total + ref[...].astype(F32)
+        refs[-1][...] = total.astype(BF16)
+
+    cut = max(1, rows // 256)
+    unit = rows // cut
+
+    def spec(place):
+        return pl.BlockSpec((unit, width), lambda i, j, ids: (place(i, ids) * cut + j, 0))
+
+    return call(
+        kernel,
+        ids,
+        (count, cut),
+        [spec(place) for place in places],
+        spec(lambda i, ids: i),
+        jax.ShapeDtypeStruct((count * rows, width), BF16),
+        tuple(arrays),
+        cost(len(arrays) * count * rows * width, 2 * (len(arrays) + 1) * count * rows * width),
+        after=after,
     )
 
 
@@ -519,33 +656,57 @@
     return flip(value, "dp", 1, size)
 
 
-def line_sum(value, chip, core, size):
-    chips = size // 2
-    depth, width = value.shape
-    chunks = value.reshape(chips, depth // chips, width)
-
-    def chunk(index):
-        return lax.dynamic_index_in_dim(chunks, jnp.clip(index, 0, chips - 1), 0, keepdims=False)
-
-    up = down = None
-    for step in range(1, chips):
-        send_up, send_down = chunk(chips - step + chip), chunk(chip + step - chips)
-        if step > 1:
-            send_up = (send_up.astype(F32) + up.astype(F32)).astype(BF16)
-            send_down = (send_down.astype(F32) + down.astype(F32)).astype(BF16)
-        pairs = [(i, i + 1) for i in range(step)]
-        up = lax.ppermute(send_up, "dp", [(2 * a + k, 2 * b + k) for a, b in pairs for k in (0, 1)])
-        pairs = [(chips - 1 - i, chips - 2 - i) for i in range(step)]
-        down = lax.ppermute(send_down, "dp", [(2 * a + k, 2 * b + k) for a, b in pairs for k in (0, 1)])
-    total = chunk(chip).astype(F32)
-    if chips > 1:
-        total = total + up.astype(F32) + down.astype(F32)
-    total = total.astype(BF16).reshape(2, depth // size, width)
-    mine = lax.dynamic_index_in_dim(total, core, 0, keepdims=False)
-    other = swap_core(lax.dynamic_index_in_dim(total, 1 - core, 0, keepdims=False), size)
-    low = jnp.where(core == 0, mine, other)
-    high = jnp.where(core == 0, other, mine)
-    return jnp.concatenate([low, high], axis=1).astype(F32)
+class LineSum:
+    def __init__(self, ids, first, mine, size):
+        self.ids, self.size = ids, size
+        self.chips = size // 2
+        self.rows = mine.shape[0] // self.chips
+        self.bit = 1
+        self.parts = [(mine, lambda i, ids: i), (swap_core(first, size), lambda i, ids: i)]
+
+    def add(self, count, place, after):
+        places = [lambda i, ids, held=held: held(place(i, ids), ids) for _, held in self.parts]
+        return add_kernel(self.ids, [array for array, _ in self.parts], places, count, self.rows, after)
+
+    def step(self, after=()):
+        count = self.chips // (2 * self.bit)
+        at = 1 + self.bit.bit_length()
+        sent = self.add(count, lambda i, ids: 2 * i + 1 - ids[at], after)
+        came = flip(sent, "dp", 2 * self.bit, self.size)
+        self.parts = [
+            (array, lambda i, ids, held=held, at=at: held(2 * i + ids[at], ids)) for array, held in self.parts
+        ]
+        self.parts.append((came, lambda i, ids: i))
+        self.bit *= 2
+        return sent
+
+    def finish(self, core, after=()):
+        total = self.add(1, lambda i, ids: i, after)
+        halves = total.reshape(2, self.rows // 2, total.shape[1])
+        mine = lax.dynamic_index_in_dim(halves, core, 0, keepdims=False)
+        other = swap_core(lax.dynamic_index_in_dim(halves, 1 - core, 0, keepdims=False), self.size)
+        low = jnp.where(core == 0, mine, other)
+        high = jnp.where(core == 0, other, mine)
+        return total, jnp.concatenate([low, high], axis=1).astype(F32)
+
+
+def line_gather(shard, chip, core, size):
+    depth, width = shard.shape
+    halves = shard.reshape(depth, 2, width // 2)
+    mine = lax.dynamic_index_in_dim(halves, core, 1, keepdims=False)
+    came = swap_core(lax.dynamic_index_in_dim(halves, 1 - core, 1, keepdims=False), size)
+    value = jnp.where(core == 0, jnp.stack([mine, came]), jnp.stack([came, mine]))
+    value = value.reshape(1, 2 * depth, width // 2)
+    bit, done = size // 4, 1
+    while bit >= 1:
+        other = flip(value, "dp", 2 * bit, size)
+        here = (chip // bit) % 2
+        value = jnp.where(here == 0, jnp.stack([value, other], axis=1), jnp.stack([other, value], axis=1))
+        done *= 2
+        value = value.reshape(done, 2 * depth, width // 2)
+        bit //= 2
+    value = value.reshape(size * depth, width // 2)
+    return value, swap_core(value, size)
 
 
 def body(
@@ -567,7 +728,8 @@
     n_dp, n_tensor = lax.axis_size("dp"), lax.axis_size("tensor")
     dp_at, tensor_at = lax.axis_index("dp"), lax.axis_index("tensor")
     chip, core = dp_at // 2, dp_at % 2
-    ids = jnp.stack([tensor_at, core]).astype(jnp.int32)
+    bits = [(chip >> bit) & 1 for bit in range((n_dp // 2).bit_length() - 1)]
+    ids = jnp.stack([tensor_at, core, *bits]).astype(jnp.int32)
     own_count, width = layer_input.shape
     group_count = own_count * n_tensor
     assert group_count == LENGTH
@@ -576,13 +738,15 @@
     mixed_width = heads * 3 * HEAD_DIM
     hidden_width = expand.shape[1]
 
+    unit = own_count // 2
     rows_pieces = gather_rows(layer_input, n_tensor)
     own_project = project.reshape(depth, mixed_width)
     w_project = lax.all_gather(own_project, "dp", axis=0, tiled=True)
-    w_merge = lax.all_gather(merging, "dp", axis=1, tiled=True)
     w_expand = lax.all_gather(expand, "dp", axis=0, tiled=True)
     w_shrink = lax.all_gather(shrink, "dp", axis=1, tiled=True)
-    seed_pieces = gather_rows(cotangent, n_tensor)
+    merge_mine, merge_other = line_gather(jnp.transpose(merging), chip, core, n_dp)
+    later = stack_kernel(ids, [cotangent], unit, after=tuple(rows_pieces[1:]))
+    seed_pieces = gather_rows(later, n_tensor)
 
     packed = jnp.concatenate(
         [firstgain, firstbias, secondgain, secondbias, mergebias, shrinkbias, expandbias, projbias.reshape(-1)]
@@ -597,35 +761,49 @@
     b_project = jnp.transpose(slots[:, at:].reshape(n_dp, heads, -1), (1, 0, 2)).reshape(1, mixed_width)
 
     tables = rotary_tables(LENGTH)
-    unit = own_count // 2
     first, second = norm_kernel(ids, rows_pieces, vectors, unit)
-    seed = jnp.concatenate(seed_pieces, axis=0)
-
     mixed = mixed_kernel(ids, first, w_project, b_project, tables, n_tensor)
     context, lse = attend_kernel(ids, mixed, n_tensor)
-    cgrad = plain_kernel(ids, seed, w_merge, "NT")
+    seed = stack_kernel(ids, seed_pieces, unit, after=(context,))
+    merge_a, merge_b = grad_kernel(ids, seed, context)
+    merge_sum = LineSum(ids, merge_a, merge_b, n_dp)
+    hidden, slope = expand_kernel(ids, second, w_expand, b_expand, after=(merge_b,))
+    last = merge_sum.step((hidden,))
+    shrink_a, shrink_b = grad_kernel(ids, seed, hidden, after=(last,))
+    shrink_sum = LineSum(ids, shrink_a, shrink_b, n_dp)
+    cgrad = halves_kernel(ids, seed, merge_mine, merge_other, after=(shrink_b,))
     mgrad, mixed_sum = attend_back_kernel(ids, mixed, cgrad, context, lse, tables, n_tensor)
-    hidden, slope = expand_kernel(ids, second, w_expand, b_expand)
-    pgrad, expand_sum = shrink_back_kernel(ids, seed, w_shrink, slope)
-
-    def grad_of(left, right):
-        other = half_grad_kernel(ids, left, right, False)
-        came = swap_core(other, n_dp)
-        return line_sum(half_grad_kernel(ids, left, right, True, came), chip, core, n_dp)
-
-    merging_grad = jnp.transpose(grad_of(seed, context))
-    project_grad = grad_of(first, mgrad)
-    shrink_grad = jnp.transpose(grad_of(seed, hidden))
-    expand_grad = grad_of(second, pgrad)
-
-    ones = jnp.ones((2, width), F32)
-    branches = pair_kernel(ids, context, w_merge, hidden, w_shrink, "NN", ones, n_tensor)
+    last = shrink_sum.step((mgrad,))
+    last = merge_sum.step((last,))
+    pgrad, expand_sum = shrink_back_kernel(ids, seed, w_shrink, slope, after=(last,))
+    expand_a, expand_b, gain_two, bias_two = grad_kernel(ids, second, pgrad, w_expand, expand_sum)
+    expand_line = LineSum(ids, expand_a, expand_b, n_dp)
+    last = shrink_sum.step((expand_b,))
+    last, merging_grad = merge_sum.finish(core, (last,))
+    branches = branches_kernel(ids, context, merge_mine, merge_other, hidden, w_shrink, n_tensor, after=(last,))
+    last = expand_line.step((branches,))
+    project_a, project_b, gain_one, bias_one = grad_kernel(ids, first, mgrad, w_project, mixed_sum, after=(last,))
+    project_line = LineSum(ids, project_a, project_b, n_dp)
+    gains = jnp.stack([vectors[0], vectors[2]])
+    last, shrink_grad = shrink_sum.finish(core, (project_b,))
+    back = []
+    for block in reversed(range(n_tensor)):
+        last = back_kernel(ids, mgrad, w_project, pgrad, w_expand, gains, block, n_tensor, after=(last,))
+        back.append(last if block == 0 else flip(last, "tensor", block, n_tensor))
+        if block == n_tensor - 1:
+            last = project_line.step((last,))
+        if block == n_tensor - 2:
+            last = expand_line.step((last,))
+    last = project_line.step((last,))
+    last, expand_grad = expand_line.finish(core, (last,))
+    last, project_grad = project_line.finish(core, (last,))
+    merging_grad = jnp.transpose(merging_grad)
+    shrink_grad = jnp.transpose(shrink_grad)
+    back = sum(value.astype(F32) for value in back)
+
     summed = lax.psum_scatter(branches, "tensor", scatter_dimension=0, tiled=True).astype(F32)
     layer_output = (layer_input.astype(F32) + summed + (vectors[4] + vectors[5])).astype(BF16)
 
-    gains = jnp.stack([vectors[0], vectors[2]])
-    back = pair_kernel(ids, mgrad, w_project, pgrad, w_expand, "NT", gains, n_tensor)
-    back = lax.psum_scatter(back, "tensor", scatter_dimension=0, tiled=True).astype(F32)
     data = layer_input.astype(F32)
     centre = data - jnp.mean(data, axis=-1, keepdims=True)
     rstd = lax.rsqrt(jnp.mean(centre * centre, axis=-1, keepdims=True) + EPSILON)
@@ -634,33 +812,27 @@
     seed_own = cotangent.astype(F32)
     input_grad = seed_own + rstd * (back - jnp.mean(back, axis=-1, keepdims=True) - scaled * inner)
 
-    seed_sum = sum_over(jnp.sum(seed_own, axis=0, keepdims=True), "tensor", n_tensor)
-    sums = sum_over(jnp.concatenate([seed_sum, expand_sum, mixed_sum], axis=1), "dp", n_dp)
-    seed_sum = lax.dynamic_slice_in_dim(sums[0, :width], dp_at * depth, depth)
-    expand_sum = sums[0, width : width + hidden_width]
-    mixed_sum = sums[0, width + hidden_width :]
+    sums = jnp.stack(
+        [jnp.sum(seed_own, axis=0)] + [jnp.sum(value, axis=1) for value in (gain_one, bias_one, gain_two, bias_two)]
+    )
+    sums = sum_over(sums, "tensor", n_tensor).reshape(1, -1)
+    sums = sum_over(jnp.concatenate([sums, expand_sum, mixed_sum], axis=1), "dp", n_dp)[0]
+    norms = lax.dynamic_slice_in_dim(sums[: 5 * width].reshape(5, width), dp_at * depth, depth, axis=1)
+    seed_sum, gain_one, bias_one, gain_two, bias_two = norms
+    gain_one = (gain_one - firstbias.astype(F32) * bias_one) / firstgain.astype(F32)
+    gain_two = (gain_two - secondbias.astype(F32) * bias_two) / secondgain.astype(F32)
+    expand_sum = sums[5 * width : 5 * width + hidden_width]
+    mixed_sum = sums[5 * width + hidden_width :]
     expandbias_grad = lax.dynamic_slice_in_dim(expand_sum, dp_at * part, part)
     piece = projbias.shape[1]
     projbias_grad = lax.dynamic_slice_in_dim(mixed_sum.reshape(heads, -1), dp_at * piece, piece, axis=1)
-
-    def norm_grads(weight, weight_grad, total, gain, bias):
-        weight = weight.astype(F32)
-        gain, bias = gain.astype(F32), bias.astype(F32)
-        scaled_sum = jnp.sum(weight * (weight_grad - bias[:, None] * total[None, :]), axis=1) / gain
-        return scaled_sum, jnp.sum(weight * total[None, :], axis=1)
-
-    norms = jnp.stack(
-        norm_grads(own_project, project_grad, mixed_sum, firstgain, firstbias)
-        + norm_grads(expand, expand_grad, expand_sum, secondgain, secondbias)
-    )
-    norms = sum_over(norms, "tensor", n_tensor)
     return (
         layer_output,
         input_grad,
-        norms[0],
-        norms[1],
-        norms[2],
-        norms[3],
+        gain_one,
+        bias_one,
+        gain_two,
+        bias_two,
         project_grad.reshape(project.shape),
         projbias_grad,
         merging_grad,

time: 748 us -> 743 us (level)
  starting transfers between devices: 128 us -> 35.9 us
  Pallas kernels: 322 us -> 387 us
  waiting for transfers between devices: 165 us -> 222 us
  other arithmetic: 55.7 us -> 34.2 us
  local copies, waits for them, and re-layouts: 50.3 us -> 39 us
    ppermute x26 -> x39, waiting for transfers between devices: 85.9 us -> 221 us  [flip(): return lax.ppermute(value, axis, [(i, i ^ bit) for i in range(size)])]
    ppermute x24 -> x0, starting transfers between devices: 88.5 us -> none  [the longest x12 74.8 us: line_sum(): lax.ppermute(send_up, 'dp', [(2 * a + k, 2 * b + k) for a, b in pairs for...]
    ppermute x24 -> x0, waiting for transfers between devices: 65.6 us -> none  [the longest x12 55.5 us: line_sum(): lax.ppermute(send_up, 'dp', [(2 * a + k, 2 * b + k) for a, b in pairs for...]
    pallas_call x17 -> x30, Pallas kernels: 322 us -> 387 us  [call(): pl.pallas_call(run, grid_spec=pltpu.PrefetchScalarGridSpec(num_scalar_pre...]
    convert_element_type x20 -> x2, other arithmetic: 28.1 us -> 0.26 us  [finish(): return (total, jnp.concatenate([low, high], axis=1).astype(F32))]
    all_gather x1, waiting for transfers between devices: 11.9 us -> 0.01 us  [body(): w_shrink = lax.all_gather(shrink, 'dp', axis=1, tiled=True)]
    dynamic_slice x4 -> x12, local copies, waits for them, and re-layouts: 1.02 us -> 10.3 us  [the longest x6 5.32 us: finish(): mine = lax.dynamic_index_in_dim(halves, core, 0, keepdims=False)]
    unnamed x96 -> x102, local copies, waits for them, and re-layouts: 25.5 us -> 18.4 us
  transfers between devices with their start and end apart: 56 -> 43, of which waited for: 20 -> 18; matrix products, arithmetic and copies ran while one was open for 13% -> 8% of each run, Pallas kernels for 35% -> 48%
where the time goes in v2:
time: 743 us; the launch traced here: 733 us
  Pallas kernels  387 us (52%)
  waiting for transfers between devices  222 us (30%)
  local copies, waits for them, and re-layouts  39 us (5%)
  starting transfers between devices  35.9 us (5%)
  other arithmetic  34.2 us (5%)
  between operations  15 us (2%)
    pallas_call x30, Pallas kernels, call(): pl.pallas_call(run, grid_spec=pltpu.PrefetchScalarGridSpec(num_scalar_pre...  387 us
    ppermute x39, waiting for transfers between devices, flip(): return lax.ppermute(value, axis, [(i, i ^ bit) for i in range(size)])  221 us
    ppermute x39, starting transfers between devices, flip(): return lax.ppermute(value, axis, [(i, i ^ bit) for i in range(size)])  35.7 us
    unnamed x102, local copies, waits for them, and re-layouts  18.4 us
  transfers between devices with their start and end apart: 43, of which 18 were waited for; matrix products, arithmetic and copies ran while one was open for 8% of the time, Pallas kernels for 48%

profile of v2, /device:TPU:0, one launch (start us, length us, event | category | flops | bytes accessed | tf_op | source)
XLA Modules:
  0.0 732.7 jit_solution(2309383423171633453)
XLA Ops:
  14.9 44.3 %collective-permute-done.1.refs_2_ = bf16[512,2048]{1,0:T(8,128)(2,1)S(1)} collective-permute-done((bf16[512,2048]{1,0:T(8,128)(2,1)}, bf16[512,2048]{1,0:T(8,128)(2,1)S(1)}, u32[]{:S(2)}, u32[]{:S(2)}) %collective-permute-start.1) | collective-permute-done | bytes 2097184 | tf_op jit(solution)/shard_map/ppermute | solution.py:633
  68.3 16.6 %collective-permute-done.2.refs_3_ = bf16[256,2048]{1,0:T(8,128)(2,1)S(1)} collective-permute-done((bf16[256,2048]{1,0:T(8,128)(2,1)}, bf16[256,2048]{1,0:T(8,128)(2,1)S(1)}, u32[]{:S(2)}, u32[]{:S(2)}) %collective-permute-start.2) | collective-permute-done | bytes 1048608 | tf_op jit(solution)/shard_map/ppermute | solution.py:633
  110.2 15.3 %shard_map.245 = (bf16[2048,2048]{1,0:T(8,128)(2,1)}, bf16[2048,2048]{1,0:T(8,128)(2,1)}) custom-call(s32[4]{0:T(128)} %pad_add_fusion.ids_ref, bf16[512,2048]{1,0:T(8,128)(2,1)} %refs_0_.2, bf16[512,2048]{1,0:T(8,128)(2,1)} %collective-permute-done.refs_1_, bf16[512,2048]{1,0:T(8,128)(2,1)} %copy-done.2, bf16[256,2048]{1,0:T(8,128)(2,1)} %copy-done.9, ...), custom_call_target="tpu_custom_call" | custom-call | flops 50331648 | bytes 25165824 | tf_op jit(solution)/shard_map/pallas_call | solution.py:50
  125.4 12.4 %collective-permute-done.12.refs_2_ = bf16[512,2048]{1,0:T(8,128)(2,1)S(1)} collective-permute-done((bf16[512,2048]{1,0:T(8,128)(2,1)}, bf16[512,2048]{1,0:T(8,128)(2,1)S(1)}, u32[]{:S(2)}, u32[]{:S(2)}) %collective-permute-start.12) | collective-permute-done | bytes 2097184 | tf_op jit(solution)/shard_map/ppermute | solution.py:633
  142.3 20.9 %shard_map.246.refs_0_ = bf16[2048,1536]{1,0:T(8,128)(2,1)} custom-call(s32[4]{0:T(128)} %pad_add_fusion.ids_ref, bf16[2048,2048]{1,0:T(8,128)(2,1)} %get-tuple-element.36.refs_0_, bf16[2048,1536]{1,0:T(8,128)(2,1)} %all-gather.4.cloned.1.call-done.refs_1_.refs_2_, f32[1,1536]{1,0:T(1,128)} %reshape.256.refs_2_, ...), custom_call_target="tpu_custom_call" | custom-call | flops 12884901888 | bytes 29360128 | tf_op jit(solution)/shard_map/pallas_call | solution.py:50
  163.2 23.0 %shard_map.247 = (bf16[2048,512]{1,0:T(8,128)(2,1)}, f32[2,4,8,512]{3,2,1,0:T(8,128)}) custom-call(s32[4]{0:T(128)} %pad_add_fusion.ids_ref, bf16[2048,1536]{1,0:T(8,128)(2,1)} %shard_map.246.refs_0_), custom_call_target="tpu_custom_call" | custom-call | flops 4294967296 | bytes 9437184 | tf_op jit(solution)/shard_map/pallas_call | solution.py:50
  186.2 10.1 %shard_map.249.refs_0_ = bf16[2048,2048]{1,0:T(8,128)(2,1)} custom-call(s32[4]{0:T(128)} %pad_add_fusion.ids_ref, bf16[512,2048]{1,0:T(8,128)(2,1)} %shard_map.248.refs_0_, bf16[512,2048]{1,0:T(8,128)(2,1)} %collective-permute-done.11.refs_1_, bf16[512,2048]{1,0:T(8,128)(2,1)} %copy-done.6, bf16[256,2048]{1,0:T(8,128)(2,1)} %collective-permute-done.13.refs_3_, ...), custom_call_target="tpu_custom_call" | custom-call | bytes 16777216 | tf_op jit(solution)/shard_map/pallas_call | solution.py:50
  196.3 13.1 %shard_map.250 = (bf16[2048,256]{1,0:T(8,128)(2,1)}, bf16[2048,256]{1,0:T(8,128)(2,1)}) custom-call(s32[4]{0:T(128)} %pad_add_fusion.ids_ref, bf16[2048,2048]{1,0:T(8,128)(2,1)} %shard_map.249.refs_0_, bf16[2048,512]{1,0:T(8,128)(2,1)} %get-tuple-element.37.refs_5_.refs_1_.refs_2_.refs_0_), custom_call_target="tpu_custom_call" | custom-call | flops 4294967296 | bytes 23068672 | tf_op jit(solution)/shard_map/pallas_call | solution.py:50
  209.4 30.2 %shard_map.251 = (bf16[2048,2048]{1,0:T(8,128)(2,1)}, bf16[2048,2048]{1,0:T(8,128)(2,1)}) custom-call(s32[4]{0:T(128)} %pad_add_fusion.ids_ref, bf16[2048,2048]{1,0:T(8,128)(2,1)} %get-tuple-element.38.refs_0_, bf16[2048,2048]{1,0:T(8,128)(2,1)} %all-gather.6.cloned.1.call-done.refs_1_.refs_2_.refs_3_, f32[1,2048]{1,0:T(1,128)} %bitcast.120, ...), custom_call_target="tpu_custom_call" | custom-call | flops 17179869184 | bytes 41943040 | tf_op jit(solution)/shard_map/pallas_call | solution.py:50
  244.6 25.5 %shard_map.253 = (bf16[2048,1024]{1,0:T(8,128)(2,1)}, bf16[2048,1024]{1,0:T(8,128)(2,1)}) custom-call(s32[4]{0:T(128)} %pad_add_fusion.ids_ref, bf16[2048,2048]{1,0:T(8,128)(2,1)} %shard_map.249.refs_0_, bf16[2048,2048]{1,0:T(8,128)(2,1)} %get-tuple-element.40.refs_2_.refs_1_.refs_4_, bf16[1024,256]{1,0:T(8,128)(2,1)} %shard_map.252.refs_2_), custom_call_target="tpu_custom_call" | custom-call | flops 17179869184 | bytes 41943040 | tf_op jit(solution)/shard_map/pallas_call | solution.py:50
  280.2 12.2 %collective-permute-done.8 = bf16[1,512,256]{2,1,0:T(8,128)(2,1)S(1)} collective-permute-done((bf16[1,512,256]{2,1,0:T(8,128)(2,1)S(1)}, bf16[1,512,256]{2,1,0:T(8,128)(2,1)S(1)}, u32[]{:S(2)}, u32[]{:S(2)}) %collective-permute-start.8) | collective-permute-done | bytes 262176 | tf_op jit(solution)/shard_map/ppermute | solution.py:633
  293.3 12.5 %collective-permute-done.9 = bf16[2,512,256]{2,1,0:T(8,128)(2,1)S(1)} collective-permute-done((bf16[2,512,256]{2,1,0:T(8,128)(2,1)S(1)}, bf16[2,512,256]{2,1,0:T(8,128)(2,1)S(1)}, u32[]{:S(2)}, u32[]{:S(2)}) %collective-permute-start.9) | collective-permute-done | bytes 524320 | tf_op jit(solution)/shard_map/ppermute | solution.py:633
  319.0 26.3 %shard_map.255 = (bf16[2048,1536]{1,0:T(8,128)(2,1)}, f32[1,1536]{1,0:T(1,128)}) custom-call(s32[4]{0:T(128)} %pad_add_fusion.ids_ref, bf16[2048,1536]{1,0:T(8,128)(2,1)} %shard_map.246.refs_0_, bf16[2048,512]{1,0:T(8,128)(2,1)} %shard_map.254.refs_1_, bf16[2048,512]{1,0:T(8,128)(2,1)} %get-tuple-element.37.refs_5_.refs_1_.refs_2_.refs_0_, ...), custom_call_target="tpu_custom_call" | custom-call | flops 10737418240 | bytes 18874368 | tf_op jit(solution)/shard_map/pallas_call | solution.py:50
  358.3 25.3 %shard_map.258 = (bf16[2048,2048]{1,0:T(8,128)(2,1)}, f32[1,2048]{1,0:T(1,128)}) custom-call(s32[4]{0:T(128)} %pad_add_fusion.ids_ref, bf16[2048,2048]{1,0:T(8,128)(2,1)} %shard_map.249.refs_0_, bf16[2048,2048]{1,0:T(8,128)(2,1)} %all-gather.8.cloned.1.call-done.refs_1_.refs_5_, bf16[2048,2048]{1,0:T(8,128)(2,1)} %get-tuple-element.46.refs_2_, ...), custom_call_target="tpu_custom_call" | custom-call | flops 17179869184 | bytes 41943040 | tf_op jit(solution)/shard_map/pallas_call | solution.py:50
  383.5 26.8 %shard_map.259 = (bf16[2048,1024]{1,0:T(8,128)(2,1)}, bf16[2048,1024]{1,0:T(8,128)(2,1)}, f32[2048,128]{1,0:T(8,128)}, f32[2048,128]{1,0:T(8,128)}) custom-call(s32[4]{0:T(128)} %pad_add_fusion.ids_ref, bf16[2048,2048]{1,0:T(8,128)(2,1)} %get-tuple-element.38.refs_0_, bf16[2048,2048]{1,0:T(8,128)(2,1)} %get-tuple-element.47.refs_1_.refs_2_, ...), custom_call_target="tpu_custom_call" | custom-call | flops 17179869184 | bytes 41943040 | tf_op jit(solution)/shard_map/pallas_call | solution.py:50
  418.6 29.5 %shard_map.262.refs_2_ = bf16[2048,2048]{1,0:T(8,128)(2,1)} custom-call(s32[4]{0:T(128)} %pad_add_fusion.ids_ref, bf16[2048,512]{1,0:T(8,128)(2,1)} %get-tuple-element.37.refs_5_.refs_1_.refs_2_.refs_0_, bf16[2048,512]{1,0:T(8,128)(2,1)} %get-tuple-element.37.refs_5_.refs_1_.refs_2_.refs_0_, bf16[2048,256]{1,0:T(8,128)(2,1)} %bitcast.90, ...), custom_call_target="tpu_custom_call" | custom-call | flops 21474836480 | bytes 39845888 | tf_op jit(solution)/shard_map/pallas_call | solution.py:50
  462.7 26.5 %shard_map.264 = (bf16[2048,768]{1,0:T(8,128)(2,1)}, bf16[2048,768]{1,0:T(8,128)(2,1)}, f32[2048,128]{1,0:T(8,128)}, f32[2048,128]{1,0:T(8,128)}) custom-call(s32[4]{0:T(128)} %pad_add_fusion.ids_ref, bf16[2048,2048]{1,0:T(8,128)(2,1)} %get-tuple-element.36.refs_0_, bf16[2048,1536]{1,0:T(8,128)(2,1)} %get-tuple-element.45.refs_2_.refs_1_.refs_0_, ...), custom_call_target="tpu_custom_call" | custom-call | flops 12884901888 | bytes 35651584 | tf_op jit(solution)/shard_map/pallas_call | solution.py:50
  494.5 43.7 %collective-permute-done.20.refs_3_ = bf16[512,1024]{1,0:T(8,128)(2,1)} collective-permute-done((bf16[512,1024]{1,0:T(8,128)(2,1)S(1)}, bf16[512,1024]{1,0:T(8,128)(2,1)}, u32[]{:S(2)}, u32[]{:S(2)}) %collective-permute-start.20) | collective-permute-done | bytes 1048608 | tf_op jit(solution)/shard_map/ppermute | solution.py:633
  542.1 13.8 %shard_map.266.refs_2_ = bf16[512,2048]{1,0:T(8,128)(2,1)} custom-call(s32[4]{0:T(128)} %pad_add_fusion.ids_ref, bf16[2048,1536]{1,0:T(8,128)(2,1)} %get-tuple-element.45.refs_2_.refs_1_.refs_0_, bf16[2048,1536]{1,0:T(8,128)(2,1)} %all-gather.4.cloned.1.call-done.refs_1_.refs_2_, bf16[2048,2048]{1,0:T(8,128)(2,1)} %get-tuple-element.47.refs_1_.refs_2_, ...), custom_call_target="tpu_custom_call" | custom-call | flops 7516192768 | bytes 20447232 | tf_op jit(solution)/shard_map/pallas_call | solution.py:50
  562.5 13.9 %shard_map.268.refs_3_ = bf16[512,2048]{1,0:T(8,128)(2,1)} custom-call(s32[4]{0:T(128)} %pad_add_fusion.ids_ref, bf16[2048,1536]{1,0:T(8,128)(2,1)} %get-tuple-element.45.refs_2_.refs_1_.refs_0_, bf16[2048,1536]{1,0:T(8,128)(2,1)} %all-gather.4.cloned.1.call-done.refs_1_.refs_2_, bf16[2048,2048]{1,0:T(8,128)(2,1)} %get-tuple-element.47.refs_1_.refs_2_, ...), custom_call_target="tpu_custom_call" | custom-call | flops 7516192768 | bytes 20447232 | tf_op jit(solution)/shard_map/pallas_call | solution.py:50
  580.9 14.2 %shard_map.270.refs_5_ = bf16[512,2048]{1,0:T(8,128)(2,1)} custom-call(s32[4]{0:T(128)} %pad_add_fusion.ids_ref, bf16[2048,1536]{1,0:T(8,128)(2,1)} %get-tuple-element.45.refs_2_.refs_1_.refs_0_, bf16[2048,1536]{1,0:T(8,128)(2,1)} %all-gather.4.cloned.1.call-done.refs_1_.refs_2_, bf16[2048,2048]{1,0:T(8,128)(2,1)} %get-tuple-element.47.refs_1_.refs_2_, ...), custom_call_target="tpu_custom_call" | custom-call | flops 7516192768 | bytes 20447232 | tf_op jit(solution)/shard_map/pallas_call | solution.py:50
  613.3 14.3 %shard_map.271.refs_3_ = bf16[512,2048]{1,0:T(8,128)(2,1)} custom-call(s32[4]{0:T(128)} %pad_add_fusion.ids_ref, bf16[2048,1536]{1,0:T(8,128)(2,1)} %get-tuple-element.45.refs_2_.refs_1_.refs_0_, bf16[2048,1536]{1,0:T(8,128)(2,1)} %all-gather.4.cloned.1.call-done.refs_1_.refs_2_, bf16[2048,2048]{1,0:T(8,128)(2,1)} %get-tuple-element.47.refs_1_.refs_2_, ...), custom_call_target="tpu_custom_call" | custom-call | flops 7516192768 | bytes 20447232 | tf_op jit(solution)/shard_map/pallas_call | solution.py:50
  627.6 35.5 %collective-permute-done.32.refs_2_ = bf16[1024,768]{1,0:T(8,128)(2,1)} collective-permute-done((bf16[1024,768]{1,0:T(8,128)(2,1)}, bf16[1024,768]{1,0:T(8,128)(2,1)}, u32[]{:S(2)}, u32[]{:S(2)}) %collective-permute-start.32) | collective-permute-done | bytes 1572896 | tf_op jit(solution)/shard_map/ppermute | solution.py:633
  689.0 13.4 %collective-permute-done.33.refs_3_ = bf16[512,768]{1,0:T(8,128)(2,1)} collective-permute-done((bf16[512,768]{1,0:T(8,128)(2,1)}, bf16[512,768]{1,0:T(8,128)(2,1)}, u32[]{:S(2)}, u32[]{:S(2)}) %collective-permute-start.33) | collective-permute-done | bytes 786464 | tf_op jit(solution)/shard_map/ppermute | solution.py:633
  (276 shorter events, 198.6 us)
Async XLA Ops:
  7.2 135.2 %all-gather.4.cloned.1.call-start = ((), (), s32[]{:S(2)}) async-start(), calls=%async_computation.1 | async-start | bytes 7077888 | tf_op jit(solution)/shard_map/all_gather | solution.py:744
  9.5 199.9 %all-gather.6.cloned.1.call-start = ((), (), s32[]{:S(2)}) async-start(), calls=%async_computation.2 | async-start | bytes 9437184 | tf_op jit(solution)/shard_map/all_gather | solution.py:745
  10.2 348.0 %all-gather.8.cloned.1.call-start = ((), (), s32[]{:S(2)}) async-start(), calls=%async_computation.3 | async-start | bytes 9437184 | tf_op jit(solution)/shard_map/all_gather | solution.py:746
  10.3 48.9 %collective-permute-start.1 = (bf16[512,2048]{1,0:T(8,128)(2,1)}, bf16[512,2048]{1,0:T(8,128)(2,1)S(1)}, u32[]{:S(2)}, u32[]{:S(2)}) collective-permute-start(bf16[512,2048]{1,0:T(8,128)(2,1)} %refs_0_.2), channel_id=1, source_target_pairs={{0,2},{1,3},{2,0},{3,1},{4,6},{5,7},{6,4},{7,5},{8,10},{9,11},{10,... | collective-permute-start | bytes 6291464 | tf_op jit(solution)/shard_map/ppermute | solution.py:633
  13.3 48.7 %collective-permute-start = (bf16[512,2048]{1,0:T(8,128)(2,1)}, bf16[512,2048]{1,0:T(8,128)(2,1)}, u32[]{:S(2)}, u32[]{:S(2)}) collective-permute-start(bf16[512,2048]{1,0:T(8,128)(2,1)} %refs_0_.2), channel_id=1, source_target_pairs={{0,1},{1,0},{2,3},{3,2},{4,5},{5,4},{6,7},{7,6},{8,9},{9,8},{10,11... | collective-permute-start | bytes 6291464 | tf_op jit(solution)/shard_map/ppermute | solution.py:633
  14.8 663.4 %reduce-scatter.2.cloned.1.call-start = ((), (), s32[]{:S(2)}) async-start(), calls=%async_computation.4 | async-start | bytes 10485760 | tf_op jit(solution)/shard_map/reduce_scatter | solution.py:804
  91.7 46.1 %collective-permute-start.12 = (bf16[512,2048]{1,0:T(8,128)(2,1)}, bf16[512,2048]{1,0:T(8,128)(2,1)S(1)}, u32[]{:S(2)}, u32[]{:S(2)}) collective-permute-start(bf16[512,2048]{1,0:T(8,128)(2,1)} %shard_map.248.refs_0_), channel_id=1, source_target_pairs={{0,2},{1,3},{2,0},{3,1},{4,6},{5,7},{6,4},{7,5},{8,10},{9,11},{10,... | collective-permute-start | bytes 6291464 | tf_op jit(solution)/shard_map/ppermute | solution.py:633
  93.2 46.5 %collective-permute-start.11 = (bf16[512,2048]{1,0:T(8,128)(2,1)}, bf16[512,2048]{1,0:T(8,128)(2,1)}, u32[]{:S(2)}, u32[]{:S(2)}) collective-permute-start(bf16[512,2048]{1,0:T(8,128)(2,1)} %shard_map.248.refs_0_), channel_id=1, source_target_pairs={{0,1},{1,0},{2,3},{3,2},{4,5},{5,4},{6,7},{7,6},{8,9},{9,8},{10,11... | collective-permute-start | bytes 6291464 | tf_op jit(solution)/shard_map/ppermute | solution.py:633
  138.0 48.2 %collective-permute-start.13 = (bf16[256,2048]{1,0:T(8,128)(2,1)S(1)}, bf16[256,2048]{1,0:T(8,128)(2,1)}, u32[]{:S(2)}, u32[]{:S(2)}) collective-permute-start(bf16[256,2048]{1,0:T(8,128)(2,1)S(1)} %slice.74), channel_id=1, source_target_pairs={{0,1},{1,0},{2,3},{3,2},{4,5},{5,4},{6,7},{7,6},{8,9},{9,8},{10,11... | collective-permute-start | bytes 3145736 | tf_op jit(solution)/shard_map/ppermute | solution.py:633
  142.0 44.2 %collective-permute-start.14 = (bf16[256,2048]{1,0:T(8,128)(2,1)}, bf16[256,2048]{1,0:T(8,128)(2,1)}, u32[]{:S(2)}, u32[]{:S(2)}) collective-permute-start(bf16[256,2048]{1,0:T(8,128)(2,1)} %slice.75), channel_id=1, source_target_pairs={{0,2},{1,3},{2,0},{3,1},{4,6},{5,7},{6,4},{7,5},{8,10},{9,11},{10,... | collective-permute-start | bytes 3145736 | tf_op jit(solution)/shard_map/ppermute | solution.py:633
  270.1 75.2 %collective-permute-start.17 = (bf16[2048,1024]{1,0:T(8,128)(2,1)}, bf16[2048,1024]{1,0:T(8,128)(2,1)}, u32[]{:S(2)}, u32[]{:S(2)}) collective-permute-start(bf16[2048,1024]{1,0:T(8,128)(2,1)} %get-tuple-element.43), channel_id=1, source_target_pairs={{0,4},{4,0},{8,12},{12,8},{16,20},{20,16},{24,28},{28,24},{1,5},{5... | collective-permute-start | bytes 12582920 | tf_op jit(solution)/shard_map/ppermute | solution.py:633
  306.0 45.5 %collective-permute-start.16 = (bf16[1024,256]{1,0:T(8,128)(2,1)}, bf16[1024,256]{1,0:T(8,128)(2,1)S(1)}, u32[]{:S(2)}, u32[]{:S(2)}) collective-permute-start(bf16[1024,256]{1,0:T(8,128)(2,1)} %shard_map.252.refs_2_), channel_id=1, source_target_pairs={{0,8},{4,12},{8,0},{12,4},{16,24},{20,28},{24,16},{28,20},{1,9},{5... | collective-permute-start | bytes 1572872 | tf_op jit(solution)/shard_map/ppermute | solution.py:633
  350.3 60.1 %collective-permute-start.19 = (bf16[1024,1024]{1,0:T(8,128)(2,1)}, bf16[1024,1024]{1,0:T(8,128)(2,1)S(1)}, u32[]{:S(2)}, u32[]{:S(2)}) collective-permute-start(bf16[1024,1024]{1,0:T(8,128)(2,1)} %shard_map.256.refs_3_), channel_id=1, source_target_pairs={{0,8},{4,12},{8,0},{12,4},{16,24},{20,28},{24,16},{28,20},{1,9},{5... | collective-permute-start | bytes 6291464 | tf_op jit(solution)/shard_map/ppermute | solution.py:633
  354.9 60.4 %collective-permute-start.18 = (bf16[512,256]{1,0:T(8,128)(2,1)}, bf16[512,256]{1,0:T(8,128)(2,1)S(1)}, u32[]{:S(2)}, u32[]{:S(2)}) collective-permute-start(bf16[512,256]{1,0:T(8,128)(2,1)} %shard_map.257.refs_3_), channel_id=1, source_target_pairs={{0,16},{4,20},{8,24},{12,28},{16,0},{20,4},{24,8},{28,12},{1,17},{... | collective-permute-start | bytes 786440 | tf_op jit(solution)/shard_map/ppermute | solution.py:633
  489.2 68.7 %collective-permute-start.23 = (bf16[2048,768]{1,0:T(8,128)(2,1)}, bf16[2048,768]{1,0:T(8,128)(2,1)}, u32[]{:S(2)}, u32[]{:S(2)}) collective-permute-start(bf16[2048,768]{1,0:T(8,128)(2,1)} %get-tuple-element.53), channel_id=1, source_target_pairs={{0,4},{4,0},{8,12},{12,8},{16,20},{20,16},{24,28},{28,24},{1,5},{5... | collective-permute-start | bytes 9437192 | tf_op jit(solution)/shard_map/ppermute | solution.py:633
  489.7 48.5 %collective-permute-start.20 = (bf16[512,1024]{1,0:T(8,128)(2,1)S(1)}, bf16[512,1024]{1,0:T(8,128)(2,1)}, u32[]{:S(2)}, u32[]{:S(2)}) collective-permute-start(bf16[512,1024]{1,0:T(8,128)(2,1)S(1)} %copy-done.7), channel_id=1, source_target_pairs={{0,16},{4,20},{8,24},{12,28},{16,0},{20,4},{24,8},{28,12},{1,17},{... | collective-permute-start | bytes 3145736 | tf_op jit(solution)/shard_map/ppermute | solution.py:633
  489.8 87.6 %collective-permute-start.25 = (bf16[1024,1024]{1,0:T(8,128)(2,1)}, bf16[1024,1024]{1,0:T(8,128)(2,1)}, u32[]{:S(2)}, u32[]{:S(2)}) collective-permute-start(bf16[1024,1024]{1,0:T(8,128)(2,1)} %shard_map.263.refs_4_), channel_id=1, source_target_pairs={{0,8},{4,12},{8,0},{12,4},{16,24},{20,28},{24,16},{28,20},{1,9},{5... | collective-permute-start | bytes 6291464 | tf_op jit(solution)/shard_map/ppermute | solution.py:633
  494.1 109.3 %collective-permute-start.36 = (bf16[256,256]{0,1:T(8,128)(2,1)}, bf16[256,256]{0,1:T(8,128)(2,1)S(1)}, u32[]{:S(2)}, u32[]{:S(2)}) collective-permute-start(bf16[256,256]{0,1:T(8,128)(2,1)} %bitcast.35), channel_id=1, source_target_pairs={{0,4},{4,0},{8,12},{12,8},{16,20},{20,16},{24,28},{28,24},{1,5},{5... | collective-permute-start | bytes 393224 | tf_op jit(solution)/shard_map/ppermute | solution.py:633
  555.9 117.7 %collective-permute-start.22 = (bf16[512,2048]{1,0:T(8,128)(2,1)}, bf16[512,2048]{1,0:T(8,128)(2,1)}, u32[]{:S(2)}, u32[]{:S(2)}) collective-permute-start(bf16[512,2048]{1,0:T(8,128)(2,1)} %shard_map.266.refs_2_), channel_id=1, source_target_pairs={{0,3},{1,2},{2,1},{3,0},{4,7},{5,6},{6,5},{7,4},{8,11},{9,10},{10,... | collective-permute-start | bytes 6291464 | tf_op jit(solution)/shard_map/ppermute | solution.py:633
  576.4 97.2 %collective-permute-start.24 = (bf16[512,2048]{1,0:T(8,128)(2,1)}, bf16[512,2048]{1,0:T(8,128)(2,1)}, u32[]{:S(2)}, u32[]{:S(2)}) collective-permute-start(bf16[512,2048]{1,0:T(8,128)(2,1)} %shard_map.268.refs_3_), channel_id=1, source_target_pairs={{0,2},{1,3},{2,0},{3,1},{4,6},{5,7},{6,4},{7,5},{8,10},{9,11},{10,... | collective-permute-start | bytes 6291464 | tf_op jit(solution)/shard_map/ppermute | solution.py:633
  595.1 78.5 %collective-permute-start.26 = (bf16[512,2048]{1,0:T(8,128)(2,1)}, bf16[512,2048]{1,0:T(8,128)(2,1)}, u32[]{:S(2)}, u32[]{:S(2)}) collective-permute-start(bf16[512,2048]{1,0:T(8,128)(2,1)} %shard_map.270.refs_5_), channel_id=1, source_target_pairs={{0,1},{1,0},{2,3},{3,2},{4,5},{5,4},{6,7},{7,6},{8,9},{9,8},{10,11... | collective-permute-start | bytes 6291464 | tf_op jit(solution)/shard_map/ppermute | solution.py:633
  603.4 59.7 %collective-permute-start.32 = (bf16[1024,768]{1,0:T(8,128)(2,1)}, bf16[1024,768]{1,0:T(8,128)(2,1)}, u32[]{:S(2)}, u32[]{:S(2)}) collective-permute-start(bf16[1024,768]{1,0:T(8,128)(2,1)} %shard_map.267.refs_5_), channel_id=1, source_target_pairs={{0,8},{4,12},{8,0},{12,4},{16,24},{20,28},{24,16},{28,20},{1,9},{5... | collective-permute-start | bytes 4718600 | tf_op jit(solution)/shard_map/ppermute | solution.py:633
  609.5 56.7 %collective-permute-start.34 = (bf16[512,1024]{1,0:T(8,128)(2,1)S(1)}, bf16[512,1024]{1,0:T(8,128)(2,1)S(1)}, u32[]{:S(2)}, u32[]{:S(2)}) collective-permute-start(bf16[512,1024]{1,0:T(8,128)(2,1)S(1)} %copy-done.10), channel_id=1, source_target_pairs={{0,16},{4,20},{8,24},{12,28},{16,0},{20,4},{24,8},{28,12},{1,17},{... | collective-permute-start | bytes 3145736 | tf_op jit(solution)/shard_map/ppermute | solution.py:633
  666.2 36.2 %collective-permute-start.33 = (bf16[512,768]{1,0:T(8,128)(2,1)}, bf16[512,768]{1,0:T(8,128)(2,1)}, u32[]{:S(2)}, u32[]{:S(2)}) collective-permute-start(bf16[512,768]{1,0:T(8,128)(2,1)} %shard_map.272.refs_4_), channel_id=1, source_target_pairs={{0,16},{4,20},{8,24},{12,28},{16,0},{20,4},{24,8},{28,12},{1,17},{... | collective-permute-start | bytes 2359304 | tf_op jit(solution)/shard_map/ppermute | solution.py:633
  (60 other events, 996.1 us)
Sparse Core Ops, SparseCore 0:
  10.2 67.4 all-gather.3
  79.3 82.0 all-gather.5
  163.0 81.1 all-gather.7
  448.2 84.1 reduce-scatter.1

commit v3 on v1

v3 whole, which is shorter than its diff:
```python
import jax
import jax.numpy as jnp
from jax import lax
from jax.experimental import pallas as pl
from jax.experimental.pallas import tpu as pltpu
from jax.sharding import PartitionSpec as P

HEAD_DIM = 256
ROTARY = 64
LENGTH = 2048
EPSILON = 1e-05
BIG = -1e30
F32 = jnp.float32
BF16 = jnp.bfloat16
DIMS = {
    "NN": (((1,), (0,)), ((), ())),
    "NT": (((1,), (1,)), ((), ())),
    "TN": (((0,), (0,)), ((), ())),
}


def product(left, right, mode):
    return lax.dot_general(left, right, DIMS[mode], preferred_element_type=F32)


def params():
    return pltpu.CompilerParams(vmem_limit_bytes=56 << 20)


def cost(lag):
    return pl.CostEstimate(flops=int(lag * 1e9), bytes_accessed=0, transcendentals=0)


def tile_of(width, most):
    best = 128
    for size in range(128, most + 1, 128):
        if width % size == 0:
            best = size
    return best


def call(kernel, ids, grid, in_specs, out_specs, out_shape, args, name, scratch=(), after=(), kept=(), lag=0.05):
    count = len(args)
    unread = tuple(kept) + tuple(after)

    def run(ids_ref, *refs):
        kernel(ids_ref, *refs[:count], *refs[count + len(unread) :])

    return pl.pallas_call(
        run,
        grid_spec=pltpu.PrefetchScalarGridSpec(
            num_scalar_prefetch=1,
            grid=grid,
            in_specs=list(in_specs) + [pl.BlockSpec(memory_space=pl.ANY)] * len(unread),
            out_specs=out_specs,
            scratch_shapes=list(scratch),
        ),
        out_shape=out_shape,
        input_output_aliases={1 + count + k: k for k in range(len(kept))},
        compiler_params=params(),
        cost_estimate=cost(lag),
        name=name,
    )(ids, *args, *unread)


def group(pieces, unit):
    blocks, filled = [], unit
    for number, piece in enumerate(pieces):
        if filled == unit:
            blocks.append([])
            filled = 0
        blocks[-1].append((number, filled))
        filled += piece.shape[0]
    return blocks


def norm_kernel(ids, pieces, vectors, unit, start, total, kept=(), after=(), lag=0.05):
    width = pieces[0].shape[1]
    blocks = group(pieces, unit)

    def kernel(ids_ref, *refs):
        vec = refs[len(pieces)]
        first_ref, second_ref = refs[len(pieces) + 1 :]
        for step, block in enumerate(blocks):

            @pl.when(pl.program_id(0) == step)
            def _(block=block):
                for number, row in block:
                    rows = slice(row, row + pieces[number].shape[0])
                    data = refs[number][...].astype(F32)
                    centre = data - jnp.mean(data, axis=-1, keepdims=True)
                    spread = jnp.mean(centre * centre, axis=-1, keepdims=True)
                    scaled = centre * lax.rsqrt(spread + EPSILON)
                    first_ref[rows, :] = (scaled * vec[0:1, :] + vec[1:2, :]).astype(BF16)
                    second_ref[rows, :] = (scaled * vec[2:3, :] + vec[3:4, :]).astype(BF16)

    out = pl.BlockSpec((unit, width), lambda i, ids: (start + i, 0))
    shape = jax.ShapeDtypeStruct((total * unit, width), BF16)
    return call(
        kernel,
        ids,
        (len(blocks),),
        [pl.BlockSpec(array.shape, lambda i, ids: (0, 0)) for array in (*pieces, vectors)],
        [out, out],
        [shape, shape],
        (*pieces, vectors),
        kept=kept,
        after=after,
        lag=lag,
        name="norm",
    )


def rotate(block, cos, sin_low, sin_high, sign):
    lead = block[:, :128]
    turned = (
        lead * cos
        + sign * (pltpu.roll(lead, 96, 1) * sin_low + pltpu.roll(lead, 32, 1) * sin_high)
    )
    return jnp.concatenate([turned, block[:, 128:]], axis=1)


def mixed_kernel(ids, first, weight, bias, tables, start, count, blocks, kept=(), after=(), lag=0.05):
    rows, depth = first.shape
    heads = weight.shape[1] // (3 * HEAD_DIM)
    unit = rows // blocks
    wide = 3 * HEAD_DIM

    def kernel(ids_ref, a_ref, w_ref, b_ref, cos, low, high, out_ref):
        for part in range(3):
            here = slice(part * HEAD_DIM, (part + 1) * HEAD_DIM)
            value = product(a_ref[...], w_ref[:, here], "NN") + b_ref[:, here]
            if part < 2:
                value = rotate(value, cos[...], low[...], high[...], 1.0)
            out_ref[:, here] = value.astype(BF16)

    table = pl.BlockSpec((unit, 128), lambda j, i, ids: (ids[0] ^ (start + i), 0))
    return call(
        kernel,
        ids,
        (heads, count),
        [
            pl.BlockSpec((unit, depth), lambda j, i, ids: (start + i, 0)),
            pl.BlockSpec((depth, wide), lambda j, i, ids: (0, j)),
            pl.BlockSpec((1, wide), lambda j, i, ids: (0, j)),
            table,
            table,
            table,
        ],
        [pl.BlockSpec((unit, wide), lambda j, i, ids: (start + i, j))],
        [jax.ShapeDtypeStruct((rows, heads * wide), BF16)],
        (first, weight, bias, *tables),
        kept=kept,
        after=after,
        lag=lag,
        name="mixed",
    )


def attend_kernel(ids, mixed, blocks, after=(), lag=0.05):
    rows, width = mixed.shape
    heads = width // (3 * HEAD_DIM)
    unit = rows // blocks
    scale = HEAD_DIM ** (-0.5)

    def kernel(ids_ref, x_ref, ctx_ref, lse_ref, top_s, total_s, acc_s):
        block = pl.program_id(0)
        me = ids_ref[0]
        here = pl.ds(pl.multiple_of((me ^ block) * unit, unit), unit)

        def step(other, diagonal):
            there = pl.ds(pl.multiple_of((me ^ other) * unit, unit), unit)
            for head in range(heads):
                at = 3 * HEAD_DIM * head
                scores = (
                    product(
                        x_ref[here, at : at + HEAD_DIM],
                        x_ref[there, at + HEAD_DIM : at + 2 * HEAD_DIM],
                        "NT",
                    )
                    * scale
                )
                value = x_ref[there, at + 2 * HEAD_DIM : at + 3 * HEAD_DIM]
                if diagonal:
                    row_at = lax.broadcasted_iota(jnp.int32, scores.shape, 0)
                    col_at = lax.broadcasted_iota(jnp.int32, scores.shape, 1)
                    scores = jnp.where(col_at <= row_at, scores, BIG)
                    top = jnp.max(scores, axis=1, keepdims=True)
                    weight = jnp.exp(scores - top)
                    top_s[head] = top
                    total_s[head] = jnp.sum(weight, axis=1, keepdims=True)
                    acc_s[head] = product(weight.astype(BF16), value, "NN")
                else:
                    before = top_s[head]
                    top = jnp.maximum(before, jnp.max(scores, axis=1, keepdims=True))
                    weight = jnp.exp(scores - top)
                    shrunk = jnp.exp(before - top)
                    top_s[head] = top
                    total_s[head] = total_s[head] * shrunk + jnp.sum(weight, axis=1, keepdims=True)
                    acc_s[head] = acc_s[head] * shrunk + product(weight.astype(BF16), value, "NN")

        step(block, True)

        @pl.loop(0, block)
        def _(other):
            step(other, False)

        for head in range(heads):
            at = HEAD_DIM * head
            ctx_ref[:, at : at + HEAD_DIM] = (acc_s[head] / total_s[head]).astype(BF16)
            log_total = top_s[head] + jnp.log(total_s[head])
            lse_ref[head, 0] = jnp.transpose(jnp.broadcast_to(log_total, (unit, 128)))[:8]

    return call(
        kernel,
        ids,
        (blocks,),
        [pl.BlockSpec((rows, width), lambda b, ids: (0, 0))],
        [
            pl.BlockSpec((unit, heads * HEAD_DIM), lambda b, ids: (ids[0] ^ b, 0)),
            pl.BlockSpec((heads, 1, 8, unit), lambda b, ids: (0, b, 0, 0)),
        ],
        [
            jax.ShapeDtypeStruct((rows, heads * HEAD_DIM), BF16),
            jax.ShapeDtypeStruct((heads, blocks, 8, unit), F32),
        ],
        (mixed,),
        scratch=[
            pltpu.VMEM((heads, unit, 1), F32),
            pltpu.VMEM((heads, unit, 1), F32),
            pltpu.VMEM((heads, unit, HEAD_DIM), F32),
        ],
        after=after,
        lag=lag,
        name="attend",
    )


def attend_back_kernel(ids, mixed, grad, context, lse, tables, blocks, after=(), lag=0.05):
    rows, width = mixed.shape
    heads = width // (3 * HEAD_DIM)
    unit = rows // blocks
    scale = HEAD_DIM ** (-0.5)

    def kernel(ids_ref, x_ref, g_ref, c_ref, lse_ref, cos, low, high, out_ref, sum_ref, dk_s, dv_s, dq_s, inner_s):
        turn = pl.program_id(0)
        block = blocks - 1 - turn
        me = ids_ref[0]

        @pl.when(turn == 0)
        def _():
            dk_s[...] = jnp.zeros_like(dk_s)
            dv_s[...] = jnp.zeros_like(dv_s)
            sum_ref[...] = jnp.zeros_like(sum_ref)

        here = pl.ds(pl.multiple_of((me ^ block) * unit, unit), unit)
        for head in range(heads):
            cols = slice(HEAD_DIM * head, HEAD_DIM * (head + 1))
            inner = jnp.sum(g_ref[here, cols].astype(F32) * c_ref[here, cols].astype(F32), axis=1, keepdims=True)
            inner_s[head] = jnp.transpose(jnp.broadcast_to(inner, (unit, 128)))[:8]

        def step(other, diagonal):
            there = pl.ds(pl.multiple_of((me ^ other) * unit, unit), unit)
            for head in range(heads):
                at = 3 * HEAD_DIM * head
                query = x_ref[here, at : at + HEAD_DIM]
                seed = g_ref[here, HEAD_DIM * head : HEAD_DIM * (head + 1)]
                key = x_ref[there, at + HEAD_DIM : at + 2 * HEAD_DIM]
                value = x_ref[there, at + 2 * HEAD_DIM : at + 3 * HEAD_DIM]
                scores = product(key, query, "NT") * scale
                prob = jnp.exp(scores - lse_ref[head, 0][:1])
                if diagonal:
                    key_at = lax.broadcasted_iota(jnp.int32, scores.shape, 0)
                    row_at = lax.broadcasted_iota(jnp.int32, scores.shape, 1)
                    prob = jnp.where(key_at <= row_at, prob, 0.0)
                dprob = product(value, seed, "NT")
                dscore = (prob * (dprob - inner_s[head][:1])).astype(BF16)
                dv_s[head, other] += product(prob.astype(BF16), seed, "NN")
                dk_s[head, other] += product(dscore, query, "NN")
                dquery = product(dscore, key, "TN")
                if diagonal:
                    dq_s[head] = dquery
                else:
                    dq_s[head] += dquery

        step(block, True)

        @pl.loop(0, block)
        def _(other):
            step(other, False)

        for head in range(heads):
            at = 3 * HEAD_DIM * head
            dquery = rotate(dq_s[head] * scale, cos[...], low[...], high[...], -1.0)
            dkey = rotate(dk_s[head, block] * scale, cos[...], low[...], high[...], -1.0)
            for part, value in enumerate((dquery, dkey, dv_s[head, block])):
                cols = slice(at + part * HEAD_DIM, at + (part + 1) * HEAD_DIM)
                rounded = value.astype(BF16)
                out_ref[:, cols] = rounded
                sum_ref[:, cols] += jnp.sum(rounded.astype(F32), axis=0, keepdims=True)

    def whole(cols):
        return pl.BlockSpec((rows, cols), lambda b, ids: (0, 0))

    table = pl.BlockSpec((unit, 128), lambda b, ids: (blocks - 1 - b, 0))
    return call(
        kernel,
        ids,
        (blocks,),
        [
            whole(width),
            whole(heads * HEAD_DIM),
            whole(heads * HEAD_DIM),
            pl.BlockSpec((heads, 1, 8, unit), lambda b, ids: (0, blocks - 1 - b, 0, 0)),
            table,
            table,
            table,
        ],
        [
            pl.BlockSpec((unit, width), lambda b, ids: (ids[0] ^ (blocks - 1 - b), 0)),
            pl.BlockSpec((1, width), lambda b, ids: (0, 0)),
        ],
        [jax.ShapeDtypeStruct((rows, width), BF16), jax.ShapeDtypeStruct((1, width), F32)],
        (mixed, grad, context, lse, *tables),
        scratch=[
            pltpu.VMEM((heads, blocks, unit, HEAD_DIM), F32),
            pltpu.VMEM((heads, blocks, unit, HEAD_DIM), F32),
            pltpu.VMEM((heads, unit, HEAD_DIM), F32),
            pltpu.VMEM((heads, 8, unit), F32),
        ],
        after=after,
        lag=lag,
        name="attend_back",
    )


def expand_kernel(ids, second, weight, bias, after=(), lag=0.05):
    rows, depth = second.shape
    width = weight.shape[1]
    tall, wide = tile_of(rows, 1024), tile_of(width, 1024)
    unit = tile_of(wide, 512)

    def kernel(ids_ref, a_ref, w_ref, b_ref, hidden_ref, slope_ref):
        for part in range(wide // unit):
            here = slice(part * unit, (part + 1) * unit)
            pre = product(a_ref[...], w_ref[:, here], "NN") + b_ref[:, here]
            phi = 0.5 + 0.5 * lax.erf(pre * 0.7071067811865476)
            hidden_ref[:, here] = (pre * phi).astype(BF16)
            slope = phi + pre * (jnp.exp(-0.5 * pre * pre) * 0.3989422804014327)
            slope_ref[:, here] = slope.astype(BF16)

    out = pl.BlockSpec((tall, wide), lambda i, j, ids: (i, j))
    shape = jax.ShapeDtypeStruct((rows, width), BF16)
    return call(
        kernel,
        ids,
        (rows // tall, width // wide),
        [
            pl.BlockSpec((tall, depth), lambda i, j, ids: (i, 0)),
            pl.BlockSpec((depth, wide), lambda i, j, ids: (0, j)),
            pl.BlockSpec((1, wide), lambda i, j, ids: (0, j)),
        ],
        [out, out],
        [shape, shape],
        (second, weight, bias),
        after=after,
        lag=lag,
        name="expand",
    )


def stack_kernel(ids, pieces, unit, after=(), lag=0.05):
    width = pieces[0].shape[1]
    blocks = group(pieces, unit)

    def kernel(ids_ref, *refs):
        for step, block in enumerate(blocks):

            @pl.when(pl.program_id(0) == step)
            def _(block=block):
                for number, row in block:
                    refs[-1][row : row + pieces[number].shape[0], :] = refs[number][...]

    return call(
        kernel,
        ids,
        (len(blocks),),
        [pl.BlockSpec(piece.shape, lambda i, ids: (0, 0)) for piece in pieces],
        pl.BlockSpec((unit, width), lambda i, ids: (i, 0)),
        jax.ShapeDtypeStruct((len(blocks) * unit, width), BF16),
        tuple(pieces),
        after=after,
        lag=lag,
        name="stack",
    )


def join_kernel(ids, mine, other, bit, chunks, after=(), lag=0.05):
    rows, width = mine.shape[0] // chunks, mine.shape[1]

    def kernel(ids_ref, a_ref, b_ref, out_ref):
        for side, ref in ((0, a_ref), (1, b_ref)):

            @pl.when(pl.program_id(0) == side)
            def _(ref=ref):
                out_ref[...] = ref[...]

    return call(
        kernel,
        ids,
        (2, chunks),
        [
            pl.BlockSpec((rows, width), lambda s, i, ids: (jnp.where(s == 0, i, chunks - 1), 0)),
            pl.BlockSpec((rows, width), lambda s, i, ids: (jnp.where(s == 0, 0, i), 0)),
        ],
        pl.BlockSpec((rows, width), lambda s, i, ids: (2 * i + (s ^ ids[bit]), 0)),
        jax.ShapeDtypeStruct((2 * chunks * rows, width), BF16),
        (mine, other),
        after=after,
        lag=lag,
        name="join",
    )


def assemble_kernel(ids, parts, bit, chunks, after=(), lag=0.05):
    rows, width = parts[0].shape[0] // chunks, parts[0].shape[1]

    def kernel(ids_ref, *refs):
        for step, ref in enumerate(refs[:4]):

            @pl.when(pl.program_id(0) == step)
            def _(ref=ref):
                refs[4][...] = ref[...]

    def spec(step):
        def place(s, i, ids):
            return jnp.where(s == step, i, jnp.where(s < step, 0, chunks - 1)), 0

        return pl.BlockSpec((rows, width), place)

    return call(
        kernel,
        ids,
        (4, chunks),
        [spec(step) for step in range(4)],
        pl.BlockSpec((rows, width), lambda s, i, ids: (2 * i + ((s & 1) ^ ids[bit]), (s >> 1) ^ ids[1])),
        jax.ShapeDtypeStruct((2 * chunks * rows, 2 * width), BF16),
        tuple(parts),
        after=after,
        lag=lag,
        name="assemble",
    )


def shrink_back_kernel(ids, seed, weight, slope, after=(), lag=0.05):
    rows, depth = seed.shape
    width = weight.shape[1]
    tall, wide = tile_of(rows, 1024), tile_of(width, 1024)
    unit = tile_of(wide, 512)

    def kernel(ids_ref, a_ref, w_ref, s_ref, out_ref, sum_ref):
        @pl.when(pl.program_id(1) == 0)
        def _():
            sum_ref[...] = jnp.zeros_like(sum_ref)

        for part in range(wide // unit):
            here = slice(part * unit, (part + 1) * unit)
            grad = product(a_ref[...], w_ref[:, here], "NN") * s_ref[:, here].astype(F32)
            rounded = grad.astype(BF16)
            out_ref[:, here] = rounded
            sum_ref[:, here] += jnp.sum(rounded.astype(F32), axis=0, keepdims=True)

    tile = pl.BlockSpec((tall, wide), lambda j, i, ids: (i, j))
    return call(
        kernel,
        ids,
        (width // wide, rows // tall),
        [
            pl.BlockSpec((tall, depth), lambda j, i, ids: (i, 0)),
            pl.BlockSpec((depth, wide), lambda j, i, ids: (0, j)),
            tile,
        ],
        [tile, pl.BlockSpec((1, wide), lambda j, i, ids: (0, j))],
        [jax.ShapeDtypeStruct((rows, width), BF16), jax.ShapeDtypeStruct((1, width), F32)],
        (seed, weight, slope),
        after=after,
        lag=lag,
        name="shrink_back",
    )


def plain_kernel(ids, left, right, after=(), lag=0.05):
    rows, depth = left.shape
    width = right.shape[1]
    tall = tile_of(rows, 1024)

    def kernel(ids_ref, a_ref, b_ref, out_ref):
        out_ref[...] = product(a_ref[...], b_ref[...], "NN").astype(BF16)

    return call(
        kernel,
        ids,
        (rows // tall,),
        [
            pl.BlockSpec((tall, depth), lambda i, ids: (i, 0)),
            pl.BlockSpec(right.shape, lambda i, ids: (0, 0)),
        ],
        pl.BlockSpec((tall, width), lambda i, ids: (i, 0)),
        jax.ShapeDtypeStruct((rows, width), BF16),
        (left, right),
        after=after,
        lag=lag,
        name="plain",
    )


def branches_kernel(ids, context, merge, hidden, shrink, blocks, after=(), lag=0.05):
    rows, deep_b = hidden.shape
    depth, deep_a = merge.shape
    tall, wide = rows // blocks, tile_of(depth, 1024)
    unit = tile_of(wide, 512)

    def kernel(ids_ref, a_ref, m_ref, h_ref, s_ref, *out_refs):
        for block, out_ref in enumerate(out_refs):

            @pl.when(pl.program_id(1) == block)
            def _(out_ref=out_ref):
                for part in range(wide // unit):
                    here = slice(part * unit, (part + 1) * unit)
                    value = product(h_ref[...], s_ref[here, :], "NT")
                    value = value + product(a_ref[...], m_ref[here, :], "NT")
                    out_ref[:, here] = value.astype(BF16)

    return call(
        kernel,
        ids,
        (depth // wide, blocks),
        [
            pl.BlockSpec((tall, deep_a), lambda j, i, ids: (i, 0)),
            pl.BlockSpec((wide, deep_a), lambda j, i, ids: (j, 0)),
            pl.BlockSpec((tall, deep_b), lambda j, i, ids: (i, 0)),
            pl.BlockSpec((wide, deep_b), lambda j, i, ids: (j, 0)),
        ],
        [pl.BlockSpec((tall, wide), lambda j, i, ids: (0, j))] * blocks,
        [jax.ShapeDtypeStruct((tall, depth), BF16)] * blocks,
        (context, merge, hidden, shrink),
        after=after,
        lag=lag,
        name="branches",
    )


def back_kernel(ids, left_a, right_a, left_b, right_b, scales, start, count, blocks, after=(), lag=0.05):
    rows = left_a.shape[0] // blocks
    width = right_a.shape[0]
    deep_a, deep_b = left_a.shape[1], left_b.shape[1]
    wide = tile_of(width, 1024)
    unit = tile_of(wide, 512)

    def kernel(ids_ref, a_ref, b_ref, c_ref, d_ref, s_ref, *out_refs):
        for block, out_ref in enumerate(out_refs):

            @pl.when(pl.program_id(1) == block)
            def _(out_ref=out_ref):
                for part in range(wide // unit):
                    here = slice(part * unit, (part + 1) * unit)
                    one = product(a_ref[...], b_ref[here, :], "NT") * s_ref[0:1, here]
                    two = product(c_ref[...], d_ref[here, :], "NT") * s_ref[1:2, here]
                    out_ref[:, here] = (one + two).astype(BF16)

    return call(
        kernel,
        ids,
        (width // wide, count),
        [
            pl.BlockSpec((rows, deep_a), lambda j, i, ids: (start + i, 0)),
            pl.BlockSpec((wide, deep_a), lambda j, i, ids: (j, 0)),
            pl.BlockSpec((rows, deep_b), lambda j, i, ids: (start + i, 0)),
            pl.BlockSpec((wide, deep_b), lambda j, i, ids: (j, 0)),
            pl.BlockSpec((2, wide), lambda j, i, ids: (0, j)),
        ],
        [pl.BlockSpec((rows, wide), lambda j, i, ids: (0, j))] * count,
        [jax.ShapeDtypeStruct((rows, width), BF16)] * count,
        (left_a, right_a, left_b, right_b, scales),
        after=after,
        lag=lag,
        name="back",
    )


def full_grad_kernel(ids, left, right, weight=None, total=None, spare=0, after=(), lag=0.05):
    rows, depth = left.shape
    width = right.shape[1]
    tall, wide = tile_of(depth, 1024), tile_of(width, 1024)
    unit = tile_of(wide, 512)
    summed = weight is not None

    def kernel(ids_ref, a_ref, b_ref, *refs):
        out_ref = refs[2 if summed else 0]
        if summed:

            @pl.when(pl.program_id(1) == 0)
            def _():
                refs[3][...] = jnp.zeros_like(refs[3])
                refs[4][...] = jnp.zeros_like(refs[4])

        for part in range(wide // unit):
            here = slice(part * unit, (part + 1) * unit)
            value = product(a_ref[...], b_ref[:, here], "TN")
            out_ref[:, here] = value.astype(BF16)
            if summed:
                held = refs[0][:, here].astype(F32)
                one, two = held * value, held * refs[1][:, here]
                refs[3][...] += sum(one[:, lane : lane + 128] for lane in range(0, unit, 128))
                refs[4][...] += sum(two[:, lane : lane + 128] for lane in range(0, unit, 128))

    tile = pl.BlockSpec((tall, wide), lambda i, j, ids: (i, j))
    in_specs = [
        pl.BlockSpec((rows, tall), lambda i, j, ids: (0, i)),
        pl.BlockSpec((rows, wide), lambda i, j, ids: (0, j)),
    ]
    out_specs = [tile]
    out_shape = [jax.ShapeDtypeStruct((depth, width + spare), BF16)]
    args = (left, right)
    if summed:
        args += (weight, total)
        in_specs += [tile, pl.BlockSpec((1, wide), lambda i, j, ids: (0, j))]
        out_specs += [pl.BlockSpec((tall, 128), lambda i, j, ids: (i, 0))] * 2
        out_shape += [jax.ShapeDtypeStruct((depth, 128), F32)] * 2
    return call(
        kernel,
        ids,
        (depth // tall, width // wide),
        in_specs,
        out_specs,
        out_shape,
        args,
        after=after,
        lag=lag,
        name="full_grad",
    )


def spare_kernel(ids, kept, wide, narrow, after=(), lag=0.05):
    depth = kept.shape[0]

    def kernel(ids_ref, *refs):
        lane = lax.broadcasted_iota(jnp.int32, (depth, 128), 1)
        value = refs[len(wide)][...]
        for number, ref in enumerate(refs[: len(wide)]):
            value = jnp.where(lane == number, jnp.sum(ref[...], axis=1, keepdims=True), value)
        rounded = value.astype(BF16).astype(F32)
        rest = pltpu.roll(value - rounded, 64, 1)
        refs[-1][...] = jnp.where(lane < 64, rounded, rest).astype(BF16)

    block = pl.BlockSpec((depth, 128), lambda i, ids: (0, 0))
    return call(
        kernel,
        ids,
        (1,),
        [block] * (len(wide) + 1),
        [pl.BlockSpec((depth, 128), lambda i, ids: (0, kept.shape[1] // 128 - 1))],
        [jax.ShapeDtypeStruct(kept.shape, BF16)],
        (*wide, narrow),
        kept=(kept,),
        after=after,
        lag=lag,
        name="spare",
    )[0]


def output_kernel(ids, rows, parts, vectors, after=(), lag=0.05):
    count, width = rows.shape

    def kernel(ids_ref, x_ref, vec, *refs):
        total = refs[0][...].astype(F32)
        for ref in refs[1:-1]:
            total = total + ref[...].astype(F32)
        refs[-1][...] = (x_ref[...].astype(F32) + total + (vec[4:5, :] + vec[5:6, :])).astype(BF16)

    unit = tile_of(count, 256)
    tile = pl.BlockSpec((unit, width), lambda i, ids: (i, 0))
    return call(
        kernel,
        ids,
        (count // unit,),
        [tile, pl.BlockSpec(vectors.shape, lambda i, ids: (0, 0))] + [tile] * len(parts),
        tile,
        jax.ShapeDtypeStruct((count, width), BF16),
        (rows, vectors, *parts),
        after=after,
        lag=lag,
        name="output",
    )


def widen_kernel(ids, rows, spare=0, after=(), lag=0.05):
    count, width = rows.shape[0], rows.shape[1] - spare

    def kernel(ids_ref, *refs):
        half = len(refs) // 2
        for in_ref, out_ref in zip(refs[:half], refs[half:]):
            out_ref[...] = in_ref[...].astype(F32)

    specs = [pl.BlockSpec((count, width), lambda i, ids: (0, 0))]
    shapes = [jax.ShapeDtypeStruct((count, width), F32)]
    if spare:
        specs.append(pl.BlockSpec((count, spare), lambda i, ids: (0, width // spare)))
        shapes.append(jax.ShapeDtypeStruct((count, spare), F32))
    out_specs = [pl.BlockSpec(shape.shape, lambda i, ids: (0, 0)) for shape in shapes]
    return call(
        kernel,
        ids,
        (1,),
        specs,
        out_specs,
        shapes,
        (rows,) * len(specs),
        after=after,
        lag=lag,
        name="widen",
    )


def total_kernel(ids, parts, after=(), lag=0.05):
    rows, width = parts[0].shape

    def kernel(ids_ref, *refs):
        total = refs[0][...].astype(F32)
        for ref in refs[1:-1]:
            total = total + ref[...].astype(F32)
        refs[-1][...] = total

    unit = min(rows, 256)
    tile = pl.BlockSpec((unit, width), lambda i, ids: (i, 0))
    return call(
        kernel,
        ids,
        (rows // unit,),
        [tile] * len(parts),
        tile,
        jax.ShapeDtypeStruct((rows, width), F32),
        tuple(parts),
        after=after,
        lag=lag,
        name="total",
    )


def input_kernel(ids, rows, seed, parts, after=(), lag=0.05):
    count, width = rows.shape

    def kernel(ids_ref, x_ref, g_ref, *refs):
        back = refs[0][...].astype(F32)
        for ref in refs[1:-1]:
            back = back + ref[...].astype(F32)
        data = x_ref[...].astype(F32)
        centre = data - jnp.mean(data, axis=-1, keepdims=True)
        rstd = lax.rsqrt(jnp.mean(centre * centre, axis=-1, keepdims=True) + EPSILON)
        scaled = centre * rstd
        inner = jnp.mean(back * scaled, axis=-1, keepdims=True)
        back = back - jnp.mean(back, axis=-1, keepdims=True) - scaled * inner
        refs[-1][...] = g_ref[...].astype(F32) + rstd * back

    unit = tile_of(count, 256)
    tile = pl.BlockSpec((unit, width), lambda i, ids: (i, 0))
    return call(
        kernel,
        ids,
        (count // unit,),
        [tile] * (2 + len(parts)),
        tile,
        jax.ShapeDtypeStruct((count, width), F32),
        (rows, seed, *parts),
        after=after,
        lag=lag,
        name="input",
    )


def rotary_tables(length):
    position = jnp.arange(length, dtype=F32)[:, None]
    lane = jnp.arange(128)
    half = ROTARY // 2
    frequency = 10000.0 ** (-2.0 * (lane % half).astype(F32) / ROTARY)
    angles = position * frequency[None, :]
    sine = jnp.sin(angles)
    return (
        jnp.where(lane < ROTARY, jnp.cos(angles), 1.0),
        jnp.where(lane < half, -sine, 0.0),
        jnp.where((lane >= half) & (lane < ROTARY), sine, 0.0),
    )


def flip(value, axis, bit, size):
    return lax.ppermute(value, axis, [(i, i ^ bit) for i in range(size)])


def sum_over(value, axis, size):
    bit = 1
    while bit < size:
        value = value + flip(value, axis, bit, size)
        bit *= 2
    return value


def half_kernel(ids, rows, number, after=(), lag=0.05):
    count, width = rows.shape[0] // 2, rows.shape[1]

    def kernel(ids_ref, in_ref, out_ref):
        out_ref[...] = in_ref[...]

    return call(
        kernel,
        ids,
        (1,),
        [pl.BlockSpec((count, width), lambda i, ids: (number, 0))],
        pl.BlockSpec((count, width), lambda i, ids: (0, 0)),
        jax.ShapeDtypeStruct((count, width), BF16),
        (rows,),
        after=after,
        lag=lag,
        name="half",
    )


def gather_rows(ids, rows, size, after=()):
    if size != 4:
        return [rows] + [flip(rows, "tensor", k, size) for k in range(1, size)]
    one = flip(rows, "tensor", 1, size)
    two = flip(rows, "tensor", 2, size)
    upper = flip(half_kernel(ids, two, 0, after), "tensor", 1, size)
    lower = flip(half_kernel(ids, one, 1, after), "tensor", 2, size)
    return [rows, one, two, upper, lower]


def swap_core(value, size):
    return flip(value, "dp", 1, size)


class LineGather:
    def __init__(self, ids, shard, core, size):
        self.ids, self.size = ids, size
        depth, width = shard.shape
        halves = jnp.transpose(shard.reshape(depth, 2, width // 2), (1, 0, 2))
        self.mine = lax.dynamic_index_in_dim(halves, core, 0, keepdims=False)
        self.other = swap_core(lax.dynamic_index_in_dim(halves, 1 - core, 0, keepdims=False), size)
        self.bit, self.place, self.chunks = size // 4, 1, 1
        self.first = True

    def step(self, after=()):
        self.mine = join_kernel(self.ids, self.mine, self.other, self.place, self.chunks, after)
        self.chunks = 1 if self.first else 2 * self.chunks
        self.first = False
        self.place = 1 + self.bit.bit_length()
        self.other = flip(self.mine, "dp", 2 * self.bit, self.size)
        self.bit //= 2
        return self.mine

    def open(self):
        return self.bit >= 1

    def cross(self, after=()):
        self.other = stack_kernel(self.ids, [self.other], self.other.shape[0], after=after)
        self.across = [swap_core(value, self.size) for value in (self.mine, self.other)]
        return self.other

    def finish(self, after=()):
        return assemble_kernel(self.ids, (self.mine, self.other, *self.across), self.place, self.chunks, after)


def body(
    layer_input,
    cotangent,
    firstgain,
    firstbias,
    secondgain,
    secondbias,
    project,
    projbias,
    merging,
    mergebias,
    expand,
    expandbias,
    shrink,
    shrinkbias,
):
    n_dp, n_tensor = lax.axis_size("dp"), lax.axis_size("tensor")
    dp_at, tensor_at = lax.axis_index("dp"), lax.axis_index("tensor")
    chip, core = dp_at // 2, dp_at % 2
    bits = [(chip >> bit) & 1 for bit in range((n_dp // 2).bit_length() - 1)]
    ids = jnp.stack([tensor_at, core, *bits]).astype(jnp.int32)
    own_count, width = layer_input.shape
    group_count = own_count * n_tensor
    assert group_count == LENGTH
    depth = width // n_dp
    heads = project.shape[1]
    mixed_width = heads * 3 * HEAD_DIM
    hidden_width = expand.shape[1]

    packed = jnp.concatenate(
        [firstgain, firstbias, secondgain, secondbias, mergebias, shrinkbias, expandbias, projbias.reshape(-1)]
    )
    slots = jnp.where(jnp.arange(n_dp)[:, None] == dp_at, packed[None, :], jnp.zeros((), BF16))
    slots = sum_over(slots, "dp", n_dp).astype(F32)
    vectors = jnp.transpose(slots[:, : 6 * depth].reshape(n_dp, 6, depth), (1, 0, 2)).reshape(6, width)
    at = 6 * depth
    part = hidden_width // n_dp
    b_expand = slots[:, at : at + part].reshape(1, hidden_width)
    at += part
    b_project = jnp.transpose(slots[:, at:].reshape(n_dp, heads, -1), (1, 0, 2)).reshape(1, mixed_width)

    tables = rotary_tables(LENGTH)
    own_project = project.reshape(depth, mixed_width)
    w_project = lax.all_gather(own_project, "dp", axis=0, tiled=True)
    w_expand = lax.all_gather(expand, "dp", axis=0, tiled=True)
    shrink_line = LineGather(ids, jnp.transpose(shrink), core, n_dp)
    merge_line = LineGather(ids, jnp.transpose(merging), core, n_dp)
    last = shrink_line.step()
    last = merge_line.step((last,))

    unit = own_count
    rows_pieces = gather_rows(ids, layer_input, n_tensor, (vectors, last))
    near, far = (rows_pieces[:-1], rows_pieces[-1:]) if n_tensor != 4 else (rows_pieces[:3], rows_pieces[3:])
    pair = norm_kernel(ids, near, vectors, unit, 0, n_tensor)
    mixed = mixed_kernel(ids, pair[0], w_project, b_project, tables, 0, n_tensor - 1, n_tensor)
    later = stack_kernel(ids, [cotangent], unit, after=(mixed[0], *far))
    seed_pieces = [later] + [flip(later, "tensor", k, n_tensor) for k in range(n_tensor - 1, 0, -1)]
    last = later
    while shrink_line.open():
        last = shrink_line.step((last,))
    first, second = norm_kernel(ids, far, vectors, unit, n_tensor - 1, n_tensor, kept=pair, after=(last,))
    (mixed,) = mixed_kernel(ids, first, w_project, b_project, tables, n_tensor - 1, 1, n_tensor, kept=mixed)
    last = mixed
    while merge_line.open():
        last = merge_line.step((last,))
    context, lse = attend_kernel(ids, mixed, n_tensor, after=(last,), lag=12)
    last = merge_line.cross((context,))
    hidden, slope = expand_kernel(ids, second, w_expand, b_expand, after=(last,))
    last = shrink_line.cross((hidden,))
    seed = stack_kernel(ids, seed_pieces[:1] + seed_pieces[:0:-1], unit, after=(last,))
    w_merge = merge_line.finish((seed,))
    w_shrink = shrink_line.finish((w_merge,))
    (merge_part,) = full_grad_kernel(ids, context, seed, after=(w_shrink,))
    merging_grad = lax.psum_scatter(merge_part, "dp", scatter_dimension=1, tiled=True)
    (shrink_part,) = full_grad_kernel(ids, hidden, seed, after=(merge_part,))
    shrink_grad = lax.psum_scatter(shrink_part, "dp", scatter_dimension=1, tiled=True)
    cgrad = plain_kernel(ids, seed, w_merge, after=(shrink_part,))
    (merging_grad,) = widen_kernel(ids, merging_grad, after=(cgrad,))
    mgrad, mixed_sum = attend_back_kernel(
        ids, mixed, cgrad, context, lse, tables, n_tensor, after=(merging_grad,), lag=30
    )
    project_part, gain_one, bias_one = full_grad_kernel(ids, first, mgrad, w_project, mixed_sum)
    project_grad = lax.psum_scatter(project_part, "dp", scatter_dimension=0, tiled=True)
    branches = branches_kernel(ids, context, w_merge, hidden, w_shrink, n_tensor, after=(project_part,))
    summed = [branches[0]] + [flip(branches[k], "tensor", k, n_tensor) for k in range(n_tensor - 1, 0, -1)]
    pgrad, expand_sum = shrink_back_kernel(ids, seed, w_shrink, slope, after=(branches[0],))
    expand_part, gain_two, bias_two = full_grad_kernel(ids, second, pgrad, w_expand, expand_sum, spare=128)

    def slots(values):
        return jnp.pad(values, ((0, 0), (0, depth - values.shape[1]))).reshape(width)

    narrow = [
        jnp.sum(cotangent.astype(F32), axis=0),
        slots(expand_sum.reshape(n_dp, -1)),
        slots(jnp.transpose(mixed_sum.reshape(heads, n_dp, -1), (1, 0, 2)).reshape(n_dp, -1)),
    ]
    narrow = jnp.pad(jnp.stack(narrow, axis=1), ((0, 0), (4, 128 - 4 - len(narrow))))
    expand_part = spare_kernel(ids, expand_part, [gain_one, bias_one, gain_two, bias_two], narrow)
    expand_grad = lax.psum_scatter(expand_part, "dp", scatter_dimension=0, tiled=True)
    (shrink_grad,) = widen_kernel(ids, shrink_grad, after=(expand_part,))
    gains = jnp.stack([vectors[0], vectors[2]])
    step = n_tensor // 2
    made = back_kernel(ids, mgrad, w_project, pgrad, w_expand, gains, step, step, n_tensor, after=(shrink_grad,))
    back_far = [flip(made[k], "tensor", step + k, n_tensor) for k in range(step - 1, -1, -1)]
    made = back_kernel(ids, mgrad, w_project, pgrad, w_expand, gains, 0, step, n_tensor, after=(made[0],))
    back = [made[0]] + [flip(made[k], "tensor", k, n_tensor) for k in range(step - 1, 0, -1)]
    layer_output = output_kernel(ids, layer_input, summed, vectors, after=(made[0],), lag=10)
    (project_grad,) = widen_kernel(ids, project_grad, after=(layer_output,))
    back_far = total_kernel(ids, back_far, after=(project_grad,), lag=4)
    input_grad = input_kernel(ids, layer_input, cotangent, back + [back_far], lag=160)

    expand_grad, sums = widen_kernel(ids, expand_grad, spare=128)
    sums = jnp.transpose(sums[:, :7] + sums[:, 64:71])
    norms = sums[:5]
    norms = norms + sum(flip(norms, "tensor", k, n_tensor) for k in range(1, n_tensor))
    gain_one, bias_one, gain_two, bias_two, seed_sum = norms
    gain_one = (gain_one - firstbias.astype(F32) * bias_one) / firstgain.astype(F32)
    gain_two = (gain_two - secondbias.astype(F32) * bias_two) / secondgain.astype(F32)
    expandbias_grad = sums[5, : expandbias.shape[0]]
    projbias_grad = sums[6, : projbias.size].reshape(projbias.shape)
    return (
        layer_output,
        input_grad,
        gain_one,
        bias_one,
        gain_two,
        bias_two,
        project_grad.reshape(project.shape),
        projbias_grad,
        merging_grad,
        seed_sum,
        expand_grad,
        expandbias_grad,
        shrink_grad,
        seed_sum,
    )


def solution(mesh):
    specs = (
        P(("dp", "tensor"), None),
        P(("dp", "tensor"), None),
        P("dp"),
        P("dp"),
        P("dp"),
        P("dp"),
        P("dp", "tensor", None),
        P("tensor", "dp"),
        P("tensor", "dp"),
        P("dp"),
        P("dp", "tensor"),
        P(("tensor", "dp")),
        P("tensor", "dp"),
        P("dp"),
    )
    return jax.shard_map(body, mesh=mesh, in_specs=specs, out_specs=specs, check_vma=False)
```

time: 748 us -> 695 us (0.929)
  starting transfers between devices: 128 us -> 36.6 us
  Pallas kernels: 322 us -> 409 us
  other arithmetic: 55.7 us -> 9.85 us
  local copies, waits for them, and re-layouts: 50.3 us -> 27.5 us
  waiting for transfers between devices: 165 us -> 187 us
    ppermute x24 -> x0, starting transfers between devices: 88.5 us -> none  [the longest x12 74.8 us: line_sum(): lax.ppermute(send_up, 'dp', [(2 * a + k, 2 * b + k) for a, b in pairs for...]
    pallas_call x17 -> x36, Pallas kernels: 322 us -> 409 us  [call(): pl.pallas_call(run, grid_spec=pltpu.PrefetchScalarGridSpec(num_scalar_pre...]
    ppermute x26 -> x29, waiting for transfers between devices: 85.9 us -> 170 us  [flip(): return lax.ppermute(value, axis, [(i, i ^ bit) for i in range(size)])]
    ppermute x24 -> x0, waiting for transfers between devices: 65.6 us -> none  [the longest x12 55.5 us: line_sum(): lax.ppermute(send_up, 'dp', [(2 * a + k, 2 * b + k) for a, b in pairs for...]
    convert_element_type x20 -> x0, other arithmetic: 28.1 us -> none  [the longest x8 13.3 us: line_sum(): send_up = (send_up.astype(F32) + up.astype(F32)).astype(BF16)]
    all_gather x1, waiting for transfers between devices: 0.01 us -> 15.6 us  [body(): w_project = lax.all_gather(own_project, 'dp', axis=0, tiled=True)]
    reduce_sum x6 -> x1, other arithmetic: 13.1 us -> 0.37 us  [body(): jnp.sum(cotangent.astype(F32), axis=0)]
    all_gather x2 -> x0, waiting for transfers between devices: 11.9 us -> none  [the longest x1 11.9 us: body(): w_shrink = lax.all_gather(shrink, 'dp', axis=1, tiled=True)]
  transfers between devices with their start and end apart: 56 -> 35, of which waited for: 20 -> 12; matrix products, arithmetic and copies ran while one was open for 13% -> 3% of each run, Pallas kernels for 35% -> 56%
where the time goes in v3:
time: 695 us; the launch traced here: 685 us
  Pallas kernels  409 us (59%)
  waiting for transfers between devices  187 us (27%)
  starting transfers between devices  36.6 us (5%)
  local copies, waits for them, and re-layouts  27.5 us (4%)
  between operations  15 us (2%)
  other arithmetic  9.85 us (1%)
    pallas_call x36, Pallas kernels, call(): pl.pallas_call(run, grid_spec=pltpu.PrefetchScalarGridSpec(num_scalar_pre...  409 us
    ppermute x29, waiting for transfers between devices, flip(): return lax.ppermute(value, axis, [(i, i ^ bit) for i in range(size)])  170 us
    ppermute x29, starting transfers between devices, flip(): return lax.ppermute(value, axis, [(i, i ^ bit) for i in range(size)])  36.4 us
    unnamed x91, local copies, waits for them, and re-layouts  18.2 us
    all_gather x1, waiting for transfers between devices, body(): w_project = lax.all_gather(own_project, 'dp', axis=0, tiled=True)  15.6 us
  transfers between devices with their start and end apart: 35, of which 12 were waited for; matrix products, arithmetic and copies ran while one was open for 3% of the time, Pallas kernels for 56%

profile of v3, /device:TPU:0, one launch (start us, length us, event | category | flops | bytes accessed | tf_op | source)
XLA Modules:
  0.0 685.0 jit_solution(3945084391819775189)
XLA Ops:
  37.0 22.1 %collective-permute-done.7.refs_0_.refs_1_ = bf16[512,2048]{1,0:T(8,128)(2,1)S(1)} collective-permute-done((bf16[512,2048]{1,0:T(8,128)(2,1)}, bf16[512,2048]{1,0:T(8,128)(2,1)S(1)}, u32[]{:S(2)}, u32[]{:S(2)}) %collective-permute-start.7) | collective-permute-done | bytes 2097184 | tf_op jit(solution)/shard_map/ppermute | solution.py:796
  78.0 11.7 %norm.2 = (bf16[2048,2048]{1,0:T(8,128)(2,1)}, bf16[2048,2048]{1,0:T(8,128)(2,1)}) custom-call(s32[4]{0:T(128)} %pad_add_fusion.ids_ref, bf16[512,2048]{1,0:T(8,128)(2,1)} %refs_0_.7, bf16[512,2048]{1,0:T(8,128)(2,1)} %copy-done.3, bf16[512,2048]{1,0:T(8,128)(2,1)} %collective-permute-done.3.refs_0_.refs_2_, f32[6,2048]{1,0:T(8,128)} %bitcast.52), custom_call_target="tpu_custom_call" | custom-call | flops 50000000 | tf_op jit(solution)/shard_map/norm/pallas_call | solution.py:49
  89.7 15.6 %all-gather.3.cloned.1.call-done.refs_1_.refs_2_ = bf16[2048,1536]{1,0:T(8,128)(2,1)} async-done(((bf16[256,1536]{1,0:T(8,128)(2,1)}), bf16[2048,1536]{1,0:T(8,128)(2,1)}) %all-gather.3.cloned.1.call-update) | async-done | bytes 6291472 | tf_op jit(solution)/shard_map/all_gather | solution.py:915
  105.2 18.1 %mixed.2.refs_1_.refs_6_ = bf16[2048,1536]{1,0:T(8,128)(2,1)} custom-call(s32[4]{0:T(128)} %pad_add_fusion.ids_ref, bf16[2048,2048]{1,0:T(8,128)(2,1)} %get-tuple-element.42.refs_0_.refs_3_, bf16[2048,1536]{1,0:T(8,128)(2,1)} %all-gather.3.cloned.1.call-done.refs_1_.refs_2_, f32[1,1536]{1,0:T(1,128)} %reshape.101.refs_2_, ...), custom_call_target="tpu_custom_call" | custom-call | flops 50000000 | tf_op jit(solution)/shard_map/mixed/pallas_call | solution.py:49
  129.0 10.8 %collective-permute-done.9.refs_1_ = bf16[512,1024]{1,0:T(8,128)(2,1)} collective-permute-done((bf16[512,1024]{1,0:T(8,128)(2,1)S(1)}, bf16[512,1024]{1,0:T(8,128)(2,1)}, u32[]{:S(2)}, u32[]{:S(2)}) %collective-permute-start.9) | collective-permute-done | bytes 1048608 | tf_op jit(solution)/shard_map/ppermute | solution.py:796
  154.3 8.2 %mixed.3.refs_2_.refs_0_ = bf16[2048,1536]{1,0:T(8,128)(2,1)} custom-call(s32[4]{0:T(128)} %pad_add_fusion.ids_ref, bf16[2048,2048]{1,0:T(8,128)(2,1)} %get-tuple-element.44.refs_0_, bf16[2048,1536]{1,0:T(8,128)(2,1)} %all-gather.3.cloned.1.call-done.refs_1_.refs_2_, f32[1,1536]{1,0:T(1,128)} %reshape.101.refs_2_, ...), custom_call_target="tpu_custom_call", output_to_operand_aliasing={{}: (7, {})} | custom-call | flops 50000000 | tf_op jit(solution)/shard_map/mixed/pallas_call | solution.py:49
  162.5 69.2 %collective-permute-done.10.refs_1_ = bf16[512,256]{1,0:T(8,128)(2,1)S(1)} collective-permute-done((bf16[512,256]{1,0:T(8,128)(2,1)S(1)}, bf16[512,256]{1,0:T(8,128)(2,1)S(1)}, u32[]{:S(2)}, u32[]{:S(2)}) %collective-permute-start.10) | collective-permute-done | bytes 262176 | tf_op jit(solution)/shard_map/ppermute | solution.py:796
  239.5 22.8 %attend.1 = (bf16[2048,512]{1,0:T(8,128)(2,1)}, f32[2,4,8,512]{3,2,1,0:T(8,128)}) custom-call(s32[4]{0:T(128)} %pad_add_fusion.ids_ref, bf16[2048,1536]{1,0:T(8,128)(2,1)} %mixed.3.refs_2_.refs_0_, bf16[1024,256]{1,0:T(8,128)(2,1)} %join.7.refs_1_.refs_0_), custom_call_target="tpu_custom_call" | custom-call | flops 12000000000 | tf_op jit(solution)/shard_map/attend/pallas_call | solution.py:49
  266.4 30.2 %expand.1 = (bf16[2048,2048]{1,0:T(8,128)(2,1)}, bf16[2048,2048]{1,0:T(8,128)(2,1)}) custom-call(s32[4]{0:T(128)} %pad_add_fusion.ids_ref, bf16[2048,2048]{1,0:T(8,128)(2,1)} %get-tuple-element.46.refs_0_, bf16[2048,2048]{1,0:T(8,128)(2,1)} %all-gather.5.cloned.1.call-done.refs_1_.refs_2_.refs_3_, f32[1,2048]{1,0:T(1,128)} %bitcast.64, ...), custom_call_target="tpu_custom_call" | custom-call | flops 50000000 | tf_op jit(solution)/shard_map/expand/pallas_call | solution.py:49
  301.0 8.3 %collective-permute-done.14.refs_1_ = bf16[512,2048]{1,0:T(8,128)(2,1)} collective-permute-done((bf16[512,2048]{1,0:T(8,128)(2,1)S(1)}, bf16[512,2048]{1,0:T(8,128)(2,1)}, u32[]{:S(2)}, u32[]{:S(2)}) %collective-permute-start.14) | collective-permute-done | bytes 2097184 | tf_op jit(solution)/shard_map/ppermute | solution.py:796
  327.0 10.8 %assemble.3.refs_2_.refs_3_.refs_1_ = bf16[2048,2048]{1,0:T(8,128)(2,1)} custom-call(s32[4]{0:T(128)} %pad_add_fusion.ids_ref, bf16[1024,1024]{1,0:T(8,128)(2,1)} %join.6.refs_5_.refs_0_, bf16[1024,1024]{1,0:T(8,128)(2,1)} %stack.38.refs_4_.refs_1_, bf16[1024,1024]{1,0:T(8,128)(2,1)} %collective-permute-done.18.refs_2_, bf16[1024,1024]{1,0:T(8,128)(2,1)} %copy-done.9, ...), custom_call_target="tpu_custom_call" | custom-call | flops 50000000 | tf_op jit(solution)/shard_map/assemble/pallas_call | solution.py:49
  337.8 9.3 %full_grad.4.refs_2_ = bf16[512,2048]{1,0:T(8,128)(2,1)} custom-call(s32[4]{0:T(128)} %pad_add_fusion.ids_ref, bf16[2048,512]{1,0:T(8,128)(2,1)} %get-tuple-element.45.refs_1_.refs_0_.refs_2_, bf16[2048,2048]{1,0:T(8,128)(2,1)} %stack.39.refs_4_.refs_1_.refs_0_, bf16[2048,2048]{1,0:T(8,128)(2,1)} %assemble.3.refs_2_.refs_3_.refs_1_), custom_call_target="tpu_custom_call" | custom-call | flops 50000000 | tf_op jit(solution)/shard_map/full_grad/pallas_call | solution.py:49
  347.1 23.7 %full_grad.5.refs_2_ = bf16[2048,2048]{1,0:T(8,128)(2,1)} custom-call(s32[4]{0:T(128)} %pad_add_fusion.ids_ref, bf16[2048,2048]{1,0:T(8,128)(2,1)} %get-tuple-element.47.refs_1_.refs_0_.refs_2_, bf16[2048,2048]{1,0:T(8,128)(2,1)} %stack.39.refs_4_.refs_1_.refs_0_, bf16[512,2048]{1,0:T(8,128)(2,1)} %full_grad.4.refs_2_), custom_call_target="tpu_custom_call" | custom-call | flops 50000000 | tf_op jit(solution)/shard_map/full_grad/pallas_call | solution.py:49
  370.9 9.6 %plain.1.refs_1_ = bf16[2048,512]{1,0:T(8,128)(2,1)} custom-call(s32[4]{0:T(128)} %pad_add_fusion.ids_ref, bf16[2048,2048]{1,0:T(8,128)(2,1)} %stack.39.refs_4_.refs_1_.refs_0_, bf16[2048,512]{1,0:T(8,128)(2,1)} %assemble.2.refs_4_.refs_1_, bf16[2048,2048]{1,0:T(8,128)(2,1)} %full_grad.5.refs_2_), custom_call_target="tpu_custom_call" | custom-call | flops 50000000 | tf_op jit(solution)/shard_map/plain/pallas_call | solution.py:49
  383.8 26.9 %attend_back.1 = (bf16[2048,1536]{1,0:T(8,128)(2,1)}, f32[1,1536]{1,0:T(1,128)}) custom-call(s32[4]{0:T(128)} %pad_add_fusion.ids_ref, bf16[2048,1536]{1,0:T(8,128)(2,1)} %mixed.3.refs_2_.refs_0_, bf16[2048,512]{1,0:T(8,128)(2,1)} %plain.1.refs_1_, bf16[2048,512]{1,0:T(8,128)(2,1)} %get-tuple-element.45.refs_1_.refs_0_.refs_2_, ...), custom_call_target="tpu_custom_call" | custom-call | flops 30000001024 | tf_op jit(solution)/shard_map/attend_back/pallas_call | solution.py:49
  410.7 24.9 %full_grad.6 = (bf16[2048,1536]{1,0:T(8,128)(2,1)}, f32[2048,128]{1,0:T(8,128)}, f32[2048,128]{1,0:T(8,128)}) custom-call(s32[4]{0:T(128)} %pad_add_fusion.ids_ref, bf16[2048,2048]{1,0:T(8,128)(2,1)} %get-tuple-element.44.refs_0_, bf16[2048,1536]{1,0:T(8,128)(2,1)} %get-tuple-element.49.refs_1_.refs_0_, ...), custom_call_target="tpu_custom_call" | custom-call | flops 50000000 | tf_op jit(solution)/shard_map/full_grad/pallas_call | solution.py:49
  435.7 30.6 %branches.1 = (bf16[512,2048]{1,0:T(8,128)(2,1)}, bf16[512,2048]{1,0:T(8,128)(2,1)}, bf16[512,2048]{1,0:T(8,128)(2,1)}, bf16[512,2048]{1,0:T(8,128)(2,1)}) custom-call(s32[4]{0:T(128)} %pad_add_fusion.ids_ref, bf16[2048,512]{1,0:T(8,128)(2,1)} %get-tuple-element.45.refs_1_.refs_0_.refs_2_, bf16[2048,512]{1,0:T(8,128)(2,1)} %assemble.2.refs_4_.refs_1_, ...), custom_call_target="tpu_custom_call" | custom-call | flops 50000000 | tf_op jit(solution)/shard_map/branches/pallas_call | solution.py:49
  470.4 25.3 %shrink_back.1 = (bf16[2048,2048]{1,0:T(8,128)(2,1)}, f32[1,2048]{1,0:T(1,128)}) custom-call(s32[4]{0:T(128)} %pad_add_fusion.ids_ref, bf16[2048,2048]{1,0:T(8,128)(2,1)} %stack.39.refs_4_.refs_1_.refs_0_, bf16[2048,2048]{1,0:T(8,128)(2,1)} %assemble.3.refs_2_.refs_3_.refs_1_, bf16[2048,2048]{1,0:T(8,128)(2,1)} %get-tuple-element.56.refs_2_, ...), custom_call_target="tpu_custom_call" | custom-call | flops 50000000 | tf_op jit(solution)/shard_map/shrink_back/pallas_call | solution.py:49
  498.2 26.4 %full_grad.7 = (bf16[2048,2176]{1,0:T(8,128)(2,1)}, f32[2048,128]{1,0:T(8,128)}, f32[2048,128]{1,0:T(8,128)}) custom-call(s32[4]{0:T(128)} %pad_add_fusion.ids_ref, bf16[2048,2048]{1,0:T(8,128)(2,1)} %get-tuple-element.46.refs_0_, bf16[2048,2048]{1,0:T(8,128)(2,1)} %get-tuple-element.57.refs_1_.refs_2_, ...), custom_call_target="tpu_custom_call" | custom-call | flops 50000000 | tf_op jit(solution)/shard_map/full_grad/pallas_call | solution.py:49
  534.6 22.6 %back.2 = (bf16[512,2048]{1,0:T(8,128)(2,1)}, bf16[512,2048]{1,0:T(8,128)(2,1)}) custom-call(s32[4]{0:T(128)} %pad_add_fusion.ids_ref, bf16[2048,1536]{1,0:T(8,128)(2,1)} %get-tuple-element.49.refs_1_.refs_0_, bf16[2048,1536]{1,0:T(8,128)(2,1)} %all-gather.3.cloned.1.call-done.refs_1_.refs_2_, bf16[2048,2048]{1,0:T(8,128)(2,1)} %get-tuple-element.57.refs_1_.refs_2_, ...), custom_call_target="tpu_custom_call" | custom-call | flops 50000000 | tf_op jit(solution)/shard_map/back/pallas_call | solution.py:49
  559.8 23.0 %back.3 = (bf16[512,2048]{1,0:T(8,128)(2,1)}, bf16[512,2048]{1,0:T(8,128)(2,1)}) custom-call(s32[4]{0:T(128)} %pad_add_fusion.ids_ref, bf16[2048,1536]{1,0:T(8,128)(2,1)} %get-tuple-element.49.refs_1_.refs_0_, bf16[2048,1536]{1,0:T(8,128)(2,1)} %all-gather.3.cloned.1.call-done.refs_1_.refs_2_, bf16[2048,2048]{1,0:T(8,128)(2,1)} %get-tuple-element.57.refs_1_.refs_2_, ...), custom_call_target="tpu_custom_call" | custom-call | flops 50000000 | tf_op jit(solution)/shard_map/back/pallas_call | solution.py:49
  596.4 10.5 %collective-permute-done.24.refs_0_ = bf16[512,2048]{1,0:T(8,128)(2,1)S(1)} collective-permute-done((bf16[512,2048]{1,0:T(8,128)(2,1)}, bf16[512,2048]{1,0:T(8,128)(2,1)S(1)}, u32[]{:S(2)}, u32[]{:S(2)}) %collective-permute-start.24) | collective-permute-done | bytes 2097184 | tf_op jit(solution)/shard_map/ppermute | solution.py:796
  606.8 41.0 %collective-permute-done.25.refs_1_ = bf16[512,2048]{1,0:T(8,128)(2,1)} collective-permute-done((bf16[512,2048]{1,0:T(8,128)(2,1)}, bf16[512,2048]{1,0:T(8,128)(2,1)}, u32[]{:S(2)}, u32[]{:S(2)}) %collective-permute-start.25) | collective-permute-done | bytes 2097184 | tf_op jit(solution)/shard_map/ppermute | solution.py:796
  652.4 8.3 %input.1 = f32[512,2048]{1,0:T(8,128)} custom-call(s32[4]{0:T(128)} %pad_add_fusion.ids_ref, bf16[512,2048]{1,0:T(8,128)(2,1)} %refs_0_.7, bf16[512,2048]{1,0:T(8,128)(2,1)} %refs_1_.1, bf16[512,2048]{1,0:T(8,128)(2,1)} %get-tuple-element.65.refs_6_.refs_2_, bf16[512,2048]{1,0:T(8,128)(2,1)} %collective-permute-done.23.refs_3_, f32[512,2048]{1,0:T(8,128)} %total.1.refs_4_), custom_call_target="tpu_custom_call" | custom-call | flops 160000000000 | tf_op jit(solution)/shard_map/input/pallas_call | solution.py:49
  (217 shorter events, 160.3 us)
Async XLA Ops:
  7.3 98.0 %all-gather.3.cloned.1.call-start = ((), (), s32[]{:S(2)}) async-start(), calls=%async_computation.4 | async-start | bytes 7077888 | tf_op jit(solution)/shard_map/all_gather | solution.py:915
  9.5 256.9 %all-gather.5.cloned.1.call-start = ((), (), s32[]{:S(2)}) async-start(), calls=%async_computation.5 | async-start | bytes 9437184 | tf_op jit(solution)/shard_map/all_gather | solution.py:916
  10.3 371.1 %reduce-scatter.5.cloned.1.call-start = ((), (), s32[]{:S(2)}) async-start(), calls=%async_computation.6 | async-start | bytes 2359296 | tf_op jit(solution)/shard_map/reduce_scatter | solution.py:945
  10.3 48.8 %collective-permute-start.7 = (bf16[512,2048]{1,0:T(8,128)(2,1)}, bf16[512,2048]{1,0:T(8,128)(2,1)S(1)}, u32[]{:S(2)}, u32[]{:S(2)}) collective-permute-start(bf16[512,2048]{1,0:T(8,128)(2,1)} %refs_0_.7), channel_id=1, source_target_pairs={{0,1},{1,0},{2,3},{3,2},{4,5},{5,4},{6,7},{7,6},{8,9},{9,8},{10,11... | collective-permute-start | bytes 6291464 | tf_op jit(solution)/shard_map/ppermute | solution.py:796
  13.3 51.9 %collective-permute-start.3 = (bf16[512,2048]{1,0:T(8,128)(2,1)}, bf16[512,2048]{1,0:T(8,128)(2,1)}, u32[]{:S(2)}, u32[]{:S(2)}) collective-permute-start(bf16[512,2048]{1,0:T(8,128)(2,1)} %refs_0_.7), channel_id=1, source_target_pairs={{0,2},{1,3},{2,0},{3,1},{4,6},{5,7},{6,4},{7,5},{8,10},{9,11},{10,... | collective-permute-start | bytes 6291464 | tf_op jit(solution)/shard_map/ppermute | solution.py:796
  63.4 59.9 %collective-permute-start.8 = (bf16[256,2048]{1,0:T(8,128)(2,1)}, bf16[256,2048]{1,0:T(8,128)(2,1)S(1)}, u32[]{:S(2)}, u32[]{:S(2)}) collective-permute-start(bf16[256,2048]{1,0:T(8,128)(2,1)} %half.3), channel_id=1, source_target_pairs={{0,2},{1,3},{2,0},{3,1},{4,6},{5,7},{6,4},{7,5},{8,10},{9,11},{10,... | collective-permute-start | bytes 3145736 | tf_op jit(solution)/shard_map/ppermute | solution.py:796
  68.1 55.2 %collective-permute-start.6 = (bf16[256,2048]{1,0:T(8,128)(2,1)}, bf16[256,2048]{1,0:T(8,128)(2,1)S(1)}, u32[]{:S(2)}, u32[]{:S(2)}) collective-permute-start(bf16[256,2048]{1,0:T(8,128)(2,1)} %half.2), channel_id=1, source_target_pairs={{0,1},{1,0},{2,3},{3,2},{4,5},{5,4},{6,7},{7,6},{8,9},{9,8},{10,11... | collective-permute-start | bytes 3145736 | tf_op jit(solution)/shard_map/ppermute | solution.py:796
  69.6 70.1 %collective-permute-start.9 = (bf16[512,1024]{1,0:T(8,128)(2,1)S(1)}, bf16[512,1024]{1,0:T(8,128)(2,1)}, u32[]{:S(2)}, u32[]{:S(2)}) collective-permute-start(bf16[512,1024]{1,0:T(8,128)(2,1)S(1)} %copy-done.1), channel_id=1, source_target_pairs={{0,16},{4,20},{8,24},{12,28},{16,0},{20,4},{24,8},{28,12},{1,17},{... | collective-permute-start | bytes 3145736 | tf_op jit(solution)/shard_map/ppermute | solution.py:796
  143.4 153.2 %collective-permute-start.17 = (bf16[1024,1024]{1,0:T(8,128)(2,1)}, bf16[1024,1024]{1,0:T(8,128)(2,1)}, u32[]{:S(2)}, u32[]{:S(2)}) collective-permute-start(bf16[1024,1024]{1,0:T(8,128)(2,1)} %join.6.refs_5_.refs_0_), channel_id=1, source_target_pairs={{0,8},{4,12},{8,0},{12,4},{16,24},{20,28},{24,16},{28,20},{1,9},{5... | collective-permute-start | bytes 6291464 | tf_op jit(solution)/shard_map/ppermute | solution.py:796
  143.4 88.4 %collective-permute-start.10 = (bf16[512,256]{1,0:T(8,128)(2,1)S(1)}, bf16[512,256]{1,0:T(8,128)(2,1)S(1)}, u32[]{:S(2)}, u32[]{:S(2)}) collective-permute-start(bf16[512,256]{1,0:T(8,128)(2,1)S(1)} %copy-done.7), channel_id=1, source_target_pairs={{0,16},{4,20},{8,24},{12,28},{16,0},{20,4},{24,8},{28,12},{1,17},{... | collective-permute-start | bytes 786440 | tf_op jit(solution)/shard_map/ppermute | solution.py:796
  145.3 180.3 %collective-permute-start.18 = (bf16[1024,1024]{1,0:T(8,128)(2,1)}, bf16[1024,1024]{1,0:T(8,128)(2,1)}, u32[]{:S(2)}, u32[]{:S(2)}) collective-permute-start(bf16[1024,1024]{1,0:T(8,128)(2,1)} %join.6.refs_5_.refs_0_), channel_id=1, source_target_pairs={{0,4},{4,0},{8,12},{12,8},{16,20},{20,16},{24,28},{28,24},{1,5},{5... | collective-permute-start | bytes 6291464 | tf_op jit(solution)/shard_map/ppermute | solution.py:796
  145.3 155.2 %collective-permute-start.16 = (bf16[512,2048]{1,0:T(8,128)(2,1)S(1)}, bf16[512,2048]{1,0:T(8,128)(2,1)}, u32[]{:S(2)}, u32[]{:S(2)}) collective-permute-start(bf16[512,2048]{1,0:T(8,128)(2,1)S(1)} %copy-done), channel_id=1, source_target_pairs={{0,3},{1,2},{2,1},{3,0},{4,7},{5,6},{6,5},{7,4},{8,11},{9,10},{10,... | collective-permute-start | bytes 6291464 | tf_op jit(solution)/shard_map/ppermute | solution.py:796
  147.5 153.4 %collective-permute-start.15 = (bf16[512,2048]{1,0:T(8,128)(2,1)S(1)}, bf16[512,2048]{1,0:T(8,128)(2,1)}, u32[]{:S(2)}, u32[]{:S(2)}) collective-permute-start(bf16[512,2048]{1,0:T(8,128)(2,1)S(1)} %copy-done), channel_id=1, source_target_pairs={{0,2},{1,3},{2,0},{3,1},{4,6},{5,7},{6,4},{7,5},{8,10},{9,11},{10,... | collective-permute-start | bytes 6291464 | tf_op jit(solution)/shard_map/ppermute | solution.py:796
  235.0 27.4 %collective-permute-start.11 = (bf16[1024,256]{1,0:T(8,128)(2,1)}, bf16[1024,256]{1,0:T(8,128)(2,1)S(1)}, u32[]{:S(2)}, u32[]{:S(2)}) collective-permute-start(bf16[1024,256]{1,0:T(8,128)(2,1)} %join.7.refs_1_.refs_0_), channel_id=1, source_target_pairs={{0,8},{4,12},{8,0},{12,4},{16,24},{20,28},{24,16},{28,20},{1,9},{5... | collective-permute-start | bytes 1572872 | tf_op jit(solution)/shard_map/ppermute | solution.py:796
  262.3 47.0 %collective-permute-start.14 = (bf16[512,2048]{1,0:T(8,128)(2,1)S(1)}, bf16[512,2048]{1,0:T(8,128)(2,1)}, u32[]{:S(2)}, u32[]{:S(2)}) collective-permute-start(bf16[512,2048]{1,0:T(8,128)(2,1)S(1)} %copy-done), channel_id=1, source_target_pairs={{0,1},{1,0},{2,3},{3,2},{4,5},{5,4},{6,7},{7,6},{8,9},{9,8},{10,11... | collective-permute-start | bytes 6291464 | tf_op jit(solution)/shard_map/ppermute | solution.py:796
  347.0 184.2 %reduce-scatter.7.cloned.1.call-start = ((), (), s32[]{:S(2)}) async-start(), calls=%async_computation.7 | async-start | bytes 9437184 | tf_op jit(solution)/shard_map/reduce_scatter | solution.py:947
  370.8 219.4 %reduce-scatter.9.cloned.1.call-start = ((), (), s32[]{:S(2)}) async-start(), calls=%async_computation.8 | async-start | bytes 7077888 | tf_op jit(solution)/shard_map/reduce_scatter | solution.py:954
  435.7 225.1 %reduce-scatter.11.cloned.1.call-start = ((), (), s32[]{:S(2)}) async-start(), calls=%async_computation.9 | async-start | bytes 10027008 | tf_op jit(solution)/shard_map/reduce_scatter | solution.py:970
  466.3 116.5 %collective-permute-start.20 = (bf16[512,2048]{1,0:T(8,128)(2,1)}, bf16[512,2048]{1,0:T(8,128)(2,1)}, u32[]{:S(2)}, u32[]{:S(2)}) collective-permute-start(bf16[512,2048]{1,0:T(8,128)(2,1)} %get-tuple-element.53), channel_id=1, source_target_pairs={{0,3},{1,2},{2,1},{3,0},{4,7},{5,6},{6,5},{7,4},{8,11},{9,10},{10,... | collective-permute-start | bytes 6291464 | tf_op jit(solution)/shard_map/ppermute | solution.py:796
  468.4 115.3 %collective-permute-start.21 = (bf16[512,2048]{1,0:T(8,128)(2,1)}, bf16[512,2048]{1,0:T(8,128)(2,1)}, u32[]{:S(2)}, u32[]{:S(2)}) collective-permute-start(bf16[512,2048]{1,0:T(8,128)(2,1)} %get-tuple-element.54), channel_id=1, source_target_pairs={{0,2},{1,3},{2,0},{3,1},{4,6},{5,7},{6,4},{7,5},{8,10},{9,11},{10,... | collective-permute-start | bytes 6291464 | tf_op jit(solution)/shard_map/ppermute | solution.py:796
  469.0 114.7 %collective-permute-start.22 = (bf16[512,2048]{1,0:T(8,128)(2,1)}, bf16[512,2048]{1,0:T(8,128)(2,1)}, u32[]{:S(2)}, u32[]{:S(2)}) collective-permute-start(bf16[512,2048]{1,0:T(8,128)(2,1)} %get-tuple-element.55), channel_id=1, source_target_pairs={{0,1},{1,0},{2,3},{3,2},{4,5},{5,4},{6,7},{7,6},{8,9},{9,8},{10,11... | collective-permute-start | bytes 6291464 | tf_op jit(solution)/shard_map/ppermute | solution.py:796
  557.2 49.7 %collective-permute-start.24 = (bf16[512,2048]{1,0:T(8,128)(2,1)}, bf16[512,2048]{1,0:T(8,128)(2,1)S(1)}, u32[]{:S(2)}, u32[]{:S(2)}) collective-permute-start(bf16[512,2048]{1,0:T(8,128)(2,1)} %get-tuple-element.67), channel_id=1, source_target_pairs={{0,3},{1,2},{2,1},{3,0},{4,7},{5,6},{6,5},{7,4},{8,11},{9,10},{10,... | collective-permute-start | bytes 6291464 | tf_op jit(solution)/shard_map/ppermute | solution.py:796
  559.3 88.6 %collective-permute-start.25 = (bf16[512,2048]{1,0:T(8,128)(2,1)}, bf16[512,2048]{1,0:T(8,128)(2,1)}, u32[]{:S(2)}, u32[]{:S(2)}) collective-permute-start(bf16[512,2048]{1,0:T(8,128)(2,1)} %get-tuple-element.64.refs_5_), channel_id=1, source_target_pairs={{0,2},{1,3},{2,0},{3,1},{4,6},{5,7},{6,4},{7,5},{8,10},{9,11},{10,... | collective-permute-start | bytes 6291464 | tf_op jit(solution)/shard_map/ppermute | solution.py:796
  582.8 69.6 %collective-permute-start.23 = (bf16[512,2048]{1,0:T(8,128)(2,1)}, bf16[512,2048]{1,0:T(8,128)(2,1)}, u32[]{:S(2)}, u32[]{:S(2)}) collective-permute-start(bf16[512,2048]{1,0:T(8,128)(2,1)} %get-tuple-element.66), channel_id=1, source_target_pairs={{0,1},{1,0},{2,3},{3,2},{4,5},{5,4},{6,7},{7,6},{8,9},{9,8},{10,11... | collective-permute-start | bytes 6291464 | tf_op jit(solution)/shard_map/ppermute | solution.py:796
  (46 other events, 423.5 us)
Sparse Core Ops, SparseCore 0:
  10.3 94.8 all-gather.2
  106.8 112.5 all-gather.4
  347.2 34.1 reduce-scatter.4
  383.5 88.2 reduce-scatter.6
  474.0 68.1 reduce-scatter.8
  544.3 92.9 reduce-scatter.10

commit v4 on v3

--- a/solution.py
+++ b/solution.py
@@ -430,31 +430,27 @@
 
             @pl.when(pl.program_id(0) == step)
             def _(ref=ref):
-                refs[4][...] = ref[...]
-
-    def spec(step):
-        def place(s, i, ids):
-            return jnp.where(s == step, i, jnp.where(s < step, 0, chunks - 1)), 0
-
-        return pl.BlockSpec((rows, width), place)
-
-    return call(
-        kernel,
-        ids,
-        (4, chunks),
-        [spec(step) for step in range(4)],
-        pl.BlockSpec((rows, width), lambda s, i, ids: (2 * i + ((s & 1) ^ ids[bit]), (s >> 1) ^ ids[1])),
-        jax.ShapeDtypeStruct((2 * chunks * rows, 2 * width), BF16),
+                refs[4][...] = ref[...].reshape(chunks, 1, rows, width)
+
+    whole = pl.BlockSpec((chunks * rows, width), lambda s, ids: (0, 0))
+    made = call(
+        kernel,
+        ids,
+        (4,),
+        [whole] * 4,
+        pl.BlockSpec((chunks, 1, rows, width), lambda s, ids: (0, (s & 1) ^ ids[bit], 0, (s >> 1) ^ ids[1])),
+        jax.ShapeDtypeStruct((chunks, 2, rows, 2 * width), BF16),
         tuple(parts),
         after=after,
         lag=lag,
         name="assemble",
     )
+    return made.reshape(2 * chunks * rows, 2 * width)
 
 
 def shrink_back_kernel(ids, seed, weight, slope, after=(), lag=0.05):
     rows, depth = seed.shape
-    width = weight.shape[1]
+    width = weight.shape[0]
     tall, wide = tile_of(rows, 1024), tile_of(width, 1024)
     unit = tile_of(wide, 512)
 
@@ -465,7 +461,7 @@
 
         for part in range(wide // unit):
             here = slice(part * unit, (part + 1) * unit)
-            grad = product(a_ref[...], w_ref[:, here], "NN") * s_ref[:, here].astype(F32)
+            grad = product(a_ref[...], w_ref[here, :], "NT") * s_ref[:, here].astype(F32)
             rounded = grad.astype(BF16)
             out_ref[:, here] = rounded
             sum_ref[:, here] += jnp.sum(rounded.astype(F32), axis=0, keepdims=True)
@@ -477,7 +473,7 @@
         (width // wide, rows // tall),
         [
             pl.BlockSpec((tall, depth), lambda j, i, ids: (i, 0)),
-            pl.BlockSpec((depth, wide), lambda j, i, ids: (0, j)),
+            pl.BlockSpec((wide, depth), lambda j, i, ids: (j, 0)),
             tile,
         ],
         [tile, pl.BlockSpec((1, wide), lambda j, i, ids: (0, j))],
@@ -527,7 +523,7 @@
             def _(out_ref=out_ref):
                 for part in range(wide // unit):
                     here = slice(part * unit, (part + 1) * unit)
-                    value = product(h_ref[...], s_ref[here, :], "NT")
+                    value = product(h_ref[...], s_ref[:, here], "NN")
                     value = value + product(a_ref[...], m_ref[here, :], "NT")
                     out_ref[:, here] = value.astype(BF16)
 
@@ -539,7 +535,7 @@
             pl.BlockSpec((tall, deep_a), lambda j, i, ids: (i, 0)),
             pl.BlockSpec((wide, deep_a), lambda j, i, ids: (j, 0)),
             pl.BlockSpec((tall, deep_b), lambda j, i, ids: (i, 0)),
-            pl.BlockSpec((wide, deep_b), lambda j, i, ids: (j, 0)),
+            pl.BlockSpec((deep_b, wide), lambda j, i, ids: (0, j)),
         ],
         [pl.BlockSpec((tall, wide), lambda j, i, ids: (0, j))] * blocks,
         [jax.ShapeDtypeStruct((tall, depth), BF16)] * blocks,
@@ -588,7 +584,7 @@
     )
 
 
-def full_grad_kernel(ids, left, right, weight=None, total=None, spare=0, after=(), lag=0.05):
+def full_grad_kernel(ids, left, right, weight=None, total=None, spare=0, start=0, count=0, kept=(), after=(), lag=0.05):
     rows, depth = left.shape
     width = right.shape[1]
     tall, wide = tile_of(depth, 1024), tile_of(width, 1024)
@@ -619,8 +615,8 @@
         pl.BlockSpec((rows, tall), lambda i, j, ids: (0, i)),
         pl.BlockSpec((rows, wide), lambda i, j, ids: (0, j)),
     ]
-    out_specs = [tile]
-    out_shape = [jax.ShapeDtypeStruct((depth, width + spare), BF16)]
+    out_specs = [pl.BlockSpec((tall, wide), lambda i, j, ids: (start // tall + i, j))]
+    out_shape = [jax.ShapeDtypeStruct((count or depth, width + spare), BF16)]
     args = (left, right)
     if summed:
         args += (weight, total)
@@ -635,6 +631,7 @@
         out_specs,
         out_shape,
         args,
+        kept=kept,
         after=after,
         lag=lag,
         name="full_grad",
@@ -914,22 +911,17 @@
     own_project = project.reshape(depth, mixed_width)
     w_project = lax.all_gather(own_project, "dp", axis=0, tiled=True)
     w_expand = lax.all_gather(expand, "dp", axis=0, tiled=True)
-    shrink_line = LineGather(ids, jnp.transpose(shrink), core, n_dp)
+    w_shrink = lax.all_gather(shrink, "dp", axis=1, tiled=True)
     merge_line = LineGather(ids, jnp.transpose(merging), core, n_dp)
-    last = shrink_line.step()
-    last = merge_line.step((last,))
-
     unit = own_count
-    rows_pieces = gather_rows(ids, layer_input, n_tensor, (vectors, last))
+    rows_pieces = gather_rows(ids, layer_input, n_tensor, (vectors,))
     near, far = (rows_pieces[:-1], rows_pieces[-1:]) if n_tensor != 4 else (rows_pieces[:3], rows_pieces[3:])
     pair = norm_kernel(ids, near, vectors, unit, 0, n_tensor)
     mixed = mixed_kernel(ids, pair[0], w_project, b_project, tables, 0, n_tensor - 1, n_tensor)
-    later = stack_kernel(ids, [cotangent], unit, after=(mixed[0], *far))
+    last = merge_line.step((mixed[0],))
+    later = stack_kernel(ids, [cotangent], unit, after=(last, *far))
     seed_pieces = [later] + [flip(later, "tensor", k, n_tensor) for k in range(n_tensor - 1, 0, -1)]
-    last = later
-    while shrink_line.open():
-        last = shrink_line.step((last,))
-    first, second = norm_kernel(ids, far, vectors, unit, n_tensor - 1, n_tensor, kept=pair, after=(last,))
+    first, second = norm_kernel(ids, far, vectors, unit, n_tensor - 1, n_tensor, kept=pair, after=(later,))
     (mixed,) = mixed_kernel(ids, first, w_project, b_project, tables, n_tensor - 1, 1, n_tensor, kept=mixed)
     last = mixed
     while merge_line.open():
@@ -937,19 +929,15 @@
     context, lse = attend_kernel(ids, mixed, n_tensor, after=(last,), lag=12)
     last = merge_line.cross((context,))
     hidden, slope = expand_kernel(ids, second, w_expand, b_expand, after=(last,))
-    last = shrink_line.cross((hidden,))
-    seed = stack_kernel(ids, seed_pieces[:1] + seed_pieces[:0:-1], unit, after=(last,))
-    w_merge = merge_line.finish((seed,))
-    w_shrink = shrink_line.finish((w_merge,))
-    (merge_part,) = full_grad_kernel(ids, context, seed, after=(w_shrink,))
-    merging_grad = lax.psum_scatter(merge_part, "dp", scatter_dimension=1, tiled=True)
-    (shrink_part,) = full_grad_kernel(ids, hidden, seed, after=(merge_part,))
-    shrink_grad = lax.psum_scatter(shrink_part, "dp", scatter_dimension=1, tiled=True)
-    cgrad = plain_kernel(ids, seed, w_merge, after=(shrink_part,))
-    (merging_grad,) = widen_kernel(ids, merging_grad, after=(cgrad,))
-    mgrad, mixed_sum = attend_back_kernel(
-        ids, mixed, cgrad, context, lse, tables, n_tensor, after=(merging_grad,), lag=30
-    )
+    w_merge = merge_line.finish((hidden,))
+    seed = stack_kernel(ids, seed_pieces[:1] + seed_pieces[:0:-1], unit, after=(w_merge,))
+    merge_width = merging.shape[0]
+    joint = hidden_width + merge_width
+    part = full_grad_kernel(ids, context, seed, start=hidden_width, count=joint)
+    part = full_grad_kernel(ids, hidden, seed, count=joint, kept=part)
+    joint_grad = lax.psum_scatter(part[0], "dp", scatter_dimension=1, tiled=True)
+    cgrad = plain_kernel(ids, seed, w_merge, after=part)
+    mgrad, mixed_sum = attend_back_kernel(ids, mixed, cgrad, context, lse, tables, n_tensor)
     project_part, gain_one, bias_one = full_grad_kernel(ids, first, mgrad, w_project, mixed_sum)
     project_grad = lax.psum_scatter(project_part, "dp", scatter_dimension=0, tiled=True)
     branches = branches_kernel(ids, context, w_merge, hidden, w_shrink, n_tensor, after=(project_part,))
@@ -968,19 +956,23 @@
     narrow = jnp.pad(jnp.stack(narrow, axis=1), ((0, 0), (4, 128 - 4 - len(narrow))))
     expand_part = spare_kernel(ids, expand_part, [gain_one, bias_one, gain_two, bias_two], narrow)
     expand_grad = lax.psum_scatter(expand_part, "dp", scatter_dimension=0, tiled=True)
-    (shrink_grad,) = widen_kernel(ids, shrink_grad, after=(expand_part,))
+    (joint_grad,) = widen_kernel(ids, joint_grad, after=(expand_part,))
+    shrink_grad, merging_grad = joint_grad[:hidden_width], joint_grad[hidden_width:]
     gains = jnp.stack([vectors[0], vectors[2]])
-    step = n_tensor // 2
-    made = back_kernel(ids, mgrad, w_project, pgrad, w_expand, gains, step, step, n_tensor, after=(shrink_grad,))
-    back_far = [flip(made[k], "tensor", step + k, n_tensor) for k in range(step - 1, -1, -1)]
-    made = back_kernel(ids, mgrad, w_project, pgrad, w_expand, gains, 0, step, n_tensor, after=(made[0],))
-    back = [made[0]] + [flip(made[k], "tensor", k, n_tensor) for k in range(step - 1, 0, -1)]
-    layer_output = output_kernel(ids, layer_input, summed, vectors, after=(made[0],), lag=10)
-    (project_grad,) = widen_kernel(ids, project_grad, after=(layer_output,))
-    back_far = total_kernel(ids, back_far, after=(project_grad,), lag=4)
-    input_grad = input_kernel(ids, layer_input, cotangent, back + [back_far], lag=160)
-
-    expand_grad, sums = widen_kernel(ids, expand_grad, spare=128)
+    back = []
+    last = joint_grad
+    half = n_tensor // 2
+    for start, count in ((half + 1, half - 1), (1, half), (0, 1)):
+        made = back_kernel(ids, mgrad, w_project, pgrad, w_expand, gains, start, count, n_tensor, after=(last,))
+        back.append([flip(made[k], "tensor", start + k, n_tensor) if start else made[k] for k in range(count - 1, -1, -1)])
+        last = made[0]
+        if len(back) == 1:
+            (project_grad,) = widen_kernel(ids, project_grad, after=(last,))
+            last = layer_output = output_kernel(ids, layer_input, summed, vectors, after=(project_grad,), lag=165)
+    far = total_kernel(ids, back[0] + back[2], after=(last,), lag=4)
+    expand_grad, sums = widen_kernel(ids, expand_grad, spare=128, after=(far,))
+    input_grad = input_kernel(ids, layer_input, cotangent, back[1] + [far], after=(expand_grad,), lag=160)
+
     sums = jnp.transpose(sums[:, :7] + sums[:, 64:71])
     norms = sums[:5]
     norms = norms + sum(flip(norms, "tensor", k, n_tensor) for k in range(1, n_tensor))

time: 695 us -> 581 us (0.84)
  waiting for transfers between devices: 187 us -> 91.4 us
  Pallas kernels: 409 us -> 401 us
    ppermute x29 -> x24, waiting for transfers between devices: 170 us -> 54.1 us  [flip(): return lax.ppermute(value, axis, [(i, i ^ bit) for i in range(size)])]
    reduce_scatter x1, waiting for transfers between devices: 0.02 us -> 31.8 us  [body(): lax.psum_scatter(expand_part, 'dp', scatter_dimension=0, tiled=True)]
    all_gather x1, waiting for transfers between devices: 15.6 us -> 0.01 us  [body(): w_project = lax.all_gather(own_project, 'dp', axis=0, tiled=True)]
    pallas_call x36 -> x32, Pallas kernels: 409 us -> 401 us  [call(): pl.pallas_call(run, grid_spec=pltpu.PrefetchScalarGridSpec(num_scalar_pre...]
    ppermute x29 -> x24, starting transfers between devices: 36.4 us -> 30.2 us  [flip(): return lax.ppermute(value, axis, [(i, i ^ bit) for i in range(size)])]
    unnamed x91 -> x77, local copies, waits for them, and re-layouts: 18.2 us -> 13.9 us
  transfers between devices with their start and end apart: 35 -> 30, of which waited for: 12 -> 8; matrix products, arithmetic and copies ran while one was open for 3% -> 4% of each run, Pallas kernels for 56% -> 70%
where the time goes in v4:
time: 581 us; the launch traced here: 576 us
  Pallas kernels  401 us (69%)
  waiting for transfers between devices  91.4 us (16%)
  starting transfers between devices  30.4 us (5%)
  local copies, waits for them, and re-layouts  26 us (4%)
  between operations  14.8 us (3%)
  other arithmetic  11.7 us (2%)
    pallas_call x32, Pallas kernels, call(): pl.pallas_call(run, grid_spec=pltpu.PrefetchScalarGridSpec(num_scalar_pre...  401 us
    ppermute x24, waiting for transfers between devices, flip(): return lax.ppermute(value, axis, [(i, i ^ bit) for i in range(size)])  54.1 us
    reduce_scatter x1, waiting for transfers between devices, body(): lax.psum_scatter(expand_part, 'dp', scatter_dimension=0, tiled=True)  31.8 us
    ppermute x24, starting transfers between devices, flip(): return lax.ppermute(value, axis, [(i, i ^ bit) for i in range(size)])  30.2 us
    unnamed x77, local copies, waits for them, and re-layouts  13.9 us
  transfers between devices with their start and end apart: 30, of which 8 were waited for; matrix products, arithmetic and copies ran while one was open for 4% of the time, Pallas kernels for 70%

profile of v4, /device:TPU:0, one launch (start us, length us, event | category | flops | bytes accessed | tf_op | source)
XLA Modules:
  0.0 575.7 jit_solution(13446116408014244370)
XLA Ops:
  30.3 29.6 %collective-permute-done.5.refs_0_.refs_1_ = bf16[512,2048]{1,0:T(8,128)(2,1)S(1)} collective-permute-done((bf16[512,2048]{1,0:T(8,128)(2,1)}, bf16[512,2048]{1,0:T(8,128)(2,1)S(1)}, u32[]{:S(2)}, u32[]{:S(2)}) %collective-permute-start.5) | collective-permute-done | bytes 2097184 | tf_op jit(solution)/shard_map/ppermute | solution.py:793
  77.1 11.9 %norm.2 = (bf16[2048,2048]{1,0:T(8,128)(2,1)}, bf16[2048,2048]{1,0:T(8,128)(2,1)}) custom-call(s32[4]{0:T(128)} %pad_add_fusion.ids_ref, bf16[512,2048]{1,0:T(8,128)(2,1)} %refs_0_.7, bf16[512,2048]{1,0:T(8,128)(2,1)} %copy-done.1, bf16[512,2048]{1,0:T(8,128)(2,1)} %collective-permute-done.3.refs_0_.refs_2_, f32[6,2048]{1,0:T(8,128)} %bitcast.47), custom_call_target="tpu_custom_call" | custom-call | flops 50000000 | tf_op jit(solution)/shard_map/norm/pallas_call | solution.py:49
  89.0 17.1 %mixed.2.refs_2_.refs_6_ = bf16[2048,1536]{1,0:T(8,128)(2,1)} custom-call(s32[4]{0:T(128)} %pad_add_fusion.ids_ref, bf16[2048,2048]{1,0:T(8,128)(2,1)} %get-tuple-element.40.refs_0_.refs_3_, bf16[2048,1536]{1,0:T(8,128)(2,1)} %all-gather.4.cloned.1.call-done.refs_1_.refs_2_, f32[1,1536]{1,0:T(1,128)} %reshape.96.refs_2_, ...), custom_call_target="tpu_custom_call" | custom-call | flops 50000000 | tf_op jit(solution)/shard_map/mixed/pallas_call | solution.py:49
  121.2 6.3 %norm.3 = (bf16[2048,2048]{1,0:T(8,128)(2,1)}, bf16[2048,2048]{1,0:T(8,128)(2,1)}) custom-call(s32[4]{0:T(128)} %pad_add_fusion.ids_ref, bf16[256,2048]{1,0:T(8,128)(2,1)} %copy-done.4, bf16[256,2048]{1,0:T(8,128)(2,1)} %copy-done.3, f32[6,2048]{1,0:T(8,128)} %bitcast.48, ...), custom_call_target="tpu_custom_call", output_to_operand_aliasing={{0}: (4, {}), {1}: (5, {})} | custom-call | flops 50000000 | tf_op jit(solution)/shard_map/norm/pallas_call | solution.py:49
  127.5 8.1 %mixed.3.refs_2_.refs_0_ = bf16[2048,1536]{1,0:T(8,128)(2,1)} custom-call(s32[4]{0:T(128)} %pad_add_fusion.ids_ref, bf16[2048,2048]{1,0:T(8,128)(2,1)} %get-tuple-element.42.refs_0_, bf16[2048,1536]{1,0:T(8,128)(2,1)} %all-gather.4.cloned.1.call-done.refs_1_.refs_2_, f32[1,1536]{1,0:T(1,128)} %reshape.96.refs_2_, ...), custom_call_target="tpu_custom_call", output_to_operand_aliasing={{}: (7, {})} | custom-call | flops 50000000 | tf_op jit(solution)/shard_map/mixed/pallas_call | solution.py:49
  135.7 13.2 %collective-permute-done.8.refs_1_ = bf16[512,256]{1,0:T(8,128)(2,1)S(1)} collective-permute-done((bf16[512,256]{1,0:T(8,128)(2,1)S(1)}, bf16[512,256]{1,0:T(8,128)(2,1)S(1)}, u32[]{:S(2)}, u32[]{:S(2)}) %collective-permute-start.8) | collective-permute-done | bytes 262176 | tf_op jit(solution)/shard_map/ppermute | solution.py:793
  154.5 22.8 %attend.1 = (bf16[2048,512]{1,0:T(8,128)(2,1)}, f32[2,4,8,512]{3,2,1,0:T(8,128)}) custom-call(s32[4]{0:T(128)} %pad_add_fusion.ids_ref, bf16[2048,1536]{1,0:T(8,128)(2,1)} %mixed.3.refs_2_.refs_0_, bf16[1024,256]{1,0:T(8,128)(2,1)} %join.3.refs_1_.refs_0_), custom_call_target="tpu_custom_call" | custom-call | flops 12000000000 | tf_op jit(solution)/shard_map/attend/pallas_call | solution.py:49
  181.8 30.7 %expand.1 = (bf16[2048,2048]{1,0:T(8,128)(2,1)}, bf16[2048,2048]{1,0:T(8,128)(2,1)}) custom-call(s32[4]{0:T(128)} %pad_add_fusion.ids_ref, bf16[2048,2048]{1,0:T(8,128)(2,1)} %get-tuple-element.44.refs_0_, bf16[2048,2048]{1,0:T(8,128)(2,1)} %all-gather.6.cloned.1.call-done.refs_1_.refs_2_.refs_3_, f32[1,2048]{1,0:T(1,128)} %bitcast.58, ...), custom_call_target="tpu_custom_call" | custom-call | flops 50000000 | tf_op jit(solution)/shard_map/expand/pallas_call | solution.py:49
  218.7 18.5 %stack.37.refs_1_.refs_0_ = bf16[2048,2048]{1,0:T(8,128)(2,1)} custom-call(s32[4]{0:T(128)} %pad_add_fusion.ids_ref, bf16[512,2048]{1,0:T(8,128)(2,1)} %stack.35.refs_5_.refs_0_, bf16[512,2048]{1,0:T(8,128)(2,1)} %copy-done.7, bf16[512,2048]{1,0:T(8,128)(2,1)} %collective-permute-done.13.refs_2_, bf16[512,2048]{1,0:T(8,128)(2,1)} %collective-permute-done.14.refs_3_, ...), custom_call_target="tpu_custom_call" | custom-call | flops 50000000 | tf_op jit(solution)/shard_map/stack/pallas_call | solution.py:49
  237.2 9.5 %full_grad.4.refs_2_ = bf16[2560,2048]{1,0:T(8,128)(2,1)} custom-call(s32[4]{0:T(128)} %pad_add_fusion.ids_ref, bf16[2048,512]{1,0:T(8,128)(2,1)} %get-tuple-element.43.refs_1_.refs_0_.refs_2_, bf16[2048,2048]{1,0:T(8,128)(2,1)} %stack.37.refs_1_.refs_0_), custom_call_target="tpu_custom_call" | custom-call | flops 50000000 | tf_op jit(solution)/shard_map/full_grad/pallas_call | solution.py:49
  246.7 23.9 %full_grad.5.refs_2_ = bf16[2560,2048]{1,0:T(8,128)(2,1)} custom-call(s32[4]{0:T(128)} %pad_add_fusion.ids_ref, bf16[2048,2048]{1,0:T(8,128)(2,1)} %get-tuple-element.45.refs_4_.refs_0_.refs_2_, bf16[2048,2048]{1,0:T(8,128)(2,1)} %stack.37.refs_1_.refs_0_, bf16[2560,2048]{1,0:T(8,128)(2,1)} %full_grad.4.refs_2_), custom_call_target="tpu_custom_call", output_to_operand_aliasing={{}: (3, {})} | custom-call | flops 50000000 | tf_op jit(solution)/shard_map/full_grad/pallas_call | solution.py:49
  270.7 9.2 %plain.1.refs_1_ = bf16[2048,512]{1,0:T(8,128)(2,1)} custom-call(s32[4]{0:T(128)} %pad_add_fusion.ids_ref, bf16[2048,2048]{1,0:T(8,128)(2,1)} %stack.37.refs_1_.refs_0_, bf16[2048,512]{1,0:T(8,128)(2,1)} %bitcast.42, bf16[2560,2048]{1,0:T(8,128)(2,1)} %full_grad.5.refs_2_), custom_call_target="tpu_custom_call" | custom-call | flops 50000000 | tf_op jit(solution)/shard_map/plain/pallas_call | solution.py:49
  279.9 26.3 %attend_back.1 = (bf16[2048,1536]{1,0:T(8,128)(2,1)}, f32[1,1536]{1,0:T(1,128)}) custom-call(s32[4]{0:T(128)} %pad_add_fusion.ids_ref, bf16[2048,1536]{1,0:T(8,128)(2,1)} %mixed.3.refs_2_.refs_0_, bf16[2048,512]{1,0:T(8,128)(2,1)} %plain.1.refs_1_, bf16[2048,512]{1,0:T(8,128)(2,1)} %get-tuple-element.43.refs_1_.refs_0_.refs_2_, ...), custom_call_target="tpu_custom_call" | custom-call | flops 50000000 | tf_op jit(solution)/shard_map/attend_back/pallas_call | solution.py:49
  306.2 25.0 %full_grad.6 = (bf16[2048,1536]{1,0:T(8,128)(2,1)}, f32[2048,128]{1,0:T(8,128)}, f32[2048,128]{1,0:T(8,128)}) custom-call(s32[4]{0:T(128)} %pad_add_fusion.ids_ref, bf16[2048,2048]{1,0:T(8,128)(2,1)} %get-tuple-element.42.refs_0_, bf16[2048,1536]{1,0:T(8,128)(2,1)} %get-tuple-element.47.refs_1_.refs_0_, ...), custom_call_target="tpu_custom_call" | custom-call | flops 50000000 | tf_op jit(solution)/shard_map/full_grad/pallas_call | solution.py:49
  331.3 30.8 %branches.1 = (bf16[512,2048]{1,0:T(8,128)(2,1)}, bf16[512,2048]{1,0:T(8,128)(2,1)}, bf16[512,2048]{1,0:T(8,128)(2,1)}, bf16[512,2048]{1,0:T(8,128)(2,1)}) custom-call(s32[4]{0:T(128)} %pad_add_fusion.ids_ref, bf16[2048,512]{1,0:T(8,128)(2,1)} %get-tuple-element.43.refs_1_.refs_0_.refs_2_, bf16[2048,512]{1,0:T(8,128)(2,1)} %bitcast.43, ...), custom_call_target="tpu_custom_call" | custom-call | flops 50000000 | tf_op jit(solution)/shard_map/branches/pallas_call | solution.py:49
  366.3 25.5 %shrink_back.1 = (bf16[2048,2048]{1,0:T(8,128)(2,1)}, f32[1,2048]{1,0:T(1,128)}) custom-call(s32[4]{0:T(128)} %pad_add_fusion.ids_ref, bf16[2048,2048]{1,0:T(8,128)(2,1)} %stack.37.refs_1_.refs_0_, bf16[2048,2048]{1,0:T(8,128)(2,1)} %all-gather.8.cloned.1.call-done.refs_3_.refs_1_, bf16[2048,2048]{1,0:T(8,128)(2,1)} %get-tuple-element.54.refs_2_, ...), custom_call_target="tpu_custom_call" | custom-call | flops 50000000 | tf_op jit(solution)/shard_map/shrink_back/pallas_call | solution.py:49
  394.2 26.3 %full_grad.7 = (bf16[2048,2176]{1,0:T(8,128)(2,1)}, f32[2048,128]{1,0:T(8,128)}, f32[2048,128]{1,0:T(8,128)}) custom-call(s32[4]{0:T(128)} %pad_add_fusion.ids_ref, bf16[2048,2048]{1,0:T(8,128)(2,1)} %get-tuple-element.44.refs_0_, bf16[2048,2048]{1,0:T(8,128)(2,1)} %get-tuple-element.55.refs_1_.refs_2_, ...), custom_call_target="tpu_custom_call" | custom-call | flops 50000000 | tf_op jit(solution)/shard_map/full_grad/pallas_call | solution.py:49
  420.5 5.4 spare.1.refs_1_
  430.3 15.2 %back.3.refs_1_ = bf16[512,2048]{1,0:T(8,128)(2,1)} custom-call(s32[4]{0:T(128)} %pad_add_fusion.ids_ref, bf16[2048,1536]{1,0:T(8,128)(2,1)} %get-tuple-element.47.refs_1_.refs_0_, bf16[2048,1536]{1,0:T(8,128)(2,1)} %all-gather.4.cloned.1.call-done.refs_1_.refs_2_, bf16[2048,2048]{1,0:T(8,128)(2,1)} %get-tuple-element.55.refs_1_.refs_2_, ...), custom_call_target="tpu_custom_call" | custom-call | flops 50000000 | tf_op jit(solution)/shard_map/back/pallas_call | solution.py:49
  456.6 6.4 %output.1.refs_5_ = bf16[512,2048]{1,0:T(8,128)(2,1)} custom-call(s32[4]{0:T(128)} %pad_add_fusion.ids_ref, bf16[512,2048]{1,0:T(8,128)(2,1)} %refs_0_.7, f32[6,2048]{1,0:T(8,128)} %bitcast.49, bf16[512,2048]{1,0:T(8,128)(2,1)} %get-tuple-element.50.refs_3_.refs_2_, bf16[512,2048]{1,0:T(8,128)(2,1)} %collective-permute-done.15.refs_3_, ...), custom_call_target="tpu_custom_call" | custom-call | flops 165000003584 | tf_op jit(solution)/shard_map/output/pallas_call | solution.py:49
  463.0 23.0 %back.4 = (bf16[512,2048]{1,0:T(8,128)(2,1)}, bf16[512,2048]{1,0:T(8,128)(2,1)}) custom-call(s32[4]{0:T(128)} %pad_add_fusion.ids_ref, bf16[2048,1536]{1,0:T(8,128)(2,1)} %get-tuple-element.47.refs_1_.refs_0_, bf16[2048,1536]{1,0:T(8,128)(2,1)} %all-gather.4.cloned.1.call-done.refs_1_.refs_2_, bf16[2048,2048]{1,0:T(8,128)(2,1)} %get-tuple-element.55.refs_1_.refs_2_, ...), custom_call_target="tpu_custom_call" | custom-call | flops 50000000 | tf_op jit(solution)/shard_map/back/pallas_call | solution.py:49
  493.3 15.2 %back.5.refs_1_.refs_2_ = bf16[512,2048]{1,0:T(8,128)(2,1)} custom-call(s32[4]{0:T(128)} %pad_add_fusion.ids_ref, bf16[2048,1536]{1,0:T(8,128)(2,1)} %get-tuple-element.47.refs_1_.refs_0_, bf16[2048,1536]{1,0:T(8,128)(2,1)} %all-gather.4.cloned.1.call-done.refs_1_.refs_2_, bf16[2048,2048]{1,0:T(8,128)(2,1)} %get-tuple-element.55.refs_1_.refs_2_, ...), custom_call_target="tpu_custom_call" | custom-call | flops 50000000 | tf_op jit(solution)/shard_map/back/pallas_call | solution.py:49
  512.9 31.8 %reduce-scatter.8.cloned.1.call-done.refs_0_.refs_1_ = bf16[256,2176]{1,0:T(8,128)(2,1)} async-done(((bf16[2048,2176]{1,0:T(8,128)(2,1)}), bf16[256,2176]{1,0:T(8,128)(2,1)}) %reduce-scatter.8.cloned.1.call-update) | async-done | bytes 1114128 | tf_op jit(solution)/shard_map/reduce_scatter | solution.py:958
  555.1 8.4 %input.1 = f32[512,2048]{1,0:T(8,128)} custom-call(s32[4]{0:T(128)} %pad_add_fusion.ids_ref, bf16[512,2048]{1,0:T(8,128)(2,1)} %refs_0_.7, bf16[512,2048]{1,0:T(8,128)(2,1)} %refs_1_.1, bf16[512,2048]{1,0:T(8,128)(2,1)} %collective-permute-done.18.refs_2_, bf16[512,2048]{1,0:T(8,128)(2,1)} %collective-permute-done.19.refs_3_, ...), custom_call_target="tpu_custom_call" | custom-call | flops 160000000000 | tf_op jit(solution)/shard_map/input/pallas_call | solution.py:49
  (190 shorter events, 120.6 us)
Async XLA Ops:
  7.2 81.8 %all-gather.4.cloned.1.call-start = ((), (), s32[]{:S(2)}) async-start(), calls=%async_computation.3 | async-start | bytes 7077888 | tf_op jit(solution)/shard_map/all_gather | solution.py:912
  9.5 172.3 %all-gather.6.cloned.1.call-start = ((), (), s32[]{:S(2)}) async-start(), calls=%async_computation.4 | async-start | bytes 9437184 | tf_op jit(solution)/shard_map/all_gather | solution.py:913
  10.2 321.0 %all-gather.8.cloned.1.call-start = ((), (), s32[]{:S(2)}) async-start(), calls=%async_computation.5 | async-start | bytes 9437184 | tf_op jit(solution)/shard_map/all_gather | solution.py:914
  11.0 415.7 %reduce-scatter.6.cloned.1.call-start = ((), (), s32[]{:S(2)}) async-start(), calls=%async_computation.7 | async-start | bytes 11796480 | tf_op jit(solution)/shard_map/reduce_scatter | solution.py:938
  11.0 48.8 %collective-permute-start.5 = (bf16[512,2048]{1,0:T(8,128)(2,1)}, bf16[512,2048]{1,0:T(8,128)(2,1)S(1)}, u32[]{:S(2)}, u32[]{:S(2)}) collective-permute-start(bf16[512,2048]{1,0:T(8,128)(2,1)} %refs_0_.7), channel_id=1, source_target_pairs={{0,1},{1,0},{2,3},{3,2},{4,5},{5,4},{6,7},{7,6},{8,9},{9,8},{10,11... | collective-permute-start | bytes 6291464 | tf_op jit(solution)/shard_map/ppermute | solution.py:793
  14.0 51.9 %collective-permute-start.3 = (bf16[512,2048]{1,0:T(8,128)(2,1)}, bf16[512,2048]{1,0:T(8,128)(2,1)}, u32[]{:S(2)}, u32[]{:S(2)}) collective-permute-start(bf16[512,2048]{1,0:T(8,128)(2,1)} %refs_0_.7), channel_id=1, source_target_pairs={{0,2},{1,3},{2,0},{3,1},{4,6},{5,7},{6,4},{7,5},{8,10},{9,11},{10,... | collective-permute-start | bytes 6291464 | tf_op jit(solution)/shard_map/ppermute | solution.py:793
  64.1 45.3 %collective-permute-start.6 = (bf16[256,2048]{1,0:T(8,128)(2,1)}, bf16[256,2048]{1,0:T(8,128)(2,1)S(1)}, u32[]{:S(2)}, u32[]{:S(2)}) collective-permute-start(bf16[256,2048]{1,0:T(8,128)(2,1)} %half.3), channel_id=1, source_target_pairs={{0,2},{1,3},{2,0},{3,1},{4,6},{5,7},{6,4},{7,5},{8,10},{9,11},{10,... | collective-permute-start | bytes 3145736 | tf_op jit(solution)/shard_map/ppermute | solution.py:793
  68.8 40.6 %collective-permute-start.4 = (bf16[256,2048]{1,0:T(8,128)(2,1)}, bf16[256,2048]{1,0:T(8,128)(2,1)S(1)}, u32[]{:S(2)}, u32[]{:S(2)}) collective-permute-start(bf16[256,2048]{1,0:T(8,128)(2,1)} %half.2), channel_id=1, source_target_pairs={{0,1},{1,0},{2,3},{3,2},{4,5},{5,4},{6,7},{7,6},{8,9},{9,8},{10,11... | collective-permute-start | bytes 3145736 | tf_op jit(solution)/shard_map/ppermute | solution.py:793
  70.4 35.7 %collective-permute-start.7 = (bf16[256,256]{1,0:T(8,128)(2,1)S(1)}, bf16[256,256]{1,0:T(8,128)(2,1)S(1)}, u32[]{:S(2)}, u32[]{:S(2)}) collective-permute-start(bf16[256,256]{1,0:T(8,128)(2,1)S(1)} %bitcast.55), channel_id=1, source_target_pairs={{0,4},{4,0},{8,12},{12,8},{16,20},{20,16},{24,28},{28,24},{1,5},{5... | collective-permute-start | bytes 393224 | tf_op jit(solution)/shard_map/ppermute | solution.py:793
  115.0 102.4 %collective-permute-start.12 = (bf16[512,2048]{1,0:T(8,128)(2,1)}, bf16[512,2048]{1,0:T(8,128)(2,1)S(1)}, u32[]{:S(2)}, u32[]{:S(2)}) collective-permute-start(bf16[512,2048]{1,0:T(8,128)(2,1)} %stack.35.refs_5_.refs_0_), channel_id=1, source_target_pairs={{0,1},{1,0},{2,3},{3,2},{4,5},{5,4},{6,7},{7,6},{8,9},{9,8},{10,11... | collective-permute-start | bytes 6291464 | tf_op jit(solution)/shard_map/ppermute | solution.py:793
  115.6 101.7 %collective-permute-start.13 = (bf16[512,2048]{1,0:T(8,128)(2,1)}, bf16[512,2048]{1,0:T(8,128)(2,1)}, u32[]{:S(2)}, u32[]{:S(2)}) collective-permute-start(bf16[512,2048]{1,0:T(8,128)(2,1)} %stack.35.refs_5_.refs_0_), channel_id=1, source_target_pairs={{0,2},{1,3},{2,0},{3,1},{4,6},{5,7},{6,4},{7,5},{8,10},{9,11},{10,... | collective-permute-start | bytes 6291464 | tf_op jit(solution)/shard_map/ppermute | solution.py:793
  116.7 100.7 %collective-permute-start.14 = (bf16[512,2048]{1,0:T(8,128)(2,1)}, bf16[512,2048]{1,0:T(8,128)(2,1)}, u32[]{:S(2)}, u32[]{:S(2)}) collective-permute-start(bf16[512,2048]{1,0:T(8,128)(2,1)} %stack.35.refs_5_.refs_0_), channel_id=1, source_target_pairs={{0,3},{1,2},{2,1},{3,0},{4,7},{5,6},{6,5},{7,4},{8,11},{9,10},{10,... | collective-permute-start | bytes 6291464 | tf_op jit(solution)/shard_map/ppermute | solution.py:793
  118.5 30.4 %collective-permute-start.8 = (bf16[512,256]{1,0:T(8,128)(2,1)S(1)}, bf16[512,256]{1,0:T(8,128)(2,1)S(1)}, u32[]{:S(2)}, u32[]{:S(2)}) collective-permute-start(bf16[512,256]{1,0:T(8,128)(2,1)S(1)} %copy-done.5), channel_id=1, source_target_pairs={{0,16},{4,20},{8,24},{12,28},{16,0},{20,4},{24,8},{28,12},{1,17},{... | collective-permute-start | bytes 786440 | tf_op jit(solution)/shard_map/ppermute | solution.py:793
  152.1 25.2 %collective-permute-start.9 = (bf16[1024,256]{1,0:T(8,128)(2,1)}, bf16[1024,256]{1,0:T(8,128)(2,1)S(1)}, u32[]{:S(2)}, u32[]{:S(2)}) collective-permute-start(bf16[1024,256]{1,0:T(8,128)(2,1)} %join.3.refs_1_.refs_0_), channel_id=1, source_target_pairs={{0,8},{4,12},{8,0},{12,4},{16,24},{20,28},{24,16},{28,20},{1,9},{5... | collective-permute-start | bytes 1572872 | tf_op jit(solution)/shard_map/ppermute | solution.py:793
  177.3 35.1 %collective-permute-start.10 = (bf16[1024,256]{1,0:T(8,128)(2,1)S(1)}, bf16[1024,256]{1,0:T(8,128)(2,1)S(1)}, u32[]{:S(2)}, u32[]{:S(2)}) collective-permute-start(bf16[1024,256]{1,0:T(8,128)(2,1)S(1)} %copy-done.6), channel_id=1, source_target_pairs={{0,4},{4,0},{8,12},{12,8},{16,20},{20,16},{24,28},{28,24},{1,5},{5... | collective-permute-start | bytes 1572872 | tf_op jit(solution)/shard_map/ppermute | solution.py:793
  180.7 31.8 %collective-permute-start.11 = (bf16[1024,256]{1,0:T(8,128)(2,1)}, bf16[1024,256]{1,0:T(8,128)(2,1)}, u32[]{:S(2)}, u32[]{:S(2)}) collective-permute-start(bf16[1024,256]{1,0:T(8,128)(2,1)} %stack.36.refs_3_.refs_1_), channel_id=1, source_target_pairs={{0,4},{4,0},{8,12},{12,8},{16,20},{20,16},{24,28},{28,24},{1,5},{5... | collective-permute-start | bytes 1572872 | tf_op jit(solution)/shard_map/ppermute | solution.py:793
  270.7 178.9 %reduce-scatter.4.cloned.1.call-start = ((), (), s32[]{:S(2)}) async-start(), calls=%async_computation.6 | async-start | bytes 7077888 | tf_op jit(solution)/shard_map/reduce_scatter | solution.py:942
  331.2 213.5 %reduce-scatter.8.cloned.1.call-start = ((), (), s32[]{:S(2)}) async-start(), calls=%async_computation.8 | async-start | bytes 10027008 | tf_op jit(solution)/shard_map/reduce_scatter | solution.py:958
  362.1 90.6 %collective-permute-start.15 = (bf16[512,2048]{1,0:T(8,128)(2,1)}, bf16[512,2048]{1,0:T(8,128)(2,1)}, u32[]{:S(2)}, u32[]{:S(2)}) collective-permute-start(bf16[512,2048]{1,0:T(8,128)(2,1)} %get-tuple-element.51), channel_id=1, source_target_pairs={{0,3},{1,2},{2,1},{3,0},{4,7},{5,6},{6,5},{7,4},{8,11},{9,10},{10,... | collective-permute-start | bytes 6291464 | tf_op jit(solution)/shard_map/ppermute | solution.py:793
  362.4 94.2 %collective-permute-start.16 = (bf16[512,2048]{1,0:T(8,128)(2,1)}, bf16[512,2048]{1,0:T(8,128)(2,1)}, u32[]{:S(2)}, u32[]{:S(2)}) collective-permute-start(bf16[512,2048]{1,0:T(8,128)(2,1)} %get-tuple-element.52), channel_id=1, source_target_pairs={{0,2},{1,3},{2,0},{3,1},{4,6},{5,7},{6,4},{7,5},{8,10},{9,11},{10,... | collective-permute-start | bytes 6291464 | tf_op jit(solution)/shard_map/ppermute | solution.py:793
  363.9 92.7 %collective-permute-start.17 = (bf16[512,2048]{1,0:T(8,128)(2,1)}, bf16[512,2048]{1,0:T(8,128)(2,1)}, u32[]{:S(2)}, u32[]{:S(2)}) collective-permute-start(bf16[512,2048]{1,0:T(8,128)(2,1)} %get-tuple-element.53), channel_id=1, source_target_pairs={{0,1},{1,0},{2,3},{3,2},{4,5},{5,4},{6,7},{7,6},{8,9},{9,8},{10,11... | collective-permute-start | bytes 6291464 | tf_op jit(solution)/shard_map/ppermute | solution.py:793
  445.5 63.0 %collective-permute-start.20 = (bf16[512,2048]{1,0:T(8,128)(2,1)}, bf16[512,2048]{1,0:T(8,128)(2,1)}, u32[]{:S(2)}, u32[]{:S(2)}) collective-permute-start(bf16[512,2048]{1,0:T(8,128)(2,1)} %back.3.refs_1_), channel_id=1, source_target_pairs={{0,3},{1,2},{2,1},{3,0},{4,7},{5,6},{6,5},{7,4},{8,11},{9,10},{10,... | collective-permute-start | bytes 6291464 | tf_op jit(solution)/shard_map/ppermute | solution.py:793
  486.1 69.0 %collective-permute-start.18 = (bf16[512,2048]{1,0:T(8,128)(2,1)}, bf16[512,2048]{1,0:T(8,128)(2,1)}, u32[]{:S(2)}, u32[]{:S(2)}) collective-permute-start(bf16[512,2048]{1,0:T(8,128)(2,1)} %get-tuple-element.62), channel_id=1, source_target_pairs={{0,2},{1,3},{2,0},{3,1},{4,6},{5,7},{6,4},{7,5},{8,10},{9,11},{10,... | collective-permute-start | bytes 6291464 | tf_op jit(solution)/shard_map/ppermute | solution.py:793
  487.1 68.0 %collective-permute-start.19 = (bf16[512,2048]{1,0:T(8,128)(2,1)}, bf16[512,2048]{1,0:T(8,128)(2,1)}, u32[]{:S(2)}, u32[]{:S(2)}) collective-permute-start(bf16[512,2048]{1,0:T(8,128)(2,1)} %get-tuple-element.63.refs_5_), channel_id=1, source_target_pairs={{0,1},{1,0},{2,3},{3,2},{4,5},{5,4},{6,7},{7,6},{8,9},{9,8},{10,11... | collective-permute-start | bytes 6291464 | tf_op jit(solution)/shard_map/ppermute | solution.py:793
  (35 other events, 270.2 us)
Sparse Core Ops, SparseCore 0:
  10.2 68.7 all-gather.3
  80.6 91.8 all-gather.5
  174.1 85.5 all-gather.7
  270.8 108.4 reduce-scatter.5
  381.4 68.1 reduce-scatter.3
  451.8 92.9 reduce-scatter.7

commit v5 on v4

--- a/solution.py
+++ b/solution.py
@@ -120,16 +120,17 @@
     return jnp.concatenate([turned, block[:, 128:]], axis=1)
 
 
-def mixed_kernel(ids, first, weight, bias, tables, start, count, blocks, kept=(), after=(), lag=0.05):
+def mixed_kernel(ids, first, weight, place, bias, tables, start, count, blocks, kept=(), after=(), lag=0.05):
     rows, depth = first.shape
-    heads = weight.shape[1] // (3 * HEAD_DIM)
+    heads = bias.shape[1] // (3 * HEAD_DIM)
     unit = rows // blocks
     wide = 3 * HEAD_DIM
 
-    def kernel(ids_ref, a_ref, w_ref, b_ref, cos, low, high, out_ref):
+    def kernel(ids_ref, a_ref, *refs):
+        b_ref, cos, low, high, out_ref = refs[3:]
         for part in range(3):
             here = slice(part * HEAD_DIM, (part + 1) * HEAD_DIM)
-            value = product(a_ref[...], w_ref[:, here], "NN") + b_ref[:, here]
+            value = product(a_ref[...], refs[part][...], "NN") + b_ref[:, here]
             if part < 2:
                 value = rotate(value, cos[...], low[...], high[...], 1.0)
             out_ref[:, here] = value.astype(BF16)
@@ -141,7 +142,10 @@
         (heads, count),
         [
             pl.BlockSpec((unit, depth), lambda j, i, ids: (start + i, 0)),
-            pl.BlockSpec((depth, wide), lambda j, i, ids: (0, j)),
+            *[
+                pl.BlockSpec((depth, HEAD_DIM), lambda j, i, ids, part=part: (0, place // HEAD_DIM + 3 * j + part))
+                for part in range(3)
+            ],
             pl.BlockSpec((1, wide), lambda j, i, ids: (0, j)),
             table,
             table,
@@ -149,7 +153,7 @@
         ],
         [pl.BlockSpec((unit, wide), lambda j, i, ids: (start + i, j))],
         [jax.ShapeDtypeStruct((rows, heads * wide), BF16)],
-        (first, weight, bias, *tables),
+        (first, weight, weight, weight, bias, *tables),
         kept=kept,
         after=after,
         lag=lag,
@@ -161,55 +165,52 @@
     rows, width = mixed.shape
     heads = width // (3 * HEAD_DIM)
     unit = rows // blocks
+    lanes = range(0, unit, 128)
     scale = HEAD_DIM ** (-0.5)
 
-    def kernel(ids_ref, x_ref, ctx_ref, lse_ref, top_s, total_s, acc_s):
-        block = pl.program_id(0)
+    def kernel(ids_ref, x_ref, ctx_ref, lse_ref):
         me = ids_ref[0]
-        here = pl.ds(pl.multiple_of((me ^ block) * unit, unit), unit)
-
-        def step(other, diagonal):
-            there = pl.ds(pl.multiple_of((me ^ other) * unit, unit), unit)
-            for head in range(heads):
-                at = 3 * HEAD_DIM * head
-                scores = (
-                    product(
-                        x_ref[here, at : at + HEAD_DIM],
-                        x_ref[there, at + HEAD_DIM : at + 2 * HEAD_DIM],
-                        "NT",
-                    )
-                    * scale
-                )
-                value = x_ref[there, at + 2 * HEAD_DIM : at + 3 * HEAD_DIM]
-                if diagonal:
+
+        def place(block):
+            return pl.ds(pl.multiple_of((me ^ block) * unit, unit), unit)
+
+        def head_of(block, head):
+            at = 3 * HEAD_DIM * head
+            query = x_ref[place(block), at : at + HEAD_DIM] * jnp.asarray(scale, BF16)
+            tiles = []
+            for other in range(block + 1):
+                scores = product(query, x_ref[place(other), at + HEAD_DIM : at + 2 * HEAD_DIM], "NT")
+                if other == block:
                     row_at = lax.broadcasted_iota(jnp.int32, scores.shape, 0)
                     col_at = lax.broadcasted_iota(jnp.int32, scores.shape, 1)
                     scores = jnp.where(col_at <= row_at, scores, BIG)
-                    top = jnp.max(scores, axis=1, keepdims=True)
-                    weight = jnp.exp(scores - top)
-                    top_s[head] = top
-                    total_s[head] = jnp.sum(weight, axis=1, keepdims=True)
-                    acc_s[head] = product(weight.astype(BF16), value, "NN")
-                else:
-                    before = top_s[head]
-                    top = jnp.maximum(before, jnp.max(scores, axis=1, keepdims=True))
-                    weight = jnp.exp(scores - top)
-                    shrunk = jnp.exp(before - top)
-                    top_s[head] = top
-                    total_s[head] = total_s[head] * shrunk + jnp.sum(weight, axis=1, keepdims=True)
-                    acc_s[head] = acc_s[head] * shrunk + product(weight.astype(BF16), value, "NN")
-
-        step(block, True)
-
-        @pl.loop(0, block)
-        def _(other):
-            step(other, False)
-
-        for head in range(heads):
-            at = HEAD_DIM * head
-            ctx_ref[:, at : at + HEAD_DIM] = (acc_s[head] / total_s[head]).astype(BF16)
-            log_total = top_s[head] + jnp.log(total_s[head])
-            lse_ref[head, 0] = jnp.transpose(jnp.broadcast_to(log_total, (unit, 128)))[:8]
+                tiles.append(scores)
+            top = None
+            for scores in tiles:
+                for lane in lanes:
+                    piece = scores[:, lane : lane + 128]
+                    top = piece if top is None else jnp.maximum(top, piece)
+            top = jnp.max(top, axis=1, keepdims=True)
+            total = acc = None
+            for other, scores in enumerate(tiles):
+                weight = jnp.exp(scores - top)
+                for lane in lanes:
+                    piece = weight[:, lane : lane + 128]
+                    total = piece if total is None else total + piece
+                value = x_ref[place(other), at + 2 * HEAD_DIM : at + 3 * HEAD_DIM]
+                made = product(weight.astype(BF16), value, "NN")
+                acc = made if acc is None else acc + made
+            total = jnp.sum(total, axis=1, keepdims=True)
+            ctx_ref[:, HEAD_DIM * head : HEAD_DIM * (head + 1)] = (acc / total).astype(BF16)
+            log_total = jnp.broadcast_to(top + jnp.log(total), (unit, 128))
+            lse_ref[head, 0] = jnp.transpose(log_total)[:8]
+
+        for block in range(blocks):
+
+            @pl.when(pl.program_id(0) == block)
+            def _(block=block):
+                for head in range(heads):
+                    head_of(block, head)
 
     return call(
         kernel,
@@ -225,11 +226,6 @@
             jax.ShapeDtypeStruct((heads, blocks, 8, unit), F32),
         ],
         (mixed,),
-        scratch=[
-            pltpu.VMEM((heads, unit, 1), F32),
-            pltpu.VMEM((heads, unit, 1), F32),
-            pltpu.VMEM((heads, unit, HEAD_DIM), F32),
-        ],
         after=after,
         lag=lag,
         name="attend",
@@ -242,62 +238,59 @@
     unit = rows // blocks
     scale = HEAD_DIM ** (-0.5)
 
-    def kernel(ids_ref, x_ref, g_ref, c_ref, lse_ref, cos, low, high, out_ref, sum_ref, dk_s, dv_s, dq_s, inner_s):
-        turn = pl.program_id(0)
-        block = blocks - 1 - turn
+    def kernel(ids_ref, x_ref, g_ref, c_ref, lse_ref, cos, low, high, out_ref, sum_ref, dk_s, dv_s):
         me = ids_ref[0]
 
-        @pl.when(turn == 0)
-        def _():
-            dk_s[...] = jnp.zeros_like(dk_s)
-            dv_s[...] = jnp.zeros_like(dv_s)
-            sum_ref[...] = jnp.zeros_like(sum_ref)
-
-        here = pl.ds(pl.multiple_of((me ^ block) * unit, unit), unit)
-        for head in range(heads):
+        def place(block):
+            return pl.ds(pl.multiple_of((me ^ block) * unit, unit), unit)
+
+        def head_of(block, head):
+            at = 3 * HEAD_DIM * head
             cols = slice(HEAD_DIM * head, HEAD_DIM * (head + 1))
-            inner = jnp.sum(g_ref[here, cols].astype(F32) * c_ref[here, cols].astype(F32), axis=1, keepdims=True)
-            inner_s[head] = jnp.transpose(jnp.broadcast_to(inner, (unit, 128)))[:8]
-
-        def step(other, diagonal):
-            there = pl.ds(pl.multiple_of((me ^ other) * unit, unit), unit)
-            for head in range(heads):
-                at = 3 * HEAD_DIM * head
-                query = x_ref[here, at : at + HEAD_DIM]
-                seed = g_ref[here, HEAD_DIM * head : HEAD_DIM * (head + 1)]
-                key = x_ref[there, at + HEAD_DIM : at + 2 * HEAD_DIM]
-                value = x_ref[there, at + 2 * HEAD_DIM : at + 3 * HEAD_DIM]
-                scores = product(key, query, "NT") * scale
-                prob = jnp.exp(scores - lse_ref[head, 0][:1])
-                if diagonal:
-                    key_at = lax.broadcasted_iota(jnp.int32, scores.shape, 0)
-                    row_at = lax.broadcasted_iota(jnp.int32, scores.shape, 1)
+            query = x_ref[place(block), at : at + HEAD_DIM] * jnp.asarray(scale, BF16)
+            seed = g_ref[place(block), cols]
+            inner = jnp.sum(seed.astype(F32) * c_ref[place(block), cols].astype(F32), axis=1, keepdims=True)
+            inner = jnp.transpose(jnp.broadcast_to(inner, (unit, 128)))[:1]
+            log_total = lse_ref[head, 0][:1]
+            dquery = None
+            for other in reversed(range(block + 1)):
+                key = x_ref[place(other), at + HEAD_DIM : at + 2 * HEAD_DIM]
+                value = x_ref[place(other), at + 2 * HEAD_DIM : at + 3 * HEAD_DIM]
+                prob = jnp.exp(product(key, query, "NT") - log_total)
+                if other == block:
+                    key_at = lax.broadcasted_iota(jnp.int32, prob.shape, 0)
+                    row_at = lax.broadcasted_iota(jnp.int32, prob.shape, 1)
                     prob = jnp.where(key_at <= row_at, prob, 0.0)
-                dprob = product(value, seed, "NT")
-                dscore = (prob * (dprob - inner_s[head][:1])).astype(BF16)
-                dv_s[head, other] += product(prob.astype(BF16), seed, "NN")
-                dk_s[head, other] += product(dscore, query, "NN")
-                dquery = product(dscore, key, "TN")
-                if diagonal:
-                    dq_s[head] = dquery
+                dscore = (prob * (product(value, seed, "NT") - inner)).astype(BF16)
+                dvalue = product(prob.astype(BF16), seed, "NN")
+                dkey = product(dscore, query, "NN")
+                if block < blocks - 1:
+                    dvalue = dvalue + dv_s[head, other]
+                    dkey = dkey + dk_s[head, other]
+                if other < block:
+                    dv_s[head, other] = dvalue
+                    dk_s[head, other] = dkey
                 else:
-                    dq_s[head] += dquery
-
-        step(block, True)
-
-        @pl.loop(0, block)
-        def _(other):
-            step(other, False)
-
-        for head in range(heads):
-            at = 3 * HEAD_DIM * head
-            dquery = rotate(dq_s[head] * scale, cos[...], low[...], high[...], -1.0)
-            dkey = rotate(dk_s[head, block] * scale, cos[...], low[...], high[...], -1.0)
-            for part, value in enumerate((dquery, dkey, dv_s[head, block])):
+                    done = (dkey, dvalue)
+                made = product(dscore, key, "TN")
+                dquery = made if dquery is None else dquery + made
+            dquery = rotate(dquery * scale, cos[...], low[...], high[...], -1.0)
+            dkey = rotate(done[0], cos[...], low[...], high[...], -1.0)
+            for part, value in enumerate((dquery, dkey, done[1])):
                 cols = slice(at + part * HEAD_DIM, at + (part + 1) * HEAD_DIM)
                 rounded = value.astype(BF16)
                 out_ref[:, cols] = rounded
-                sum_ref[:, cols] += jnp.sum(rounded.astype(F32), axis=0, keepdims=True)
+                column = jnp.sum(rounded.astype(F32), axis=0, keepdims=True)
+                if block < blocks - 1:
+                    column = column + sum_ref[:, cols]
+                sum_ref[:, cols] = column
+
+        for turn in range(blocks):
+
+            @pl.when(pl.program_id(0) == turn)
+            def _(turn=turn):
+                for head in range(heads):
+                    head_of(blocks - 1 - turn, head)
 
     def whole(cols):
         return pl.BlockSpec((rows, cols), lambda b, ids: (0, 0))
@@ -325,8 +318,6 @@
         scratch=[
             pltpu.VMEM((heads, blocks, unit, HEAD_DIM), F32),
             pltpu.VMEM((heads, blocks, unit, HEAD_DIM), F32),
-            pltpu.VMEM((heads, unit, HEAD_DIM), F32),
-            pltpu.VMEM((heads, 8, unit), F32),
         ],
         after=after,
         lag=lag,
@@ -336,7 +327,7 @@
 
 def expand_kernel(ids, second, weight, bias, after=(), lag=0.05):
     rows, depth = second.shape
-    width = weight.shape[1]
+    width = bias.shape[1]
     tall, wide = tile_of(rows, 1024), tile_of(width, 1024)
     unit = tile_of(wide, 512)
 
@@ -395,62 +386,9 @@
     )
 
 
-def join_kernel(ids, mine, other, bit, chunks, after=(), lag=0.05):
-    rows, width = mine.shape[0] // chunks, mine.shape[1]
-
-    def kernel(ids_ref, a_ref, b_ref, out_ref):
-        for side, ref in ((0, a_ref), (1, b_ref)):
-
-            @pl.when(pl.program_id(0) == side)
-            def _(ref=ref):
-                out_ref[...] = ref[...]
-
-    return call(
-        kernel,
-        ids,
-        (2, chunks),
-        [
-            pl.BlockSpec((rows, width), lambda s, i, ids: (jnp.where(s == 0, i, chunks - 1), 0)),
-            pl.BlockSpec((rows, width), lambda s, i, ids: (jnp.where(s == 0, 0, i), 0)),
-        ],
-        pl.BlockSpec((rows, width), lambda s, i, ids: (2 * i + (s ^ ids[bit]), 0)),
-        jax.ShapeDtypeStruct((2 * chunks * rows, width), BF16),
-        (mine, other),
-        after=after,
-        lag=lag,
-        name="join",
-    )
-
-
-def assemble_kernel(ids, parts, bit, chunks, after=(), lag=0.05):
-    rows, width = parts[0].shape[0] // chunks, parts[0].shape[1]
-
-    def kernel(ids_ref, *refs):
-        for step, ref in enumerate(refs[:4]):
-
-            @pl.when(pl.program_id(0) == step)
-            def _(ref=ref):
-                refs[4][...] = ref[...].reshape(chunks, 1, rows, width)
-
-    whole = pl.BlockSpec((chunks * rows, width), lambda s, ids: (0, 0))
-    made = call(
-        kernel,
-        ids,
-        (4,),
-        [whole] * 4,
-        pl.BlockSpec((chunks, 1, rows, width), lambda s, ids: (0, (s & 1) ^ ids[bit], 0, (s >> 1) ^ ids[1])),
-        jax.ShapeDtypeStruct((chunks, 2, rows, 2 * width), BF16),
-        tuple(parts),
-        after=after,
-        lag=lag,
-        name="assemble",
-    )
-    return made.reshape(2 * chunks * rows, 2 * width)
-
-
 def shrink_back_kernel(ids, seed, weight, slope, after=(), lag=0.05):
     rows, depth = seed.shape
-    width = weight.shape[0]
+    width = slope.shape[1]
     tall, wide = tile_of(rows, 1024), tile_of(width, 1024)
     unit = tile_of(wide, 512)
 
@@ -485,34 +423,51 @@
     )
 
 
-def plain_kernel(ids, left, right, after=(), lag=0.05):
-    rows, depth = left.shape
-    width = right.shape[1]
-    tall = tile_of(rows, 1024)
-
-    def kernel(ids_ref, a_ref, b_ref, out_ref):
-        out_ref[...] = product(a_ref[...], b_ref[...], "NN").astype(BF16)
-
-    return call(
-        kernel,
-        ids,
-        (rows // tall,),
+def merge_kernel(ids, seed, context, weight, place, start, span, blocks, after=(), lag=0.05):
+    rows, depth = seed.shape
+    width = context.shape[1]
+    unit = rows // blocks
+
+    def kernel(ids_ref, g_ref, c_ref, w_ref, back_ref, out_ref, acc_s):
+        step = pl.program_id(0)
+        back_ref[...] = product(g_ref[...], w_ref[...], "NT").astype(BF16)
+        made = product(g_ref[...], c_ref[...], "TN")
+
+        @pl.when(step == 0)
+        def _():
+            acc_s[...] = made
+
+        @pl.when((step > 0) & (step < blocks - 1))
+        def _():
+            acc_s[...] += made
+
+        @pl.when(step == blocks - 1)
+        def _():
+            out_ref[...] = (acc_s[...] + made).astype(BF16)
+
+    tile = pl.BlockSpec((unit, width), lambda i, ids: (i, 0))
+    return call(
+        kernel,
+        ids,
+        (blocks,),
         [
-            pl.BlockSpec((tall, depth), lambda i, ids: (i, 0)),
-            pl.BlockSpec(right.shape, lambda i, ids: (0, 0)),
-        ],
-        pl.BlockSpec((tall, width), lambda i, ids: (i, 0)),
-        jax.ShapeDtypeStruct((rows, width), BF16),
-        (left, right),
-        after=after,
-        lag=lag,
-        name="plain",
-    )
-
-
-def branches_kernel(ids, context, merge, hidden, shrink, blocks, after=(), lag=0.05):
+            pl.BlockSpec((unit, depth), lambda i, ids: (i, 0)),
+            tile,
+            pl.BlockSpec((width, depth), lambda i, ids: (place // width, 0)),
+        ],
+        [tile, pl.BlockSpec((depth, width), lambda i, ids: (0, start // width))],
+        [jax.ShapeDtypeStruct((rows, width), BF16), jax.ShapeDtypeStruct((depth, span), BF16)],
+        (seed, context, weight),
+        scratch=[pltpu.VMEM((depth, width), F32)],
+        after=after,
+        lag=lag,
+        name="merge",
+    )
+
+
+def branches_kernel(ids, context, hidden, weight, blocks, after=(), lag=0.05):
     rows, deep_b = hidden.shape
-    depth, deep_a = merge.shape
+    depth, deep_a = weight.shape[1], context.shape[1]
     tall, wide = rows // blocks, tile_of(depth, 1024)
     unit = tile_of(wide, 512)
 
@@ -524,7 +479,7 @@
                 for part in range(wide // unit):
                     here = slice(part * unit, (part + 1) * unit)
                     value = product(h_ref[...], s_ref[:, here], "NN")
-                    value = value + product(a_ref[...], m_ref[here, :], "NT")
+                    value = value + product(a_ref[...], m_ref[:, here], "NN")
                     out_ref[:, here] = value.astype(BF16)
 
     return call(
@@ -533,24 +488,24 @@
         (depth // wide, blocks),
         [
             pl.BlockSpec((tall, deep_a), lambda j, i, ids: (i, 0)),
-            pl.BlockSpec((wide, deep_a), lambda j, i, ids: (j, 0)),
+            pl.BlockSpec((deep_a, wide), lambda j, i, ids: (deep_b // deep_a, j)),
             pl.BlockSpec((tall, deep_b), lambda j, i, ids: (i, 0)),
             pl.BlockSpec((deep_b, wide), lambda j, i, ids: (0, j)),
         ],
         [pl.BlockSpec((tall, wide), lambda j, i, ids: (0, j))] * blocks,
         [jax.ShapeDtypeStruct((tall, depth), BF16)] * blocks,
-        (context, merge, hidden, shrink),
+        (context, weight, hidden, weight),
         after=after,
         lag=lag,
         name="branches",
     )
 
 
-def back_kernel(ids, left_a, right_a, left_b, right_b, scales, start, count, blocks, after=(), lag=0.05):
+def back_kernel(ids, left_a, left_b, right, scales, start, count, blocks, after=(), lag=0.05):
     rows = left_a.shape[0] // blocks
-    width = right_a.shape[0]
+    width = right.shape[0]
     deep_a, deep_b = left_a.shape[1], left_b.shape[1]
-    wide = tile_of(width, 1024)
+    wide = tile_of(width, 512)
     unit = tile_of(wide, 512)
 
     def kernel(ids_ref, a_ref, b_ref, c_ref, d_ref, s_ref, *out_refs):
@@ -570,24 +525,24 @@
         (width // wide, count),
         [
             pl.BlockSpec((rows, deep_a), lambda j, i, ids: (start + i, 0)),
-            pl.BlockSpec((wide, deep_a), lambda j, i, ids: (j, 0)),
+            pl.BlockSpec((pl.Element(wide), pl.Element(deep_a)), lambda j, i, ids: (j * wide, deep_b)),
             pl.BlockSpec((rows, deep_b), lambda j, i, ids: (start + i, 0)),
             pl.BlockSpec((wide, deep_b), lambda j, i, ids: (j, 0)),
             pl.BlockSpec((2, wide), lambda j, i, ids: (0, j)),
         ],
         [pl.BlockSpec((rows, wide), lambda j, i, ids: (0, j))] * count,
         [jax.ShapeDtypeStruct((rows, width), BF16)] * count,
-        (left_a, right_a, left_b, right_b, scales),
+        (left_a, right, left_b, right, scales),
         after=after,
         lag=lag,
         name="back",
     )
 
 
-def full_grad_kernel(ids, left, right, weight=None, total=None, spare=0, start=0, count=0, kept=(), after=(), lag=0.05):
+def full_grad_kernel(ids, left, right, weight=None, total=None, place=0, spare=0, start=0, span=0, kept=(), after=(), lag=0.05):
     rows, depth = left.shape
     width = right.shape[1]
-    tall, wide = tile_of(depth, 1024), tile_of(width, 1024)
+    tall, wide = tile_of(depth, 1024), tile_of(width, 512 if span else 1024)
     unit = tile_of(wide, 512)
     summed = weight is not None
 
@@ -615,12 +570,15 @@
         pl.BlockSpec((rows, tall), lambda i, j, ids: (0, i)),
         pl.BlockSpec((rows, wide), lambda i, j, ids: (0, j)),
     ]
-    out_specs = [pl.BlockSpec((tall, wide), lambda i, j, ids: (start // tall + i, j))]
-    out_shape = [jax.ShapeDtypeStruct((count or depth, width + spare), BF16)]
+    out_specs = [pl.BlockSpec((tall, wide), lambda i, j, ids: (i, start // wide + j))]
+    out_shape = [jax.ShapeDtypeStruct((depth, span or width + spare), BF16)]
     args = (left, right)
     if summed:
         args += (weight, total)
-        in_specs += [tile, pl.BlockSpec((1, wide), lambda i, j, ids: (0, j))]
+        in_specs += [
+            pl.BlockSpec((tall, wide), lambda i, j, ids: (i, place // wide + j)),
+            pl.BlockSpec((1, wide), lambda i, j, ids: (0, j)),
+        ]
         out_specs += [pl.BlockSpec((tall, 128), lambda i, j, ids: (i, 0))] * 2
         out_shape += [jax.ShapeDtypeStruct((depth, 128), F32)] * 2
     return call(
@@ -638,27 +596,55 @@
     )
 
 
-def spare_kernel(ids, kept, wide, narrow, after=(), lag=0.05):
-    depth = kept.shape[0]
+def sums_kernel(ids, wide, rows, after=(), lag=0.05):
+    depth = rows.shape[1]
+    count = len(wide)
 
     def kernel(ids_ref, *refs):
         lane = lax.broadcasted_iota(jnp.int32, (depth, 128), 1)
-        value = refs[len(wide)][...]
-        for number, ref in enumerate(refs[: len(wide)]):
+        value = jnp.zeros((depth, 128), F32)
+        for number, ref in enumerate(refs[:count]):
             value = jnp.where(lane == number, jnp.sum(ref[...], axis=1, keepdims=True), value)
+        refs[-1][...] = refs[count][...] + jnp.transpose(value)[:8]
+
+    def whole(shape):
+        return pl.BlockSpec(shape, lambda i, ids: (0, 0))
+
+    return call(
+        kernel,
+        ids,
+        (1,),
+        [whole((depth, 128))] * count + [whole((8, depth))],
+        whole((8, depth)),
+        jax.ShapeDtypeStruct((8, depth), F32),
+        (*wide, rows),
+        after=after,
+        lag=lag,
+        name="sums",
+    )
+
+
+def spare_kernel(ids, kept, parts, after=(), lag=0.05):
+    depth = kept.shape[0]
+
+    def kernel(ids_ref, *refs):
+        total = refs[0][...]
+        for ref in refs[1:-1]:
+            total = total + ref[...]
+        value = jnp.transpose(jnp.concatenate([total, jnp.zeros((120, depth), F32)], axis=0))
+        lane = lax.broadcasted_iota(jnp.int32, (depth, 128), 1)
         rounded = value.astype(BF16).astype(F32)
         rest = pltpu.roll(value - rounded, 64, 1)
         refs[-1][...] = jnp.where(lane < 64, rounded, rest).astype(BF16)
 
-    block = pl.BlockSpec((depth, 128), lambda i, ids: (0, 0))
     return call(
         kernel,
         ids,
         (1,),
-        [block] * (len(wide) + 1),
+        [pl.BlockSpec((8, depth), lambda i, ids: (0, 0))] * len(parts),
         [pl.BlockSpec((depth, 128), lambda i, ids: (0, kept.shape[1] // 128 - 1))],
         [jax.ShapeDtypeStruct(kept.shape, BF16)],
-        (*wide, narrow),
+        tuple(parts),
         kept=(kept,),
         after=after,
         lag=lag,
@@ -691,26 +677,24 @@
     )
 
 
-def widen_kernel(ids, rows, spare=0, after=(), lag=0.05):
-    count, width = rows.shape[0], rows.shape[1] - spare
+def widen_kernel(ids, rows, widths, after=(), lag=0.05):
+    count = rows.shape[0]
+    specs, shapes, place = [], [], 0
+    for width in widths:
+        specs.append(pl.BlockSpec((pl.Element(count), pl.Element(width)), lambda i, ids, place=place: (0, place)))
+        shapes.append(jax.ShapeDtypeStruct((count, width), F32))
+        place += width
 
     def kernel(ids_ref, *refs):
-        half = len(refs) // 2
-        for in_ref, out_ref in zip(refs[:half], refs[half:]):
+        for in_ref, out_ref in zip(refs[: len(specs)], refs[len(specs) :]):
             out_ref[...] = in_ref[...].astype(F32)
 
-    specs = [pl.BlockSpec((count, width), lambda i, ids: (0, 0))]
-    shapes = [jax.ShapeDtypeStruct((count, width), F32)]
-    if spare:
-        specs.append(pl.BlockSpec((count, spare), lambda i, ids: (0, width // spare)))
-        shapes.append(jax.ShapeDtypeStruct((count, spare), F32))
-    out_specs = [pl.BlockSpec(shape.shape, lambda i, ids: (0, 0)) for shape in shapes]
     return call(
         kernel,
         ids,
         (1,),
         specs,
-        out_specs,
+        [pl.BlockSpec(shape.shape, lambda i, ids: (0, 0)) for shape in shapes],
         shapes,
         (rows,) * len(specs),
         after=after,
@@ -829,41 +813,6 @@
     upper = flip(half_kernel(ids, two, 0, after), "tensor", 1, size)
     lower = flip(half_kernel(ids, one, 1, after), "tensor", 2, size)
     return [rows, one, two, upper, lower]
-
-
-def swap_core(value, size):
-    return flip(value, "dp", 1, size)
-
-
-class LineGather:
-    def __init__(self, ids, shard, core, size):
-        self.ids, self.size = ids, size
-        depth, width = shard.shape
-        halves = jnp.transpose(shard.reshape(depth, 2, width // 2), (1, 0, 2))
-        self.mine = lax.dynamic_index_in_dim(halves, core, 0, keepdims=False)
-        self.other = swap_core(lax.dynamic_index_in_dim(halves, 1 - core, 0, keepdims=False), size)
-        self.bit, self.place, self.chunks = size // 4, 1, 1
-        self.first = True
-
-    def step(self, after=()):
-        self.mine = join_kernel(self.ids, self.mine, self.other, self.place, self.chunks, after)
-        self.chunks = 1 if self.first else 2 * self.chunks
-        self.first = False
-        self.place = 1 + self.bit.bit_length()
-        self.other = flip(self.mine, "dp", 2 * self.bit, self.size)
-        self.bit //= 2
-        return self.mine
-
-    def open(self):
-        return self.bit >= 1
-
-    def cross(self, after=()):
-        self.other = stack_kernel(self.ids, [self.other], self.other.shape[0], after=after)
-        self.across = [swap_core(value, self.size) for value in (self.mine, self.other)]
-        return self.other
-
-    def finish(self, after=()):
-        return assemble_kernel(self.ids, (self.mine, self.other, *self.across), self.place, self.chunks, after)
 
 
 def body(
@@ -909,74 +858,72 @@
 
     tables = rotary_tables(LENGTH)
     own_project = project.reshape(depth, mixed_width)
-    w_project = lax.all_gather(own_project, "dp", axis=0, tiled=True)
-    w_expand = lax.all_gather(expand, "dp", axis=0, tiled=True)
-    w_shrink = lax.all_gather(shrink, "dp", axis=1, tiled=True)
-    merge_line = LineGather(ids, jnp.transpose(merging), core, n_dp)
+    w_in = lax.all_gather(jnp.concatenate([expand, own_project], axis=1), "dp", axis=0, tiled=True)
+    w_out = lax.all_gather(jnp.concatenate([shrink, merging], axis=0), "dp", axis=1, tiled=True)
+
     unit = own_count
-    rows_pieces = gather_rows(ids, layer_input, n_tensor, (vectors,))
+    rows_pieces = gather_rows(ids, layer_input, n_tensor, (vectors, tables[0]))
     near, far = (rows_pieces[:-1], rows_pieces[-1:]) if n_tensor != 4 else (rows_pieces[:3], rows_pieces[3:])
     pair = norm_kernel(ids, near, vectors, unit, 0, n_tensor)
-    mixed = mixed_kernel(ids, pair[0], w_project, b_project, tables, 0, n_tensor - 1, n_tensor)
-    last = merge_line.step((mixed[0],))
-    later = stack_kernel(ids, [cotangent], unit, after=(last, *far))
+    later = stack_kernel(ids, [cotangent], unit, after=(pair[0], *far))
     seed_pieces = [later] + [flip(later, "tensor", k, n_tensor) for k in range(n_tensor - 1, 0, -1)]
     first, second = norm_kernel(ids, far, vectors, unit, n_tensor - 1, n_tensor, kept=pair, after=(later,))
-    (mixed,) = mixed_kernel(ids, first, w_project, b_project, tables, n_tensor - 1, 1, n_tensor, kept=mixed)
-    last = mixed
-    while merge_line.open():
-        last = merge_line.step((last,))
-    context, lse = attend_kernel(ids, mixed, n_tensor, after=(last,), lag=12)
-    last = merge_line.cross((context,))
-    hidden, slope = expand_kernel(ids, second, w_expand, b_expand, after=(last,))
-    w_merge = merge_line.finish((hidden,))
-    seed = stack_kernel(ids, seed_pieces[:1] + seed_pieces[:0:-1], unit, after=(w_merge,))
+    hidden, slope = expand_kernel(ids, second, w_in, b_expand)
+    (mixed,) = mixed_kernel(
+        ids, first, w_in, hidden_width, b_project, tables, 0, n_tensor, n_tensor, after=(hidden,)
+    )
+    seed = stack_kernel(ids, seed_pieces[:1] + seed_pieces[:0:-1], unit, after=(mixed,))
+    (shrink_part,) = full_grad_kernel(ids, hidden, seed)
+    shrink_grad = lax.psum_scatter(shrink_part, "dp", scatter_dimension=1, tiled=True)
+    context, lse = attend_kernel(ids, mixed, n_tensor, after=(shrink_part,))
+    branches = branches_kernel(ids, context, hidden, w_out, n_tensor)
+    summed = [branches[0]] + [flip(branches[k], "tensor", k, n_tensor) for k in range(n_tensor - 1, 0, -1)]
+    pgrad, expand_sum = shrink_back_kernel(ids, seed, w_out, slope, after=(branches[0],))
+    expand_part, gain_two, bias_two = full_grad_kernel(ids, second, pgrad, w_in, expand_sum)
+    expand_grad = lax.psum_scatter(expand_part, "dp", scatter_dimension=0, tiled=True)
+
     merge_width = merging.shape[0]
-    joint = hidden_width + merge_width
-    part = full_grad_kernel(ids, context, seed, start=hidden_width, count=joint)
-    part = full_grad_kernel(ids, hidden, seed, count=joint, kept=part)
-    joint_grad = lax.psum_scatter(part[0], "dp", scatter_dimension=1, tiled=True)
-    cgrad = plain_kernel(ids, seed, w_merge, after=part)
+    joint = mixed_width + merge_width + 128
+    cgrad, part = merge_kernel(ids, seed, context, w_out, hidden_width, mixed_width, joint, 2, after=(expand_part,))
     mgrad, mixed_sum = attend_back_kernel(ids, mixed, cgrad, context, lse, tables, n_tensor)
-    project_part, gain_one, bias_one = full_grad_kernel(ids, first, mgrad, w_project, mixed_sum)
-    project_grad = lax.psum_scatter(project_part, "dp", scatter_dimension=0, tiled=True)
-    branches = branches_kernel(ids, context, w_merge, hidden, w_shrink, n_tensor, after=(project_part,))
-    summed = [branches[0]] + [flip(branches[k], "tensor", k, n_tensor) for k in range(n_tensor - 1, 0, -1)]
-    pgrad, expand_sum = shrink_back_kernel(ids, seed, w_shrink, slope, after=(branches[0],))
-    expand_part, gain_two, bias_two = full_grad_kernel(ids, second, pgrad, w_expand, expand_sum, spare=128)
+    project_part, gain_one, bias_one = full_grad_kernel(
+        ids, first, mgrad, w_in, mixed_sum, place=hidden_width, span=joint, kept=(part,)
+    )
+    (shrink_grad,) = widen_kernel(ids, shrink_grad, [shrink.shape[1]], after=(project_part,))
 
     def slots(values):
-        return jnp.pad(values, ((0, 0), (0, depth - values.shape[1]))).reshape(width)
-
-    narrow = [
-        jnp.sum(cotangent.astype(F32), axis=0),
+        return jnp.pad(values, ((0, 0), (0, depth - values.shape[1]))).reshape(1, width)
+
+    seed_sum = jnp.sum(cotangent.astype(F32), axis=0, keepdims=True)
+    over_all = jnp.pad(seed_sum, ((4, 3), (0, 0)))
+    over_all = sums_kernel(ids, [gain_one, bias_one, gain_two, bias_two], over_all, after=(shrink_grad,))
+    over_dp = [
         slots(expand_sum.reshape(n_dp, -1)),
         slots(jnp.transpose(mixed_sum.reshape(heads, n_dp, -1), (1, 0, 2)).reshape(n_dp, -1)),
     ]
-    narrow = jnp.pad(jnp.stack(narrow, axis=1), ((0, 0), (4, 128 - 4 - len(narrow))))
-    expand_part = spare_kernel(ids, expand_part, [gain_one, bias_one, gain_two, bias_two], narrow)
-    expand_grad = lax.psum_scatter(expand_part, "dp", scatter_dimension=0, tiled=True)
-    (joint_grad,) = widen_kernel(ids, joint_grad, after=(expand_part,))
-    shrink_grad, merging_grad = joint_grad[:hidden_width], joint_grad[hidden_width:]
+    over_dp = jnp.pad(jnp.concatenate(over_dp, axis=0), ((5, 1), (0, 0)))
+    over_tensor = [over_all] + [flip(over_all, "tensor", k, n_tensor) for k in range(n_tensor - 1, 0, -1)]
+
     gains = jnp.stack([vectors[0], vectors[2]])
     back = []
-    last = joint_grad
+    last = over_all
     half = n_tensor // 2
     for start, count in ((half + 1, half - 1), (1, half), (0, 1)):
-        made = back_kernel(ids, mgrad, w_project, pgrad, w_expand, gains, start, count, n_tensor, after=(last,))
+        made = back_kernel(ids, mgrad, pgrad, w_in, gains, start, count, n_tensor, after=(last,))
         back.append([flip(made[k], "tensor", start + k, n_tensor) if start else made[k] for k in range(count - 1, -1, -1)])
         last = made[0]
         if len(back) == 1:
-            (project_grad,) = widen_kernel(ids, project_grad, after=(last,))
-            last = layer_output = output_kernel(ids, layer_input, summed, vectors, after=(project_grad,), lag=165)
-    far = total_kernel(ids, back[0] + back[2], after=(last,), lag=4)
-    expand_grad, sums = widen_kernel(ids, expand_grad, spare=128, after=(far,))
-    input_grad = input_kernel(ids, layer_input, cotangent, back[1] + [far], after=(expand_grad,), lag=160)
-
+            layer_output = output_kernel(ids, layer_input, summed, vectors, after=(last,), lag=160)
+            last = spare_kernel(ids, project_part, over_tensor + [over_dp], after=(layer_output,))
+            project_grad = lax.psum_scatter(last, "dp", scatter_dimension=0, tiled=True)
+    (expand_grad,) = widen_kernel(ids, expand_grad, [hidden_width], after=(last,))
+    far = total_kernel(ids, back[0] + back[2], after=(expand_grad,), lag=8)
+    input_grad = input_kernel(ids, layer_input, cotangent, back[1] + [far], lag=162)
+    project_grad, merging_grad, sums = widen_kernel(
+        ids, project_grad, [mixed_width, merge_width, 128], after=(input_grad,)
+    )
     sums = jnp.transpose(sums[:, :7] + sums[:, 64:71])
-    norms = sums[:5]
-    norms = norms + sum(flip(norms, "tensor", k, n_tensor) for k in range(1, n_tensor))
-    gain_one, bias_one, gain_two, bias_two, seed_sum = norms
+    gain_one, bias_one, gain_two, bias_two, seed_sum = sums[:5]
     gain_one = (gain_one - firstbias.astype(F32) * bias_one) / firstgain.astype(F32)
     gain_two = (gain_two - secondbias.astype(F32) * bias_two) / secondgain.astype(F32)
     expandbias_grad = sums[5, : expandbias.shape[0]]
@@ -990,7 +937,7 @@
         bias_two,
         project_grad.reshape(project.shape),
         projbias_grad,
-        merging_grad,
+        jnp.transpose(merging_grad),
         seed_sum,
         expand_grad,
         expandbias_grad,

time: 581 us -> 556 us (0.957)
  Pallas kernels: 401 us -> 359 us
  waiting for transfers between devices: 91.4 us -> 116 us
  local copies, waits for them, and re-layouts: 26 us -> 19.5 us
    pallas_call x32 -> x27, Pallas kernels: 401 us -> 359 us  [call(): pl.pallas_call(run, grid_spec=pltpu.PrefetchScalarGridSpec(num_scalar_pre...]
    all_gather x3 -> x2, waiting for transfers between devices: 0.02 us -> 39.9 us  [the longest x1 38.9 us: body(): lax.all_gather(jnp.concatenate([expand, own_project], axis=1), 'dp', axis...]
    reduce_scatter x1, waiting for transfers between devices: 31.8 us -> 0.01 us  [body(): lax.psum_scatter(expand_part, 'dp', scatter_dimension=0, tiled=True)]
    ppermute x24 -> x19, waiting for transfers between devices: 54.1 us -> 75.8 us  [flip(): return lax.ppermute(value, axis, [(i, i ^ bit) for i in range(size)])]
    ppermute x24 -> x19, starting transfers between devices: 30.2 us -> 24.8 us  [flip(): return lax.ppermute(value, axis, [(i, i ^ bit) for i in range(size)])]
    unnamed x77 -> x70, local copies, waits for them, and re-layouts: 13.9 us -> 13.7 us
  transfers between devices with their start and end apart: 30 -> 24, of which waited for: 8 -> 9; matrix products, arithmetic and copies ran while one was open for 4% -> 3% of each run, Pallas kernels for 70% -> 65%
where the time goes in v5:
time: 556 us; the launch traced here: 548 us
  Pallas kernels  359 us (65%)
  waiting for transfers between devices  116 us (21%)
  starting transfers between devices  25 us (4%)
  local copies, waits for them, and re-layouts  19.5 us (4%)
  between operations  14.3 us (3%)
  other arithmetic  13 us (2%)
    pallas_call x27, Pallas kernels, call(): pl.pallas_call(run, grid_spec=pltpu.PrefetchScalarGridSpec(num_scalar_pre...  359 us
    ppermute x19, waiting for transfers between devices, flip(): return lax.ppermute(value, axis, [(i, i ^ bit) for i in range(size)])  75.8 us
    all_gather x1, waiting for transfers between devices, body(): lax.all_gather(jnp.concatenate([expand, own_project], axis=1), 'dp', axis...  38.9 us
    ppermute x19, starting transfers between devices, flip(): return lax.ppermute(value, axis, [(i, i ^ bit) for i in range(size)])  24.8 us
    unnamed x70, local copies, waits for them, and re-layouts  13.7 us
  transfers between devices with their start and end apart: 24, of which 9 were waited for; matrix products, arithmetic and copies ran while one was open for 3% of the time, Pallas kernels for 65%

profile of v5, /device:TPU:0, one launch (start us, length us, event | category | flops | bytes accessed | tf_op | source)
XLA Modules:
  0.0 547.7 jit_solution(17978735920594605886)
XLA Ops:
  21.0 5.0 fusion.1
  34.5 27.6 %collective-permute-done.3.refs_0_.refs_2_ = bf16[512,2048]{1,0:T(8,128)(2,1)} collective-permute-done((bf16[512,2048]{1,0:T(8,128)(2,1)}, bf16[512,2048]{1,0:T(8,128)(2,1)}, u32[]{:S(2)}, u32[]{:S(2)}) %collective-permute-start.3) | collective-permute-done | bytes 2097184 | tf_op jit(solution)/shard_map/ppermute | solution.py:777
  71.4 12.1 %norm.2 = (bf16[2048,2048]{1,0:T(8,128)(2,1)}, bf16[2048,2048]{1,0:T(8,128)(2,1)}) custom-call(s32[4]{0:T(128)} %pad_add_fusion.ids_ref, bf16[512,2048]{1,0:T(8,128)(2,1)} %refs_0_.7, bf16[512,2048]{1,0:T(8,128)(2,1)} %copy-done, bf16[512,2048]{1,0:T(8,128)(2,1)} %collective-permute-done.3.refs_0_.refs_2_, f32[6,2048]{1,0:T(8,128)} %bitcast.34), custom_call_target="tpu_custom_call" | custom-call | flops 50000000 | tf_op jit(solution)/shard_map/norm/pallas_call | solution.py:49
  83.4 5.5 %collective-permute-done.4.refs_2_.refs_0_ = bf16[256,2048]{1,0:T(8,128)(2,1)S(1)} collective-permute-done((bf16[256,2048]{1,0:T(8,128)(2,1)}, bf16[256,2048]{1,0:T(8,128)(2,1)S(1)}, u32[]{:S(2)}, u32[]{:S(2)}) %collective-permute-start.4) | collective-permute-done | bytes 1048608 | tf_op jit(solution)/shard_map/ppermute | solution.py:777
  103.2 6.2 %norm.3 = (bf16[2048,2048]{1,0:T(8,128)(2,1)}, bf16[2048,2048]{1,0:T(8,128)(2,1)}) custom-call(s32[4]{0:T(128)} %pad_add_fusion.ids_ref, bf16[256,2048]{1,0:T(8,128)(2,1)} %copy-done.2, bf16[256,2048]{1,0:T(8,128)(2,1)} %copy-done.3, f32[6,2048]{1,0:T(8,128)} %bitcast.35, ...), custom_call_target="tpu_custom_call", output_to_operand_aliasing={{0}: (4, {}), {1}: (5, {})} | custom-call | flops 50000000 | tf_op jit(solution)/shard_map/norm/pallas_call | solution.py:49
  109.4 38.9 %all-gather.3.cloned.1.call-done.refs_1_.refs_2_.refs_3_ = bf16[2048,3584]{1,0:T(8,128)(2,1)} async-done(((bf16[256,3584]{1,0:T(8,128)(2,1)}), bf16[2048,3584]{1,0:T(8,128)(2,1)}) %all-gather.3.cloned.1.call-update) | async-done | bytes 14680080 | tf_op jit(solution)/shard_map/all_gather | solution.py:861
  148.3 30.0 %expand.1 = (bf16[2048,2048]{1,0:T(8,128)(2,1)}, bf16[2048,2048]{1,0:T(8,128)(2,1)}) custom-call(s32[4]{0:T(128)} %pad_add_fusion.ids_ref, bf16[2048,2048]{1,0:T(8,128)(2,1)} %get-tuple-element.46.refs_0_, bf16[2048,3584]{1,0:T(8,128)(2,1)} %all-gather.3.cloned.1.call-done.refs_1_.refs_2_.refs_3_, f32[1,2048]{1,0:T(1,128)} %bitcast.42), custom_call_target="tpu_custom_call" | custom-call | flops 50000000 | tf_op jit(solution)/shard_map/expand/pallas_call | solution.py:49
  178.3 21.5 %mixed.1.refs_4_.refs_0_ = bf16[2048,1536]{1,0:T(8,128)(2,1)} custom-call(s32[4]{0:T(128)} %pad_add_fusion.ids_ref, bf16[2048,2048]{1,0:T(8,128)(2,1)} %get-tuple-element.45.refs_0_, bf16[2048,3584]{1,0:T(8,128)(2,1)} %all-gather.3.cloned.1.call-done.refs_1_.refs_2_.refs_3_, bf16[2048,3584]{1,0:T(8,128)(2,1)} %all-gather.3.cloned.1.call-done.refs_1_.refs_2_.refs_3_, ...), custom_call_target="tpu_custom_call" | custom-call | flops 50000000 | tf_op jit(solution)/shard_map/mixed/pallas_call | solution.py:49
  201.1 7.8 %stack.27.refs_1_.refs_0_ = bf16[2048,2048]{1,0:T(8,128)(2,1)} custom-call(s32[4]{0:T(128)} %pad_add_fusion.ids_ref, bf16[512,2048]{1,0:T(8,128)(2,1)} %stack.26.refs_5_.refs_0_, bf16[512,2048]{1,0:T(8,128)(2,1)} %collective-permute-done.7.refs_1_, bf16[512,2048]{1,0:T(8,128)(2,1)} %collective-permute-done.8.refs_2_, bf16[512,2048]{1,0:T(8,128)(2,1)} %copy-done.4, ...), custom_call_target="tpu_custom_call" | custom-call | flops 50000000 | tf_op jit(solution)/shard_map/stack/pallas_call | solution.py:49
  208.9 23.8 %full_grad.3.refs_1_ = bf16[2048,2048]{1,0:T(8,128)(2,1)} custom-call(s32[4]{0:T(128)} %pad_add_fusion.ids_ref, bf16[2048,2048]{1,0:T(8,128)(2,1)} %get-tuple-element.47.refs_8_.refs_0_.refs_2_, bf16[2048,2048]{1,0:T(8,128)(2,1)} %stack.27.refs_1_.refs_0_), custom_call_target="tpu_custom_call" | custom-call | flops 50000000 | tf_op jit(solution)/shard_map/full_grad/pallas_call | solution.py:49
  232.8 14.7 %attend.1 = (bf16[2048,512]{1,0:T(8,128)(2,1)}, f32[2,4,8,512]{3,2,1,0:T(8,128)}) custom-call(s32[4]{0:T(128)} %pad_add_fusion.ids_ref, bf16[2048,1536]{1,0:T(8,128)(2,1)} %mixed.1.refs_4_.refs_0_, bf16[2048,2048]{1,0:T(8,128)(2,1)} %full_grad.3.refs_1_), custom_call_target="tpu_custom_call" | custom-call | flops 50000000 | tf_op jit(solution)/shard_map/attend/pallas_call | solution.py:49
  248.5 30.4 %branches.1 = (bf16[512,2048]{1,0:T(8,128)(2,1)}, bf16[512,2048]{1,0:T(8,128)(2,1)}, bf16[512,2048]{1,0:T(8,128)(2,1)}, bf16[512,2048]{1,0:T(8,128)(2,1)}) custom-call(s32[4]{0:T(128)} %pad_add_fusion.ids_ref, bf16[2048,512]{1,0:T(8,128)(2,1)} %get-tuple-element.48.refs_0_.refs_1_.refs_2_, ...), custom_call_target="tpu_custom_call" | custom-call | flops 50000000 | tf_op jit(solution)/shard_map/branches/pallas_call | solution.py:49
  282.4 25.3 %shrink_back.1 = (bf16[2048,2048]{1,0:T(8,128)(2,1)}, f32[1,2048]{1,0:T(1,128)}) custom-call(s32[4]{0:T(128)} %pad_add_fusion.ids_ref, bf16[2048,2048]{1,0:T(8,128)(2,1)} %stack.27.refs_1_.refs_0_, bf16[2560,2048]{1,0:T(8,128)(2,1)} %all-gather.5.cloned.1.call-done.refs_1_.refs_3_.refs_2_, bf16[2048,2048]{1,0:T(8,128)(2,1)} %get-tuple-element.53.refs_2_, ...), custom_call_target="tpu_custom_call" | custom-call | flops 50000000 | tf_op jit(solution)/shard_map/shrink_back/pallas_call | solution.py:49
  307.7 26.5 %full_grad.4 = (bf16[2048,2048]{1,0:T(8,128)(2,1)}, f32[2048,128]{1,0:T(8,128)}, f32[2048,128]{1,0:T(8,128)}) custom-call(s32[4]{0:T(128)} %pad_add_fusion.ids_ref, bf16[2048,2048]{1,0:T(8,128)(2,1)} %get-tuple-element.46.refs_0_, bf16[2048,2048]{1,0:T(8,128)(2,1)} %get-tuple-element.54.refs_1_.refs_2_, ...), custom_call_target="tpu_custom_call" | custom-call | flops 50000000 | tf_op jit(solution)/shard_map/full_grad/pallas_call | solution.py:49
  337.4 15.3 %merge.1 = (bf16[2048,512]{1,0:T(8,128)(2,1)}, bf16[2048,2176]{1,0:T(8,128)(2,1)}) custom-call(s32[4]{0:T(128)} %pad_add_fusion.ids_ref, bf16[2048,2048]{1,0:T(8,128)(2,1)} %stack.27.refs_1_.refs_0_, bf16[2048,512]{1,0:T(8,128)(2,1)} %get-tuple-element.48.refs_0_.refs_1_.refs_2_, bf16[2560,2048]{1,0:T(8,128)(2,1)} %all-gather.5.cloned.1.call-done.refs_1_.refs_3_.refs_2_, ...), custom_call_target="tpu_custom_call" | custom-call | flops 50000000 | tf_op jit(solution)/shard_map/merge/pallas_call | solution.py:49
  352.8 23.1 %attend_back.1 = (bf16[2048,1536]{1,0:T(8,128)(2,1)}, f32[1,1536]{1,0:T(1,128)}) custom-call(s32[4]{0:T(128)} %pad_add_fusion.ids_ref, bf16[2048,1536]{1,0:T(8,128)(2,1)} %mixed.1.refs_4_.refs_0_, bf16[2048,512]{1,0:T(8,128)(2,1)} %get-tuple-element.57.refs_1_, bf16[2048,512]{1,0:T(8,128)(2,1)} %get-tuple-element.48.refs_0_.refs_1_.refs_2_, ...), custom_call_target="tpu_custom_call" | custom-call | flops 50000000 | tf_op jit(solution)/shard_map/attend_back/pallas_call | solution.py:49
  376.8 21.5 %full_grad.5 = (bf16[2048,2176]{1,0:T(8,128)(2,1)}, f32[2048,128]{1,0:T(8,128)}, f32[2048,128]{1,0:T(8,128)}) custom-call(s32[4]{0:T(128)} %pad_add_fusion.ids_ref, bf16[2048,2048]{1,0:T(8,128)(2,1)} %get-tuple-element.45.refs_0_, bf16[2048,1536]{1,0:T(8,128)(2,1)} %get-tuple-element.59.refs_1_.refs_0_, ...), custom_call_target="tpu_custom_call", output_to_operand_aliasing={{0}: (5, {})} | custom-call | flops 50000000 | tf_op jit(solution)/shard_map/full_grad/pallas_call | solution.py:49
  402.3 4.9 sums.1.refs_5_.refs_0_
  410.1 14.1 %back.3.refs_6_ = bf16[512,2048]{1,0:T(8,128)(2,1)} custom-call(s32[4]{0:T(128)} %pad_add_fusion.ids_ref, bf16[2048,1536]{1,0:T(8,128)(2,1)} %get-tuple-element.59.refs_1_.refs_0_, bf16[2048,3584]{1,0:T(8,128)(2,1)} %all-gather.3.cloned.1.call-done.refs_1_.refs_2_.refs_3_, bf16[2048,2048]{1,0:T(8,128)(2,1)} %get-tuple-element.54.refs_1_.refs_2_, ...), custom_call_target="tpu_custom_call" | custom-call | flops 50000000 | tf_op jit(solution)/shard_map/back/pallas_call | solution.py:49
  427.1 6.5 %output.1.refs_6_ = bf16[512,2048]{1,0:T(8,128)(2,1)} custom-call(s32[4]{0:T(128)} %pad_add_fusion.ids_ref, bf16[512,2048]{1,0:T(8,128)(2,1)} %refs_0_.7, f32[6,2048]{1,0:T(8,128)} %bitcast.36, bf16[512,2048]{1,0:T(8,128)(2,1)} %get-tuple-element.49.refs_3_.refs_2_, bf16[512,2048]{1,0:T(8,128)(2,1)} %collective-permute-done.10.refs_3_, ...), custom_call_target="tpu_custom_call" | custom-call | flops 160000000000 | tf_op jit(solution)/shard_map/output/pallas_call | solution.py:49
  436.7 26.0 %back.4 = (bf16[512,2048]{1,0:T(8,128)(2,1)}, bf16[512,2048]{1,0:T(8,128)(2,1)}) custom-call(s32[4]{0:T(128)} %pad_add_fusion.ids_ref, bf16[2048,1536]{1,0:T(8,128)(2,1)} %get-tuple-element.59.refs_1_.refs_0_, bf16[2048,3584]{1,0:T(8,128)(2,1)} %all-gather.3.cloned.1.call-done.refs_1_.refs_2_.refs_3_, bf16[2048,2048]{1,0:T(8,128)(2,1)} %get-tuple-element.54.refs_1_.refs_2_, ...), custom_call_target="tpu_custom_call" | custom-call | flops 50000000 | tf_op jit(solution)/shard_map/back/pallas_call | solution.py:49
  464.0 14.1 %back.5.refs_1_ = bf16[512,2048]{1,0:T(8,128)(2,1)} custom-call(s32[4]{0:T(128)} %pad_add_fusion.ids_ref, bf16[2048,1536]{1,0:T(8,128)(2,1)} %get-tuple-element.59.refs_1_.refs_0_, bf16[2048,3584]{1,0:T(8,128)(2,1)} %all-gather.3.cloned.1.call-done.refs_1_.refs_2_.refs_3_, bf16[2048,2048]{1,0:T(8,128)(2,1)} %get-tuple-element.54.refs_1_.refs_2_, ...), custom_call_target="tpu_custom_call" | custom-call | flops 50000000 | tf_op jit(solution)/shard_map/back/pallas_call | solution.py:49
  485.9 32.1 %collective-permute-done.16.refs_2_ = bf16[512,2048]{1,0:T(8,128)(2,1)S(1)} collective-permute-done((bf16[512,2048]{1,0:T(8,128)(2,1)}, bf16[512,2048]{1,0:T(8,128)(2,1)S(1)}, u32[]{:S(2)}, u32[]{:S(2)}) %collective-permute-start.16) | collective-permute-done | bytes 2097184 | tf_op jit(solution)/shard_map/ppermute | solution.py:777
  519.4 8.6 %input.1.refs_3_ = f32[512,2048]{1,0:T(8,128)} custom-call(s32[4]{0:T(128)} %pad_add_fusion.ids_ref, bf16[512,2048]{1,0:T(8,128)(2,1)} %refs_0_.7, bf16[512,2048]{1,0:T(8,128)(2,1)} %refs_1_.1, bf16[512,2048]{1,0:T(8,128)(2,1)} %copy-done.24, bf16[512,2048]{1,0:T(8,128)(2,1)} %collective-permute-done.17.refs_3_, f32[512,2048]{1,0:T(8,128)} %total.1.refs_4_), custom_call_target="tpu_custom_call" | custom-call | flops 161999994880 | tf_op jit(solution)/shard_map/input/pallas_call | solution.py:49
  (161 shorter events, 91.8 us)
Async XLA Ops:
  7.2 141.1 %all-gather.3.cloned.1.call-start = ((), (), s32[]{:S(2)}) async-start(), calls=%async_computation.3 | async-start | bytes 16515072 | tf_op jit(solution)/shard_map/all_gather | solution.py:861
  10.1 238.4 %all-gather.5.cloned.1.call-start = ((), (), s32[]{:S(2)}) async-start(), calls=%async_computation.4 | async-start | bytes 11796480 | tf_op jit(solution)/shard_map/all_gather | solution.py:862
  11.7 387.3 %reduce-scatter.4.cloned.1.call-start = ((), (), s32[]{:S(2)}) async-start(), calls=%async_computation.5 | async-start | bytes 9437184 | tf_op jit(solution)/shard_map/reduce_scatter | solution.py:877
  11.7 53.7 %collective-permute-start.5 = (bf16[512,2048]{1,0:T(8,128)(2,1)}, bf16[512,2048]{1,0:T(8,128)(2,1)S(1)}, u32[]{:S(2)}, u32[]{:S(2)}) collective-permute-start(bf16[512,2048]{1,0:T(8,128)(2,1)} %refs_0_.7), channel_id=1, source_target_pairs={{0,1},{1,0},{2,3},{3,2},{4,5},{5,4},{6,7},{7,6},{8,9},{9,8},{10,11... | collective-permute-start | bytes 6291464 | tf_op jit(solution)/shard_map/ppermute | solution.py:777
  14.7 47.4 %collective-permute-start.3 = (bf16[512,2048]{1,0:T(8,128)(2,1)}, bf16[512,2048]{1,0:T(8,128)(2,1)}, u32[]{:S(2)}, u32[]{:S(2)}) collective-permute-start(bf16[512,2048]{1,0:T(8,128)(2,1)} %refs_0_.7), channel_id=1, source_target_pairs={{0,2},{1,3},{2,0},{3,1},{4,6},{5,7},{6,4},{7,5},{8,10},{9,11},{10,... | collective-permute-start | bytes 6291464 | tf_op jit(solution)/shard_map/ppermute | solution.py:777
  18.1 1.2 collective-permute-start
  19.4 6.6 %collective-permute-start.1 = (bf16[8,1984]{1,0:T(8,128)(2,1)S(1)}, bf16[8,1984]{1,0:T(8,128)(2,1)S(1)}, u32[]{:S(2)}, u32[]{:S(2)}) collective-permute-start(bf16[8,1984]{1,0:T(8,128)(2,1)S(1)} %fusion.3), channel_id=1, source_target_pairs={{0,8},{4,12},{8,0},{12,4},{16,24},{20,28},{24,16},{28,20},{1,9},{5... | collective-permute-start | bytes 95240 | tf_op jit(solution)/shard_map/ppermute | solution.py:777
  26.0 7.8 %collective-permute-start.2 = (bf16[8,1984]{1,0:T(8,128)(2,1)S(1)}, bf16[8,1984]{1,0:T(8,128)(2,1)S(1)}, u32[]{:S(2)}, u32[]{:S(2)}) collective-permute-start(bf16[8,1984]{1,0:T(8,128)(2,1)S(1)} %fusion.7), channel_id=1, source_target_pairs={{0,16},{4,20},{8,24},{12,28},{16,0},{20,4},{24,8},{28,12},{1,17},{... | collective-permute-start | bytes 95240 | tf_op jit(solution)/shard_map/ppermute | solution.py:777
  65.1 23.9 %collective-permute-start.4 = (bf16[256,2048]{1,0:T(8,128)(2,1)}, bf16[256,2048]{1,0:T(8,128)(2,1)S(1)}, u32[]{:S(2)}, u32[]{:S(2)}) collective-permute-start(bf16[256,2048]{1,0:T(8,128)(2,1)} %half.2), channel_id=1, source_target_pairs={{0,1},{1,0},{2,3},{3,2},{4,5},{5,4},{6,7},{7,6},{8,9},{9,8},{10,11... | collective-permute-start | bytes 3145736 | tf_op jit(solution)/shard_map/ppermute | solution.py:777
  69.7 24.0 %collective-permute-start.6 = (bf16[256,2048]{1,0:T(8,128)(2,1)}, bf16[256,2048]{1,0:T(8,128)(2,1)S(1)}, u32[]{:S(2)}, u32[]{:S(2)}) collective-permute-start(bf16[256,2048]{1,0:T(8,128)(2,1)} %half.3), channel_id=1, source_target_pairs={{0,2},{1,3},{2,0},{3,1},{4,6},{5,7},{6,4},{7,5},{8,10},{9,11},{10,... | collective-permute-start | bytes 3145736 | tf_op jit(solution)/shard_map/ppermute | solution.py:777
  98.3 101.4 %collective-permute-start.9 = (bf16[512,2048]{1,0:T(8,128)(2,1)}, bf16[512,2048]{1,0:T(8,128)(2,1)S(1)}, u32[]{:S(2)}, u32[]{:S(2)}) collective-permute-start(bf16[512,2048]{1,0:T(8,128)(2,1)} %stack.26.refs_5_.refs_0_), channel_id=1, source_target_pairs={{0,3},{1,2},{2,1},{3,0},{4,7},{5,6},{6,5},{7,4},{8,11},{9,10},{10,... | collective-permute-start | bytes 6291464 | tf_op jit(solution)/shard_map/ppermute | solution.py:777
  100.6 99.2 %collective-permute-start.8 = (bf16[512,2048]{1,0:T(8,128)(2,1)}, bf16[512,2048]{1,0:T(8,128)(2,1)}, u32[]{:S(2)}, u32[]{:S(2)}) collective-permute-start(bf16[512,2048]{1,0:T(8,128)(2,1)} %stack.26.refs_5_.refs_0_), channel_id=1, source_target_pairs={{0,2},{1,3},{2,0},{3,1},{4,6},{5,7},{6,4},{7,5},{8,10},{9,11},{10,... | collective-permute-start | bytes 6291464 | tf_op jit(solution)/shard_map/ppermute | solution.py:777
  101.1 98.7 %collective-permute-start.7 = (bf16[512,2048]{1,0:T(8,128)(2,1)}, bf16[512,2048]{1,0:T(8,128)(2,1)}, u32[]{:S(2)}, u32[]{:S(2)}) collective-permute-start(bf16[512,2048]{1,0:T(8,128)(2,1)} %stack.26.refs_5_.refs_0_), channel_id=1, source_target_pairs={{0,1},{1,0},{2,3},{3,2},{4,5},{5,4},{6,7},{7,6},{8,9},{9,8},{10,11... | collective-permute-start | bytes 6291464 | tf_op jit(solution)/shard_map/ppermute | solution.py:777
  232.7 245.4 %reduce-scatter.6.cloned.1.call-start = ((), (), s32[]{:S(2)}) async-start(), calls=%async_computation.6 | async-start | bytes 9437184 | tf_op jit(solution)/shard_map/reduce_scatter | solution.py:883
  278.9 145.3 %collective-permute-start.10 = (bf16[512,2048]{1,0:T(8,128)(2,1)}, bf16[512,2048]{1,0:T(8,128)(2,1)}, u32[]{:S(2)}, u32[]{:S(2)}) collective-permute-start(bf16[512,2048]{1,0:T(8,128)(2,1)} %get-tuple-element.50), channel_id=1, source_target_pairs={{0,3},{1,2},{2,1},{3,0},{4,7},{5,6},{6,5},{7,4},{8,11},{9,10},{10,... | collective-permute-start | bytes 6291464 | tf_op jit(solution)/shard_map/ppermute | solution.py:777
  281.3 143.5 %collective-permute-start.11 = (bf16[512,2048]{1,0:T(8,128)(2,1)}, bf16[512,2048]{1,0:T(8,128)(2,1)}, u32[]{:S(2)}, u32[]{:S(2)}) collective-permute-start(bf16[512,2048]{1,0:T(8,128)(2,1)} %get-tuple-element.51), channel_id=1, source_target_pairs={{0,2},{1,3},{2,0},{3,1},{4,6},{5,7},{6,4},{7,5},{8,10},{9,11},{10,... | collective-permute-start | bytes 6291464 | tf_op jit(solution)/shard_map/ppermute | solution.py:777
  281.8 145.3 %collective-permute-start.12 = (bf16[512,2048]{1,0:T(8,128)(2,1)}, bf16[512,2048]{1,0:T(8,128)(2,1)}, u32[]{:S(2)}, u32[]{:S(2)}) collective-permute-start(bf16[512,2048]{1,0:T(8,128)(2,1)} %get-tuple-element.52), channel_id=1, source_target_pairs={{0,1},{1,0},{2,3},{3,2},{4,5},{5,4},{6,7},{7,6},{8,9},{9,8},{10,11... | collective-permute-start | bytes 6291464 | tf_op jit(solution)/shard_map/ppermute | solution.py:777
  334.2 194.4 %reduce-scatter.8.cloned.1.call-start = ((), (), s32[]{:S(2)}) async-start(), calls=%async_computation.7 | async-start | bytes 10027008 | tf_op jit(solution)/shard_map/reduce_scatter | solution.py:918
  407.2 26.4 %collective-permute-start.15 = (f32[8,2048]{1,0:T(8,128)}, f32[8,2048]{1,0:T(8,128)}, u32[]{:S(2)}, u32[]{:S(2)}) collective-permute-start(f32[8,2048]{1,0:T(8,128)} %sums.1.refs_5_.refs_0_), channel_id=1, source_target_pairs={{0,1},{1,0},{2,3},{3,2},{4,5},{5,4},{6,7},{7,6},{8,9},{9,8},{10,11... | collective-permute-start | bytes 196616 | tf_op jit(solution)/shard_map/ppermute | solution.py:777
  408.6 25.0 %collective-permute-start.14 = (f32[8,2048]{1,0:T(8,128)}, f32[8,2048]{1,0:T(8,128)}, u32[]{:S(2)}, u32[]{:S(2)}) collective-permute-start(f32[8,2048]{1,0:T(8,128)} %sums.1.refs_5_.refs_0_), channel_id=1, source_target_pairs={{0,2},{1,3},{2,0},{3,1},{4,6},{5,7},{6,4},{7,5},{8,10},{9,11},{10,... | collective-permute-start | bytes 196616 | tf_op jit(solution)/shard_map/ppermute | solution.py:777
  424.2 9.5 %collective-permute-start.13 = (f32[8,2048]{1,0:T(8,128)}, f32[8,2048]{1,0:T(8,128)}, u32[]{:S(2)}, u32[]{:S(2)}) collective-permute-start(f32[8,2048]{1,0:T(8,128)} %sums.1.refs_5_.refs_0_), channel_id=1, source_target_pairs={{0,3},{1,2},{2,1},{3,0},{4,7},{5,6},{6,5},{7,4},{8,11},{9,10},{10,... | collective-permute-start | bytes 196616 | tf_op jit(solution)/shard_map/ppermute | solution.py:777
  424.7 56.7 %collective-permute-start.18 = (bf16[512,2048]{1,0:T(8,128)(2,1)}, bf16[512,2048]{1,0:T(8,128)(2,1)}, u32[]{:S(2)}, u32[]{:S(2)}) collective-permute-start(bf16[512,2048]{1,0:T(8,128)(2,1)} %back.3.refs_6_), channel_id=1, source_target_pairs={{0,3},{1,2},{2,1},{3,0},{4,7},{5,6},{6,5},{7,4},{8,11},{9,10},{10,... | collective-permute-start | bytes 6291464 | tf_op jit(solution)/shard_map/ppermute | solution.py:777
  462.7 55.3 %collective-permute-start.16 = (bf16[512,2048]{1,0:T(8,128)(2,1)}, bf16[512,2048]{1,0:T(8,128)(2,1)S(1)}, u32[]{:S(2)}, u32[]{:S(2)}) collective-permute-start(bf16[512,2048]{1,0:T(8,128)(2,1)} %get-tuple-element.67), channel_id=1, source_target_pairs={{0,2},{1,3},{2,0},{3,1},{4,6},{5,7},{6,4},{7,5},{8,10},{9,11},{10,... | collective-permute-start | bytes 6291464 | tf_op jit(solution)/shard_map/ppermute | solution.py:777
  463.1 54.9 %collective-permute-start.17 = (bf16[512,2048]{1,0:T(8,128)(2,1)}, bf16[512,2048]{1,0:T(8,128)(2,1)}, u32[]{:S(2)}, u32[]{:S(2)}) collective-permute-start(bf16[512,2048]{1,0:T(8,128)(2,1)} %get-tuple-element.68.refs_5_), channel_id=1, source_target_pairs={{0,1},{1,0},{2,3},{3,2},{4,5},{5,4},{6,7},{7,6},{8,9},{9,8},{10,11... | collective-permute-start | bytes 6291464 | tf_op jit(solution)/shard_map/ppermute | solution.py:777
  (26 other events, 132.3 us)
Sparse Core Ops, SparseCore 0:
  10.2 138.0 all-gather.2
  150.5 98.0 all-gather.4
  250.8 87.7 reduce-scatter.3
  340.8 87.9 reduce-scatter.5
  436.8 91.7 reduce-scatter.7

commit v6 on v5

--- a/solution.py
+++ b/solution.py
@@ -10,6 +10,7 @@
 LENGTH = 2048
 EPSILON = 1e-05
 BIG = -1e30
+SUMS = 7
 F32 = jnp.float32
 BF16 = jnp.bfloat16
 DIMS = {
@@ -111,7 +112,8 @@
     )
 
 
-def rotate(block, cos, sin_low, sin_high, sign):
+def rotate(block, table, sign):
+    cos, sin_low, sin_high = table[:, :128], table[:, 128:256], table[:, 256:]
     lead = block[:, :128]
     turned = (
         lead * cos
@@ -120,41 +122,37 @@
     return jnp.concatenate([turned, block[:, 128:]], axis=1)
 
 
-def mixed_kernel(ids, first, weight, place, bias, tables, start, count, blocks, kept=(), after=(), lag=0.05):
+def mixed_kernel(ids, first, weight, place, bias, tables, blocks, after=(), lag=0.05):
     rows, depth = first.shape
     heads = bias.shape[1] // (3 * HEAD_DIM)
     unit = rows // blocks
     wide = 3 * HEAD_DIM
 
-    def kernel(ids_ref, a_ref, *refs):
-        b_ref, cos, low, high, out_ref = refs[3:]
+    def kernel(ids_ref, a_ref, w_ref, b_ref, low_ref, high_ref, out_ref):
         for part in range(3):
             here = slice(part * HEAD_DIM, (part + 1) * HEAD_DIM)
-            value = product(a_ref[...], refs[part][...], "NN") + b_ref[:, here]
+            value = product(a_ref[...], w_ref[:, here], "NN") + b_ref[:, here]
             if part < 2:
-                value = rotate(value, cos[...], low[...], high[...], 1.0)
+                value = rotate(value, jnp.concatenate([low_ref[...], high_ref[...]], axis=0), 1.0)
             out_ref[:, here] = value.astype(BF16)
 
-    table = pl.BlockSpec((unit, 128), lambda j, i, ids: (ids[0] ^ (start + i), 0))
-    return call(
-        kernel,
-        ids,
-        (heads, count),
+    def table(block):
+        return pl.BlockSpec((unit, 3 * 128), lambda j, i, ids: (ids[0] ^ (2 * i + block), 0))
+
+    return call(
+        kernel,
+        ids,
+        (heads, blocks // 2),
         [
-            pl.BlockSpec((unit, depth), lambda j, i, ids: (start + i, 0)),
-            *[
-                pl.BlockSpec((depth, HEAD_DIM), lambda j, i, ids, part=part: (0, place // HEAD_DIM + 3 * j + part))
-                for part in range(3)
-            ],
+            pl.BlockSpec((2 * unit, depth), lambda j, i, ids: (i, 0)),
+            pl.BlockSpec((pl.Element(depth), pl.Element(wide)), lambda j, i, ids: (0, pl.multiple_of(place + wide * j, 128))),
             pl.BlockSpec((1, wide), lambda j, i, ids: (0, j)),
-            table,
-            table,
-            table,
-        ],
-        [pl.BlockSpec((unit, wide), lambda j, i, ids: (start + i, j))],
-        [jax.ShapeDtypeStruct((rows, heads * wide), BF16)],
-        (first, weight, weight, weight, bias, *tables),
-        kept=kept,
+            table(0),
+            table(1),
+        ],
+        pl.BlockSpec((2 * unit, wide), lambda j, i, ids: (i, j)),
+        jax.ShapeDtypeStruct((rows, heads * wide), BF16),
+        (first, weight, bias, tables, tables),
         after=after,
         lag=lag,
         name="mixed",
@@ -238,7 +236,7 @@
     unit = rows // blocks
     scale = HEAD_DIM ** (-0.5)
 
-    def kernel(ids_ref, x_ref, g_ref, c_ref, lse_ref, cos, low, high, out_ref, sum_ref, dk_s, dv_s):
+    def kernel(ids_ref, x_ref, g_ref, c_ref, lse_ref, t_ref, out_ref, sum_ref, dk_s, dv_s):
         me = ids_ref[0]
 
         def place(block):
@@ -274,8 +272,8 @@
                     done = (dkey, dvalue)
                 made = product(dscore, key, "TN")
                 dquery = made if dquery is None else dquery + made
-            dquery = rotate(dquery * scale, cos[...], low[...], high[...], -1.0)
-            dkey = rotate(done[0], cos[...], low[...], high[...], -1.0)
+            dquery = rotate(dquery * scale, t_ref[...], -1.0)
+            dkey = rotate(done[0], t_ref[...], -1.0)
             for part, value in enumerate((dquery, dkey, done[1])):
                 cols = slice(at + part * HEAD_DIM, at + (part + 1) * HEAD_DIM)
                 rounded = value.astype(BF16)
@@ -295,7 +293,7 @@
     def whole(cols):
         return pl.BlockSpec((rows, cols), lambda b, ids: (0, 0))
 
-    table = pl.BlockSpec((unit, 128), lambda b, ids: (blocks - 1 - b, 0))
+    table = pl.BlockSpec((unit, 3 * 128), lambda b, ids: (blocks - 1 - b, 0))
     return call(
         kernel,
         ids,
@@ -306,15 +304,13 @@
             whole(heads * HEAD_DIM),
             pl.BlockSpec((heads, 1, 8, unit), lambda b, ids: (0, blocks - 1 - b, 0, 0)),
             table,
-            table,
-            table,
         ],
         [
             pl.BlockSpec((unit, width), lambda b, ids: (ids[0] ^ (blocks - 1 - b), 0)),
             pl.BlockSpec((1, width), lambda b, ids: (0, 0)),
         ],
         [jax.ShapeDtypeStruct((rows, width), BF16), jax.ShapeDtypeStruct((1, width), F32)],
-        (mixed, grad, context, lse, *tables),
+        (mixed, grad, context, lse, tables),
         scratch=[
             pltpu.VMEM((heads, blocks, unit, HEAD_DIM), F32),
             pltpu.VMEM((heads, blocks, unit, HEAD_DIM), F32),
@@ -472,24 +468,25 @@
     unit = tile_of(wide, 512)
 
     def kernel(ids_ref, a_ref, m_ref, h_ref, s_ref, *out_refs):
-        for block, out_ref in enumerate(out_refs):
-
-            @pl.when(pl.program_id(1) == block)
-            def _(out_ref=out_ref):
+        for block in range(0, blocks, 2):
+
+            @pl.when(pl.program_id(1) == block // 2)
+            def _(block=block):
                 for part in range(wide // unit):
                     here = slice(part * unit, (part + 1) * unit)
                     value = product(h_ref[...], s_ref[:, here], "NN")
                     value = value + product(a_ref[...], m_ref[:, here], "NN")
-                    out_ref[:, here] = value.astype(BF16)
-
-    return call(
-        kernel,
-        ids,
-        (depth // wide, blocks),
+                    out_refs[block][:, here] = value[:tall].astype(BF16)
+                    out_refs[block + 1][:, here] = value[tall:].astype(BF16)
+
+    return call(
+        kernel,
+        ids,
+        (depth // wide, blocks // 2),
         [
-            pl.BlockSpec((tall, deep_a), lambda j, i, ids: (i, 0)),
+            pl.BlockSpec((2 * tall, deep_a), lambda j, i, ids: (i, 0)),
             pl.BlockSpec((deep_a, wide), lambda j, i, ids: (deep_b // deep_a, j)),
-            pl.BlockSpec((tall, deep_b), lambda j, i, ids: (i, 0)),
+            pl.BlockSpec((2 * tall, deep_b), lambda j, i, ids: (i, 0)),
             pl.BlockSpec((deep_b, wide), lambda j, i, ids: (0, j)),
         ],
         [pl.BlockSpec((tall, wide), lambda j, i, ids: (0, j))] * blocks,
@@ -505,7 +502,7 @@
     rows = left_a.shape[0] // blocks
     width = right.shape[0]
     deep_a, deep_b = left_a.shape[1], left_b.shape[1]
-    wide = tile_of(width, 512)
+    wide = tile_of(width, 512 if count == 1 else 1024)
     unit = tile_of(wide, 512)
 
     def kernel(ids_ref, a_ref, b_ref, c_ref, d_ref, s_ref, *out_refs):
@@ -539,10 +536,49 @@
     )
 
 
+def piece_grad_kernel(ids, left, pieces, after=(), lag=0.05):
+    rows, width = left.shape
+    unit, depth = pieces[0].shape
+    tall, wide = tile_of(width, 1024), tile_of(depth, 1024)
+    cut = tile_of(wide, 512)
+
+    def kernel(ids_ref, a_ref, *refs):
+        grad_ref, right_ref = refs[len(pieces) :]
+        for part in range(wide // cut):
+            here = slice(part * cut, (part + 1) * cut)
+            total = None
+            for number in range(len(pieces)):
+                made = product(a_ref[number * unit : (number + 1) * unit, :], refs[number][:, here], "TN")
+                total = made if total is None else total + made
+            grad_ref[:, here] = total.astype(BF16)
+
+        @pl.when(pl.program_id(1) == 0)
+        def _():
+            for number in range(len(pieces)):
+                right_ref[number * unit : (number + 1) * unit, :] = refs[number][...]
+
+    return call(
+        kernel,
+        ids,
+        (depth // wide, width // tall),
+        [pl.BlockSpec((rows, tall), lambda j, i, ids: (0, i))]
+        + [pl.BlockSpec((unit, wide), lambda j, i, ids: (0, j))] * len(pieces),
+        [
+            pl.BlockSpec((tall, wide), lambda j, i, ids: (i, j)),
+            pl.BlockSpec((rows, wide), lambda j, i, ids: (0, j)),
+        ],
+        [jax.ShapeDtypeStruct((width, depth), BF16), jax.ShapeDtypeStruct((rows, depth), BF16)],
+        (left, *pieces),
+        after=after,
+        lag=lag,
+        name="piece_grad",
+    )
+
+
 def full_grad_kernel(ids, left, right, weight=None, total=None, place=0, spare=0, start=0, span=0, kept=(), after=(), lag=0.05):
     rows, depth = left.shape
     width = right.shape[1]
-    tall, wide = tile_of(depth, 1024), tile_of(width, 512 if span else 1024)
+    tall, wide = (tile_of(depth, 512), width) if span else (tile_of(depth, 1024), tile_of(width, 1024))
     unit = tile_of(wide, 512)
     summed = weight is not None
 
@@ -576,7 +612,7 @@
     if summed:
         args += (weight, total)
         in_specs += [
-            pl.BlockSpec((tall, wide), lambda i, j, ids: (i, place // wide + j)),
+            pl.BlockSpec((pl.Element(tall), pl.Element(wide)), lambda i, j, ids: (i * tall, pl.multiple_of(place + j * wide, 128))),
             pl.BlockSpec((1, wide), lambda i, j, ids: (0, j)),
         ]
         out_specs += [pl.BlockSpec((tall, 128), lambda i, j, ids: (i, 0))] * 2
@@ -601,11 +637,14 @@
     count = len(wide)
 
     def kernel(ids_ref, *refs):
-        lane = lax.broadcasted_iota(jnp.int32, (depth, 128), 1)
-        value = jnp.zeros((depth, 128), F32)
+        total = refs[count][...]
         for number, ref in enumerate(refs[:count]):
-            value = jnp.where(lane == number, jnp.sum(ref[...], axis=1, keepdims=True), value)
-        refs[-1][...] = refs[count][...] + jnp.transpose(value)[:8]
+            row = lax.broadcasted_iota(jnp.int32, (8, 128), 0)
+            pick = jnp.where(row == number, 1.0, 0.0).astype(BF16)
+            high = ref[...].astype(BF16)
+            rest = (ref[...] - high.astype(F32)).astype(BF16)
+            total = total + product(pick, high, "NT") + product(pick, rest, "NT")
+        refs[-1][...] = total
 
     def whole(shape):
         return pl.BlockSpec(shape, lambda i, ids: (0, 0))
@@ -624,18 +663,22 @@
     )
 
 
-def spare_kernel(ids, kept, parts, after=(), lag=0.05):
+def spare_kernel(ids, kept, parts, slots, after=(), lag=0.05):
     depth = kept.shape[0]
 
     def kernel(ids_ref, *refs):
         total = refs[0][...]
         for ref in refs[1:-1]:
             total = total + ref[...]
-        value = jnp.transpose(jnp.concatenate([total, jnp.zeros((120, depth), F32)], axis=0))
-        lane = lax.broadcasted_iota(jnp.int32, (depth, 128), 1)
-        rounded = value.astype(BF16).astype(F32)
-        rest = pltpu.roll(value - rounded, 64, 1)
-        refs[-1][...] = jnp.where(lane < 64, rounded, rest).astype(BF16)
+        rounded = total.astype(BF16).astype(F32)
+        row = lax.broadcasted_iota(jnp.int32, (128, depth), 0)
+        value = jnp.zeros((128, depth), F32)
+        for number in range(SUMS):
+            place = number * slots + ids_ref[1]
+            value = jnp.where(row == place, rounded[number : number + 1], value)
+            if SUMS * slots <= 64:
+                value = jnp.where(row == place + 64, (total - rounded)[number : number + 1], value)
+        refs[-1][...] = jnp.transpose(value).astype(BF16)
 
     return call(
         kernel,
@@ -700,6 +743,40 @@
         after=after,
         lag=lag,
         name="widen",
+    )
+
+
+def finish_kernel(ids, rows, widths, heads, slots, after=(), lag=0.05):
+    count = rows.shape[0]
+    one, two = widths
+    each = one // heads
+
+    def kernel(ids_ref, in_ref, one_ref, two_ref, sums_ref):
+        for head in range(heads):
+            one_ref[:, head, :] = in_ref[:, head * each : (head + 1) * each].astype(F32)
+        two_ref[...] = jnp.transpose(in_ref[:, one : one + two].astype(F32))
+        number = lax.broadcasted_iota(jnp.int32, (8, 128), 0)
+        lane = lax.broadcasted_iota(jnp.int32, (8, 128), 1)
+        if SUMS * slots <= 64:
+            lane = lane % 64
+        mine = (lane // slots == number) & (number < SUMS)
+        sums_ref[...] = product(jnp.where(mine, 1.0, 0.0).astype(BF16), in_ref[:, one + two :], "NT")
+
+    def whole(shape):
+        return pl.BlockSpec(shape, lambda i, ids: (0,) * len(shape))
+
+    shapes = [(count, heads, each), (two, count), (8, count)]
+    return call(
+        kernel,
+        ids,
+        (1,),
+        [whole(rows.shape)],
+        [whole(shape) for shape in shapes],
+        [jax.ShapeDtypeStruct(shape, F32) for shape in shapes],
+        (rows,),
+        after=after,
+        lag=lag,
+        name="finish",
     )
 
 
@@ -766,11 +843,12 @@
     frequency = 10000.0 ** (-2.0 * (lane % half).astype(F32) / ROTARY)
     angles = position * frequency[None, :]
     sine = jnp.sin(angles)
-    return (
+    tables = (
         jnp.where(lane < ROTARY, jnp.cos(angles), 1.0),
         jnp.where(lane < half, -sine, 0.0),
         jnp.where((lane >= half) & (lane < ROTARY), sine, 0.0),
     )
+    return jnp.concatenate(tables, axis=1)
 
 
 def flip(value, axis, bit, size):
@@ -833,9 +911,8 @@
 ):
     n_dp, n_tensor = lax.axis_size("dp"), lax.axis_size("tensor")
     dp_at, tensor_at = lax.axis_index("dp"), lax.axis_index("tensor")
-    chip, core = dp_at // 2, dp_at % 2
-    bits = [(chip >> bit) & 1 for bit in range((n_dp // 2).bit_length() - 1)]
-    ids = jnp.stack([tensor_at, core, *bits]).astype(jnp.int32)
+    assert SUMS * n_dp <= 128
+    ids = jnp.stack([tensor_at, dp_at]).astype(jnp.int32)
     own_count, width = layer_input.shape
     group_count = own_count * n_tensor
     assert group_count == LENGTH
@@ -862,18 +939,15 @@
     w_out = lax.all_gather(jnp.concatenate([shrink, merging], axis=0), "dp", axis=1, tiled=True)
 
     unit = own_count
-    rows_pieces = gather_rows(ids, layer_input, n_tensor, (vectors, tables[0]))
+    rows_pieces = gather_rows(ids, layer_input, n_tensor, (vectors, tables))
     near, far = (rows_pieces[:-1], rows_pieces[-1:]) if n_tensor != 4 else (rows_pieces[:3], rows_pieces[3:])
     pair = norm_kernel(ids, near, vectors, unit, 0, n_tensor)
     later = stack_kernel(ids, [cotangent], unit, after=(pair[0], *far))
     seed_pieces = [later] + [flip(later, "tensor", k, n_tensor) for k in range(n_tensor - 1, 0, -1)]
     first, second = norm_kernel(ids, far, vectors, unit, n_tensor - 1, n_tensor, kept=pair, after=(later,))
     hidden, slope = expand_kernel(ids, second, w_in, b_expand)
-    (mixed,) = mixed_kernel(
-        ids, first, w_in, hidden_width, b_project, tables, 0, n_tensor, n_tensor, after=(hidden,)
-    )
-    seed = stack_kernel(ids, seed_pieces[:1] + seed_pieces[:0:-1], unit, after=(mixed,))
-    (shrink_part,) = full_grad_kernel(ids, hidden, seed)
+    mixed = mixed_kernel(ids, first, w_in, hidden_width, b_project, tables, n_tensor, after=(hidden,))
+    shrink_part, seed = piece_grad_kernel(ids, hidden, seed_pieces[:1] + seed_pieces[:0:-1], after=(mixed,))
     shrink_grad = lax.psum_scatter(shrink_part, "dp", scatter_dimension=1, tiled=True)
     context, lse = attend_kernel(ids, mixed, n_tensor, after=(shrink_part,))
     branches = branches_kernel(ids, context, hidden, w_out, n_tensor)
@@ -889,14 +963,13 @@
     project_part, gain_one, bias_one = full_grad_kernel(
         ids, first, mgrad, w_in, mixed_sum, place=hidden_width, span=joint, kept=(part,)
     )
-    (shrink_grad,) = widen_kernel(ids, shrink_grad, [shrink.shape[1]], after=(project_part,))
 
     def slots(values):
         return jnp.pad(values, ((0, 0), (0, depth - values.shape[1]))).reshape(1, width)
 
     seed_sum = jnp.sum(cotangent.astype(F32), axis=0, keepdims=True)
     over_all = jnp.pad(seed_sum, ((4, 3), (0, 0)))
-    over_all = sums_kernel(ids, [gain_one, bias_one, gain_two, bias_two], over_all, after=(shrink_grad,))
+    over_all = sums_kernel(ids, [gain_one, bias_one, gain_two, bias_two], over_all)
     over_dp = [
         slots(expand_sum.reshape(n_dp, -1)),
         slots(jnp.transpose(mixed_sum.reshape(heads, n_dp, -1), (1, 0, 2)).reshape(n_dp, -1)),
@@ -914,15 +987,16 @@
         last = made[0]
         if len(back) == 1:
             layer_output = output_kernel(ids, layer_input, summed, vectors, after=(last,), lag=160)
-            last = spare_kernel(ids, project_part, over_tensor + [over_dp], after=(layer_output,))
+            last = spare_kernel(ids, project_part, over_tensor + [over_dp], n_dp, after=(layer_output,))
             project_grad = lax.psum_scatter(last, "dp", scatter_dimension=0, tiled=True)
+            (shrink_grad,) = widen_kernel(ids, shrink_grad, [shrink.shape[1]], after=(last,), lag=0.05)
+            last = shrink_grad
     (expand_grad,) = widen_kernel(ids, expand_grad, [hidden_width], after=(last,))
     far = total_kernel(ids, back[0] + back[2], after=(expand_grad,), lag=8)
     input_grad = input_kernel(ids, layer_input, cotangent, back[1] + [far], lag=162)
-    project_grad, merging_grad, sums = widen_kernel(
-        ids, project_grad, [mixed_width, merge_width, 128], after=(input_grad,)
-    )
-    sums = jnp.transpose(sums[:, :7] + sums[:, 64:71])
+    project_grad, merging_grad, sums = finish_kernel(
+        ids, project_grad, [mixed_width, merge_width], heads, n_dp, after=(input_grad,)
+    )
     gain_one, bias_one, gain_two, bias_two, seed_sum = sums[:5]
     gain_one = (gain_one - firstbias.astype(F32) * bias_one) / firstgain.astype(F32)
     gain_two = (gain_two - secondbias.astype(F32) * bias_two) / secondgain.astype(F32)
@@ -935,9 +1009,9 @@
         bias_one,
         gain_two,
         bias_two,
-        project_grad.reshape(project.shape),
+        project_grad,
         projbias_grad,
-        jnp.transpose(merging_grad),
+        merging_grad,
         seed_sum,
         expand_grad,
         expandbias_grad,

time: 556 us -> 546 us (0.982)
  Pallas kernels: 359 us -> 347 us
  waiting for transfers between devices: 116 us -> 124 us
    pallas_call x27 -> x26, Pallas kernels: 359 us -> 347 us  [call(): pl.pallas_call(run, grid_spec=pltpu.PrefetchScalarGridSpec(num_scalar_pre...]
    all_gather x1, waiting for transfers between devices: 1.03 us -> 8.49 us  [body(): lax.all_gather(jnp.concatenate([shrink, merging], axis=0), 'dp', axis=1,...]
    unnamed x70 -> x69, local copies, waits for them, and re-layouts: 13.7 us -> 11.6 us
  transfers between devices with their start and end apart: 24 -> 24, of which waited for: 9 -> 9; matrix products, arithmetic and copies ran while one was open for 3% -> 3% of each run, Pallas kernels for 65% -> 64%
where the time goes in v6:
time: 546 us; the launch traced here: 539 us
  Pallas kernels  347 us (64%)
  waiting for transfers between devices  124 us (23%)
  starting transfers between devices  25.3 us (5%)
  local copies, waits for them, and re-layouts  16.3 us (3%)
  between operations  14.5 us (3%)
  other arithmetic  12 us (2%)
    pallas_call x26, Pallas kernels, call(): pl.pallas_call(run, grid_spec=pltpu.PrefetchScalarGridSpec(num_scalar_pre...  347 us
    ppermute x19, waiting for transfers between devices, flip(): return lax.ppermute(value, axis, [(i, i ^ bit) for i in range(size)])  74.3 us
    all_gather x1, waiting for transfers between devices, body(): lax.all_gather(jnp.concatenate([expand, own_project], axis=1), 'dp', axis...  38.8 us
    ppermute x19, starting transfers between devices, flip(): return lax.ppermute(value, axis, [(i, i ^ bit) for i in range(size)])  25.1 us
    unnamed x69, local copies, waits for them, and re-layouts  11.6 us
  transfers between devices with their start and end apart: 24, of which 9 were waited for; matrix products, arithmetic and copies ran while one was open for 3% of the time, Pallas kernels for 64%

profile of v6, /device:TPU:0, one launch (start us, length us, event | category | flops | bytes accessed | tf_op | source)
XLA Modules:
  0.0 539.2 jit_solution(14237237106378648087)
XLA Ops:
  35.1 27.1 %collective-permute-done.3.refs_0_.refs_2_ = bf16[512,2048]{1,0:T(8,128)(2,1)} collective-permute-done((bf16[512,2048]{1,0:T(8,128)(2,1)}, bf16[512,2048]{1,0:T(8,128)(2,1)}, u32[]{:S(2)}, u32[]{:S(2)}) %collective-permute-start.3) | collective-permute-done | bytes 2097184 | tf_op jit(solution)/shard_map/ppermute | solution.py:855
  71.4 11.9 %norm.2 = (bf16[2048,2048]{1,0:T(8,128)(2,1)}, bf16[2048,2048]{1,0:T(8,128)(2,1)}) custom-call(s32[2]{0:T(128)} %pad_add_fusion.ids_ref, bf16[512,2048]{1,0:T(8,128)(2,1)} %refs_0_.7, bf16[512,2048]{1,0:T(8,128)(2,1)} %copy-done, bf16[512,2048]{1,0:T(8,128)(2,1)} %collective-permute-done.3.refs_0_.refs_2_, f32[6,2048]{1,0:T(8,128)} %bitcast.35), custom_call_target="tpu_custom_call" | custom-call | flops 50000000 | tf_op jit(solution)/shard_map/norm/pallas_call | solution.py:50
  83.4 5.6 %collective-permute-done.4.refs_2_.refs_0_ = bf16[256,2048]{1,0:T(8,128)(2,1)S(1)} collective-permute-done((bf16[256,2048]{1,0:T(8,128)(2,1)}, bf16[256,2048]{1,0:T(8,128)(2,1)S(1)}, u32[]{:S(2)}, u32[]{:S(2)}) %collective-permute-start.4) | collective-permute-done | bytes 1048608 | tf_op jit(solution)/shard_map/ppermute | solution.py:855
  89.0 4.7 collective-permute-done.6.refs_3_.refs_1_
  103.3 6.2 %norm.3 = (bf16[2048,2048]{1,0:T(8,128)(2,1)}, bf16[2048,2048]{1,0:T(8,128)(2,1)}) custom-call(s32[2]{0:T(128)} %pad_add_fusion.ids_ref, bf16[256,2048]{1,0:T(8,128)(2,1)} %copy-done.2, bf16[256,2048]{1,0:T(8,128)(2,1)} %copy-done.3, f32[6,2048]{1,0:T(8,128)} %bitcast.36, ...), custom_call_target="tpu_custom_call", output_to_operand_aliasing={{0}: (4, {}), {1}: (5, {})} | custom-call | flops 50000000 | tf_op jit(solution)/shard_map/norm/pallas_call | solution.py:50
  109.5 38.8 %all-gather.3.cloned.1.call-done.refs_1_.refs_2_.refs_3_ = bf16[2048,3584]{1,0:T(8,128)(2,1)} async-done(((bf16[256,3584]{1,0:T(8,128)(2,1)}), bf16[2048,3584]{1,0:T(8,128)(2,1)}) %all-gather.3.cloned.1.call-update) | async-done | bytes 14680080 | tf_op jit(solution)/shard_map/all_gather | solution.py:938
  148.3 30.3 %expand.1 = (bf16[2048,2048]{1,0:T(8,128)(2,1)}, bf16[2048,2048]{1,0:T(8,128)(2,1)}) custom-call(s32[2]{0:T(128)} %pad_add_fusion.ids_ref, bf16[2048,2048]{1,0:T(8,128)(2,1)} %get-tuple-element.48.refs_0_, bf16[2048,3584]{1,0:T(8,128)(2,1)} %all-gather.3.cloned.1.call-done.refs_1_.refs_2_.refs_3_, f32[1,2048]{1,0:T(1,128)} %bitcast.42), custom_call_target="tpu_custom_call" | custom-call | flops 50000000 | tf_op jit(solution)/shard_map/expand/pallas_call | solution.py:50
  178.6 20.2 %mixed.1.refs_5_.refs_0_ = bf16[2048,1536]{1,0:T(8,128)(2,1)} custom-call(s32[2]{0:T(128)} %pad_add_fusion.ids_ref, bf16[2048,2048]{1,0:T(8,128)(2,1)} %get-tuple-element.47.refs_0_, bf16[2048,3584]{1,0:T(8,128)(2,1)} %all-gather.3.cloned.1.call-done.refs_1_.refs_2_.refs_3_, f32[1,1536]{1,0:T(1,128)} %reshape.85.refs_2_, ...), custom_call_target="tpu_custom_call" | custom-call | flops 50000000 | tf_op jit(solution)/shard_map/mixed/pallas_call | solution.py:50
  200.1 25.6 %piece_grad.1 = (bf16[2048,2048]{1,0:T(8,128)(2,1)}, bf16[2048,2048]{1,0:T(8,128)(2,1)}) custom-call(s32[2]{0:T(128)} %pad_add_fusion.ids_ref, bf16[2048,2048]{1,0:T(8,128)(2,1)} %get-tuple-element.49.refs_5_.refs_0_.refs_2_, bf16[512,2048]{1,0:T(8,128)(2,1)} %stack.17.refs_5_.refs_1_, bf16[512,2048]{1,0:T(8,128)(2,1)} %collective-permute-done.7.refs_2_, ...), custom_call_target="tpu_custom_call" | custom-call | flops 50000000 | tf_op jit(solution)/shard_map/piece_grad/pallas_call | solution.py:50
  225.8 14.5 %attend.1 = (bf16[2048,512]{1,0:T(8,128)(2,1)}, f32[2,4,8,512]{3,2,1,0:T(8,128)}) custom-call(s32[2]{0:T(128)} %pad_add_fusion.ids_ref, bf16[2048,1536]{1,0:T(8,128)(2,1)} %mixed.1.refs_5_.refs_0_, bf16[2048,2048]{1,0:T(8,128)(2,1)} %get-tuple-element.50.refs_1_), custom_call_target="tpu_custom_call" | custom-call | flops 50000000 | tf_op jit(solution)/shard_map/attend/pallas_call | solution.py:50
  240.3 8.5 %all-gather.5.cloned.1.call-done.refs_1_.refs_3_.refs_2_ = bf16[2560,2048]{1,0:T(8,128)(2,1)} async-done(((bf16[2560,256]{1,0:T(8,128)(2,1)}), bf16[2560,2048]{1,0:T(8,128)(2,1)}) %all-gather.5.cloned.1.call-update) | async-done | bytes 10485776 | tf_op jit(solution)/shard_map/all_gather | solution.py:939
  248.8 29.5 %branches.1 = (bf16[512,2048]{1,0:T(8,128)(2,1)}, bf16[512,2048]{1,0:T(8,128)(2,1)}, bf16[512,2048]{1,0:T(8,128)(2,1)}, bf16[512,2048]{1,0:T(8,128)(2,1)}) custom-call(s32[2]{0:T(128)} %pad_add_fusion.ids_ref, bf16[2048,512]{1,0:T(8,128)(2,1)} %get-tuple-element.51.refs_0_.refs_1_.refs_2_, ...), custom_call_target="tpu_custom_call" | custom-call | flops 50000000 | tf_op jit(solution)/shard_map/branches/pallas_call | solution.py:50
  281.8 25.3 %shrink_back.1 = (bf16[2048,2048]{1,0:T(8,128)(2,1)}, f32[1,2048]{1,0:T(1,128)}) custom-call(s32[2]{0:T(128)} %pad_add_fusion.ids_ref, bf16[2048,2048]{1,0:T(8,128)(2,1)} %get-tuple-element.56.refs_0_, bf16[2560,2048]{1,0:T(8,128)(2,1)} %all-gather.5.cloned.1.call-done.refs_1_.refs_3_.refs_2_, bf16[2048,2048]{1,0:T(8,128)(2,1)} %get-tuple-element.57.refs_2_, ...), custom_call_target="tpu_custom_call" | custom-call | flops 50000000 | tf_op jit(solution)/shard_map/shrink_back/pallas_call | solution.py:50
  307.1 26.7 %full_grad.2 = (bf16[2048,2048]{1,0:T(8,128)(2,1)}, f32[2048,128]{1,0:T(8,128)}, f32[2048,128]{1,0:T(8,128)}) custom-call(s32[2]{0:T(128)} %pad_add_fusion.ids_ref, bf16[2048,2048]{1,0:T(8,128)(2,1)} %get-tuple-element.48.refs_0_, bf16[2048,2048]{1,0:T(8,128)(2,1)} %get-tuple-element.58.refs_1_.refs_2_, ...), custom_call_target="tpu_custom_call" | custom-call | flops 50000000 | tf_op jit(solution)/shard_map/full_grad/pallas_call | solution.py:50
  337.1 15.5 %merge.1 = (bf16[2048,512]{1,0:T(8,128)(2,1)}, bf16[2048,2176]{1,0:T(8,128)(2,1)}) custom-call(s32[2]{0:T(128)} %pad_add_fusion.ids_ref, bf16[2048,2048]{1,0:T(8,128)(2,1)} %get-tuple-element.56.refs_0_, bf16[2048,512]{1,0:T(8,128)(2,1)} %get-tuple-element.51.refs_0_.refs_1_.refs_2_, bf16[2560,2048]{1,0:T(8,128)(2,1)} %all-gather.5.cloned.1.call-done.refs_1_.refs_3_.refs_2_, ...), custom_call_target="tpu_custom_call" | custom-call | flops 50000000 | tf_op jit(solution)/shard_map/merge/pallas_call | solution.py:50
  352.5 22.7 %attend_back.1 = (bf16[2048,1536]{1,0:T(8,128)(2,1)}, f32[1,1536]{1,0:T(1,128)}) custom-call(s32[2]{0:T(128)} %pad_add_fusion.ids_ref, bf16[2048,1536]{1,0:T(8,128)(2,1)} %mixed.1.refs_5_.refs_0_, bf16[2048,512]{1,0:T(8,128)(2,1)} %get-tuple-element.61.refs_1_, bf16[2048,512]{1,0:T(8,128)(2,1)} %get-tuple-element.51.refs_0_.refs_1_.refs_2_, ...), custom_call_target="tpu_custom_call" | custom-call | flops 50000000 | tf_op jit(solution)/shard_map/attend_back/pallas_call | solution.py:50
  375.3 20.2 %full_grad.3 = (bf16[2048,2176]{1,0:T(8,128)(2,1)}, f32[2048,128]{1,0:T(8,128)}, f32[2048,128]{1,0:T(8,128)}) custom-call(s32[2]{0:T(128)} %pad_add_fusion.ids_ref, bf16[2048,2048]{1,0:T(8,128)(2,1)} %get-tuple-element.47.refs_0_, bf16[2048,1536]{1,0:T(8,128)(2,1)} %get-tuple-element.63.refs_1_.refs_0_, ...), custom_call_target="tpu_custom_call", output_to_operand_aliasing={{0}: (5, {})} | custom-call | flops 50000000 | tf_op jit(solution)/shard_map/full_grad/pallas_call | solution.py:50
  395.4 4.8 sums.1.refs_5_.refs_0_
  403.4 14.1 %back.3.refs_6_ = bf16[512,2048]{1,0:T(8,128)(2,1)} custom-call(s32[2]{0:T(128)} %pad_add_fusion.ids_ref, bf16[2048,1536]{1,0:T(8,128)(2,1)} %get-tuple-element.63.refs_1_.refs_0_, bf16[2048,3584]{1,0:T(8,128)(2,1)} %all-gather.3.cloned.1.call-done.refs_1_.refs_2_.refs_3_, bf16[2048,2048]{1,0:T(8,128)(2,1)} %get-tuple-element.58.refs_1_.refs_2_, ...), custom_call_target="tpu_custom_call" | custom-call | flops 50000000 | tf_op jit(solution)/shard_map/back/pallas_call | solution.py:50
  421.1 6.5 %output.1.refs_6_ = bf16[512,2048]{1,0:T(8,128)(2,1)} custom-call(s32[2]{0:T(128)} %pad_add_fusion.ids_ref, bf16[512,2048]{1,0:T(8,128)(2,1)} %refs_0_.7, f32[6,2048]{1,0:T(8,128)} %bitcast.37, bf16[512,2048]{1,0:T(8,128)(2,1)} %get-tuple-element.52.refs_3_.refs_2_, bf16[512,2048]{1,0:T(8,128)(2,1)} %collective-permute-done.10.refs_3_, ...), custom_call_target="tpu_custom_call" | custom-call | flops 160000000000 | tf_op jit(solution)/shard_map/output/pallas_call | solution.py:50
  434.4 23.1 %back.4 = (bf16[512,2048]{1,0:T(8,128)(2,1)}, bf16[512,2048]{1,0:T(8,128)(2,1)}) custom-call(s32[2]{0:T(128)} %pad_add_fusion.ids_ref, bf16[2048,1536]{1,0:T(8,128)(2,1)} %get-tuple-element.63.refs_1_.refs_0_, bf16[2048,3584]{1,0:T(8,128)(2,1)} %all-gather.3.cloned.1.call-done.refs_1_.refs_2_.refs_3_, bf16[2048,2048]{1,0:T(8,128)(2,1)} %get-tuple-element.58.refs_1_.refs_2_, ...), custom_call_target="tpu_custom_call" | custom-call | flops 50000000 | tf_op jit(solution)/shard_map/back/pallas_call | solution.py:50
  459.0 14.0 %back.5.refs_1_ = bf16[512,2048]{1,0:T(8,128)(2,1)} custom-call(s32[2]{0:T(128)} %pad_add_fusion.ids_ref, bf16[2048,1536]{1,0:T(8,128)(2,1)} %get-tuple-element.63.refs_1_.refs_0_, bf16[2048,3584]{1,0:T(8,128)(2,1)} %all-gather.3.cloned.1.call-done.refs_1_.refs_2_.refs_3_, bf16[2048,2048]{1,0:T(8,128)(2,1)} %get-tuple-element.58.refs_1_.refs_2_, ...), custom_call_target="tpu_custom_call" | custom-call | flops 50000000 | tf_op jit(solution)/shard_map/back/pallas_call | solution.py:50
  480.8 31.3 %collective-permute-done.16.refs_2_ = bf16[512,2048]{1,0:T(8,128)(2,1)S(1)} collective-permute-done((bf16[512,2048]{1,0:T(8,128)(2,1)}, bf16[512,2048]{1,0:T(8,128)(2,1)S(1)}, u32[]{:S(2)}, u32[]{:S(2)}) %collective-permute-start.16) | collective-permute-done | bytes 2097184 | tf_op jit(solution)/shard_map/ppermute | solution.py:855
  513.5 8.5 %input.1.refs_1_ = f32[512,2048]{1,0:T(8,128)} custom-call(s32[2]{0:T(128)} %pad_add_fusion.ids_ref, bf16[512,2048]{1,0:T(8,128)(2,1)} %refs_0_.7, bf16[512,2048]{1,0:T(8,128)(2,1)} %refs_1_.1, bf16[512,2048]{1,0:T(8,128)(2,1)} %copy-done.24, bf16[512,2048]{1,0:T(8,128)(2,1)} %collective-permute-done.17.refs_3_, f32[512,2048]{1,0:T(8,128)} %total.1.refs_4_), custom_call_target="tpu_custom_call" | custom-call | flops 161999994880 | tf_op jit(solution)/shard_map/input/pallas_call | solution.py:50
  (158 shorter events, 89.0 us)
Async XLA Ops:
  7.2 141.1 %all-gather.3.cloned.1.call-start = ((), (), s32[]{:S(2)}) async-start(), calls=%async_computation.3 | async-start | bytes 16515072 | tf_op jit(solution)/shard_map/all_gather | solution.py:938
  10.1 238.7 %all-gather.5.cloned.1.call-start = ((), (), s32[]{:S(2)}) async-start(), calls=%async_computation.4 | async-start | bytes 11796480 | tf_op jit(solution)/shard_map/all_gather | solution.py:939
  11.7 419.3 %reduce-scatter.4.cloned.1.call-start = ((), (), s32[]{:S(2)}) async-start(), calls=%async_computation.5 | async-start | bytes 9437184 | tf_op jit(solution)/shard_map/reduce_scatter | solution.py:951
  11.7 53.7 %collective-permute-start.5 = (bf16[512,2048]{1,0:T(8,128)(2,1)}, bf16[512,2048]{1,0:T(8,128)(2,1)S(1)}, u32[]{:S(2)}, u32[]{:S(2)}) collective-permute-start(bf16[512,2048]{1,0:T(8,128)(2,1)} %refs_0_.7), channel_id=1, source_target_pairs={{0,1},{1,0},{2,3},{3,2},{4,5},{5,4},{6,7},{7,6},{8,9},{9,8},{10,11... | collective-permute-start | bytes 6291464 | tf_op jit(solution)/shard_map/ppermute | solution.py:855
  14.7 47.4 %collective-permute-start.3 = (bf16[512,2048]{1,0:T(8,128)(2,1)}, bf16[512,2048]{1,0:T(8,128)(2,1)}, u32[]{:S(2)}, u32[]{:S(2)}) collective-permute-start(bf16[512,2048]{1,0:T(8,128)(2,1)} %refs_0_.7), channel_id=1, source_target_pairs={{0,2},{1,3},{2,0},{3,1},{4,6},{5,7},{6,4},{7,5},{8,10},{9,11},{10,... | collective-permute-start | bytes 6291464 | tf_op jit(solution)/shard_map/ppermute | solution.py:855
  18.1 4.1 collective-permute-start
  22.2 4.4 collective-permute-start.1
  26.7 7.7 %collective-permute-start.2 = (bf16[8,1984]{1,0:T(8,128)(2,1)S(1)}, bf16[8,1984]{1,0:T(8,128)(2,1)S(1)}, u32[]{:S(2)}, u32[]{:S(2)}) collective-permute-start(bf16[8,1984]{1,0:T(8,128)(2,1)S(1)} %fusion.8), channel_id=1, source_target_pairs={{0,16},{4,20},{8,24},{12,28},{16,0},{20,4},{24,8},{28,12},{1,17},{... | collective-permute-start | bytes 95240 | tf_op jit(solution)/shard_map/ppermute | solution.py:855
  65.1 23.9 %collective-permute-start.4 = (bf16[256,2048]{1,0:T(8,128)(2,1)}, bf16[256,2048]{1,0:T(8,128)(2,1)S(1)}, u32[]{:S(2)}, u32[]{:S(2)}) collective-permute-start(bf16[256,2048]{1,0:T(8,128)(2,1)} %half.2), channel_id=1, source_target_pairs={{0,1},{1,0},{2,3},{3,2},{4,5},{5,4},{6,7},{7,6},{8,9},{9,8},{10,11... | collective-permute-start | bytes 3145736 | tf_op jit(solution)/shard_map/ppermute | solution.py:855
  69.8 24.0 %collective-permute-start.6 = (bf16[256,2048]{1,0:T(8,128)(2,1)}, bf16[256,2048]{1,0:T(8,128)(2,1)S(1)}, u32[]{:S(2)}, u32[]{:S(2)}) collective-permute-start(bf16[256,2048]{1,0:T(8,128)(2,1)} %half.3), channel_id=1, source_target_pairs={{0,2},{1,3},{2,0},{3,1},{4,6},{5,7},{6,4},{7,5},{8,10},{9,11},{10,... | collective-permute-start | bytes 3145736 | tf_op jit(solution)/shard_map/ppermute | solution.py:855
  98.4 100.4 %collective-permute-start.9 = (bf16[512,2048]{1,0:T(8,128)(2,1)}, bf16[512,2048]{1,0:T(8,128)(2,1)S(1)}, u32[]{:S(2)}, u32[]{:S(2)}) collective-permute-start(bf16[512,2048]{1,0:T(8,128)(2,1)} %stack.17.refs_5_.refs_1_), channel_id=1, source_target_pairs={{0,3},{1,2},{2,1},{3,0},{4,7},{5,6},{6,5},{7,4},{8,11},{9,10},{10,... | collective-permute-start | bytes 6291464 | tf_op jit(solution)/shard_map/ppermute | solution.py:855
  100.7 98.1 %collective-permute-start.8 = (bf16[512,2048]{1,0:T(8,128)(2,1)}, bf16[512,2048]{1,0:T(8,128)(2,1)}, u32[]{:S(2)}, u32[]{:S(2)}) collective-permute-start(bf16[512,2048]{1,0:T(8,128)(2,1)} %stack.17.refs_5_.refs_1_), channel_id=1, source_target_pairs={{0,2},{1,3},{2,0},{3,1},{4,6},{5,7},{6,4},{7,5},{8,10},{9,11},{10,... | collective-permute-start | bytes 6291464 | tf_op jit(solution)/shard_map/ppermute | solution.py:855
  101.2 97.6 %collective-permute-start.7 = (bf16[512,2048]{1,0:T(8,128)(2,1)}, bf16[512,2048]{1,0:T(8,128)(2,1)}, u32[]{:S(2)}, u32[]{:S(2)}) collective-permute-start(bf16[512,2048]{1,0:T(8,128)(2,1)} %stack.17.refs_5_.refs_1_), channel_id=1, source_target_pairs={{0,1},{1,0},{2,3},{3,2},{4,5},{5,4},{6,7},{7,6},{8,9},{9,8},{10,11... | collective-permute-start | bytes 6291464 | tf_op jit(solution)/shard_map/ppermute | solution.py:855
  225.7 247.3 %reduce-scatter.6.cloned.1.call-start = ((), (), s32[]{:S(2)}) async-start(), calls=%async_computation.6 | async-start | bytes 9437184 | tf_op jit(solution)/shard_map/reduce_scatter | solution.py:957
  278.3 139.9 %collective-permute-start.10 = (bf16[512,2048]{1,0:T(8,128)(2,1)}, bf16[512,2048]{1,0:T(8,128)(2,1)}, u32[]{:S(2)}, u32[]{:S(2)}) collective-permute-start(bf16[512,2048]{1,0:T(8,128)(2,1)} %get-tuple-element.53), channel_id=1, source_target_pairs={{0,3},{1,2},{2,1},{3,0},{4,7},{5,6},{6,5},{7,4},{8,11},{9,10},{10,... | collective-permute-start | bytes 6291464 | tf_op jit(solution)/shard_map/ppermute | solution.py:855
  280.7 138.1 %collective-permute-start.11 = (bf16[512,2048]{1,0:T(8,128)(2,1)}, bf16[512,2048]{1,0:T(8,128)(2,1)}, u32[]{:S(2)}, u32[]{:S(2)}) collective-permute-start(bf16[512,2048]{1,0:T(8,128)(2,1)} %get-tuple-element.54), channel_id=1, source_target_pairs={{0,2},{1,3},{2,0},{3,1},{4,6},{5,7},{6,4},{7,5},{8,10},{9,11},{10,... | collective-permute-start | bytes 6291464 | tf_op jit(solution)/shard_map/ppermute | solution.py:855
  281.2 139.9 %collective-permute-start.12 = (bf16[512,2048]{1,0:T(8,128)(2,1)}, bf16[512,2048]{1,0:T(8,128)(2,1)}, u32[]{:S(2)}, u32[]{:S(2)}) collective-permute-start(bf16[512,2048]{1,0:T(8,128)(2,1)} %get-tuple-element.55), channel_id=1, source_target_pairs={{0,1},{1,0},{2,3},{3,2},{4,5},{5,4},{6,7},{7,6},{8,9},{9,8},{10,11... | collective-permute-start | bytes 6291464 | tf_op jit(solution)/shard_map/ppermute | solution.py:855
  333.9 190.3 %reduce-scatter.8.cloned.1.call-start = ((), (), s32[]{:S(2)}) async-start(), calls=%async_computation.7 | async-start | bytes 10027008 | tf_op jit(solution)/shard_map/reduce_scatter | solution.py:991
  400.2 27.4 %collective-permute-start.15 = (f32[8,2048]{1,0:T(8,128)}, f32[8,2048]{1,0:T(8,128)}, u32[]{:S(2)}, u32[]{:S(2)}) collective-permute-start(f32[8,2048]{1,0:T(8,128)} %sums.1.refs_5_.refs_0_), channel_id=1, source_target_pairs={{0,1},{1,0},{2,3},{3,2},{4,5},{5,4},{6,7},{7,6},{8,9},{9,8},{10,11... | collective-permute-start | bytes 196616 | tf_op jit(solution)/shard_map/ppermute | solution.py:855
  401.7 25.9 %collective-permute-start.14 = (f32[8,2048]{1,0:T(8,128)}, f32[8,2048]{1,0:T(8,128)}, u32[]{:S(2)}, u32[]{:S(2)}) collective-permute-start(f32[8,2048]{1,0:T(8,128)} %sums.1.refs_5_.refs_0_), channel_id=1, source_target_pairs={{0,2},{1,3},{2,0},{3,1},{4,6},{5,7},{6,4},{7,5},{8,10},{9,11},{10,... | collective-permute-start | bytes 196616 | tf_op jit(solution)/shard_map/ppermute | solution.py:855
  418.2 9.5 %collective-permute-start.13 = (f32[8,2048]{1,0:T(8,128)}, f32[8,2048]{1,0:T(8,128)}, u32[]{:S(2)}, u32[]{:S(2)}) collective-permute-start(f32[8,2048]{1,0:T(8,128)} %sums.1.refs_5_.refs_0_), channel_id=1, source_target_pairs={{0,3},{1,2},{2,1},{3,0},{4,7},{5,6},{6,5},{7,4},{8,11},{9,10},{10,... | collective-permute-start | bytes 196616 | tf_op jit(solution)/shard_map/ppermute | solution.py:855
  418.7 57.6 %collective-permute-start.18 = (bf16[512,2048]{1,0:T(8,128)(2,1)}, bf16[512,2048]{1,0:T(8,128)(2,1)}, u32[]{:S(2)}, u32[]{:S(2)}) collective-permute-start(bf16[512,2048]{1,0:T(8,128)(2,1)} %back.3.refs_6_), channel_id=1, source_target_pairs={{0,3},{1,2},{2,1},{3,0},{4,7},{5,6},{6,5},{7,4},{8,11},{9,10},{10,... | collective-permute-start | bytes 6291464 | tf_op jit(solution)/shard_map/ppermute | solution.py:855
  457.4 54.7 %collective-permute-start.16 = (bf16[512,2048]{1,0:T(8,128)(2,1)}, bf16[512,2048]{1,0:T(8,128)(2,1)S(1)}, u32[]{:S(2)}, u32[]{:S(2)}) collective-permute-start(bf16[512,2048]{1,0:T(8,128)(2,1)} %get-tuple-element.71), channel_id=1, source_target_pairs={{0,2},{1,3},{2,0},{3,1},{4,6},{5,7},{6,4},{7,5},{8,10},{9,11},{10,... | collective-permute-start | bytes 6291464 | tf_op jit(solution)/shard_map/ppermute | solution.py:855
  458.4 53.7 %collective-permute-start.17 = (bf16[512,2048]{1,0:T(8,128)(2,1)}, bf16[512,2048]{1,0:T(8,128)(2,1)}, u32[]{:S(2)}, u32[]{:S(2)}) collective-permute-start(bf16[512,2048]{1,0:T(8,128)(2,1)} %get-tuple-element.72.refs_5_), channel_id=1, source_target_pairs={{0,1},{1,0},{2,3},{3,2},{4,5},{5,4},{6,7},{7,6},{8,9},{9,8},{10,11... | collective-permute-start | bytes 6291464 | tf_op jit(solution)/shard_map/ppermute | solution.py:855
  (26 other events, 135.4 us)
Sparse Core Ops, SparseCore 0:
  10.2 137.9 all-gather.2
  150.4 98.3 all-gather.4
  251.1 87.8 reduce-scatter.3
  341.1 87.9 reduce-scatter.5
  431.2 92.9 reduce-scatter.7

commit v7 on v6

--- a/solution.py
+++ b/solution.py
@@ -419,45 +419,27 @@
     )
 
 
-def merge_kernel(ids, seed, context, weight, place, start, span, blocks, after=(), lag=0.05):
-    rows, depth = seed.shape
-    width = context.shape[1]
-    unit = rows // blocks
-
-    def kernel(ids_ref, g_ref, c_ref, w_ref, back_ref, out_ref, acc_s):
-        step = pl.program_id(0)
-        back_ref[...] = product(g_ref[...], w_ref[...], "NT").astype(BF16)
-        made = product(g_ref[...], c_ref[...], "TN")
-
-        @pl.when(step == 0)
-        def _():
-            acc_s[...] = made
-
-        @pl.when((step > 0) & (step < blocks - 1))
-        def _():
-            acc_s[...] += made
-
-        @pl.when(step == blocks - 1)
-        def _():
-            out_ref[...] = (acc_s[...] + made).astype(BF16)
-
-    tile = pl.BlockSpec((unit, width), lambda i, ids: (i, 0))
-    return call(
-        kernel,
-        ids,
-        (blocks,),
+def plain_kernel(ids, left, right, place, width, after=(), lag=0.05):
+    rows, depth = left.shape
+    tall = tile_of(rows, 1024)
+
+    def kernel(ids_ref, a_ref, b_ref, out_ref):
+        out_ref[...] = product(a_ref[...], b_ref[...], "NT").astype(BF16)
+
+    return call(
+        kernel,
+        ids,
+        (rows // tall,),
         [
-            pl.BlockSpec((unit, depth), lambda i, ids: (i, 0)),
-            tile,
+            pl.BlockSpec((tall, depth), lambda i, ids: (i, 0)),
             pl.BlockSpec((width, depth), lambda i, ids: (place // width, 0)),
         ],
-        [tile, pl.BlockSpec((depth, width), lambda i, ids: (0, start // width))],
-        [jax.ShapeDtypeStruct((rows, width), BF16), jax.ShapeDtypeStruct((depth, span), BF16)],
-        (seed, context, weight),
-        scratch=[pltpu.VMEM((depth, width), F32)],
-        after=after,
-        lag=lag,
-        name="merge",
+        pl.BlockSpec((tall, width), lambda i, ids: (i, 0)),
+        jax.ShapeDtypeStruct((rows, width), BF16),
+        (left, right),
+        after=after,
+        lag=lag,
+        name="plain",
     )
 
 
@@ -746,12 +728,12 @@
     )
 
 
-def finish_kernel(ids, rows, widths, heads, slots, after=(), lag=0.05):
+def finish_kernel(ids, rows, widths, heads, slots, scales, last, after=(), lag=0.05):
     count = rows.shape[0]
     one, two = widths
     each = one // heads
 
-    def kernel(ids_ref, in_ref, one_ref, two_ref, sums_ref):
+    def kernel(ids_ref, in_ref, v_ref, one_ref, two_ref, *sum_refs):
         for head in range(heads):
             one_ref[:, head, :] = in_ref[:, head * each : (head + 1) * each].astype(F32)
         two_ref[...] = jnp.transpose(in_ref[:, one : one + two].astype(F32))
@@ -760,20 +742,27 @@
         if SUMS * slots <= 64:
             lane = lane % 64
         mine = (lane // slots == number) & (number < SUMS)
-        sums_ref[...] = product(jnp.where(mine, 1.0, 0.0).astype(BF16), in_ref[:, one + two :], "NT")
+        sums = product(jnp.where(mine, 1.0, 0.0).astype(BF16), in_ref[:, one + two :], "NT")
+        for number, sum_ref in zip((0, 1, 2, 3, 4, 4, 5, 6), sum_refs):
+            value = sums[number : number + 1]
+            if number in (0, 2):
+                value = (value - v_ref[number + 1 : number + 2, :] * sums[number + 1 : number + 2]) / v_ref[number : number + 1, :]
+            wide = sum_ref.shape[1]
+            for row in range(sum_ref.shape[0]):
+                sum_ref[row : row + 1, :] = value[:, row * wide : (row + 1) * wide]
 
     def whole(shape):
         return pl.BlockSpec(shape, lambda i, ids: (0,) * len(shape))
 
-    shapes = [(count, heads, each), (two, count), (8, count)]
+    shapes = [(count, heads, each), (two, count)] + [(1, count)] * 6 + last
     return call(
         kernel,
         ids,
         (1,),
-        [whole(rows.shape)],
+        [whole(rows.shape), whole(scales.shape)],
         [whole(shape) for shape in shapes],
         [jax.ShapeDtypeStruct(shape, F32) for shape in shapes],
-        (rows,),
+        (rows, scales),
         after=after,
         lag=lag,
         name="finish",
@@ -950,18 +939,18 @@
     shrink_part, seed = piece_grad_kernel(ids, hidden, seed_pieces[:1] + seed_pieces[:0:-1], after=(mixed,))
     shrink_grad = lax.psum_scatter(shrink_part, "dp", scatter_dimension=1, tiled=True)
     context, lse = attend_kernel(ids, mixed, n_tensor, after=(shrink_part,))
-    branches = branches_kernel(ids, context, hidden, w_out, n_tensor)
+    merge_width = merging.shape[0]
+    joint = mixed_width + merge_width + 128
+    part = full_grad_kernel(ids, seed, context, start=mixed_width, span=joint)
+    branches = branches_kernel(ids, context, hidden, w_out, n_tensor, after=part)
     summed = [branches[0]] + [flip(branches[k], "tensor", k, n_tensor) for k in range(n_tensor - 1, 0, -1)]
     pgrad, expand_sum = shrink_back_kernel(ids, seed, w_out, slope, after=(branches[0],))
     expand_part, gain_two, bias_two = full_grad_kernel(ids, second, pgrad, w_in, expand_sum)
     expand_grad = lax.psum_scatter(expand_part, "dp", scatter_dimension=0, tiled=True)
-
-    merge_width = merging.shape[0]
-    joint = mixed_width + merge_width + 128
-    cgrad, part = merge_kernel(ids, seed, context, w_out, hidden_width, mixed_width, joint, 2, after=(expand_part,))
+    cgrad = plain_kernel(ids, seed, w_out, hidden_width, merge_width, after=(expand_part,))
     mgrad, mixed_sum = attend_back_kernel(ids, mixed, cgrad, context, lse, tables, n_tensor)
     project_part, gain_one, bias_one = full_grad_kernel(
-        ids, first, mgrad, w_in, mixed_sum, place=hidden_width, span=joint, kept=(part,)
+        ids, first, mgrad, w_in, mixed_sum, place=hidden_width, span=joint, kept=part
     )
 
     def slots(values):
@@ -994,14 +983,12 @@
     (expand_grad,) = widen_kernel(ids, expand_grad, [hidden_width], after=(last,))
     far = total_kernel(ids, back[0] + back[2], after=(expand_grad,), lag=8)
     input_grad = input_kernel(ids, layer_input, cotangent, back[1] + [far], lag=162)
-    project_grad, merging_grad, sums = finish_kernel(
-        ids, project_grad, [mixed_width, merge_width], heads, n_dp, after=(input_grad,)
-    )
-    gain_one, bias_one, gain_two, bias_two, seed_sum = sums[:5]
-    gain_one = (gain_one - firstbias.astype(F32) * bias_one) / firstgain.astype(F32)
-    gain_two = (gain_two - secondbias.astype(F32) * bias_two) / secondgain.astype(F32)
-    expandbias_grad = sums[5, : expandbias.shape[0]]
-    projbias_grad = sums[6, : projbias.size].reshape(projbias.shape)
+    scales = jnp.stack([firstgain, firstbias, secondgain, secondbias]).astype(F32)
+    project_grad, merging_grad, *sums = finish_kernel(
+        ids, project_grad, [mixed_width, merge_width], heads, n_dp, scales, [(1, expandbias.shape[0]), projbias.shape], after=(input_grad,)
+    )
+    projbias_grad = sums.pop()
+    gain_one, bias_one, gain_two, bias_two, seed_sum, seed_sum_again, expandbias_grad = [value[0] for value in sums]
     return (
         layer_output,
         input_grad,
@@ -1016,7 +1003,7 @@
         expand_grad,
         expandbias_grad,
         shrink_grad,
-        seed_sum,
+        seed_sum_again,
     )
 
 

time: 546 us -> 542 us (level)
    all_gather x1, waiting for transfers between devices: 8.49 us -> 0.01 us  [body(): lax.all_gather(jnp.concatenate([shrink, merging], axis=0), 'dp', axis=1,...]
    reduce_scatter x1, waiting for transfers between devices: 2.15 us -> 8.09 us  [body(): project_grad = lax.psum_scatter(last, 'dp', scatter_dimension=0, tiled=True)]
    pallas_call x26 -> x27, Pallas kernels: 347 us -> 350 us  [call(): pl.pallas_call(run, grid_spec=pltpu.PrefetchScalarGridSpec(num_scalar_pre...]
    unnamed x69 -> x62, local copies, waits for them, and re-layouts: 11.6 us -> 11 us
  transfers between devices with their start and end apart: 24 -> 24, of which waited for: 9 -> 8; matrix products, arithmetic and copies ran while one was open for 3% -> 3% of each run, Pallas kernels for 64% -> 65%
where the time goes in v7:
time: 542 us; the launch traced here: 535 us
  Pallas kernels  350 us (65%)
  waiting for transfers between devices  121 us (22%)
  starting transfers between devices  25.3 us (5%)
  between operations  14.5 us (3%)
  local copies, waits for them, and re-layouts  12.9 us (2%)
  other arithmetic  11.5 us (2%)
    pallas_call x27, Pallas kernels, call(): pl.pallas_call(run, grid_spec=pltpu.PrefetchScalarGridSpec(num_scalar_pre...  350 us
    ppermute x19, waiting for transfers between devices, flip(): return lax.ppermute(value, axis, [(i, i ^ bit) for i in range(size)])  73.8 us
    all_gather x1, waiting for transfers between devices, body(): lax.all_gather(jnp.concatenate([expand, own_project], axis=1), 'dp', axis...  38.8 us
    ppermute x19, starting transfers between devices, flip(): return lax.ppermute(value, axis, [(i, i ^ bit) for i in range(size)])  25.1 us
    unnamed x62, local copies, waits for them, and re-layouts  11 us
  transfers between devices with their start and end apart: 24, of which 8 were waited for; matrix products, arithmetic and copies ran while one was open for 3% of the time, Pallas kernels for 65%

profile of v7, /device:TPU:0, one launch (start us, length us, event | category | flops | bytes accessed | tf_op | source)
XLA Modules:
  0.0 534.8 jit_solution(9849715429655974840)
XLA Ops:
  35.1 27.1 %collective-permute-done.3.refs_0_.refs_2_ = bf16[512,2048]{1,0:T(8,128)(2,1)} collective-permute-done((bf16[512,2048]{1,0:T(8,128)(2,1)}, bf16[512,2048]{1,0:T(8,128)(2,1)}, u32[]{:S(2)}, u32[]{:S(2)}) %collective-permute-start.3) | collective-permute-done | bytes 2097184 | tf_op jit(solution)/shard_map/ppermute | solution.py:844
  71.4 11.9 %norm.2 = (bf16[2048,2048]{1,0:T(8,128)(2,1)}, bf16[2048,2048]{1,0:T(8,128)(2,1)}) custom-call(s32[2]{0:T(128)} %pad_add_fusion.ids_ref, bf16[512,2048]{1,0:T(8,128)(2,1)} %refs_0_.7, bf16[512,2048]{1,0:T(8,128)(2,1)} %copy-done, bf16[512,2048]{1,0:T(8,128)(2,1)} %collective-permute-done.3.refs_0_.refs_2_, f32[6,2048]{1,0:T(8,128)} %bitcast.36), custom_call_target="tpu_custom_call" | custom-call | flops 50000000 | tf_op jit(solution)/shard_map/norm/pallas_call | solution.py:50
  83.3 5.7 %collective-permute-done.4.refs_2_.refs_0_ = bf16[256,2048]{1,0:T(8,128)(2,1)S(1)} collective-permute-done((bf16[256,2048]{1,0:T(8,128)(2,1)}, bf16[256,2048]{1,0:T(8,128)(2,1)S(1)}, u32[]{:S(2)}, u32[]{:S(2)}) %collective-permute-start.4) | collective-permute-done | bytes 1048608 | tf_op jit(solution)/shard_map/ppermute | solution.py:844
  103.2 6.3 %norm.3 = (bf16[2048,2048]{1,0:T(8,128)(2,1)}, bf16[2048,2048]{1,0:T(8,128)(2,1)}) custom-call(s32[2]{0:T(128)} %pad_add_fusion.ids_ref, bf16[256,2048]{1,0:T(8,128)(2,1)} %copy-done.2, bf16[256,2048]{1,0:T(8,128)(2,1)} %copy-done.3, f32[6,2048]{1,0:T(8,128)} %bitcast.37, ...), custom_call_target="tpu_custom_call", output_to_operand_aliasing={{0}: (4, {}), {1}: (5, {})} | custom-call | flops 50000000 | tf_op jit(solution)/shard_map/norm/pallas_call | solution.py:50
  109.5 38.8 %all-gather.3.cloned.1.call-done.refs_1_.refs_2_.refs_3_ = bf16[2048,3584]{1,0:T(8,128)(2,1)} async-done(((bf16[256,3584]{1,0:T(8,128)(2,1)}), bf16[2048,3584]{1,0:T(8,128)(2,1)}) %all-gather.3.cloned.1.call-update) | async-done | bytes 14680080 | tf_op jit(solution)/shard_map/all_gather | solution.py:927
  148.3 30.3 %expand.1 = (bf16[2048,2048]{1,0:T(8,128)(2,1)}, bf16[2048,2048]{1,0:T(8,128)(2,1)}) custom-call(s32[2]{0:T(128)} %pad_add_fusion.ids_ref, bf16[2048,2048]{1,0:T(8,128)(2,1)} %get-tuple-element.53.refs_0_, bf16[2048,3584]{1,0:T(8,128)(2,1)} %all-gather.3.cloned.1.call-done.refs_1_.refs_2_.refs_3_, f32[1,2048]{1,0:T(1,128)} %bitcast.43), custom_call_target="tpu_custom_call" | custom-call | flops 50000000 | tf_op jit(solution)/shard_map/expand/pallas_call | solution.py:50
  178.6 20.1 %mixed.1.refs_5_.refs_0_ = bf16[2048,1536]{1,0:T(8,128)(2,1)} custom-call(s32[2]{0:T(128)} %pad_add_fusion.ids_ref, bf16[2048,2048]{1,0:T(8,128)(2,1)} %get-tuple-element.52.refs_0_, bf16[2048,3584]{1,0:T(8,128)(2,1)} %all-gather.3.cloned.1.call-done.refs_1_.refs_2_.refs_3_, f32[1,1536]{1,0:T(1,128)} %reshape.85.refs_2_, ...), custom_call_target="tpu_custom_call" | custom-call | flops 50000000 | tf_op jit(solution)/shard_map/mixed/pallas_call | solution.py:50
  200.0 25.6 %piece_grad.1 = (bf16[2048,2048]{1,0:T(8,128)(2,1)}, bf16[2048,2048]{1,0:T(8,128)(2,1)}) custom-call(s32[2]{0:T(128)} %pad_add_fusion.ids_ref, bf16[2048,2048]{1,0:T(8,128)(2,1)} %get-tuple-element.54.refs_5_.refs_0_.refs_2_, bf16[512,2048]{1,0:T(8,128)(2,1)} %stack.37.refs_5_.refs_1_, bf16[512,2048]{1,0:T(8,128)(2,1)} %collective-permute-done.7.refs_2_, ...), custom_call_target="tpu_custom_call" | custom-call | flops 50000000 | tf_op jit(solution)/shard_map/piece_grad/pallas_call | solution.py:50
  225.7 14.5 %attend.1 = (bf16[2048,512]{1,0:T(8,128)(2,1)}, f32[2,4,8,512]{3,2,1,0:T(8,128)}) custom-call(s32[2]{0:T(128)} %pad_add_fusion.ids_ref, bf16[2048,1536]{1,0:T(8,128)(2,1)} %mixed.1.refs_5_.refs_0_, bf16[2048,2048]{1,0:T(8,128)(2,1)} %get-tuple-element.55.refs_1_), custom_call_target="tpu_custom_call" | custom-call | flops 50000000 | tf_op jit(solution)/shard_map/attend/pallas_call | solution.py:50
  240.2 9.5 %full_grad.3.refs_4_ = bf16[2048,2176]{1,0:T(8,128)(2,1)} custom-call(s32[2]{0:T(128)} %pad_add_fusion.ids_ref, bf16[2048,2048]{1,0:T(8,128)(2,1)} %get-tuple-element.57.refs_0_, bf16[2048,512]{1,0:T(8,128)(2,1)} %get-tuple-element.56.refs_1_.refs_0_.refs_2_), custom_call_target="tpu_custom_call" | custom-call | flops 50000000 | tf_op jit(solution)/shard_map/full_grad/pallas_call | solution.py:50
  249.7 29.6 %branches.1 = (bf16[512,2048]{1,0:T(8,128)(2,1)}, bf16[512,2048]{1,0:T(8,128)(2,1)}, bf16[512,2048]{1,0:T(8,128)(2,1)}, bf16[512,2048]{1,0:T(8,128)(2,1)}) custom-call(s32[2]{0:T(128)} %pad_add_fusion.ids_ref, bf16[2048,512]{1,0:T(8,128)(2,1)} %get-tuple-element.56.refs_1_.refs_0_.refs_2_, bf16[2560,2048]{1,0:T(8,128)(2,1)} %all-gather.5.cloned.1.call-done.refs_1_.refs_3_, ...), custom_call_target="tpu_custom_call" | custom-call | flops 50000000 | tf_op jit(solution)/shard_map/branches/pallas_call | solution.py:50
  282.8 25.3 %shrink_back.1 = (bf16[2048,2048]{1,0:T(8,128)(2,1)}, f32[1,2048]{1,0:T(1,128)}) custom-call(s32[2]{0:T(128)} %pad_add_fusion.ids_ref, bf16[2048,2048]{1,0:T(8,128)(2,1)} %get-tuple-element.57.refs_0_, bf16[2560,2048]{1,0:T(8,128)(2,1)} %all-gather.5.cloned.1.call-done.refs_1_.refs_3_, bf16[2048,2048]{1,0:T(8,128)(2,1)} %get-tuple-element.62.refs_2_, ...), custom_call_target="tpu_custom_call" | custom-call | flops 50000000 | tf_op jit(solution)/shard_map/shrink_back/pallas_call | solution.py:50
  308.1 26.3 %full_grad.4 = (bf16[2048,2048]{1,0:T(8,128)(2,1)}, f32[2048,128]{1,0:T(8,128)}, f32[2048,128]{1,0:T(8,128)}) custom-call(s32[2]{0:T(128)} %pad_add_fusion.ids_ref, bf16[2048,2048]{1,0:T(8,128)(2,1)} %get-tuple-element.53.refs_0_, bf16[2048,2048]{1,0:T(8,128)(2,1)} %get-tuple-element.63.refs_1_.refs_2_, ...), custom_call_target="tpu_custom_call" | custom-call | flops 50000000 | tf_op jit(solution)/shard_map/full_grad/pallas_call | solution.py:50
  337.6 9.3 %plain.1.refs_1_ = bf16[2048,512]{1,0:T(8,128)(2,1)} custom-call(s32[2]{0:T(128)} %pad_add_fusion.ids_ref, bf16[2048,2048]{1,0:T(8,128)(2,1)} %get-tuple-element.57.refs_0_, bf16[2560,2048]{1,0:T(8,128)(2,1)} %all-gather.5.cloned.1.call-done.refs_1_.refs_3_, bf16[2048,2048]{1,0:T(8,128)(2,1)} %get-tuple-element.65.refs_2_), custom_call_target="tpu_custom_call" | custom-call | flops 50000000 | tf_op jit(solution)/shard_map/plain/pallas_call | solution.py:50
  347.0 22.6 %attend_back.1 = (bf16[2048,1536]{1,0:T(8,128)(2,1)}, f32[1,1536]{1,0:T(1,128)}) custom-call(s32[2]{0:T(128)} %pad_add_fusion.ids_ref, bf16[2048,1536]{1,0:T(8,128)(2,1)} %mixed.1.refs_5_.refs_0_, bf16[2048,512]{1,0:T(8,128)(2,1)} %plain.1.refs_1_, bf16[2048,512]{1,0:T(8,128)(2,1)} %get-tuple-element.56.refs_1_.refs_0_.refs_2_, ...), custom_call_target="tpu_custom_call" | custom-call | flops 50000000 | tf_op jit(solution)/shard_map/attend_back/pallas_call | solution.py:50
  369.6 20.2 %full_grad.5 = (bf16[2048,2176]{1,0:T(8,128)(2,1)}, f32[2048,128]{1,0:T(8,128)}, f32[2048,128]{1,0:T(8,128)}) custom-call(s32[2]{0:T(128)} %pad_add_fusion.ids_ref, bf16[2048,2048]{1,0:T(8,128)(2,1)} %get-tuple-element.52.refs_0_, bf16[2048,1536]{1,0:T(8,128)(2,1)} %get-tuple-element.67.refs_1_.refs_0_, ...), custom_call_target="tpu_custom_call", output_to_operand_aliasing={{0}: (5, {})} | custom-call | flops 50000000 | tf_op jit(solution)/shard_map/full_grad/pallas_call | solution.py:50
  389.8 4.8 sums.1.refs_5_.refs_0_
  397.7 14.1 %back.3.refs_6_ = bf16[512,2048]{1,0:T(8,128)(2,1)} custom-call(s32[2]{0:T(128)} %pad_add_fusion.ids_ref, bf16[2048,1536]{1,0:T(8,128)(2,1)} %get-tuple-element.67.refs_1_.refs_0_, bf16[2048,3584]{1,0:T(8,128)(2,1)} %all-gather.3.cloned.1.call-done.refs_1_.refs_2_.refs_3_, bf16[2048,2048]{1,0:T(8,128)(2,1)} %get-tuple-element.63.refs_1_.refs_2_, ...), custom_call_target="tpu_custom_call" | custom-call | flops 50000000 | tf_op jit(solution)/shard_map/back/pallas_call | solution.py:50
  415.4 6.5 %output.1.refs_6_ = bf16[512,2048]{1,0:T(8,128)(2,1)} custom-call(s32[2]{0:T(128)} %pad_add_fusion.ids_ref, bf16[512,2048]{1,0:T(8,128)(2,1)} %refs_0_.7, f32[6,2048]{1,0:T(8,128)} %bitcast.38, bf16[512,2048]{1,0:T(8,128)(2,1)} %get-tuple-element.58.refs_3_.refs_2_, bf16[512,2048]{1,0:T(8,128)(2,1)} %collective-permute-done.10.refs_3_, ...), custom_call_target="tpu_custom_call" | custom-call | flops 160000000000 | tf_op jit(solution)/shard_map/output/pallas_call | solution.py:50
  428.7 22.7 %back.4 = (bf16[512,2048]{1,0:T(8,128)(2,1)}, bf16[512,2048]{1,0:T(8,128)(2,1)}) custom-call(s32[2]{0:T(128)} %pad_add_fusion.ids_ref, bf16[2048,1536]{1,0:T(8,128)(2,1)} %get-tuple-element.67.refs_1_.refs_0_, bf16[2048,3584]{1,0:T(8,128)(2,1)} %all-gather.3.cloned.1.call-done.refs_1_.refs_2_.refs_3_, bf16[2048,2048]{1,0:T(8,128)(2,1)} %get-tuple-element.63.refs_1_.refs_2_, ...), custom_call_target="tpu_custom_call" | custom-call | flops 50000000 | tf_op jit(solution)/shard_map/back/pallas_call | solution.py:50
  453.5 14.1 %back.5.refs_1_ = bf16[512,2048]{1,0:T(8,128)(2,1)} custom-call(s32[2]{0:T(128)} %pad_add_fusion.ids_ref, bf16[2048,1536]{1,0:T(8,128)(2,1)} %get-tuple-element.67.refs_1_.refs_0_, bf16[2048,3584]{1,0:T(8,128)(2,1)} %all-gather.3.cloned.1.call-done.refs_1_.refs_2_.refs_3_, bf16[2048,2048]{1,0:T(8,128)(2,1)} %get-tuple-element.63.refs_1_.refs_2_, ...), custom_call_target="tpu_custom_call" | custom-call | flops 50000000 | tf_op jit(solution)/shard_map/back/pallas_call | solution.py:50
  475.4 30.9 %collective-permute-done.16.refs_2_ = bf16[512,2048]{1,0:T(8,128)(2,1)S(1)} collective-permute-done((bf16[512,2048]{1,0:T(8,128)(2,1)}, bf16[512,2048]{1,0:T(8,128)(2,1)S(1)}, u32[]{:S(2)}, u32[]{:S(2)}) %collective-permute-start.16) | collective-permute-done | bytes 2097184 | tf_op jit(solution)/shard_map/ppermute | solution.py:844
  507.7 8.4 %input.1.refs_2_ = f32[512,2048]{1,0:T(8,128)} custom-call(s32[2]{0:T(128)} %pad_add_fusion.ids_ref, bf16[512,2048]{1,0:T(8,128)(2,1)} %refs_0_.7, bf16[512,2048]{1,0:T(8,128)(2,1)} %refs_1_.1, bf16[512,2048]{1,0:T(8,128)(2,1)} %copy-done.21, bf16[512,2048]{1,0:T(8,128)(2,1)} %collective-permute-done.17.refs_3_, f32[512,2048]{1,0:T(8,128)} %total.1.refs_4_), custom_call_target="tpu_custom_call" | custom-call | flops 161999994880 | tf_op jit(solution)/shard_map/input/pallas_call | solution.py:50
  516.1 8.1 %reduce-scatter.8.cloned.1.call-done.refs_0_ = bf16[256,2176]{1,0:T(8,128)(2,1)} async-done(((bf16[2048,2176]{1,0:T(8,128)(2,1)}), bf16[256,2176]{1,0:T(8,128)(2,1)}) %reduce-scatter.8.cloned.1.call-update) | async-done | bytes 1114128 | tf_op jit(solution)/shard_map/reduce_scatter | solution.py:980
  (152 shorter events, 87.6 us)
Async XLA Ops:
  7.2 141.1 %all-gather.3.cloned.1.call-start = ((), (), s32[]{:S(2)}) async-start(), calls=%async_computation.3 | async-start | bytes 16515072 | tf_op jit(solution)/shard_map/all_gather | solution.py:927
  10.1 239.6 %all-gather.5.cloned.1.call-start = ((), (), s32[]{:S(2)}) async-start(), calls=%async_computation.4 | async-start | bytes 11796480 | tf_op jit(solution)/shard_map/all_gather | solution.py:928
  11.7 413.6 %reduce-scatter.4.cloned.1.call-start = ((), (), s32[]{:S(2)}) async-start(), calls=%async_computation.5 | async-start | bytes 9437184 | tf_op jit(solution)/shard_map/reduce_scatter | solution.py:940
  11.7 53.7 %collective-permute-start.5 = (bf16[512,2048]{1,0:T(8,128)(2,1)}, bf16[512,2048]{1,0:T(8,128)(2,1)S(1)}, u32[]{:S(2)}, u32[]{:S(2)}) collective-permute-start(bf16[512,2048]{1,0:T(8,128)(2,1)} %refs_0_.7), channel_id=1, source_target_pairs={{0,1},{1,0},{2,3},{3,2},{4,5},{5,4},{6,7},{7,6},{8,9},{9,8},{10,11... | collective-permute-start | bytes 6291464 | tf_op jit(solution)/shard_map/ppermute | solution.py:844
  14.7 47.4 %collective-permute-start.3 = (bf16[512,2048]{1,0:T(8,128)(2,1)}, bf16[512,2048]{1,0:T(8,128)(2,1)}, u32[]{:S(2)}, u32[]{:S(2)}) collective-permute-start(bf16[512,2048]{1,0:T(8,128)(2,1)} %refs_0_.7), channel_id=1, source_target_pairs={{0,2},{1,3},{2,0},{3,1},{4,6},{5,7},{6,4},{7,5},{8,10},{9,11},{10,... | collective-permute-start | bytes 6291464 | tf_op jit(solution)/shard_map/ppermute | solution.py:844
  18.1 4.1 collective-permute-start
  22.2 4.4 collective-permute-start.1
  26.7 7.7 %collective-permute-start.2 = (bf16[8,1984]{1,0:T(8,128)(2,1)S(1)}, bf16[8,1984]{1,0:T(8,128)(2,1)S(1)}, u32[]{:S(2)}, u32[]{:S(2)}) collective-permute-start(bf16[8,1984]{1,0:T(8,128)(2,1)S(1)} %fusion.7), channel_id=1, source_target_pairs={{0,16},{4,20},{8,24},{12,28},{16,0},{20,4},{24,8},{28,12},{1,17},{... | collective-permute-start | bytes 95240 | tf_op jit(solution)/shard_map/ppermute | solution.py:844
  65.1 23.9 %collective-permute-start.4 = (bf16[256,2048]{1,0:T(8,128)(2,1)}, bf16[256,2048]{1,0:T(8,128)(2,1)S(1)}, u32[]{:S(2)}, u32[]{:S(2)}) collective-permute-start(bf16[256,2048]{1,0:T(8,128)(2,1)} %half.2), channel_id=1, source_target_pairs={{0,1},{1,0},{2,3},{3,2},{4,5},{5,4},{6,7},{7,6},{8,9},{9,8},{10,11... | collective-permute-start | bytes 3145736 | tf_op jit(solution)/shard_map/ppermute | solution.py:844
  69.7 24.0 %collective-permute-start.6 = (bf16[256,2048]{1,0:T(8,128)(2,1)}, bf16[256,2048]{1,0:T(8,128)(2,1)S(1)}, u32[]{:S(2)}, u32[]{:S(2)}) collective-permute-start(bf16[256,2048]{1,0:T(8,128)(2,1)} %half.3), channel_id=1, source_target_pairs={{0,2},{1,3},{2,0},{3,1},{4,6},{5,7},{6,4},{7,5},{8,10},{9,11},{10,... | collective-permute-start | bytes 3145736 | tf_op jit(solution)/shard_map/ppermute | solution.py:844
  98.3 100.4 %collective-permute-start.9 = (bf16[512,2048]{1,0:T(8,128)(2,1)}, bf16[512,2048]{1,0:T(8,128)(2,1)S(1)}, u32[]{:S(2)}, u32[]{:S(2)}) collective-permute-start(bf16[512,2048]{1,0:T(8,128)(2,1)} %stack.37.refs_5_.refs_1_), channel_id=1, source_target_pairs={{0,3},{1,2},{2,1},{3,0},{4,7},{5,6},{6,5},{7,4},{8,11},{9,10},{10,... | collective-permute-start | bytes 6291464 | tf_op jit(solution)/shard_map/ppermute | solution.py:844
  100.6 98.1 %collective-permute-start.8 = (bf16[512,2048]{1,0:T(8,128)(2,1)}, bf16[512,2048]{1,0:T(8,128)(2,1)}, u32[]{:S(2)}, u32[]{:S(2)}) collective-permute-start(bf16[512,2048]{1,0:T(8,128)(2,1)} %stack.37.refs_5_.refs_1_), channel_id=1, source_target_pairs={{0,2},{1,3},{2,0},{3,1},{4,6},{5,7},{6,4},{7,5},{8,10},{9,11},{10,... | collective-permute-start | bytes 6291464 | tf_op jit(solution)/shard_map/ppermute | solution.py:844
  101.1 97.6 %collective-permute-start.7 = (bf16[512,2048]{1,0:T(8,128)(2,1)}, bf16[512,2048]{1,0:T(8,128)(2,1)}, u32[]{:S(2)}, u32[]{:S(2)}) collective-permute-start(bf16[512,2048]{1,0:T(8,128)(2,1)} %stack.37.refs_5_.refs_1_), channel_id=1, source_target_pairs={{0,1},{1,0},{2,3},{3,2},{4,5},{5,4},{6,7},{7,6},{8,9},{9,8},{10,11... | collective-permute-start | bytes 6291464 | tf_op jit(solution)/shard_map/ppermute | solution.py:844
  225.6 242.0 %reduce-scatter.6.cloned.1.call-start = ((), (), s32[]{:S(2)}) async-start(), calls=%async_computation.6 | async-start | bytes 9437184 | tf_op jit(solution)/shard_map/reduce_scatter | solution.py:949
  279.3 133.1 %collective-permute-start.10 = (bf16[512,2048]{1,0:T(8,128)(2,1)}, bf16[512,2048]{1,0:T(8,128)(2,1)}, u32[]{:S(2)}, u32[]{:S(2)}) collective-permute-start(bf16[512,2048]{1,0:T(8,128)(2,1)} %get-tuple-element.59), channel_id=1, source_target_pairs={{0,3},{1,2},{2,1},{3,0},{4,7},{5,6},{6,5},{7,4},{8,11},{9,10},{10,... | collective-permute-start | bytes 6291464 | tf_op jit(solution)/shard_map/ppermute | solution.py:844
  281.7 131.4 %collective-permute-start.11 = (bf16[512,2048]{1,0:T(8,128)(2,1)}, bf16[512,2048]{1,0:T(8,128)(2,1)}, u32[]{:S(2)}, u32[]{:S(2)}) collective-permute-start(bf16[512,2048]{1,0:T(8,128)(2,1)} %get-tuple-element.60), channel_id=1, source_target_pairs={{0,2},{1,3},{2,0},{3,1},{4,6},{5,7},{6,4},{7,5},{8,10},{9,11},{10,... | collective-permute-start | bytes 6291464 | tf_op jit(solution)/shard_map/ppermute | solution.py:844
  282.3 133.1 %collective-permute-start.12 = (bf16[512,2048]{1,0:T(8,128)(2,1)}, bf16[512,2048]{1,0:T(8,128)(2,1)}, u32[]{:S(2)}, u32[]{:S(2)}) collective-permute-start(bf16[512,2048]{1,0:T(8,128)(2,1)} %get-tuple-element.61), channel_id=1, source_target_pairs={{0,1},{1,0},{2,3},{3,2},{4,5},{5,4},{6,7},{7,6},{8,9},{9,8},{10,11... | collective-permute-start | bytes 6291464 | tf_op jit(solution)/shard_map/ppermute | solution.py:844
  334.4 189.8 %reduce-scatter.8.cloned.1.call-start = ((), (), s32[]{:S(2)}) async-start(), calls=%async_computation.7 | async-start | bytes 10027008 | tf_op jit(solution)/shard_map/reduce_scatter | solution.py:980
  394.6 27.3 %collective-permute-start.15 = (f32[8,2048]{1,0:T(8,128)}, f32[8,2048]{1,0:T(8,128)}, u32[]{:S(2)}, u32[]{:S(2)}) collective-permute-start(f32[8,2048]{1,0:T(8,128)} %sums.1.refs_5_.refs_0_), channel_id=1, source_target_pairs={{0,1},{1,0},{2,3},{3,2},{4,5},{5,4},{6,7},{7,6},{8,9},{9,8},{10,11... | collective-permute-start | bytes 196616 | tf_op jit(solution)/shard_map/ppermute | solution.py:844
  396.1 25.8 %collective-permute-start.14 = (f32[8,2048]{1,0:T(8,128)}, f32[8,2048]{1,0:T(8,128)}, u32[]{:S(2)}, u32[]{:S(2)}) collective-permute-start(f32[8,2048]{1,0:T(8,128)} %sums.1.refs_5_.refs_0_), channel_id=1, source_target_pairs={{0,2},{1,3},{2,0},{3,1},{4,6},{5,7},{6,4},{7,5},{8,10},{9,11},{10,... | collective-permute-start | bytes 196616 | tf_op jit(solution)/shard_map/ppermute | solution.py:844
  412.5 9.4 %collective-permute-start.13 = (f32[8,2048]{1,0:T(8,128)}, f32[8,2048]{1,0:T(8,128)}, u32[]{:S(2)}, u32[]{:S(2)}) collective-permute-start(f32[8,2048]{1,0:T(8,128)} %sums.1.refs_5_.refs_0_), channel_id=1, source_target_pairs={{0,3},{1,2},{2,1},{3,0},{4,7},{5,6},{6,5},{7,4},{8,11},{9,10},{10,... | collective-permute-start | bytes 196616 | tf_op jit(solution)/shard_map/ppermute | solution.py:844
  413.1 57.8 %collective-permute-start.18 = (bf16[512,2048]{1,0:T(8,128)(2,1)}, bf16[512,2048]{1,0:T(8,128)(2,1)}, u32[]{:S(2)}, u32[]{:S(2)}) collective-permute-start(bf16[512,2048]{1,0:T(8,128)(2,1)} %back.3.refs_6_), channel_id=1, source_target_pairs={{0,3},{1,2},{2,1},{3,0},{4,7},{5,6},{6,5},{7,4},{8,11},{9,10},{10,... | collective-permute-start | bytes 6291464 | tf_op jit(solution)/shard_map/ppermute | solution.py:844
  451.4 55.0 %collective-permute-start.16 = (bf16[512,2048]{1,0:T(8,128)(2,1)}, bf16[512,2048]{1,0:T(8,128)(2,1)S(1)}, u32[]{:S(2)}, u32[]{:S(2)}) collective-permute-start(bf16[512,2048]{1,0:T(8,128)(2,1)} %get-tuple-element.74), channel_id=1, source_target_pairs={{0,2},{1,3},{2,0},{3,1},{4,6},{5,7},{6,4},{7,5},{8,10},{9,11},{10,... | collective-permute-start | bytes 6291464 | tf_op jit(solution)/shard_map/ppermute | solution.py:844
  452.0 54.3 %collective-permute-start.17 = (bf16[512,2048]{1,0:T(8,128)(2,1)}, bf16[512,2048]{1,0:T(8,128)(2,1)}, u32[]{:S(2)}, u32[]{:S(2)}) collective-permute-start(bf16[512,2048]{1,0:T(8,128)(2,1)} %get-tuple-element.75.refs_5_), channel_id=1, source_target_pairs={{0,1},{1,0},{2,3},{3,2},{4,5},{5,4},{6,7},{7,6},{8,9},{9,8},{10,11... | collective-permute-start | bytes 6291464 | tf_op jit(solution)/shard_map/ppermute | solution.py:844
  (23 other events, 189.6 us)
Sparse Core Ops, SparseCore 0:
  10.2 137.9 all-gather.2
  150.4 98.3 all-gather.4
  251.1 87.8 reduce-scatter.3
  341.2 87.9 reduce-scatter.5
  431.3 92.8 reduce-scatter.7

commit v8 on v7

--- a/solution.py
+++ b/solution.py
@@ -10,7 +10,6 @@
 LENGTH = 2048
 EPSILON = 1e-05
 BIG = -1e30
-SUMS = 7
 F32 = jnp.float32
 BF16 = jnp.bfloat16
 DIMS = {
@@ -645,36 +644,34 @@
     )
 
 
-def spare_kernel(ids, kept, parts, slots, after=(), lag=0.05):
-    depth = kept.shape[0]
+def slots_kernel(ids, kept, parts, size, after=(), lag=0.05):
+    count, width = parts[0].shape
+    each = width // size
 
     def kernel(ids_ref, *refs):
         total = refs[0][...]
-        for ref in refs[1:-1]:
+        for ref in refs[1 : len(parts)]:
             total = total + ref[...]
-        rounded = total.astype(BF16).astype(F32)
-        row = lax.broadcasted_iota(jnp.int32, (128, depth), 0)
-        value = jnp.zeros((128, depth), F32)
-        for number in range(SUMS):
-            place = number * slots + ids_ref[1]
-            value = jnp.where(row == place, rounded[number : number + 1], value)
-            if SUMS * slots <= 64:
-                value = jnp.where(row == place + 64, (total - rounded)[number : number + 1], value)
-        refs[-1][...] = jnp.transpose(value).astype(BF16)
+        held = refs[-1]
+        held[...] = total
+        for number in range(size):
+            place = pl.multiple_of((ids_ref[1] ^ number) * each, 128)
+            refs[len(parts) + 1 + number][...] = held[:, pl.ds(place, each)]
 
     return call(
         kernel,
         ids,
         (1,),
-        [pl.BlockSpec((8, depth), lambda i, ids: (0, 0))] * len(parts),
-        [pl.BlockSpec((depth, 128), lambda i, ids: (0, kept.shape[1] // 128 - 1))],
-        [jax.ShapeDtypeStruct(kept.shape, BF16)],
+        [pl.BlockSpec((count, width), lambda i, ids: (0, 0))] * len(parts),
+        [pl.BlockSpec(memory_space=pl.ANY)] + [pl.BlockSpec((count, each), lambda i, ids: (0, 0))] * size,
+        [jax.ShapeDtypeStruct(kept.shape, BF16)] + [jax.ShapeDtypeStruct((count, each), F32)] * size,
         tuple(parts),
+        scratch=[pltpu.VMEM((count, width), F32)],
         kept=(kept,),
         after=after,
         lag=lag,
-        name="spare",
-    )[0]
+        name="slots",
+    )
 
 
 def output_kernel(ids, rows, parts, vectors, after=(), lag=0.05):
@@ -728,21 +725,19 @@
     )
 
 
-def finish_kernel(ids, rows, widths, heads, slots, scales, last, after=(), lag=0.05):
+def finish_kernel(ids, rows, widths, heads, parts, scales, last, after=(), lag=0.05):
     count = rows.shape[0]
     one, two = widths
     each = one // heads
 
-    def kernel(ids_ref, in_ref, v_ref, one_ref, two_ref, *sum_refs):
+    def kernel(ids_ref, in_ref, v_ref, *refs):
+        one_ref, two_ref, *sum_refs = refs[len(parts) :]
         for head in range(heads):
             one_ref[:, head, :] = in_ref[:, head * each : (head + 1) * each].astype(F32)
         two_ref[...] = jnp.transpose(in_ref[:, one : one + two].astype(F32))
-        number = lax.broadcasted_iota(jnp.int32, (8, 128), 0)
-        lane = lax.broadcasted_iota(jnp.int32, (8, 128), 1)
-        if SUMS * slots <= 64:
-            lane = lane % 64
-        mine = (lane // slots == number) & (number < SUMS)
-        sums = product(jnp.where(mine, 1.0, 0.0).astype(BF16), in_ref[:, one + two :], "NT")
+        sums = refs[0][...]
+        for ref in refs[1 : len(parts)]:
+            sums = sums + ref[...]
         for number, sum_ref in zip((0, 1, 2, 3, 4, 4, 5, 6), sum_refs):
             value = sums[number : number + 1]
             if number in (0, 2):
@@ -759,10 +754,10 @@
         kernel,
         ids,
         (1,),
-        [whole(rows.shape), whole(scales.shape)],
+        [whole(array.shape) for array in (rows, scales, *parts)],
         [whole(shape) for shape in shapes],
         [jax.ShapeDtypeStruct(shape, F32) for shape in shapes],
-        (rows, scales),
+        (rows, scales, *parts),
         after=after,
         lag=lag,
         name="finish",
@@ -900,7 +895,6 @@
 ):
     n_dp, n_tensor = lax.axis_size("dp"), lax.axis_size("tensor")
     dp_at, tensor_at = lax.axis_index("dp"), lax.axis_index("tensor")
-    assert SUMS * n_dp <= 128
     ids = jnp.stack([tensor_at, dp_at]).astype(jnp.int32)
     own_count, width = layer_input.shape
     group_count = own_count * n_tensor
@@ -940,7 +934,7 @@
     shrink_grad = lax.psum_scatter(shrink_part, "dp", scatter_dimension=1, tiled=True)
     context, lse = attend_kernel(ids, mixed, n_tensor, after=(shrink_part,))
     merge_width = merging.shape[0]
-    joint = mixed_width + merge_width + 128
+    joint = mixed_width + merge_width
     part = full_grad_kernel(ids, seed, context, start=mixed_width, span=joint)
     branches = branches_kernel(ids, context, hidden, w_out, n_tensor, after=part)
     summed = [branches[0]] + [flip(branches[k], "tensor", k, n_tensor) for k in range(n_tensor - 1, 0, -1)]
@@ -976,16 +970,17 @@
         last = made[0]
         if len(back) == 1:
             layer_output = output_kernel(ids, layer_input, summed, vectors, after=(last,), lag=160)
-            last = spare_kernel(ids, project_part, over_tensor + [over_dp], n_dp, after=(layer_output,))
-            project_grad = lax.psum_scatter(last, "dp", scatter_dimension=0, tiled=True)
-            (shrink_grad,) = widen_kernel(ids, shrink_grad, [shrink.shape[1]], after=(last,), lag=0.05)
+            project_part, *sums = slots_kernel(ids, project_part, over_tensor + [over_dp], n_dp, after=(layer_output,))
+            project_grad = lax.psum_scatter(project_part, "dp", scatter_dimension=0, tiled=True)
+            (shrink_grad,) = widen_kernel(ids, shrink_grad, [shrink.shape[1]], after=(sums[0],))
             last = shrink_grad
     (expand_grad,) = widen_kernel(ids, expand_grad, [hidden_width], after=(last,))
     far = total_kernel(ids, back[0] + back[2], after=(expand_grad,), lag=8)
-    input_grad = input_kernel(ids, layer_input, cotangent, back[1] + [far], lag=162)
+    input_grad = input_kernel(ids, layer_input, cotangent, back[1] + [far], lag=154)
     scales = jnp.stack([firstgain, firstbias, secondgain, secondbias]).astype(F32)
+    sums = [sums[0]] + [flip(sums[k], "dp", k, n_dp) for k in range(1, n_dp)]
     project_grad, merging_grad, *sums = finish_kernel(
-        ids, project_grad, [mixed_width, merge_width], heads, n_dp, scales, [(1, expandbias.shape[0]), projbias.shape], after=(input_grad,)
+        ids, project_grad, [mixed_width, merge_width], heads, sums, scales, [(1, expandbias.shape[0]), projbias.shape], after=(input_grad,)
     )
     projbias_grad = sums.pop()
     gain_one, bias_one, gain_two, bias_two, seed_sum, seed_sum_again, expandbias_grad = [value[0] for value in sums]

time: 542 us -> 538 us (level)
  waiting for transfers between devices: 121 us -> 111 us
  starting transfers between devices: 25.3 us -> 33.2 us
    ppermute x19 -> x26, starting transfers between devices: 25.1 us -> 33 us  [flip(): return lax.ppermute(value, axis, [(i, i ^ bit) for i in range(size)])]
    reduce_scatter x1, waiting for transfers between devices: 8.09 us -> 1.62 us  [body(): lax.psum_scatter(project_part, 'dp', scatter_dimension=0, tiled=True)]
    ppermute x19 -> x26, waiting for transfers between devices: 73.8 us -> 70.3 us  [flip(): return lax.ppermute(value, axis, [(i, i ^ bit) for i in range(size)])]
    unnamed x62 -> x70, local copies, waits for them, and re-layouts: 11 us -> 9.68 us
  transfers between devices with their start and end apart: 24 -> 31, of which waited for: 8 -> 8; matrix products, arithmetic and copies ran while one was open for 3% -> 3% of each run, Pallas kernels for 65% -> 65%
where the time goes in v8:
time: 538 us; the launch traced here: 531 us
  Pallas kernels  349 us (65%)
  waiting for transfers between devices  111 us (21%)
  starting transfers between devices  33.2 us (6%)
  between operations  14.6 us (3%)
  local copies, waits for them, and re-layouts  11.5 us (2%)
  other arithmetic  11.4 us (2%)
    pallas_call x27, Pallas kernels, call(): pl.pallas_call(run, grid_spec=pltpu.PrefetchScalarGridSpec(num_scalar_pre...  349 us
    ppermute x26, waiting for transfers between devices, flip(): return lax.ppermute(value, axis, [(i, i ^ bit) for i in range(size)])  70.3 us
    all_gather x1, waiting for transfers between devices, body(): lax.all_gather(jnp.concatenate([expand, own_project], axis=1), 'dp', axis...  38.8 us
    ppermute x26, starting transfers between devices, flip(): return lax.ppermute(value, axis, [(i, i ^ bit) for i in range(size)])  33 us
  transfers between devices with their start and end apart: 31, of which 8 were waited for; matrix products, arithmetic and copies ran while one was open for 3% of the time, Pallas kernels for 65%

profile of v8, /device:TPU:0, one launch (start us, length us, event | category | flops | bytes accessed | tf_op | source)
XLA Modules:
  0.0 530.8 jit_solution(8243457219443791958)
XLA Ops:
  35.1 27.1 %collective-permute-done.3.refs_0_.refs_2_ = bf16[512,2048]{1,0:T(8,128)(2,1)} collective-permute-done((bf16[512,2048]{1,0:T(8,128)(2,1)}, bf16[512,2048]{1,0:T(8,128)(2,1)}, u32[]{:S(2)}, u32[]{:S(2)}) %collective-permute-start.3) | collective-permute-done | bytes 2097184 | tf_op jit(solution)/shard_map/ppermute | solution.py:839
  71.4 12.0 %norm.2 = (bf16[2048,2048]{1,0:T(8,128)(2,1)}, bf16[2048,2048]{1,0:T(8,128)(2,1)}) custom-call(s32[2]{0:T(128)} %pad_add_fusion.ids_ref, bf16[512,2048]{1,0:T(8,128)(2,1)} %refs_0_.7, bf16[512,2048]{1,0:T(8,128)(2,1)} %copy-done, bf16[512,2048]{1,0:T(8,128)(2,1)} %collective-permute-done.3.refs_0_.refs_2_, f32[6,2048]{1,0:T(8,128)} %bitcast.36), custom_call_target="tpu_custom_call" | custom-call | flops 50000000 | tf_op jit(solution)/shard_map/norm/pallas_call | solution.py:49
  83.4 5.6 %collective-permute-done.4.refs_2_.refs_0_ = bf16[256,2048]{1,0:T(8,128)(2,1)S(1)} collective-permute-done((bf16[256,2048]{1,0:T(8,128)(2,1)}, bf16[256,2048]{1,0:T(8,128)(2,1)S(1)}, u32[]{:S(2)}, u32[]{:S(2)}) %collective-permute-start.4) | collective-permute-done | bytes 1048608 | tf_op jit(solution)/shard_map/ppermute | solution.py:839
  89.0 4.7 collective-permute-done.6.refs_3_.refs_1_
  103.2 6.3 %norm.3 = (bf16[2048,2048]{1,0:T(8,128)(2,1)}, bf16[2048,2048]{1,0:T(8,128)(2,1)}) custom-call(s32[2]{0:T(128)} %pad_add_fusion.ids_ref, bf16[256,2048]{1,0:T(8,128)(2,1)} %copy-done.2, bf16[256,2048]{1,0:T(8,128)(2,1)} %copy-done.3, f32[6,2048]{1,0:T(8,128)} %bitcast.37, ...), custom_call_target="tpu_custom_call", output_to_operand_aliasing={{0}: (4, {}), {1}: (5, {})} | custom-call | flops 50000000 | tf_op jit(solution)/shard_map/norm/pallas_call | solution.py:49
  109.5 38.8 %all-gather.3.cloned.1.call-done.refs_1_.refs_2_.refs_3_ = bf16[2048,3584]{1,0:T(8,128)(2,1)} async-done(((bf16[256,3584]{1,0:T(8,128)(2,1)}), bf16[2048,3584]{1,0:T(8,128)(2,1)}) %all-gather.3.cloned.1.call-update) | async-done | bytes 14680080 | tf_op jit(solution)/shard_map/all_gather | solution.py:921
  148.3 30.3 %expand.1 = (bf16[2048,2048]{1,0:T(8,128)(2,1)}, bf16[2048,2048]{1,0:T(8,128)(2,1)}) custom-call(s32[2]{0:T(128)} %pad_add_fusion.ids_ref, bf16[2048,2048]{1,0:T(8,128)(2,1)} %get-tuple-element.62.refs_0_, bf16[2048,3584]{1,0:T(8,128)(2,1)} %all-gather.3.cloned.1.call-done.refs_1_.refs_2_.refs_3_, f32[1,2048]{1,0:T(1,128)} %bitcast.43), custom_call_target="tpu_custom_call" | custom-call | flops 50000000 | tf_op jit(solution)/shard_map/expand/pallas_call | solution.py:49
  178.6 20.2 %mixed.1.refs_5_.refs_0_ = bf16[2048,1536]{1,0:T(8,128)(2,1)} custom-call(s32[2]{0:T(128)} %pad_add_fusion.ids_ref, bf16[2048,2048]{1,0:T(8,128)(2,1)} %get-tuple-element.61.refs_0_, bf16[2048,3584]{1,0:T(8,128)(2,1)} %all-gather.3.cloned.1.call-done.refs_1_.refs_2_.refs_3_, f32[1,1536]{1,0:T(1,128)} %reshape.85.refs_2_, ...), custom_call_target="tpu_custom_call" | custom-call | flops 50000000 | tf_op jit(solution)/shard_map/mixed/pallas_call | solution.py:49
  200.1 25.7 %piece_grad.1 = (bf16[2048,2048]{1,0:T(8,128)(2,1)}, bf16[2048,2048]{1,0:T(8,128)(2,1)}) custom-call(s32[2]{0:T(128)} %pad_add_fusion.ids_ref, bf16[2048,2048]{1,0:T(8,128)(2,1)} %get-tuple-element.63.refs_5_.refs_0_.refs_2_, bf16[512,2048]{1,0:T(8,128)(2,1)} %stack.37.refs_5_.refs_1_, bf16[512,2048]{1,0:T(8,128)(2,1)} %collective-permute-done.7.refs_2_, ...), custom_call_target="tpu_custom_call" | custom-call | flops 50000000 | tf_op jit(solution)/shard_map/piece_grad/pallas_call | solution.py:49
  225.9 14.5 %attend.1 = (bf16[2048,512]{1,0:T(8,128)(2,1)}, f32[2,4,8,512]{3,2,1,0:T(8,128)}) custom-call(s32[2]{0:T(128)} %pad_add_fusion.ids_ref, bf16[2048,1536]{1,0:T(8,128)(2,1)} %mixed.1.refs_5_.refs_0_, bf16[2048,2048]{1,0:T(8,128)(2,1)} %get-tuple-element.64.refs_1_), custom_call_target="tpu_custom_call" | custom-call | flops 50000000 | tf_op jit(solution)/shard_map/attend/pallas_call | solution.py:49
  240.4 9.5 %full_grad.3.refs_4_ = bf16[2048,2048]{1,0:T(8,128)(2,1)} custom-call(s32[2]{0:T(128)} %pad_add_fusion.ids_ref, bf16[2048,2048]{1,0:T(8,128)(2,1)} %get-tuple-element.66.refs_0_, bf16[2048,512]{1,0:T(8,128)(2,1)} %get-tuple-element.65.refs_1_.refs_0_.refs_2_), custom_call_target="tpu_custom_call" | custom-call | flops 50000000 | tf_op jit(solution)/shard_map/full_grad/pallas_call | solution.py:49
  249.9 29.6 %branches.1 = (bf16[512,2048]{1,0:T(8,128)(2,1)}, bf16[512,2048]{1,0:T(8,128)(2,1)}, bf16[512,2048]{1,0:T(8,128)(2,1)}, bf16[512,2048]{1,0:T(8,128)(2,1)}) custom-call(s32[2]{0:T(128)} %pad_add_fusion.ids_ref, bf16[2048,512]{1,0:T(8,128)(2,1)} %get-tuple-element.65.refs_1_.refs_0_.refs_2_, bf16[2560,2048]{1,0:T(8,128)(2,1)} %all-gather.5.cloned.1.call-done.refs_1_.refs_3_, ...), custom_call_target="tpu_custom_call" | custom-call | flops 50000000 | tf_op jit(solution)/shard_map/branches/pallas_call | solution.py:49
  283.0 25.3 %shrink_back.1 = (bf16[2048,2048]{1,0:T(8,128)(2,1)}, f32[1,2048]{1,0:T(1,128)}) custom-call(s32[2]{0:T(128)} %pad_add_fusion.ids_ref, bf16[2048,2048]{1,0:T(8,128)(2,1)} %get-tuple-element.66.refs_0_, bf16[2560,2048]{1,0:T(8,128)(2,1)} %all-gather.5.cloned.1.call-done.refs_1_.refs_3_, bf16[2048,2048]{1,0:T(8,128)(2,1)} %get-tuple-element.71.refs_2_, ...), custom_call_target="tpu_custom_call" | custom-call | flops 50000000 | tf_op jit(solution)/shard_map/shrink_back/pallas_call | solution.py:49
  308.3 26.3 %full_grad.4 = (bf16[2048,2048]{1,0:T(8,128)(2,1)}, f32[2048,128]{1,0:T(8,128)}, f32[2048,128]{1,0:T(8,128)}) custom-call(s32[2]{0:T(128)} %pad_add_fusion.ids_ref, bf16[2048,2048]{1,0:T(8,128)(2,1)} %get-tuple-element.62.refs_0_, bf16[2048,2048]{1,0:T(8,128)(2,1)} %get-tuple-element.72.refs_1_.refs_2_, ...), custom_call_target="tpu_custom_call" | custom-call | flops 50000000 | tf_op jit(solution)/shard_map/full_grad/pallas_call | solution.py:49
  337.9 9.3 %plain.1.refs_1_ = bf16[2048,512]{1,0:T(8,128)(2,1)} custom-call(s32[2]{0:T(128)} %pad_add_fusion.ids_ref, bf16[2048,2048]{1,0:T(8,128)(2,1)} %get-tuple-element.66.refs_0_, bf16[2560,2048]{1,0:T(8,128)(2,1)} %all-gather.5.cloned.1.call-done.refs_1_.refs_3_, bf16[2048,2048]{1,0:T(8,128)(2,1)} %get-tuple-element.74.refs_2_), custom_call_target="tpu_custom_call" | custom-call | flops 50000000 | tf_op jit(solution)/shard_map/plain/pallas_call | solution.py:49
  347.2 22.7 %attend_back.1 = (bf16[2048,1536]{1,0:T(8,128)(2,1)}, f32[1,1536]{1,0:T(1,128)}) custom-call(s32[2]{0:T(128)} %pad_add_fusion.ids_ref, bf16[2048,1536]{1,0:T(8,128)(2,1)} %mixed.1.refs_5_.refs_0_, bf16[2048,512]{1,0:T(8,128)(2,1)} %plain.1.refs_1_, bf16[2048,512]{1,0:T(8,128)(2,1)} %get-tuple-element.65.refs_1_.refs_0_.refs_2_, ...), custom_call_target="tpu_custom_call" | custom-call | flops 50000000 | tf_op jit(solution)/shard_map/attend_back/pallas_call | solution.py:49
  369.9 20.2 %full_grad.5 = (bf16[2048,2048]{1,0:T(8,128)(2,1)}, f32[2048,128]{1,0:T(8,128)}, f32[2048,128]{1,0:T(8,128)}) custom-call(s32[2]{0:T(128)} %pad_add_fusion.ids_ref, bf16[2048,2048]{1,0:T(8,128)(2,1)} %get-tuple-element.61.refs_0_, bf16[2048,1536]{1,0:T(8,128)(2,1)} %get-tuple-element.76.refs_1_.refs_0_, ...), custom_call_target="tpu_custom_call", output_to_operand_aliasing={{0}: (5, {})} | custom-call | flops 50000000 | tf_op jit(solution)/shard_map/full_grad/pallas_call | solution.py:49
  390.1 4.8 sums.1.refs_5_.refs_0_
  398.1 14.1 %back.3.refs_6_ = bf16[512,2048]{1,0:T(8,128)(2,1)} custom-call(s32[2]{0:T(128)} %pad_add_fusion.ids_ref, bf16[2048,1536]{1,0:T(8,128)(2,1)} %get-tuple-element.76.refs_1_.refs_0_, bf16[2048,3584]{1,0:T(8,128)(2,1)} %all-gather.3.cloned.1.call-done.refs_1_.refs_2_.refs_3_, bf16[2048,2048]{1,0:T(8,128)(2,1)} %get-tuple-element.72.refs_1_.refs_2_, ...), custom_call_target="tpu_custom_call" | custom-call | flops 50000000 | tf_op jit(solution)/shard_map/back/pallas_call | solution.py:49
  415.7 6.4 %output.1.refs_6_ = bf16[512,2048]{1,0:T(8,128)(2,1)} custom-call(s32[2]{0:T(128)} %pad_add_fusion.ids_ref, bf16[512,2048]{1,0:T(8,128)(2,1)} %refs_0_.7, f32[6,2048]{1,0:T(8,128)} %bitcast.38, bf16[512,2048]{1,0:T(8,128)(2,1)} %get-tuple-element.67.refs_3_.refs_2_, bf16[512,2048]{1,0:T(8,128)(2,1)} %collective-permute-done.10.refs_3_, ...), custom_call_target="tpu_custom_call" | custom-call | flops 160000000000 | tf_op jit(solution)/shard_map/output/pallas_call | solution.py:49
  427.9 22.7 %back.4 = (bf16[512,2048]{1,0:T(8,128)(2,1)}, bf16[512,2048]{1,0:T(8,128)(2,1)}) custom-call(s32[2]{0:T(128)} %pad_add_fusion.ids_ref, bf16[2048,1536]{1,0:T(8,128)(2,1)} %get-tuple-element.76.refs_1_.refs_0_, bf16[2048,3584]{1,0:T(8,128)(2,1)} %all-gather.3.cloned.1.call-done.refs_1_.refs_2_.refs_3_, bf16[2048,2048]{1,0:T(8,128)(2,1)} %get-tuple-element.72.refs_1_.refs_2_, ...), custom_call_target="tpu_custom_call" | custom-call | flops 50000000 | tf_op jit(solution)/shard_map/back/pallas_call | solution.py:49
  453.1 14.1 %back.5.refs_1_ = bf16[512,2048]{1,0:T(8,128)(2,1)} custom-call(s32[2]{0:T(128)} %pad_add_fusion.ids_ref, bf16[2048,1536]{1,0:T(8,128)(2,1)} %get-tuple-element.76.refs_1_.refs_0_, bf16[2048,3584]{1,0:T(8,128)(2,1)} %all-gather.3.cloned.1.call-done.refs_1_.refs_2_.refs_3_, bf16[2048,2048]{1,0:T(8,128)(2,1)} %get-tuple-element.72.refs_1_.refs_2_, ...), custom_call_target="tpu_custom_call" | custom-call | flops 50000000 | tf_op jit(solution)/shard_map/back/pallas_call | solution.py:49
  479.4 27.4 %collective-permute-done.16.refs_2_ = bf16[512,2048]{1,0:T(8,128)(2,1)S(1)} collective-permute-done((bf16[512,2048]{1,0:T(8,128)(2,1)}, bf16[512,2048]{1,0:T(8,128)(2,1)S(1)}, u32[]{:S(2)}, u32[]{:S(2)}) %collective-permute-start.16) | collective-permute-done | bytes 2097184 | tf_op jit(solution)/shard_map/ppermute | solution.py:839
  510.1 8.4 %input.1.refs_10_ = f32[512,2048]{1,0:T(8,128)} custom-call(s32[2]{0:T(128)} %pad_add_fusion.ids_ref, bf16[512,2048]{1,0:T(8,128)(2,1)} %refs_0_.7, bf16[512,2048]{1,0:T(8,128)(2,1)} %refs_1_.1, bf16[512,2048]{1,0:T(8,128)(2,1)} %copy-done.23, bf16[512,2048]{1,0:T(8,128)(2,1)} %collective-permute-done.17.refs_3_, f32[512,2048]{1,0:T(8,128)} %total.1.refs_4_), custom_call_target="tpu_custom_call" | custom-call | flops 153999998976 | tf_op jit(solution)/shard_map/input/pallas_call | solution.py:49
  (174 shorter events, 90.2 us)
Async XLA Ops:
  7.2 141.1 %all-gather.3.cloned.1.call-start = ((), (), s32[]{:S(2)}) async-start(), calls=%async_computation.3 | async-start | bytes 16515072 | tf_op jit(solution)/shard_map/all_gather | solution.py:921
  10.1 239.8 %all-gather.5.cloned.1.call-start = ((), (), s32[]{:S(2)}) async-start(), calls=%async_computation.4 | async-start | bytes 11796480 | tf_op jit(solution)/shard_map/all_gather | solution.py:922
  11.7 412.8 %reduce-scatter.4.cloned.1.call-start = ((), (), s32[]{:S(2)}) async-start(), calls=%async_computation.5 | async-start | bytes 9437184 | tf_op jit(solution)/shard_map/reduce_scatter | solution.py:934
  11.7 53.7 %collective-permute-start.5 = (bf16[512,2048]{1,0:T(8,128)(2,1)}, bf16[512,2048]{1,0:T(8,128)(2,1)S(1)}, u32[]{:S(2)}, u32[]{:S(2)}) collective-permute-start(bf16[512,2048]{1,0:T(8,128)(2,1)} %refs_0_.7), channel_id=1, source_target_pairs={{0,1},{1,0},{2,3},{3,2},{4,5},{5,4},{6,7},{7,6},{8,9},{9,8},{10,11... | collective-permute-start | bytes 6291464 | tf_op jit(solution)/shard_map/ppermute | solution.py:839
  14.7 47.4 %collective-permute-start.3 = (bf16[512,2048]{1,0:T(8,128)(2,1)}, bf16[512,2048]{1,0:T(8,128)(2,1)}, u32[]{:S(2)}, u32[]{:S(2)}) collective-permute-start(bf16[512,2048]{1,0:T(8,128)(2,1)} %refs_0_.7), channel_id=1, source_target_pairs={{0,2},{1,3},{2,0},{3,1},{4,6},{5,7},{6,4},{7,5},{8,10},{9,11},{10,... | collective-permute-start | bytes 6291464 | tf_op jit(solution)/shard_map/ppermute | solution.py:839
  65.1 23.9 %collective-permute-start.4 = (bf16[256,2048]{1,0:T(8,128)(2,1)}, bf16[256,2048]{1,0:T(8,128)(2,1)S(1)}, u32[]{:S(2)}, u32[]{:S(2)}) collective-permute-start(bf16[256,2048]{1,0:T(8,128)(2,1)} %half.2), channel_id=1, source_target_pairs={{0,1},{1,0},{2,3},{3,2},{4,5},{5,4},{6,7},{7,6},{8,9},{9,8},{10,11... | collective-permute-start | bytes 3145736 | tf_op jit(solution)/shard_map/ppermute | solution.py:839
  69.7 24.0 %collective-permute-start.6 = (bf16[256,2048]{1,0:T(8,128)(2,1)}, bf16[256,2048]{1,0:T(8,128)(2,1)S(1)}, u32[]{:S(2)}, u32[]{:S(2)}) collective-permute-start(bf16[256,2048]{1,0:T(8,128)(2,1)} %half.3), channel_id=1, source_target_pairs={{0,2},{1,3},{2,0},{3,1},{4,6},{5,7},{6,4},{7,5},{8,10},{9,11},{10,... | collective-permute-start | bytes 3145736 | tf_op jit(solution)/shard_map/ppermute | solution.py:839
  98.3 100.5 %collective-permute-start.9 = (bf16[512,2048]{1,0:T(8,128)(2,1)}, bf16[512,2048]{1,0:T(8,128)(2,1)S(1)}, u32[]{:S(2)}, u32[]{:S(2)}) collective-permute-start(bf16[512,2048]{1,0:T(8,128)(2,1)} %stack.37.refs_5_.refs_1_), channel_id=1, source_target_pairs={{0,3},{1,2},{2,1},{3,0},{4,7},{5,6},{6,5},{7,4},{8,11},{9,10},{10,... | collective-permute-start | bytes 6291464 | tf_op jit(solution)/shard_map/ppermute | solution.py:839
  100.6 98.2 %collective-permute-start.8 = (bf16[512,2048]{1,0:T(8,128)(2,1)}, bf16[512,2048]{1,0:T(8,128)(2,1)}, u32[]{:S(2)}, u32[]{:S(2)}) collective-permute-start(bf16[512,2048]{1,0:T(8,128)(2,1)} %stack.37.refs_5_.refs_1_), channel_id=1, source_target_pairs={{0,2},{1,3},{2,0},{3,1},{4,6},{5,7},{6,4},{7,5},{8,10},{9,11},{10,... | collective-permute-start | bytes 6291464 | tf_op jit(solution)/shard_map/ppermute | solution.py:839
  101.1 97.7 %collective-permute-start.7 = (bf16[512,2048]{1,0:T(8,128)(2,1)}, bf16[512,2048]{1,0:T(8,128)(2,1)}, u32[]{:S(2)}, u32[]{:S(2)}) collective-permute-start(bf16[512,2048]{1,0:T(8,128)(2,1)} %stack.37.refs_5_.refs_1_), channel_id=1, source_target_pairs={{0,1},{1,0},{2,3},{3,2},{4,5},{5,4},{6,7},{7,6},{8,9},{9,8},{10,11... | collective-permute-start | bytes 6291464 | tf_op jit(solution)/shard_map/ppermute | solution.py:839
  225.8 241.4 %reduce-scatter.6.cloned.1.call-start = ((), (), s32[]{:S(2)}) async-start(), calls=%async_computation.6 | async-start | bytes 9437184 | tf_op jit(solution)/shard_map/reduce_scatter | solution.py:943
  279.5 133.3 %collective-permute-start.10 = (bf16[512,2048]{1,0:T(8,128)(2,1)}, bf16[512,2048]{1,0:T(8,128)(2,1)}, u32[]{:S(2)}, u32[]{:S(2)}) collective-permute-start(bf16[512,2048]{1,0:T(8,128)(2,1)} %get-tuple-element.68), channel_id=1, source_target_pairs={{0,3},{1,2},{2,1},{3,0},{4,7},{5,6},{6,5},{7,4},{8,11},{9,10},{10,... | collective-permute-start | bytes 6291464 | tf_op jit(solution)/shard_map/ppermute | solution.py:839
  281.9 131.5 %collective-permute-start.11 = (bf16[512,2048]{1,0:T(8,128)(2,1)}, bf16[512,2048]{1,0:T(8,128)(2,1)}, u32[]{:S(2)}, u32[]{:S(2)}) collective-permute-start(bf16[512,2048]{1,0:T(8,128)(2,1)} %get-tuple-element.69), channel_id=1, source_target_pairs={{0,2},{1,3},{2,0},{3,1},{4,6},{5,7},{6,4},{7,5},{8,10},{9,11},{10,... | collective-permute-start | bytes 6291464 | tf_op jit(solution)/shard_map/ppermute | solution.py:839
  282.6 133.2 %collective-permute-start.12 = (bf16[512,2048]{1,0:T(8,128)(2,1)}, bf16[512,2048]{1,0:T(8,128)(2,1)}, u32[]{:S(2)}, u32[]{:S(2)}) collective-permute-start(bf16[512,2048]{1,0:T(8,128)(2,1)} %get-tuple-element.70), channel_id=1, source_target_pairs={{0,1},{1,0},{2,3},{3,2},{4,5},{5,4},{6,7},{7,6},{8,9},{9,8},{10,11... | collective-permute-start | bytes 6291464 | tf_op jit(solution)/shard_map/ppermute | solution.py:839
  334.7 185.6 %reduce-scatter.8.cloned.1.call-start = ((), (), s32[]{:S(2)}) async-start(), calls=%async_computation.7 | async-start | bytes 9437184 | tf_op jit(solution)/shard_map/reduce_scatter | solution.py:974
  394.9 27.2 %collective-permute-start.15 = (f32[8,2048]{1,0:T(8,128)}, f32[8,2048]{1,0:T(8,128)}, u32[]{:S(2)}, u32[]{:S(2)}) collective-permute-start(f32[8,2048]{1,0:T(8,128)} %sums.1.refs_5_.refs_0_), channel_id=1, source_target_pairs={{0,1},{1,0},{2,3},{3,2},{4,5},{5,4},{6,7},{7,6},{8,9},{9,8},{10,11... | collective-permute-start | bytes 196616 | tf_op jit(solution)/shard_map/ppermute | solution.py:839
  396.4 25.7 %collective-permute-start.14 = (f32[8,2048]{1,0:T(8,128)}, f32[8,2048]{1,0:T(8,128)}, u32[]{:S(2)}, u32[]{:S(2)}) collective-permute-start(f32[8,2048]{1,0:T(8,128)} %sums.1.refs_5_.refs_0_), channel_id=1, source_target_pairs={{0,2},{1,3},{2,0},{3,1},{4,6},{5,7},{6,4},{7,5},{8,10},{9,11},{10,... | collective-permute-start | bytes 196616 | tf_op jit(solution)/shard_map/ppermute | solution.py:839
  413.5 57.1 %collective-permute-start.18 = (bf16[512,2048]{1,0:T(8,128)(2,1)}, bf16[512,2048]{1,0:T(8,128)(2,1)}, u32[]{:S(2)}, u32[]{:S(2)}) collective-permute-start(bf16[512,2048]{1,0:T(8,128)(2,1)} %back.3.refs_6_), channel_id=1, source_target_pairs={{0,3},{1,2},{2,1},{3,0},{4,7},{5,6},{6,5},{7,4},{8,11},{9,10},{10,... | collective-permute-start | bytes 6291464 | tf_op jit(solution)/shard_map/ppermute | solution.py:839
  450.6 56.2 %collective-permute-start.16 = (bf16[512,2048]{1,0:T(8,128)(2,1)}, bf16[512,2048]{1,0:T(8,128)(2,1)S(1)}, u32[]{:S(2)}, u32[]{:S(2)}) collective-permute-start(bf16[512,2048]{1,0:T(8,128)(2,1)} %get-tuple-element.84), channel_id=1, source_target_pairs={{0,2},{1,3},{2,0},{3,1},{4,6},{5,7},{6,4},{7,5},{8,10},{9,11},{10,... | collective-permute-start | bytes 6291464 | tf_op jit(solution)/shard_map/ppermute | solution.py:839
  451.4 56.9 %collective-permute-start.17 = (bf16[512,2048]{1,0:T(8,128)(2,1)}, bf16[512,2048]{1,0:T(8,128)(2,1)}, u32[]{:S(2)}, u32[]{:S(2)}) collective-permute-start(bf16[512,2048]{1,0:T(8,128)(2,1)} %get-tuple-element.85.refs_5_), channel_id=1, source_target_pairs={{0,1},{1,0},{2,3},{3,2},{4,5},{5,4},{6,7},{7,6},{8,9},{9,8},{10,11... | collective-permute-start | bytes 6291464 | tf_op jit(solution)/shard_map/ppermute | solution.py:839
  453.0 24.9 %collective-permute-start.20 = (f32[8,256]{1,0:T(8,128)S(1)}, f32[8,256]{1,0:T(8,128)S(1)}, u32[]{:S(2)}, u32[]{:S(2)}) collective-permute-start(f32[8,256]{1,0:T(8,128)S(1)} %copy-done.24), channel_id=1, source_target_pairs={{0,8},{4,12},{8,0},{12,4},{16,24},{20,28},{24,16},{28,20},{1,9},{5... | collective-permute-start | bytes 24584 | tf_op jit(solution)/shard_map/ppermute | solution.py:839
  470.6 48.0 %collective-permute-start.21 = (f32[8,256]{1,0:T(8,128)}, f32[8,256]{1,0:T(8,128)}, u32[]{:S(2)}, u32[]{:S(2)}) collective-permute-start(f32[8,256]{1,0:T(8,128)} %get-tuple-element.89), channel_id=1, source_target_pairs={{0,12},{4,8},{8,4},{12,0},{16,28},{20,24},{24,20},{28,16},{1,13},{... | collective-permute-start | bytes 24584 | tf_op jit(solution)/shard_map/ppermute | solution.py:839
  476.8 41.8 %collective-permute-start.22 = (f32[8,256]{1,0:T(8,128)}, f32[8,256]{1,0:T(8,128)}, u32[]{:S(2)}, u32[]{:S(2)}) collective-permute-start(f32[8,256]{1,0:T(8,128)} %get-tuple-element.90), channel_id=1, source_target_pairs={{0,16},{4,20},{8,24},{12,28},{16,0},{20,4},{24,8},{28,12},{1,17},{... | collective-permute-start | bytes 24584 | tf_op jit(solution)/shard_map/ppermute | solution.py:839
  477.9 40.6 %collective-permute-start.23 = (f32[8,256]{1,0:T(8,128)}, f32[8,256]{1,0:T(8,128)}, u32[]{:S(2)}, u32[]{:S(2)}) collective-permute-start(f32[8,256]{1,0:T(8,128)} %get-tuple-element.91), channel_id=1, source_target_pairs={{0,20},{4,16},{8,28},{12,24},{16,4},{20,0},{24,12},{28,8},{1,21},{... | collective-permute-start | bytes 24584 | tf_op jit(solution)/shard_map/ppermute | solution.py:839
  (34 other events, 396.4 us)
Sparse Core Ops, SparseCore 0:
  10.2 137.9 all-gather.2
  150.4 98.3 all-gather.4
  251.1 87.7 reduce-scatter.3
  341.1 87.9 reduce-scatter.5
  431.2 88.9 reduce-scatter.7

commit v9 on v8

--- a/solution.py
+++ b/solution.py
@@ -729,6 +729,7 @@
     count = rows.shape[0]
     one, two = widths
     each = one // heads
+    unit = tile_of(count, 128)
 
     def kernel(ids_ref, in_ref, v_ref, *refs):
         one_ref, two_ref, *sum_refs = refs[len(parts) :]
@@ -753,9 +754,14 @@
     return call(
         kernel,
         ids,
-        (1,),
-        [whole(array.shape) for array in (rows, scales, *parts)],
-        [whole(shape) for shape in shapes],
+        (count // unit,),
+        [pl.BlockSpec((unit, rows.shape[1]), lambda i, ids: (i, 0))]
+        + [whole(array.shape) for array in (scales, *parts)],
+        [
+            pl.BlockSpec((unit, heads, each), lambda i, ids: (i, 0, 0)),
+            pl.BlockSpec((two, unit), lambda i, ids: (0, i)),
+        ]
+        + [whole(shape) for shape in shapes[2:]],
         [jax.ShapeDtypeStruct(shape, F32) for shape in shapes],
         (rows, scales, *parts),
         after=after,

time: 538 us -> 537 us (level)
  no operation moved by 1% of the time
where the time goes in v9:
time: 537 us; the launch traced here: 530 us
  Pallas kernels  349 us (65%)
  waiting for transfers between devices  111 us (21%)
  starting transfers between devices  33.2 us (6%)
  between operations  14.6 us (3%)
  local copies, waits for them, and re-layouts  11.5 us (2%)
  other arithmetic  11.4 us (2%)
    pallas_call x27, Pallas kernels, call(): pl.pallas_call(run, grid_spec=pltpu.PrefetchScalarGridSpec(num_scalar_pre...  349 us
    ppermute x26, waiting for transfers between devices, flip(): return lax.ppermute(value, axis, [(i, i ^ bit) for i in range(size)])  70.3 us
    all_gather x1, waiting for transfers between devices, body(): lax.all_gather(jnp.concatenate([expand, own_project], axis=1), 'dp', axis...  38.8 us
    ppermute x26, starting transfers between devices, flip(): return lax.ppermute(value, axis, [(i, i ^ bit) for i in range(size)])  33 us
  transfers between devices with their start and end apart: 31, of which 8 were waited for; matrix products, arithmetic and copies ran while one was open for 3% of the time, Pallas kernels for 65%

profile of v9, /device:TPU:0, one launch (start us, length us, event | category | flops | bytes accessed | tf_op | source)
XLA Modules:
  0.0 530.4 jit_solution(5100810958113056121)
XLA Ops:
  35.1 27.1 %collective-permute-done.3.refs_0_.refs_2_ = bf16[512,2048]{1,0:T(8,128)(2,1)} collective-permute-done((bf16[512,2048]{1,0:T(8,128)(2,1)}, bf16[512,2048]{1,0:T(8,128)(2,1)}, u32[]{:S(2)}, u32[]{:S(2)}) %collective-permute-start.3) | collective-permute-done | bytes 2097184 | tf_op jit(solution)/shard_map/ppermute | solution.py:845
  71.4 12.0 %norm.2 = (bf16[2048,2048]{1,0:T(8,128)(2,1)}, bf16[2048,2048]{1,0:T(8,128)(2,1)}) custom-call(s32[2]{0:T(128)} %pad_add_fusion.ids_ref, bf16[512,2048]{1,0:T(8,128)(2,1)} %refs_0_.7, bf16[512,2048]{1,0:T(8,128)(2,1)} %copy-done, bf16[512,2048]{1,0:T(8,128)(2,1)} %collective-permute-done.3.refs_0_.refs_2_, f32[6,2048]{1,0:T(8,128)} %bitcast.36), custom_call_target="tpu_custom_call" | custom-call | flops 50000000 | tf_op jit(solution)/shard_map/norm/pallas_call | solution.py:49
  83.4 5.6 %collective-permute-done.4.refs_2_.refs_0_ = bf16[256,2048]{1,0:T(8,128)(2,1)S(1)} collective-permute-done((bf16[256,2048]{1,0:T(8,128)(2,1)}, bf16[256,2048]{1,0:T(8,128)(2,1)S(1)}, u32[]{:S(2)}, u32[]{:S(2)}) %collective-permute-start.4) | collective-permute-done | bytes 1048608 | tf_op jit(solution)/shard_map/ppermute | solution.py:845
  89.0 4.7 collective-permute-done.6.refs_3_.refs_1_
  103.2 6.3 %norm.3 = (bf16[2048,2048]{1,0:T(8,128)(2,1)}, bf16[2048,2048]{1,0:T(8,128)(2,1)}) custom-call(s32[2]{0:T(128)} %pad_add_fusion.ids_ref, bf16[256,2048]{1,0:T(8,128)(2,1)} %copy-done.2, bf16[256,2048]{1,0:T(8,128)(2,1)} %copy-done.3, f32[6,2048]{1,0:T(8,128)} %bitcast.37, ...), custom_call_target="tpu_custom_call", output_to_operand_aliasing={{0}: (4, {}), {1}: (5, {})} | custom-call | flops 50000000 | tf_op jit(solution)/shard_map/norm/pallas_call | solution.py:49
  109.5 38.8 %all-gather.3.cloned.1.call-done.refs_1_.refs_2_.refs_3_ = bf16[2048,3584]{1,0:T(8,128)(2,1)} async-done(((bf16[256,3584]{1,0:T(8,128)(2,1)}), bf16[2048,3584]{1,0:T(8,128)(2,1)}) %all-gather.3.cloned.1.call-update) | async-done | bytes 14680080 | tf_op jit(solution)/shard_map/all_gather | solution.py:927
  148.3 30.3 %expand.1 = (bf16[2048,2048]{1,0:T(8,128)(2,1)}, bf16[2048,2048]{1,0:T(8,128)(2,1)}) custom-call(s32[2]{0:T(128)} %pad_add_fusion.ids_ref, bf16[2048,2048]{1,0:T(8,128)(2,1)} %get-tuple-element.62.refs_0_, bf16[2048,3584]{1,0:T(8,128)(2,1)} %all-gather.3.cloned.1.call-done.refs_1_.refs_2_.refs_3_, f32[1,2048]{1,0:T(1,128)} %bitcast.43), custom_call_target="tpu_custom_call" | custom-call | flops 50000000 | tf_op jit(solution)/shard_map/expand/pallas_call | solution.py:49
  178.6 20.2 %mixed.1.refs_5_.refs_0_ = bf16[2048,1536]{1,0:T(8,128)(2,1)} custom-call(s32[2]{0:T(128)} %pad_add_fusion.ids_ref, bf16[2048,2048]{1,0:T(8,128)(2,1)} %get-tuple-element.61.refs_0_, bf16[2048,3584]{1,0:T(8,128)(2,1)} %all-gather.3.cloned.1.call-done.refs_1_.refs_2_.refs_3_, f32[1,1536]{1,0:T(1,128)} %reshape.85.refs_2_, ...), custom_call_target="tpu_custom_call" | custom-call | flops 50000000 | tf_op jit(solution)/shard_map/mixed/pallas_call | solution.py:49
  200.1 25.7 %piece_grad.1 = (bf16[2048,2048]{1,0:T(8,128)(2,1)}, bf16[2048,2048]{1,0:T(8,128)(2,1)}) custom-call(s32[2]{0:T(128)} %pad_add_fusion.ids_ref, bf16[2048,2048]{1,0:T(8,128)(2,1)} %get-tuple-element.63.refs_5_.refs_0_.refs_2_, bf16[512,2048]{1,0:T(8,128)(2,1)} %stack.37.refs_5_.refs_1_, bf16[512,2048]{1,0:T(8,128)(2,1)} %collective-permute-done.7.refs_2_, ...), custom_call_target="tpu_custom_call" | custom-call | flops 50000000 | tf_op jit(solution)/shard_map/piece_grad/pallas_call | solution.py:49
  225.9 14.5 %attend.1 = (bf16[2048,512]{1,0:T(8,128)(2,1)}, f32[2,4,8,512]{3,2,1,0:T(8,128)}) custom-call(s32[2]{0:T(128)} %pad_add_fusion.ids_ref, bf16[2048,1536]{1,0:T(8,128)(2,1)} %mixed.1.refs_5_.refs_0_, bf16[2048,2048]{1,0:T(8,128)(2,1)} %get-tuple-element.64.refs_1_), custom_call_target="tpu_custom_call" | custom-call | flops 50000000 | tf_op jit(solution)/shard_map/attend/pallas_call | solution.py:49
  240.4 9.5 %full_grad.3.refs_4_ = bf16[2048,2048]{1,0:T(8,128)(2,1)} custom-call(s32[2]{0:T(128)} %pad_add_fusion.ids_ref, bf16[2048,2048]{1,0:T(8,128)(2,1)} %get-tuple-element.66.refs_0_, bf16[2048,512]{1,0:T(8,128)(2,1)} %get-tuple-element.65.refs_1_.refs_0_.refs_2_), custom_call_target="tpu_custom_call" | custom-call | flops 50000000 | tf_op jit(solution)/shard_map/full_grad/pallas_call | solution.py:49
  249.9 29.6 %branches.1 = (bf16[512,2048]{1,0:T(8,128)(2,1)}, bf16[512,2048]{1,0:T(8,128)(2,1)}, bf16[512,2048]{1,0:T(8,128)(2,1)}, bf16[512,2048]{1,0:T(8,128)(2,1)}) custom-call(s32[2]{0:T(128)} %pad_add_fusion.ids_ref, bf16[2048,512]{1,0:T(8,128)(2,1)} %get-tuple-element.65.refs_1_.refs_0_.refs_2_, bf16[2560,2048]{1,0:T(8,128)(2,1)} %all-gather.5.cloned.1.call-done.refs_1_.refs_3_, ...), custom_call_target="tpu_custom_call" | custom-call | flops 50000000 | tf_op jit(solution)/shard_map/branches/pallas_call | solution.py:49
  283.0 25.3 %shrink_back.1 = (bf16[2048,2048]{1,0:T(8,128)(2,1)}, f32[1,2048]{1,0:T(1,128)}) custom-call(s32[2]{0:T(128)} %pad_add_fusion.ids_ref, bf16[2048,2048]{1,0:T(8,128)(2,1)} %get-tuple-element.66.refs_0_, bf16[2560,2048]{1,0:T(8,128)(2,1)} %all-gather.5.cloned.1.call-done.refs_1_.refs_3_, bf16[2048,2048]{1,0:T(8,128)(2,1)} %get-tuple-element.71.refs_2_, ...), custom_call_target="tpu_custom_call" | custom-call | flops 50000000 | tf_op jit(solution)/shard_map/shrink_back/pallas_call | solution.py:49
  308.3 26.3 %full_grad.4 = (bf16[2048,2048]{1,0:T(8,128)(2,1)}, f32[2048,128]{1,0:T(8,128)}, f32[2048,128]{1,0:T(8,128)}) custom-call(s32[2]{0:T(128)} %pad_add_fusion.ids_ref, bf16[2048,2048]{1,0:T(8,128)(2,1)} %get-tuple-element.62.refs_0_, bf16[2048,2048]{1,0:T(8,128)(2,1)} %get-tuple-element.72.refs_1_.refs_2_, ...), custom_call_target="tpu_custom_call" | custom-call | flops 50000000 | tf_op jit(solution)/shard_map/full_grad/pallas_call | solution.py:49
  337.9 9.3 %plain.1.refs_1_ = bf16[2048,512]{1,0:T(8,128)(2,1)} custom-call(s32[2]{0:T(128)} %pad_add_fusion.ids_ref, bf16[2048,2048]{1,0:T(8,128)(2,1)} %get-tuple-element.66.refs_0_, bf16[2560,2048]{1,0:T(8,128)(2,1)} %all-gather.5.cloned.1.call-done.refs_1_.refs_3_, bf16[2048,2048]{1,0:T(8,128)(2,1)} %get-tuple-element.74.refs_2_), custom_call_target="tpu_custom_call" | custom-call | flops 50000000 | tf_op jit(solution)/shard_map/plain/pallas_call | solution.py:49
  347.2 22.7 %attend_back.1 = (bf16[2048,1536]{1,0:T(8,128)(2,1)}, f32[1,1536]{1,0:T(1,128)}) custom-call(s32[2]{0:T(128)} %pad_add_fusion.ids_ref, bf16[2048,1536]{1,0:T(8,128)(2,1)} %mixed.1.refs_5_.refs_0_, bf16[2048,512]{1,0:T(8,128)(2,1)} %plain.1.refs_1_, bf16[2048,512]{1,0:T(8,128)(2,1)} %get-tuple-element.65.refs_1_.refs_0_.refs_2_, ...), custom_call_target="tpu_custom_call" | custom-call | flops 50000000 | tf_op jit(solution)/shard_map/attend_back/pallas_call | solution.py:49
  369.9 20.2 %full_grad.5 = (bf16[2048,2048]{1,0:T(8,128)(2,1)}, f32[2048,128]{1,0:T(8,128)}, f32[2048,128]{1,0:T(8,128)}) custom-call(s32[2]{0:T(128)} %pad_add_fusion.ids_ref, bf16[2048,2048]{1,0:T(8,128)(2,1)} %get-tuple-element.61.refs_0_, bf16[2048,1536]{1,0:T(8,128)(2,1)} %get-tuple-element.76.refs_1_.refs_0_, ...), custom_call_target="tpu_custom_call", output_to_operand_aliasing={{0}: (5, {})} | custom-call | flops 50000000 | tf_op jit(solution)/shard_map/full_grad/pallas_call | solution.py:49
  390.1 4.8 sums.1.refs_5_.refs_0_
  398.1 14.1 %back.3.refs_6_ = bf16[512,2048]{1,0:T(8,128)(2,1)} custom-call(s32[2]{0:T(128)} %pad_add_fusion.ids_ref, bf16[2048,1536]{1,0:T(8,128)(2,1)} %get-tuple-element.76.refs_1_.refs_0_, bf16[2048,3584]{1,0:T(8,128)(2,1)} %all-gather.3.cloned.1.call-done.refs_1_.refs_2_.refs_3_, bf16[2048,2048]{1,0:T(8,128)(2,1)} %get-tuple-element.72.refs_1_.refs_2_, ...), custom_call_target="tpu_custom_call" | custom-call | flops 50000000 | tf_op jit(solution)/shard_map/back/pallas_call | solution.py:49
  415.7 6.4 %output.1.refs_6_ = bf16[512,2048]{1,0:T(8,128)(2,1)} custom-call(s32[2]{0:T(128)} %pad_add_fusion.ids_ref, bf16[512,2048]{1,0:T(8,128)(2,1)} %refs_0_.7, f32[6,2048]{1,0:T(8,128)} %bitcast.38, bf16[512,2048]{1,0:T(8,128)(2,1)} %get-tuple-element.67.refs_3_.refs_2_, bf16[512,2048]{1,0:T(8,128)(2,1)} %collective-permute-done.10.refs_3_, ...), custom_call_target="tpu_custom_call" | custom-call | flops 160000000000 | tf_op jit(solution)/shard_map/output/pallas_call | solution.py:49
  427.9 22.7 %back.4 = (bf16[512,2048]{1,0:T(8,128)(2,1)}, bf16[512,2048]{1,0:T(8,128)(2,1)}) custom-call(s32[2]{0:T(128)} %pad_add_fusion.ids_ref, bf16[2048,1536]{1,0:T(8,128)(2,1)} %get-tuple-element.76.refs_1_.refs_0_, bf16[2048,3584]{1,0:T(8,128)(2,1)} %all-gather.3.cloned.1.call-done.refs_1_.refs_2_.refs_3_, bf16[2048,2048]{1,0:T(8,128)(2,1)} %get-tuple-element.72.refs_1_.refs_2_, ...), custom_call_target="tpu_custom_call" | custom-call | flops 50000000 | tf_op jit(solution)/shard_map/back/pallas_call | solution.py:49
  453.1 14.1 %back.5.refs_1_ = bf16[512,2048]{1,0:T(8,128)(2,1)} custom-call(s32[2]{0:T(128)} %pad_add_fusion.ids_ref, bf16[2048,1536]{1,0:T(8,128)(2,1)} %get-tuple-element.76.refs_1_.refs_0_, bf16[2048,3584]{1,0:T(8,128)(2,1)} %all-gather.3.cloned.1.call-done.refs_1_.refs_2_.refs_3_, bf16[2048,2048]{1,0:T(8,128)(2,1)} %get-tuple-element.72.refs_1_.refs_2_, ...), custom_call_target="tpu_custom_call" | custom-call | flops 50000000 | tf_op jit(solution)/shard_map/back/pallas_call | solution.py:49
  479.4 27.4 %collective-permute-done.16.refs_2_ = bf16[512,2048]{1,0:T(8,128)(2,1)S(1)} collective-permute-done((bf16[512,2048]{1,0:T(8,128)(2,1)}, bf16[512,2048]{1,0:T(8,128)(2,1)S(1)}, u32[]{:S(2)}, u32[]{:S(2)}) %collective-permute-start.16) | collective-permute-done | bytes 2097184 | tf_op jit(solution)/shard_map/ppermute | solution.py:845
  510.1 8.4 %input.1.refs_10_ = f32[512,2048]{1,0:T(8,128)} custom-call(s32[2]{0:T(128)} %pad_add_fusion.ids_ref, bf16[512,2048]{1,0:T(8,128)(2,1)} %refs_0_.7, bf16[512,2048]{1,0:T(8,128)(2,1)} %refs_1_.1, bf16[512,2048]{1,0:T(8,128)(2,1)} %copy-done.23, bf16[512,2048]{1,0:T(8,128)(2,1)} %collective-permute-done.17.refs_3_, f32[512,2048]{1,0:T(8,128)} %total.1.refs_4_), custom_call_target="tpu_custom_call" | custom-call | flops 153999998976 | tf_op jit(solution)/shard_map/input/pallas_call | solution.py:49
  (174 shorter events, 89.8 us)
Async XLA Ops:
  7.2 141.1 %all-gather.3.cloned.1.call-start = ((), (), s32[]{:S(2)}) async-start(), calls=%async_computation.3 | async-start | bytes 16515072 | tf_op jit(solution)/shard_map/all_gather | solution.py:927
  10.1 239.8 %all-gather.5.cloned.1.call-start = ((), (), s32[]{:S(2)}) async-start(), calls=%async_computation.4 | async-start | bytes 11796480 | tf_op jit(solution)/shard_map/all_gather | solution.py:928
  11.7 412.8 %reduce-scatter.4.cloned.1.call-start = ((), (), s32[]{:S(2)}) async-start(), calls=%async_computation.5 | async-start | bytes 9437184 | tf_op jit(solution)/shard_map/reduce_scatter | solution.py:940
  11.7 53.7 %collective-permute-start.5 = (bf16[512,2048]{1,0:T(8,128)(2,1)}, bf16[512,2048]{1,0:T(8,128)(2,1)S(1)}, u32[]{:S(2)}, u32[]{:S(2)}) collective-permute-start(bf16[512,2048]{1,0:T(8,128)(2,1)} %refs_0_.7), channel_id=1, source_target_pairs={{0,1},{1,0},{2,3},{3,2},{4,5},{5,4},{6,7},{7,6},{8,9},{9,8},{10,11... | collective-permute-start | bytes 6291464 | tf_op jit(solution)/shard_map/ppermute | solution.py:845
  14.7 47.4 %collective-permute-start.3 = (bf16[512,2048]{1,0:T(8,128)(2,1)}, bf16[512,2048]{1,0:T(8,128)(2,1)}, u32[]{:S(2)}, u32[]{:S(2)}) collective-permute-start(bf16[512,2048]{1,0:T(8,128)(2,1)} %refs_0_.7), channel_id=1, source_target_pairs={{0,2},{1,3},{2,0},{3,1},{4,6},{5,7},{6,4},{7,5},{8,10},{9,11},{10,... | collective-permute-start | bytes 6291464 | tf_op jit(solution)/shard_map/ppermute | solution.py:845
  65.1 23.9 %collective-permute-start.4 = (bf16[256,2048]{1,0:T(8,128)(2,1)}, bf16[256,2048]{1,0:T(8,128)(2,1)S(1)}, u32[]{:S(2)}, u32[]{:S(2)}) collective-permute-start(bf16[256,2048]{1,0:T(8,128)(2,1)} %half.2), channel_id=1, source_target_pairs={{0,1},{1,0},{2,3},{3,2},{4,5},{5,4},{6,7},{7,6},{8,9},{9,8},{10,11... | collective-permute-start | bytes 3145736 | tf_op jit(solution)/shard_map/ppermute | solution.py:845
  69.7 24.0 %collective-permute-start.6 = (bf16[256,2048]{1,0:T(8,128)(2,1)}, bf16[256,2048]{1,0:T(8,128)(2,1)S(1)}, u32[]{:S(2)}, u32[]{:S(2)}) collective-permute-start(bf16[256,2048]{1,0:T(8,128)(2,1)} %half.3), channel_id=1, source_target_pairs={{0,2},{1,3},{2,0},{3,1},{4,6},{5,7},{6,4},{7,5},{8,10},{9,11},{10,... | collective-permute-start | bytes 3145736 | tf_op jit(solution)/shard_map/ppermute | solution.py:845
  98.3 100.5 %collective-permute-start.9 = (bf16[512,2048]{1,0:T(8,128)(2,1)}, bf16[512,2048]{1,0:T(8,128)(2,1)S(1)}, u32[]{:S(2)}, u32[]{:S(2)}) collective-permute-start(bf16[512,2048]{1,0:T(8,128)(2,1)} %stack.37.refs_5_.refs_1_), channel_id=1, source_target_pairs={{0,3},{1,2},{2,1},{3,0},{4,7},{5,6},{6,5},{7,4},{8,11},{9,10},{10,... | collective-permute-start | bytes 6291464 | tf_op jit(solution)/shard_map/ppermute | solution.py:845
  100.6 98.2 %collective-permute-start.8 = (bf16[512,2048]{1,0:T(8,128)(2,1)}, bf16[512,2048]{1,0:T(8,128)(2,1)}, u32[]{:S(2)}, u32[]{:S(2)}) collective-permute-start(bf16[512,2048]{1,0:T(8,128)(2,1)} %stack.37.refs_5_.refs_1_), channel_id=1, source_target_pairs={{0,2},{1,3},{2,0},{3,1},{4,6},{5,7},{6,4},{7,5},{8,10},{9,11},{10,... | collective-permute-start | bytes 6291464 | tf_op jit(solution)/shard_map/ppermute | solution.py:845
  101.1 97.7 %collective-permute-start.7 = (bf16[512,2048]{1,0:T(8,128)(2,1)}, bf16[512,2048]{1,0:T(8,128)(2,1)}, u32[]{:S(2)}, u32[]{:S(2)}) collective-permute-start(bf16[512,2048]{1,0:T(8,128)(2,1)} %stack.37.refs_5_.refs_1_), channel_id=1, source_target_pairs={{0,1},{1,0},{2,3},{3,2},{4,5},{5,4},{6,7},{7,6},{8,9},{9,8},{10,11... | collective-permute-start | bytes 6291464 | tf_op jit(solution)/shard_map/ppermute | solution.py:845
  225.8 241.4 %reduce-scatter.6.cloned.1.call-start = ((), (), s32[]{:S(2)}) async-start(), calls=%async_computation.6 | async-start | bytes 9437184 | tf_op jit(solution)/shard_map/reduce_scatter | solution.py:949
  279.5 133.3 %collective-permute-start.10 = (bf16[512,2048]{1,0:T(8,128)(2,1)}, bf16[512,2048]{1,0:T(8,128)(2,1)}, u32[]{:S(2)}, u32[]{:S(2)}) collective-permute-start(bf16[512,2048]{1,0:T(8,128)(2,1)} %get-tuple-element.68), channel_id=1, source_target_pairs={{0,3},{1,2},{2,1},{3,0},{4,7},{5,6},{6,5},{7,4},{8,11},{9,10},{10,... | collective-permute-start | bytes 6291464 | tf_op jit(solution)/shard_map/ppermute | solution.py:845
  281.9 131.5 %collective-permute-start.11 = (bf16[512,2048]{1,0:T(8,128)(2,1)}, bf16[512,2048]{1,0:T(8,128)(2,1)}, u32[]{:S(2)}, u32[]{:S(2)}) collective-permute-start(bf16[512,2048]{1,0:T(8,128)(2,1)} %get-tuple-element.69), channel_id=1, source_target_pairs={{0,2},{1,3},{2,0},{3,1},{4,6},{5,7},{6,4},{7,5},{8,10},{9,11},{10,... | collective-permute-start | bytes 6291464 | tf_op jit(solution)/shard_map/ppermute | solution.py:845
  282.6 133.2 %collective-permute-start.12 = (bf16[512,2048]{1,0:T(8,128)(2,1)}, bf16[512,2048]{1,0:T(8,128)(2,1)}, u32[]{:S(2)}, u32[]{:S(2)}) collective-permute-start(bf16[512,2048]{1,0:T(8,128)(2,1)} %get-tuple-element.70), channel_id=1, source_target_pairs={{0,1},{1,0},{2,3},{3,2},{4,5},{5,4},{6,7},{7,6},{8,9},{9,8},{10,11... | collective-permute-start | bytes 6291464 | tf_op jit(solution)/shard_map/ppermute | solution.py:845
  334.7 185.6 %reduce-scatter.8.cloned.1.call-start = ((), (), s32[]{:S(2)}) async-start(), calls=%async_computation.7 | async-start | bytes 9437184 | tf_op jit(solution)/shard_map/reduce_scatter | solution.py:980
  394.9 27.2 %collective-permute-start.15 = (f32[8,2048]{1,0:T(8,128)}, f32[8,2048]{1,0:T(8,128)}, u32[]{:S(2)}, u32[]{:S(2)}) collective-permute-start(f32[8,2048]{1,0:T(8,128)} %sums.1.refs_5_.refs_0_), channel_id=1, source_target_pairs={{0,1},{1,0},{2,3},{3,2},{4,5},{5,4},{6,7},{7,6},{8,9},{9,8},{10,11... | collective-permute-start | bytes 196616 | tf_op jit(solution)/shard_map/ppermute | solution.py:845
  396.4 25.7 %collective-permute-start.14 = (f32[8,2048]{1,0:T(8,128)}, f32[8,2048]{1,0:T(8,128)}, u32[]{:S(2)}, u32[]{:S(2)}) collective-permute-start(f32[8,2048]{1,0:T(8,128)} %sums.1.refs_5_.refs_0_), channel_id=1, source_target_pairs={{0,2},{1,3},{2,0},{3,1},{4,6},{5,7},{6,4},{7,5},{8,10},{9,11},{10,... | collective-permute-start | bytes 196616 | tf_op jit(solution)/shard_map/ppermute | solution.py:845
  413.5 57.1 %collective-permute-start.18 = (bf16[512,2048]{1,0:T(8,128)(2,1)}, bf16[512,2048]{1,0:T(8,128)(2,1)}, u32[]{:S(2)}, u32[]{:S(2)}) collective-permute-start(bf16[512,2048]{1,0:T(8,128)(2,1)} %back.3.refs_6_), channel_id=1, source_target_pairs={{0,3},{1,2},{2,1},{3,0},{4,7},{5,6},{6,5},{7,4},{8,11},{9,10},{10,... | collective-permute-start | bytes 6291464 | tf_op jit(solution)/shard_map/ppermute | solution.py:845
  450.6 56.2 %collective-permute-start.16 = (bf16[512,2048]{1,0:T(8,128)(2,1)}, bf16[512,2048]{1,0:T(8,128)(2,1)S(1)}, u32[]{:S(2)}, u32[]{:S(2)}) collective-permute-start(bf16[512,2048]{1,0:T(8,128)(2,1)} %get-tuple-element.84), channel_id=1, source_target_pairs={{0,2},{1,3},{2,0},{3,1},{4,6},{5,7},{6,4},{7,5},{8,10},{9,11},{10,... | collective-permute-start | bytes 6291464 | tf_op jit(solution)/shard_map/ppermute | solution.py:845
  451.4 56.9 %collective-permute-start.17 = (bf16[512,2048]{1,0:T(8,128)(2,1)}, bf16[512,2048]{1,0:T(8,128)(2,1)}, u32[]{:S(2)}, u32[]{:S(2)}) collective-permute-start(bf16[512,2048]{1,0:T(8,128)(2,1)} %get-tuple-element.85.refs_5_), channel_id=1, source_target_pairs={{0,1},{1,0},{2,3},{3,2},{4,5},{5,4},{6,7},{7,6},{8,9},{9,8},{10,11... | collective-permute-start | bytes 6291464 | tf_op jit(solution)/shard_map/ppermute | solution.py:845
  453.0 24.9 %collective-permute-start.20 = (f32[8,256]{1,0:T(8,128)S(1)}, f32[8,256]{1,0:T(8,128)S(1)}, u32[]{:S(2)}, u32[]{:S(2)}) collective-permute-start(f32[8,256]{1,0:T(8,128)S(1)} %copy-done.24), channel_id=1, source_target_pairs={{0,8},{4,12},{8,0},{12,4},{16,24},{20,28},{24,16},{28,20},{1,9},{5... | collective-permute-start | bytes 24584 | tf_op jit(solution)/shard_map/ppermute | solution.py:845
  470.6 48.0 %collective-permute-start.21 = (f32[8,256]{1,0:T(8,128)}, f32[8,256]{1,0:T(8,128)}, u32[]{:S(2)}, u32[]{:S(2)}) collective-permute-start(f32[8,256]{1,0:T(8,128)} %get-tuple-element.89), channel_id=1, source_target_pairs={{0,12},{4,8},{8,4},{12,0},{16,28},{20,24},{24,20},{28,16},{1,13},{... | collective-permute-start | bytes 24584 | tf_op jit(solution)/shard_map/ppermute | solution.py:845
  476.8 41.8 %collective-permute-start.22 = (f32[8,256]{1,0:T(8,128)}, f32[8,256]{1,0:T(8,128)}, u32[]{:S(2)}, u32[]{:S(2)}) collective-permute-start(f32[8,256]{1,0:T(8,128)} %get-tuple-element.90), channel_id=1, source_target_pairs={{0,16},{4,20},{8,24},{12,28},{16,0},{20,4},{24,8},{28,12},{1,17},{... | collective-permute-start | bytes 24584 | tf_op jit(solution)/shard_map/ppermute | solution.py:845
  477.9 40.6 %collective-permute-start.23 = (f32[8,256]{1,0:T(8,128)}, f32[8,256]{1,0:T(8,128)}, u32[]{:S(2)}, u32[]{:S(2)}) collective-permute-start(f32[8,256]{1,0:T(8,128)} %get-tuple-element.91), channel_id=1, source_target_pairs={{0,20},{4,16},{8,28},{12,24},{16,4},{20,0},{24,12},{28,8},{1,21},{... | collective-permute-start | bytes 24584 | tf_op jit(solution)/shard_map/ppermute | solution.py:845
  (34 other events, 396.4 us)
Sparse Core Ops, SparseCore 0:
  10.2 137.9 all-gather.2
  150.4 98.3 all-gather.4
  251.1 87.7 reduce-scatter.3
  341.1 87.9 reduce-scatter.5
  431.2 88.9 reduce-scatter.7
